TPU v7x, 32 devices: a whole 2x2x4 slice. The times are simulated.
32 devices in a mesh: dp: 4 (over y, core), seq: 8 (over z, x).
Axes of the slice: x: 2, y: 2, z: 4, core: 2. Of those that a mesh axis runs over, the one named last changes fastest.
Arguments:
- hidden: bfloat16 [4, 2048, 2048], P('dp', 'seq'), may hold values from -6 to 6
- targets: int32 [4, 2048], P('dp'), may hold values from 0 to 26623
- lengths: int32 [4, 8], P('dp'), may hold values from 1 to 1024, 2048 in all within a row
- labels: int32 [4, 8], P('dp'), may hold values 0 or 1
- ref_logps: float32 [4, 8], P('dp'), may hold values from -26 to -1
- ln1_gain: bfloat16 [2048], replicated, may hold values from 0.5 to 1.5
- ln1_bias: bfloat16 [2048], replicated, may hold values from -1.796875 to 1.796875
- ln2_gain: bfloat16 [2048], replicated, may hold values from 0.5 to 1.5
- ln2_bias: bfloat16 [2048], replicated, may hold values from -1.796875 to 1.796875
- qkv_weight: bfloat16 [2048, 16, 384], P(None, 'seq'), may hold values from -0.125 to 0.125
- qv_bias: bfloat16 [16, 256], P('seq'), may hold values from -1.796875 to 1.796875
- out_weight: bfloat16 [16, 128, 2048], P('seq'), may hold values from -0.5 to 0.5
- up_weight: bfloat16 [2048, 8192], P(None, 'seq'), may hold values from -0.125 to 0.125
- up_bias: bfloat16 [8192], P('seq'), may hold values from -1.796875 to 1.796875
- down_weight: bfloat16 [8192, 2048], P('seq'), may hold values from -0.0625 to 0.0625
- branch_bias: bfloat16 [2048], replicated, may hold values from -1.796875 to 1.796875
- lnf_gain: bfloat16 [2048], replicated, may hold values from 0.5 to 1.5
- lnf_bias: bfloat16 [2048], replicated, may hold values from -1.796875 to 1.796875
- head_weight: bfloat16 [2048, 26624], P(None, 'seq'), may hold values from -0.25 to 0.25
Outputs:
- losses: float32 [4, 8], P('dp')
- output: bfloat16 [4, 2048, 2048], P('dp', 'seq')
- grad_hidden: float32 [4, 2048, 2048], P('dp', 'seq')
- grad_ln1_gain: float32 [2048], replicated
- grad_ln1_bias: float32 [2048], replicated
- grad_ln2_gain: float32 [2048], replicated
- grad_ln2_bias: float32 [2048], replicated
- grad_qkv_weight: float32 [2048, 16, 384], P(None, 'seq')
- grad_qv_bias: float32 [16, 256], P('seq')
- grad_out_weight: float32 [16, 128, 2048], P('seq')
- grad_up_weight: float32 [2048, 8192], P(None, 'seq')
- grad_up_bias: float32 [8192], P('seq')
- grad_down_weight: float32 [8192, 2048], P('seq')
- grad_branch_bias: float32 [2048], replicated
- grad_lnf_gain: float32 [2048], replicated
- grad_lnf_bias: float32 [2048], replicated
- grad_head_weight: float32 [2048, 26624], P(None, 'seq')
Inputs may be any that keep to these rules, and one draw needn't show every extreme that they name: Each block's lengths sum to 2048; the longest example of every block has exactly 1024 rows. `labels`: 1 marks a desirable example, 0 an undesirable one.
All inputs are finite; a program needn't handle non-finite values. No bound on the sum of `labels` on one device may be relied on, other than what follows from the above.
Results may differ from a plain program's by a relative error of at most 0.018.
Values may be sent and summed in bfloat16 or wider, within the bound.
A program may use at most 256 MiB of HBM per device.

v0:
```python
import jax
import jax.numpy as jnp
from jax import lax
from jax.sharding import PartitionSpec as P

D = 2048
HEAD_DIM = 128
ROT = 32
BLOCK = 2048
EXB = 8
ATT_BLK = 512


EPSILON = 1e-05
BETA = 0.25
LOSS_SCALE = 65536.0


def joined(value, axis, join):
    pieces = jax.tree.map(lambda part: lax.all_gather(part, axis), value)
    head = jax.tree.map(lambda part: part[0], pieces)
    tail = jax.tree.map(lambda part: part[1:], pieces)
    so_far, _ = lax.scan(lambda so_far, piece: (join(so_far, piece), None), head, tail)
    return so_far


def norm_parts(values, norm_gain, norm_shift):
    centered = values - jnp.mean(values, axis=-1, keepdims=True)
    inverse = lax.rsqrt(jnp.mean(centered * centered, axis=-1, keepdims=True) + EPSILON)
    normed = centered * inverse
    return (normed * norm_gain + norm_shift, normed, inverse)


def norm_back(grad_rows, normed, inverse, norm_gain):
    scaled = grad_rows * norm_gain
    inner_part = (
        scaled
        - jnp.mean(scaled, axis=-1, keepdims=True)
        - normed * jnp.mean(scaled * normed, axis=-1, keepdims=True)
    )
    return (inner_part * inverse, jnp.sum(grad_rows * normed, axis=0), jnp.sum(grad_rows, axis=0))


def exact_gelu(vector):
    return jax.nn.gelu(vector, approximate=False)


def segment_rows(block_lengths):
    row_ends = jnp.cumsum(block_lengths)
    row_ids = jnp.arange(BLOCK, dtype=jnp.int32)
    passed = (row_ids[:, None] >= row_ends[None, :]).astype(jnp.int32)
    segment = jnp.sum(passed, axis=1)
    position = row_ids - jnp.sum(passed * block_lengths[None, :], axis=1)
    return (segment, position)


def rotary_tables(position):
    half_rot = ROT // 2
    frequency = 10000.0 ** (-2.0 * jnp.arange(half_rot, dtype=jnp.float32) / ROT)
    angles = position.astype(jnp.float32)[:, None] * frequency[None, :]
    return (jnp.cos(angles)[:, None, :], jnp.sin(angles)[:, None, :])


def rotate(vector, cos_table, sin_table, direction):
    half_rot = ROT // 2
    first_half = vector[..., :half_rot]
    second_half = vector[..., half_rot:ROT]
    return jnp.concatenate(
        [
            first_half * cos_table - direction * second_half * sin_table,
            second_half * cos_table + direction * first_half * sin_table,
            vector[..., ROT:],
        ],
        axis=-1,
    )


def block_scores(query_block, key_rows, segment, first_row):
    row_ids = jnp.arange(BLOCK, dtype=jnp.int32)
    raw_scores = jnp.einsum(
        "qhd,khd->hqk", query_block, key_rows, preferred_element_type=jnp.float32
    ) * HEAD_DIM ** (-0.5)
    query_ids = lax.dynamic_slice_in_dim(row_ids, first_row, ATT_BLK, 0)
    query_seg = lax.dynamic_slice_in_dim(segment, first_row, ATT_BLK, 0)
    allowed = (query_seg[:, None] == segment[None, :]) & (row_ids[None, :] <= query_ids[:, None])
    return jnp.where(allowed[None], raw_scores, -1e30)


def attention_forward(queries, key_rows, values, segment):

    def one_block(block_index):
        first_row = block_index * ATT_BLK
        query_block = lax.dynamic_slice_in_dim(queries, first_row, ATT_BLK, 0)
        scores = block_scores(query_block, key_rows, segment, first_row)
        row_top = jnp.max(scores, axis=-1, keepdims=True)
        weights = jnp.exp(scores - row_top)
        summed = jnp.sum(weights, axis=-1, keepdims=True)
        prob_rows = (weights / summed).astype(jnp.bfloat16)
        context = jnp.einsum("hqk,khd->qhd", prob_rows, values, preferred_element_type=jnp.float32)
        return (context, (row_top + jnp.log(summed))[..., 0])

    contexts, row_lse = lax.map(one_block, jnp.arange(BLOCK // ATT_BLK, dtype=jnp.int32))
    return (contexts.reshape(BLOCK, queries.shape[1], HEAD_DIM), row_lse)


def attention_backward(queries, key_rows, values, segment, row_lse, grad_context):

    def one_block(carry, block_index):
        grad_keys, grad_values = carry
        first_row = block_index * ATT_BLK
        query_block = lax.dynamic_slice_in_dim(queries, first_row, ATT_BLK, 0)
        grad_block = lax.dynamic_slice_in_dim(grad_context, first_row, ATT_BLK, 0)
        scores = block_scores(query_block, key_rows, segment, first_row)
        block_lse = lax.dynamic_index_in_dim(row_lse, block_index, 0, keepdims=False)
        prob_rows = jnp.exp(scores - block_lse[:, :, None])
        grad_probs = jnp.einsum(
            "qhd,khd->hqk", grad_block, values, preferred_element_type=jnp.float32
        )
        inner_sum = jnp.sum(prob_rows * grad_probs, axis=-1, keepdims=True)
        grad_scores = (prob_rows * (grad_probs - inner_sum)).astype(jnp.bfloat16)
        grad_query = jnp.einsum(
            "hqk,khd->qhd", grad_scores, key_rows, preferred_element_type=jnp.float32
        ) * HEAD_DIM ** (-0.5)
        grad_keys = grad_keys + jnp.einsum(
            "hqk,qhd->khd", grad_scores, query_block, preferred_element_type=jnp.float32
        ) * HEAD_DIM ** (-0.5)
        grad_values = grad_values + jnp.einsum(
            "hqk,qhd->khd",
            prob_rows.astype(jnp.bfloat16),
            grad_block,
            preferred_element_type=jnp.float32,
        )
        return ((grad_keys, grad_values), grad_query)

    empty = jnp.zeros(key_rows.shape, jnp.float32)
    (grad_keys, grad_values), grad_queries = lax.scan(
        one_block, (empty, empty), jnp.arange(BLOCK // ATT_BLK, dtype=jnp.int32)
    )
    return (grad_queries.reshape(key_rows.shape), grad_keys, grad_values)


def merge_stats(left_stats, right_stats):
    left_top, left_sum, left_pick = left_stats
    right_top, right_sum, right_pick = right_stats
    joint_top = jnp.maximum(left_top, right_top)
    joint_sum = left_sum * jnp.exp(left_top - joint_top) + right_sum * jnp.exp(
        right_top - joint_top
    )
    return (joint_top, joint_sum, left_pick + right_pick)


def per_device(
    hidden,
    targets,
    lengths,
    labels,
    ref_logps,
    ln1_gain,
    ln1_bias,
    ln2_gain,
    ln2_bias,
    qkv_weight,
    qv_bias,
    out_weight,
    up_weight,
    up_bias,
    down_weight,
    branch_bias,
    lnf_gain,
    lnf_bias,
    head_weight,
):
    num_blocks = hidden.shape[0]
    shard_rows = hidden.shape[1]
    local_heads = qkv_weight.shape[1]
    local_vocab = head_weight.shape[1]
    row_blocks = BLOCK // ATT_BLK
    gain_one = ln1_gain.astype(jnp.float32)
    shift_one = ln1_bias.astype(jnp.float32)
    gain_two = ln2_gain.astype(jnp.float32)
    shift_two = ln2_bias.astype(jnp.float32)
    gain_final = lnf_gain.astype(jnp.float32)
    shift_final = lnf_bias.astype(jnp.float32)
    branch_float = branch_bias.astype(jnp.float32)
    up_float = up_bias.astype(jnp.float32)
    qv_float = qv_bias.astype(jnp.float32)
    full_bias = jnp.concatenate(
        [qv_float[:, :HEAD_DIM], jnp.zeros_like(qv_float[:, :HEAD_DIM]), qv_float[:, HEAD_DIM:]],
        axis=-1,
    )
    qkv_flat = qkv_weight.reshape(D, local_heads * 3 * HEAD_DIM)
    out_flat = out_weight.reshape(local_heads * HEAD_DIM, D)
    vocab_ids = lax.axis_index("seq") * local_vocab + jnp.arange(local_vocab, dtype=jnp.int32)
    block_num = 0
    own_rows = hidden[block_num].astype(jnp.float32)
    segment, position = segment_rows(lengths[block_num])
    gathered = lax.all_gather(hidden[block_num], "seq", axis=0, tiled=True).astype(jnp.float32)
    first_norm, normed_one, inverse_one = norm_parts(gathered, gain_one, shift_one)
    second_norm, normed_two, inverse_two = norm_parts(gathered, gain_two, shift_two)
    first_full = first_norm.astype(jnp.bfloat16)
    second_full = second_norm.astype(jnp.bfloat16)
    projected = (
        jnp.dot(first_full, qkv_flat, preferred_element_type=jnp.float32).reshape(
            BLOCK, local_heads, 3 * HEAD_DIM
        )
        + full_bias
    )
    cos_table, sin_table = rotary_tables(position)
    queries = rotate(projected[..., :HEAD_DIM], cos_table, sin_table, 1.0).astype(jnp.bfloat16)
    key_rows = rotate(projected[..., HEAD_DIM : 2 * HEAD_DIM], cos_table, sin_table, 1.0).astype(
        jnp.bfloat16
    )
    values = projected[..., 2 * HEAD_DIM :].astype(jnp.bfloat16)
    context, row_lse = attention_forward(queries, key_rows, values, segment)
    context = context.reshape(BLOCK, local_heads * HEAD_DIM).astype(jnp.bfloat16)
    up_pre = jnp.dot(second_full, up_weight, preferred_element_type=jnp.float32) + up_float
    activated = exact_gelu(up_pre).astype(jnp.bfloat16)

    def branch_term(first_row, row_count, context=context, activated=activated):
        return jnp.dot(context, out_flat, preferred_element_type=jnp.float32) + jnp.dot(
            activated, down_weight, preferred_element_type=jnp.float32
        )

    stream = (
        own_rows
        + lax.psum_scatter(
            branch_term(jnp.int32(0), shard_rows * lax.axis_size("seq")),
            "seq",
            scatter_dimension=0,
            tiled=True,
        )
        + branch_float
    )
    final_norm, normed_final, inverse_final = norm_parts(stream, gain_final, shift_final)
    final_full = lax.all_gather(final_norm.astype(jnp.bfloat16), "seq", axis=0, tiled=True)
    block_targets = targets[block_num]

    def logit_stats(row_block, final_full=final_full, block_targets=block_targets):
        first_row = row_block * ATT_BLK
        rows_in = lax.dynamic_slice_in_dim(final_full, first_row, ATT_BLK, 0)
        row_targets = lax.dynamic_slice_in_dim(block_targets, first_row, ATT_BLK, 0)
        logits = jnp.dot(rows_in, head_weight, preferred_element_type=jnp.float32)
        row_top = jnp.max(logits, axis=-1)
        summed = jnp.sum(jnp.exp(logits - row_top[:, None]), axis=-1)
        picked = jnp.sum(
            jnp.where(vocab_ids[None, :] == row_targets[:, None], logits, 0.0), axis=-1
        )
        return (row_top, summed, picked)

    row_tops, row_sums, row_picks = lax.map(logit_stats, jnp.arange(row_blocks, dtype=jnp.int32))
    top_all, sum_all, pick_all = joined(
        (row_tops.reshape(BLOCK), row_sums.reshape(BLOCK), row_picks.reshape(BLOCK)),
        "seq",
        merge_stats,
    )
    log_total = top_all + jnp.log(sum_all)
    token_logp = pick_all - log_total
    member = (segment[:, None] == jnp.arange(EXB, dtype=jnp.int32)[None, :]).astype(jnp.float32)
    mean_rows = [
        jnp.sum(member * token_logp[:, None], axis=0) / lengths[block_num].astype(jnp.float32)
    ]
    saved = [
        {
            "own_rows": own_rows,
            "segment": segment,
            "cos_table": cos_table,
            "sin_table": sin_table,
            "normed_one": normed_one,
            "inverse_one": inverse_one,
            "normed_two": normed_two,
            "inverse_two": inverse_two,
            "first_full": first_full,
            "second_full": second_full,
            "queries": queries,
            "key_rows": key_rows,
            "values": values,
            "row_lse": row_lse,
            "context": context,
            "up_pre": up_pre,
            "activated": activated,
            "stream": stream,
            "normed_final": normed_final,
            "inverse_final": inverse_final,
            "final_full": final_full,
            "log_total": log_total,
            "member": member,
        }
    ]
    log_ratio = jnp.stack(mean_rows) - ref_logps
    total_ratio = lax.psum(jnp.sum(log_ratio), "dp")
    center = total_ratio / (num_blocks * lax.axis_size("dp") * EXB)
    label_sign = (2 * labels - 1).astype(jnp.float32)
    squashed = jax.nn.sigmoid(BETA * label_sign * (log_ratio - center))
    losses = 1.0 - squashed
    grad_ratio = -LOSS_SCALE * BETA * label_sign * squashed * (1.0 - squashed)
    block_num = 0
    kept = saved[block_num]
    example_grad = grad_ratio[block_num] / lengths[block_num].astype(jnp.float32)
    token_grad = jnp.sum(kept["member"] * example_grad[None, :], axis=1)
    block_targets = targets[block_num]

    def logit_grads(row_block, kept=kept, token_grad=token_grad, block_targets=block_targets):
        first_row = row_block * ATT_BLK
        rows_in = lax.dynamic_slice_in_dim(kept["final_full"], first_row, ATT_BLK, 0)
        row_targets = lax.dynamic_slice_in_dim(block_targets, first_row, ATT_BLK, 0)
        row_total = lax.dynamic_slice_in_dim(kept["log_total"], first_row, ATT_BLK, 0)
        row_scale = lax.dynamic_slice_in_dim(token_grad, first_row, ATT_BLK, 0)
        logits = jnp.dot(rows_in, head_weight, preferred_element_type=jnp.float32)
        prob_rows = jnp.exp(logits - row_total[:, None])
        onehot = (vocab_ids[None, :] == row_targets[:, None]).astype(jnp.float32)
        return (row_scale[:, None] * (onehot - prob_rows)).astype(jnp.bfloat16)

    grad_logits = lax.map(logit_grads, jnp.arange(row_blocks, dtype=jnp.int32)).reshape(
        BLOCK, local_vocab
    )
    head_grad = jnp.einsum(
        "nd,nv->dv", kept["final_full"], grad_logits, preferred_element_type=jnp.float32
    )

    def final_term(first_row, row_count, grad_logits=grad_logits):
        return jnp.einsum("nv,dv->nd", grad_logits, head_weight, preferred_element_type=jnp.float32)

    grad_final = lax.psum_scatter(
        final_term(jnp.int32(0), shard_rows * lax.axis_size("seq")),
        "seq",
        scatter_dimension=0,
        tiled=True,
    )
    grad_stream, part_gain, part_shift = norm_back(
        grad_final, kept["normed_final"], kept["inverse_final"], gain_final
    )
    branch_grad = jnp.sum(grad_stream, axis=0)
    grad_full = lax.all_gather(grad_stream.astype(jnp.bfloat16), "seq", axis=0, tiled=True)
    out_grad = jnp.einsum(
        "nc,nd->cd", kept["context"], grad_full, preferred_element_type=jnp.float32
    )
    down_grad = jnp.einsum(
        "nf,nd->fd", kept["activated"], grad_full, preferred_element_type=jnp.float32
    )
    grad_context = (
        jnp.einsum("nd,cd->nc", grad_full, out_flat, preferred_element_type=jnp.float32)
        .astype(jnp.bfloat16)
        .reshape(BLOCK, local_heads, HEAD_DIM)
    )
    grad_active = jnp.einsum(
        "nd,fd->nf", grad_full, down_weight, preferred_element_type=jnp.float32
    )
    gelu_pull = jax.vjp(exact_gelu, kept["up_pre"])[1]
    grad_up = gelu_pull(grad_active)[0].astype(jnp.bfloat16)
    up_grad = jnp.einsum(
        "nd,nf->df", kept["second_full"], grad_up, preferred_element_type=jnp.float32
    )
    up_bias_grad = jnp.sum(grad_up, axis=0, dtype=jnp.float32)
    grad_query, grad_keys, grad_values = attention_backward(
        kept["queries"],
        kept["key_rows"],
        kept["values"],
        kept["segment"],
        kept["row_lse"],
        grad_context,
    )
    grad_qkv = jnp.concatenate(
        [
            rotate(grad_query, kept["cos_table"], kept["sin_table"], -1.0),
            rotate(grad_keys, kept["cos_table"], kept["sin_table"], -1.0),
            grad_values,
        ],
        axis=-1,
    ).astype(jnp.bfloat16)
    qkv_sums = jnp.sum(grad_qkv, axis=0, dtype=jnp.float32)
    qv_grad = jnp.concatenate([qkv_sums[:, :HEAD_DIM], qkv_sums[:, 2 * HEAD_DIM :]], axis=-1)
    qkv_grad = jnp.einsum(
        "nd,nhe->dhe", kept["first_full"], grad_qkv, preferred_element_type=jnp.float32
    )
    grad_first = jnp.einsum("nhe,dhe->nd", grad_qkv, qkv_weight, preferred_element_type=jnp.float32)
    grad_second = jnp.einsum("nf,df->nd", grad_up, up_weight, preferred_element_type=jnp.float32)
    part_one, gain_part_one, shift_part_one = norm_back(
        grad_first, kept["normed_one"], kept["inverse_one"], gain_one
    )
    part_two, gain_part_two, shift_part_two = norm_back(
        grad_second, kept["normed_two"], kept["inverse_two"], gain_two
    )
    grad_input = grad_stream + lax.psum_scatter(
        (part_one + part_two).astype(jnp.bfloat16), "seq", scatter_dimension=0, tiled=True
    ).astype(jnp.float32)
    outputs = [kept["stream"].astype(jnp.bfloat16)]
    input_grads = [grad_input]
    small_sums = lax.psum(
        (
            gain_part_one,
            shift_part_one,
            gain_part_two,
            shift_part_two,
            part_gain,
            part_shift,
            branch_grad,
        ),
        ("dp", "seq"),
    )
    large_sums = (
        lax.psum(qkv_grad.astype(jnp.bfloat16), "dp").astype(jnp.float32),
        lax.psum(qv_grad.astype(jnp.bfloat16), "dp").astype(jnp.float32),
        lax.psum(out_grad.astype(jnp.bfloat16), "dp").astype(jnp.float32),
        lax.psum(up_grad.astype(jnp.bfloat16), "dp").astype(jnp.float32),
        lax.psum(up_bias_grad.astype(jnp.bfloat16), "dp").astype(jnp.float32),
        lax.psum(down_grad.astype(jnp.bfloat16), "dp").astype(jnp.float32),
        lax.psum(head_grad.astype(jnp.bfloat16), "dp").astype(jnp.float32),
    )
    return (
        losses,
        jnp.stack(outputs),
        jnp.stack(input_grads),
        small_sums[0],
        small_sums[1],
        small_sums[2],
        small_sums[3],
        large_sums[0],
        large_sums[1],
        large_sums[2].reshape(out_weight.shape),
        large_sums[3],
        large_sums[4],
        large_sums[5],
        small_sums[6],
        small_sums[4],
        small_sums[5],
        large_sums[6],
    )


def solution(mesh):
    return jax.shard_map(
        per_device,
        mesh=mesh,
        in_specs=(
            P("dp", "seq", None),
            P("dp", None),
            P("dp", None),
            P("dp", None),
            P("dp", None),
            P(),
            P(),
            P(),
            P(),
            P(None, "seq", None),
            P("seq", None),
            P("seq", None, None),
            P(None, "seq"),
            P("seq"),
            P("seq", None),
            P(),
            P(),
            P(),
            P(None, "seq"),
        ),
        out_specs=(
            P("dp", None),
            P("dp", "seq", None),
            P("dp", "seq", None),
            P(),
            P(),
            P(),
            P(),
            P(None, "seq", None),
            P("seq", None),
            P("seq", None, None),
            P(None, "seq"),
            P("seq"),
            P("seq", None),
            P(),
            P(),
            P(),
            P(None, "seq"),
        ),
        check_vma=False,
    )
```

profile of v0, /device:TPU:0, one launch (start us, length us, event | category | flops | bytes accessed | tf_op | source)
XLA Modules:
  0.0 2213.9 jit_solution(8481005598364883140)
XLA Ops:
  22.6 115.3 %all-gather.12.cloned.1.call-done = bf16[1,2048,2048]{2,1,0:T(8,128)(2,1)} async-done(((bf16[1,256,2048]{2,1,0:T(8,128)(2,1)}), bf16[1,2048,2048]{2,1,0:T(8,128)(2,1)}) %all-gather.12.cloned.1.call-update) | async-done | bytes 8388624 | tf_op jit(solution)/shard_map/all_gather | solution.py:197
  165.8 53.5 %while.67 = (s32[]{:T(128)}, bf16[4,512,2,128]{3,1,2,0:T(8,128)(2,1)}, f32[4,2,512]{2,1,0:T(2,128)}, s32[4]{0:T(128)S(1)}, s32[2048]{0:T(1024)S(1)}, /*index=5*/...) while((s32[]{:T(128)}, ...), condition=%wide.region_8.9_spmd, body=%wide.region_5.0_spmd.sunk | while | flops 1102052864 | bytes 40683776 | solution.py:102
  222.1 32.5 %multiply_convert_fusion.2 = (bf16[2048,1024]{1,0:T(8,128)(2,1)S(1)}, f32[2048,1024]{1,0:T(8,128)}, f32[2048,1024]{1,0:T(8,128)}) fusion(f32[1024]{0:T(1024)S(1)} %convert_element_type.163, bf16[2048,1024]{1,0:T(8,128)(2,1)} %param.41, bf16[1,2048,2048]{2,1,0:T(8,128)(2,1)} %all-gather.12.cloned.1.call-done, f32[2048]{0:T(1024)S(1)} %convert_element_type.161, ...), kind=kOutput, calls=%fused_computation.101 | convolution fusion | flops 8753512448 | bytes 33591296 | tf_op jit(solution)/shard_map/dot_general | solution.py:216
  273.2 280.3 %reduce-scatter.4.cloned.1.call-done = f32[256,2048]{1,0:T(8,128)} async-done(((f32[2048,2048]{1,0:T(8,128)}), f32[256,2048]{1,0:T(8,128)}) %reduce-scatter.4.cloned.1.call-update) | async-done | bytes 2097168 | tf_op jit(solution)/shard_map/reduce_scatter | solution.py:226
  559.6 124.1 %all-gather.8.cloned.1.call-done = bf16[2048,2048]{1,0:T(8,128)(2,1)} async-done(((bf16[256,2048]{1,0:T(8,128)(2,1)}), bf16[2048,2048]{1,0:T(8,128)(2,1)}) %all-gather.8.cloned.1.call-update) | async-done | bytes 8388624 | tf_op jit(solution)/shard_map/all_gather | solution.py:235
  683.7 62.2 %while.69 = (s32[]{:T(128)}, f32[4,512]{1,0:T(4,128)S(1)}, f32[4,512]{1,0:T(4,128)S(1)}, f32[4,512]{1,0:T(4,128)S(1)}, s32[4]{0:T(128)S(1)}, /*index=5*/bf16[204...) while((s32[]{:T(128)}, f32[4,512]{1,0:T(4,128)S(1)}, ...), condition=%wide.region_16.17_spmd.clone, body=%wide.region_12.16_spmd.clone.sunk | while | flops 6989547520 | bytes 29413592 | solution.py:250
  685.2 11.7 fusion.172
  700.7 11.8 fusion.172
  716.2 11.7 fusion.172
  731.7 11.7 fusion.172
  745.9 30.5 %all-gather.2 = f32[8,1,2048]{2,1,0:T(1,128)S(1)} all-gather(f32[1,1,2048]{2,1,0:T(1,128)S(1)} %reshape.347), channel_id=1, replica_groups=mesh['dp'=4,'seq'=8] {'seq'}, dimensions={0}, use_global_device_ids=true | all-gather | bytes 73728 | tf_op jit(solution)/shard_map/all_gather | solution.py:20
  776.4 30.5 %all-gather.1 = f32[8,1,2048]{2,1,0:T(1,128)S(1)} all-gather(f32[1,1,2048]{2,1,0:T(1,128)S(1)} %reshape.345), channel_id=1, replica_groups=mesh['dp'=4,'seq'=8] {'seq'}, dimensions={0}, use_global_device_ids=true | all-gather | bytes 73728 | tf_op jit(solution)/shard_map/all_gather | solution.py:20
  807.0 30.5 %all-gather.3 = f32[8,1,2048]{2,1,0:T(1,128)S(1)} all-gather(f32[1,1,2048]{2,1,0:T(1,128)S(1)} %reshape.349), channel_id=1, replica_groups=mesh['dp'=4,'seq'=8] {'seq'}, dimensions={0}, use_global_device_ids=true | all-gather | bytes 73728 | tf_op jit(solution)/shard_map/all_gather | solution.py:20
  846.6 62.2 %while.70 = (s32[]{:T(128)}, bf16[4,512,3328]{2,1,0:T(8,128)(2,1)}, s32[4]{0:T(128)S(1)}, f32[2048]{0:T(1024)S(1)}, s32[2048]{0:T(1024)S(1)}, /*index=5*/bf16[20...) while((s32[]{:T(128)}, bf16[4,512,3328]{2,1,0:T(8,128)(2,1)}, ...), condition=%wide.region_24.25_spmd.clone, body=%wide.region_23.24_spmd.clone.sunk | while | flops 6989549056 | bytes 19181784 | solution.py:313
  848.1 14.0 fusion.175
  863.6 14.1 fusion.175
  879.1 14.1 fusion.175
  894.7 14.1 fusion.175
  908.8 35.8 %fusion.106 = f32[2048,2048]{1,0:T(8,128)} fusion(bf16[2048,3328]{1,0:T(8,128)(2,1)} %bitcast.272, bf16[2048,3328]{1,0:T(8,128)(2,1)} %get-tuple-element.1187), kind=kOutput, calls=%fused_computation.195 | convolution fusion | flops 27917287424 | bytes 44040192 | tf_op jit(solution)/shard_map/nv,dv->nd/dot_general | solution.py:321
  944.7 280.9 %reduce-scatter.6.cloned.1.call-done = f32[256,2048]{1,0:T(8,128)} async-done(((f32[2048,2048]{1,0:T(8,128)}), f32[256,2048]{1,0:T(8,128)}) %reduce-scatter.6.cloned.1.call-update) | async-done | bytes 2097168 | tf_op jit(solution)/shard_map/reduce_scatter | solution.py:323
  1234.2 37.1 %convolution_convert_fusion = bf16[2048,3328]{1,0:T(8,128)(2,1)} fusion(bf16[2048,2048]{1,0:T(8,128)(2,1)} %get-tuple-element.1190, bf16[2048,3328]{1,0:T(8,128)(2,1)} %bitcast.273), kind=kOutput, calls=%fused_computation.93 | convolution fusion | flops 27924103168 | bytes 35651584 | tf_op jit(solution)/shard_map/nd,nv->dv/dot_general | solution.py:316
  1271.3 87.0 %all-gather.10.cloned.1.call-done = bf16[2048,2048]{1,0:T(8,128)(2,1)} async-done(((bf16[256,2048]{1,0:T(8,128)(2,1)}), bf16[2048,2048]{1,0:T(8,128)(2,1)}) %all-gather.10.cloned.1.call-update) | async-done | bytes 8388624 | tf_op jit(solution)/shard_map/all_gather | solution.py:333
  1365.0 144.8 %while.71 = (s32[]{:T(128)}, f32[2048,2,128]{0,2,1:T(8,128)}, f32[2048,2,128]{0,2,1:T(8,128)}, f32[4,512,2,128]{1,0,3,2:T(4,128)}, s32[4]{0:T(128)S(1)}, /*index...) while((s32[]{:T(128)}, f32[2048,2,128]{0,2,1:T(8,128)}, ...), condition=%wide.region_30.31_spmd.clone, body=%wide.region_28.30_spmd.clone.sunk | while | flops 2721709568 | bytes 82360616 | solution.py:136
  1551.9 13.2 convolution_convert_fusion.1
  1572.0 22.1 fusion.93
  1594.2 14.0 convolution_convert_fusion.2
  1608.3 15.7 fusion.107
  1624.0 20.9 fusion.70
  1645.0 17.1 fusion.67
  1672.2 41.3 %all-reduce = (f32[2048]{0:T(1024)}, f32[2048]{0:T(1024)}, f32[2048]{0:T(1024)}, f32[2048]{0:T(1024)}, f32[2048]{0:T(1024)}, /*index=5*/f32[2048]{0:T(1024)}, f32[2048]{0:T(1024)}) all-reduce(f32[2048]{0:T(1024)S(1)} %get-tuple-element.492, f32[2048]{0:T(1024)S(1)} %get-tuple-element.497, ...), channel_id=1, replica_groups=mesh['dp'=4,'seq'=8] {'dp','seq'}, use_global_device_ids=true, to_apply=%region_37.38 | all-reduce | flops 14336 | bytes 114688 | tf_op jit(solution)/shard_map/psum | solution.py:388
  1713.5 337.2 %all-reduce.5.cloned.1.call-done = (bf16[2048,2,384]{2,0,1:T(8,128)(2,1)}, bf16[2,128,2048]{2,1,0:T(8,128)(2,1)}, bf16[2048,1024]{1,0:T(8,128)(2,1)}, bf16[1024,2048]{1,0:T(8,128)(2,1)}, bf16[2048,3328]{1,0:T(8,128)(2,1)}) async-done(((bf16[2048,2,384]{2,0,1:T(8,128)(2,1)}, bf16[2,128,2048]{2,1,0:T(8,128)(2,1)}, bf16[2048,1024]{1,0:T(8,128)(2,1)}, bf16[1024,2048]{1,0:T(8,128)(2,1)}, ...) | async-done | bytes 26214416 | tf_op jit(solution)/shard_map/psum | solution.py:401
  2082.7 121.3 %reduce-scatter.8.cloned.1.call-done = bf16[256,2048]{1,0:T(8,128)(2,1)} async-done(((bf16[2048,2048]{1,0:T(8,128)(2,1)}), bf16[256,2048]{1,0:T(8,128)(2,1)}) %reduce-scatter.8.cloned.1.call-update) | async-done | bytes 1048592 | tf_op jit(solution)/shard_map/reduce_scatter | solution.py:383
  (426 shorter events, 388.3 us)
Async XLA Ops:
  7.2 256.7 %copy-start = (bf16[2,128,2048]{2,1,0:T(8,128)(2,1)S(1)}, bf16[2,128,2048]{2,1,0:T(8,128)(2,1)}, u32[]{:S(2)}) copy-start(bf16[2,128,2048]{2,1,0:T(8,128)(2,1)} %param.40) | copy-start | bytes 3145732
  7.2 130.6 %all-gather.12.cloned.1.call-start = ((), (), s32[]{:S(2)}) async-start(), calls=%async_computation.8 | async-start | bytes 9437184 | tf_op jit(solution)/shard_map/all_gather | solution.py:197
  8.0 545.6 %reduce-scatter.4.cloned.1.call-start = ((), (), s32[]{:S(2)}) async-start(), calls=%async_computation.3 | async-start | bytes 18874368 | tf_op jit(solution)/shard_map/reduce_scatter | solution.py:226
  9.5 212.4 %copy-start.48 = (f32[1024]{0:T(1024)}, f32[1024]{0:T(1024)S(1)}, u32[]{:S(2)}) copy-start(f32[1024]{0:T(1024)S(1)} %convert_element_type.163) | copy-start | bytes 12292
  10.2 211.8 %copy-start.35 = (f32[2048]{0:T(1024)}, f32[2048]{0:T(1024)S(1)}, u32[]{:S(2)}) copy-start(f32[2048]{0:T(1024)S(1)} %convert_element_type.160) | copy-start | bytes 24580
  10.9 135.0 %copy-start.27 = (f32[2048]{0:T(1024)}, f32[2048]{0:T(1024)S(1)}, u32[]{:S(2)}) copy-start(f32[2048]{0:T(1024)S(1)} %convert_element_type.153) | copy-start | bytes 24580
  11.6 210.4 %copy-start.41 = (f32[2048]{0:T(1024)}, f32[2048]{0:T(1024)S(1)}, u32[]{:S(2)}) copy-start(f32[2048]{0:T(1024)S(1)} %convert_element_type.161) | copy-start | bytes 24580
  22.6 138.3 %copy-start.19 = (f32[2048,16]{0,1:T(8,128)}, f32[2048,16]{0,1:T(8,128)S(1)}, u32[]{:S(2)}) copy-start(f32[2048,16]{0,1:T(8,128)S(1)} %get-tuple-element.648) | copy-start | bytes 393220
  143.6 78.4 %copy-start.25 = (f32[2048]{0:T(1024)}, f32[2048]{0:T(1024)S(1)}, u32[]{:S(2)}) copy-start(f32[2048]{0:T(1024)S(1)} %broadcast_multiply_fusion.5) | copy-start | bytes 24580
  146.0 76.1 %copy-start.29 = (f32[2048]{0:T(1024)}, f32[2048]{0:T(1024)S(1)}, u32[]{:S(2)}) copy-start(f32[2048]{0:T(1024)S(1)} %add_rsqrt_fusion) | copy-start | bytes 24580
  222.0 41.9 %copy-start.6 = (bf16[4,512,2,128]{3,2,1,0:T(2,128)(2,1)}, bf16[4,512,2,128]{3,2,1,0:T(2,128)(2,1)S(1)}, u32[]{:S(2)}) copy-start(bf16[4,512,2,128]{3,2,1,0:T(2,128)(2,1)S(1)} %copy.113) | copy-start | bytes 3145732
  272.6 411.1 %copy-start.31 = (s32[1,2048]{1,0:T(1,128)S(1)}, s32[1,2048]{1,0:T(1,128)}, u32[]{:S(2)}) copy-start(s32[1,2048]{1,0:T(1,128)} %param.30) | copy-start | bytes 24580
  272.6 411.0 %all-gather.8.cloned.1.call-start = ((), (), s32[]{:S(2)}) async-start(), calls=%async_computation.4 | async-start | bytes 9437184 | tf_op jit(solution)/shard_map/all_gather | solution.py:235
  273.2 410.4 %copy-start.23 = (f32[2048]{0:T(1024)}, f32[2048]{0:T(1024)S(1)}, u32[]{:S(2)}) copy-start(f32[2048]{0:T(1024)S(1)} %convert_element_type.166) | copy-start | bytes 24580
  556.8 126.9 %copy-start.4 = (f32[256,2048]{1,0:T(8,128)}, f32[256,2048]{1,0:T(8,128)S(1)}, u32[]{:S(2)}) copy-start(f32[256,2048]{1,0:T(8,128)S(1)} %get-tuple-element.619) | copy-start | bytes 6291460
  557.0 126.7 %copy-start.37 = (f32[256]{0:T(256)}, f32[256]{0:T(256)S(1)}, u32[]{:S(2)}) copy-start(f32[256]{0:T(256)S(1)} %broadcast_multiply_fusion.8) | copy-start | bytes 3076
  559.5 666.2 %reduce-scatter.6.cloned.1.call-start = ((), (), s32[]{:S(2)}) async-start(), calls=%async_computation.5 | async-start | bytes 18874368 | tf_op jit(solution)/shard_map/reduce_scatter | solution.py:323
  683.6 154.7 %copy-start.17 = (s32[2048]{0:T(1024)S(1)}, s32[2048]{0:T(1024)}, u32[]{:S(2)}) copy-start(s32[2048]{0:T(1024)} %copy-done.16) | copy-start | bytes 24580
  683.6 154.8 %copy-start.44 = (s32[1,8]{1,0:T(1,128)S(1)}, s32[1,8]{1,0:T(1,128)}, u32[]{:S(2)}) copy-start(s32[1,8]{1,0:T(1,128)} %param.31) | copy-start | bytes 100
  683.6 154.8 %copy-start.51 = (f32[1,8]{1,0:T(1,128)S(1)}, f32[1,8]{1,0:T(1,128)}, u32[]{:S(2)}) copy-start(f32[1,8]{1,0:T(1,128)} %param.33) | copy-start | bytes 100
  683.7 162.3 %copy-start.52 = (s32[1,8]{1,0:T(1,128)S(1)}, s32[1,8]{1,0:T(1,128)}, u32[]{:S(2)}) copy-start(s32[1,8]{1,0:T(1,128)} %param.32) | copy-start | bytes 100
  944.6 281.0 %copy-start.5 = (f32[256,2048]{1,0:T(8,128)S(1)}, f32[256,2048]{1,0:T(8,128)}, u32[]{:S(2)}) copy-start(f32[256,2048]{1,0:T(8,128)} %copy-done.4) | copy-start | bytes 6291460
  944.6 281.0 %copy-start.24 = (f32[2048]{0:T(1024)S(1)}, f32[2048]{0:T(1024)}, u32[]{:S(2)}) copy-start(f32[2048]{0:T(1024)} %copy-done.23) | copy-start | bytes 24580
  944.6 281.0 %copy-start.38 = (f32[256]{0:T(256)S(1)}, f32[256]{0:T(256)}, u32[]{:S(2)}) copy-start(f32[256]{0:T(256)} %copy-done.37) | copy-start | bytes 3076
  944.6 281.0 %copy-start.40 = (f32[256]{0:T(256)S(1)}, f32[256]{0:T(256)}, u32[]{:S(2)}) copy-start(f32[256]{0:T(256)} %copy-done.39) | copy-start | bytes 3076
  944.7 413.6 %all-gather.10.cloned.1.call-start = ((), (), s32[]{:S(2)}) async-start(), calls=%async_computation.6 | async-start | bytes 9437184 | tf_op jit(solution)/shard_map/all_gather | solution.py:333
  1234.1 816.6 %all-reduce.5.cloned.1.call-start = ((), (), s32[]{:S(2)}) async-start(), calls=%async_computation.9 | async-start | bytes 52428800 | tf_op jit(solution)/shard_map/psum | solution.py:401
  1271.3 93.7 %copy-start.3 = (bf16[2048,2,128]{2,0,1:T(8,128)(2,1)S(1)}, bf16[2048,2,128]{2,0,1:T(8,128)(2,1)}, u32[]{:S(2)}) copy-start(bf16[2048,2,128]{2,0,1:T(8,128)(2,1)} %copy-done.2) | copy-start | bytes 3145732
  1271.3 93.7 %copy-start.18 = (s32[2048]{0:T(1024)S(1)}, s32[2048]{0:T(1024)}, u32[]{:S(2)}) copy-start(s32[2048]{0:T(1024)} %copy-done.16) | copy-start | bytes 24580
  1608.2 595.8 %reduce-scatter.8.cloned.1.call-start = ((), (), s32[]{:S(2)}) async-start(), calls=%async_computation.7 | async-start | bytes 9437184 | tf_op jit(solution)/shard_map/reduce_scatter | solution.py:383
  1608.3 36.6 %slice-start.2 = ((s8[8388608]{0:T(1024)(128)(4,1)}), s8[4194304]{0:T(1024)(128)(4,1)S(1)}, s32[]{:S(2)}) async-start(s8[8388608]{0:T(1024)(128)(4,1)} %bitcast.246), calls=%async_computation.12 | async-start | bytes 8388608
  2073.3 130.7 %copy-start.9 = (f32[256,2048]{1,0:T(8,128)S(1)}, f32[256,2048]{1,0:T(8,128)}, u32[]{:S(2)}) copy-start(f32[256,2048]{1,0:T(8,128)} %copy-done.8) | copy-start | bytes 6291460
  (45 other events, 537.2 us)
Sparse Core Ops, SparseCore 0:
  10.2 127.6 all-gather.11
  272.7 280.8 reduce-scatter.3
  559.6 123.9 all-gather.7
  944.8 280.8 reduce-scatter.5
  1234.2 123.9 all-gather.9
  1608.3 442.3 all-reduce.4
  2054.8 149.2 reduce-scatter.7
where the time goes:
time: 2220 us; the launch traced here: 2210 us
  waiting for transfers between devices  1350 us (61%)
  matrix products  443 us (20%)
  blocking collectives  146 us (7%)
  other arithmetic  122 us (5%)
  local copies, waits for them, and re-layouts  121 us (5%)
    psum x1, waiting for transfers between devices, per_device(): lax.psum(qkv_grad.astype(jnp.bfloat16), 'dp').astype(jnp.float32)  337 us
    reduce_scatter x1, waiting for transfers between devices, per_device(): lax.psum_scatter(final_term(jnp.int32(0), shard_rows * lax.axis_size('seq...  281 us
    reduce_scatter x1, waiting for transfers between devices, per_device(): lax.psum_scatter(branch_term(jnp.int32(0), shard_rows * lax.axis_size('se...  280 us
    all_gather x1, waiting for transfers between devices, per_device(): lax.all_gather(final_norm.astype(jnp.bfloat16), 'seq', axis=0, tiled=True)  124 us
    reduce_scatter x1, waiting for transfers between devices, per_device(): lax.psum_scatter((part_one + part_two).astype(jnp.bfloat16), 'seq', scatt...  121 us
    all_gather x1, waiting for transfers between devices, per_device(): lax.all_gather(hidden[block_num], 'seq', axis=0, tiled=True)  115 us
    all_gather x3, blocking collectives, joined(): pieces = jax.tree.map(lambda part: lax.all_gather(part, axis), value)  91.5 us
    all_gather x1, waiting for transfers between devices, per_device(): lax.all_gather(grad_stream.astype(jnp.bfloat16), 'seq', axis=0, tiled=True)  87 us
  transfers between devices with their start and end apart: 7, of which 7 were waited for; matrix products, arithmetic and copies ran while one was open for 6% of the time, Pallas kernels for 0%

commit v1 on v0

--- a/solution.py
+++ b/solution.py
@@ -1,6 +1,8 @@
 import jax
 import jax.numpy as jnp
 from jax import lax
+from jax.experimental import pallas as pl
+from jax.experimental.pallas import tpu as pltpu
 from jax.sharding import PartitionSpec as P
 
 D = 2048
@@ -16,10 +18,397 @@
 LOSS_SCALE = 65536.0
 
 
+MESH = pl.DeviceIdType.MESH
+
+
+class Grid2:
+    def __init__(self, sizes):
+        self.n = sizes
+        place = lax.axis_index("seq")
+        self.me = (place // sizes[1], lax.rem(place, sizes[1]))
+
+    def index(self, slow, fast):
+        return slow * self.n[1] + fast
+
+    def device(self, axis, spot):
+        here = list(self.me)
+        here[axis] = spot
+        return {"seq": self.index(*here)}
+
+    def nearest(self, axis, rank):
+        n, m = self.n[axis], self.me[axis]
+        if rank == 0:
+            return m
+        if n == 2:
+            return 1 - m
+        after = n - 1 - m
+        both = jnp.minimum(m, after)
+        dist = (rank + 1) // 2
+        near = m - dist if rank % 2 else m + dist
+        far = jnp.where(m < after, m + (rank - both), m - (rank - both))
+        return jnp.where(rank <= 2 * both, near, far)
+
+    def neighbours(self):
+        found = []
+        for axis in (0, 1):
+            m, n = self.me[axis], self.n[axis]
+            if n == 2:
+                found.append((None, self.device(axis, 1 - m)))
+            elif n > 2:
+                found.append((m > 0, self.device(axis, m - 1)))
+                found.append((m < n - 1, self.device(axis, m + 1)))
+        return found
+
+    def barrier(self):
+        sem = pltpu.get_barrier_semaphore()
+        amount = jnp.int32(0)
+        for there, device in self.neighbours():
+            def tell(device=device):
+                pl.semaphore_signal(sem, inc=1, device_id=device, device_id_type=MESH)
+            if there is None:
+                tell()
+                amount = amount + 1
+            else:
+                pl.when(there)(tell)
+                amount = amount + there.astype(jnp.int32)
+        pl.semaphore_wait(sem, amount)
+
+
+class Sender:
+    def __init__(self, send_sems):
+        self.sems = send_sems
+        self.used = 0
+        self.open = []
+
+    def send(self, src, dst, recv_sem, device, when=None):
+        copy = pltpu.make_async_remote_copy(
+            src_ref=src, dst_ref=dst, send_sem=self.sems.at[self.used], recv_sem=recv_sem,
+            device_id=device, device_id_type=MESH)
+        self.used += 1
+        if when is None:
+            copy.start()
+        else:
+            pl.when(when)(copy.start)
+        self.open.append((when, copy))
+
+    def finish(self):
+        for when, copy in self.open:
+            if when is None:
+                copy.wait_send()
+            else:
+                pl.when(when)(copy.wait_send)
+        self.open = []
+
+
+def gather_sends(sizes, halves):
+    return halves * 2 * (sizes[0] * sizes[1] * 2 + 8)
+
+
+def gather_rounds(grid, sender, piece, recv_sems, halves, cut, ready):
+    n, me = grid.n, grid.me
+
+    def arrived(slow, fast, half, kind):
+        ref = piece(grid.index(slow, fast), half, kind)
+        sem = recv_sems.at[kind, half, grid.index(slow, fast)]
+        pltpu.make_async_copy(ref, ref, sem).wait()
+
+    def push(slow, fast, half, kind, axis, spot, when):
+        ref = piece(grid.index(slow, fast), half, kind)
+        sem = recv_sems.at[kind, half, grid.index(slow, fast)]
+        sender.send(ref, ref, sem, grid.device(axis, spot), when)
+
+    def spread(slow, fast, half, kind, axis):
+        m, size = me[axis], n[axis]
+        if size == 2:
+            push(slow, fast, half, kind, axis, 1 - m, None)
+        elif size > 2:
+            push(slow, fast, half, kind, axis, m + 1, m < size - 1)
+            push(slow, fast, half, kind, axis, m - 1, m > 0)
+
+    def onward(slow, fast, half, kind, axis):
+        m, size = me[axis], n[axis]
+        if size <= 2:
+            return
+        source = (slow, fast)[axis]
+        below = source < m
+        when = (below & (m < size - 1)) | (jnp.logical_not(below) & (m > 0))
+        push(slow, fast, half, kind, axis, jnp.where(below, m + 1, m - 1), when)
+
+    todo = []
+
+    def work(count=1):
+        for _ in range(count):
+            if todo:
+                ready(*todo.pop(0))
+
+    def settle(k):
+        slow = grid.nearest(0, k)
+        for half in range(halves):
+            for l in range(n[1]):
+                fast = grid.nearest(1, l)
+                if k > 0:
+                    arrived(slow, fast, half, 1)
+                    onward(slow, fast, half, 1, 0)
+                else:
+                    spread(slow, fast, half, 1, 0)
+
+    def complete(k):
+        slow = grid.nearest(0, k)
+        if k > 0:
+            todo.append((slow, me[1], k * n[1]))
+        for l in range(1, n[1]):
+            fast = grid.nearest(1, l)
+            if cut[0]:
+                for half in range(halves):
+                    arrived(slow, fast, half, 0)
+                    onward(slow, fast, half, 0, 1)
+            todo.append((slow, fast, k * n[1] + l))
+
+    for half in range(halves):
+        for kind in (1, 0):
+            if cut[kind]:
+                spread(me[0], me[1], half, kind, kind)
+        if cut[0]:
+            spread(me[0], me[1], half, 0, 1)
+    todo.append((me[0], me[1], 0))
+    work()
+    if cut[1]:
+        for half in range(halves):
+            for l in range(1, n[1]):
+                fast = grid.nearest(1, l)
+                arrived(me[0], fast, half, 1)
+                onward(me[0], fast, half, 1, 1)
+    for k in range(1, n[0]):
+        slow = grid.nearest(0, k)
+        for half in range(halves):
+            if cut[0]:
+                arrived(slow, me[1], half, 0)
+                onward(slow, me[1], half, 0, 0)
+                spread(slow, me[1], half, 0, 1)
+            if half < halves - 1:
+                work()
+        if cut[1]:
+            settle(k - 1)
+        complete(k - 1)
+        work()
+    if cut[1]:
+        settle(n[0] - 1)
+    work(len(todo))
+    complete(n[0] - 1)
+    work(len(todo))
+
+
+def scatter_slots(n):
+    return 1 if n == 2 else n + 1
+
+
+class Scatter:
+    def __init__(self, grid, sender, part, bufs, sems, halves, cut):
+        self.grid, self.sender, self.part = grid, sender, part
+        self.bufs, self.sems, self.halves, self.cut = bufs, sems, halves, cut
+
+    def slot(self, axis, target, from_below):
+        if self.grid.n[axis] == 2:
+            return 0
+        return target + jnp.where(from_below, 1, 0)
+
+    def take(self, kind, stage, axis, other, target, from_below, half, when, slot_index):
+        buf, sem = self.bufs[kind][stage], self.sems[kind][stage]
+        slot = self.slot(axis, target, from_below)
+
+        def add():
+            ref = buf.at[other, slot, half]
+            pltpu.make_async_copy(ref, ref, sem.at[other, slot, half]).wait()
+            mine = self.part(slot_index, half, kind)
+            mine[...] = (mine[...].astype(jnp.float32) + ref[...].astype(jnp.float32)).astype(mine.dtype)
+
+        if when is None:
+            add()
+        else:
+            pl.when(when)(add)
+
+    def toward(self, kind, stage, axis, other, target, half, slow, fast):
+        grid = self.grid
+        m, n = grid.me[axis], grid.n[axis]
+        up = target > m
+        index = grid.index(slow, fast)
+        if n > 2:
+            incoming = (up & (m > 0)) | (jnp.logical_not(up) & (m < n - 1))
+            self.take(kind, stage, axis, other, target, up, half, incoming, index)
+        buf, sem = self.bufs[kind][stage], self.sems[kind][stage]
+        slot = self.slot(axis, target, up)
+        spot = 1 - m if n == 2 else jnp.where(up, m + 1, m - 1)
+        self.sender.send(
+            self.part(index, half, kind), buf.at[other, slot, half], sem.at[other, slot, half],
+            grid.device(axis, spot))
+
+    def last(self, kind, stage, axis, other, half, slow, fast):
+        grid = self.grid
+        m, n = grid.me[axis], grid.n[axis]
+        index = grid.index(slow, fast)
+        if n == 2:
+            self.take(kind, stage, axis, other, m, m > 0, half, None, index)
+        elif n > 2:
+            self.take(kind, stage, axis, other, m, jnp.bool_(True), half, m > 0, index)
+            self.take(kind, stage, axis, other, m, jnp.bool_(False), half, m < n - 1, index)
+
+    def run(self, produce):
+        grid, n, me = self.grid, self.grid.n, self.grid.me
+        for k in reversed(range(n[0])):
+            slow = grid.nearest(0, k)
+            for l in reversed(range(n[1])):
+                fast = grid.nearest(1, l)
+                produce(slow, fast)
+                for half in range(self.halves):
+                    if self.cut[0] and l > 0:
+                        self.toward(0, 0, 1, slow, fast, half, slow, fast)
+                    if self.cut[1] and k > 0:
+                        self.toward(1, 0, 0, fast, slow, half, slow, fast)
+        if self.cut[1]:
+            for half in range(self.halves):
+                for l in reversed(range(n[1])):
+                    fast = grid.nearest(1, l)
+                    self.last(1, 0, 0, fast, half, me[0], fast)
+                    if l > 0:
+                        self.toward(1, 1, 1, 0, fast, half, me[0], fast)
+        if self.cut[0]:
+            for k in reversed(range(1, n[0])):
+                slow = grid.nearest(0, k)
+                for half in range(self.halves):
+                    self.last(0, 0, 1, slow, half, slow, me[1])
+                    self.toward(0, 1, 0, 0, slow, half, slow, me[1])
+            for half in range(self.halves):
+                self.last(0, 0, 1, me[0], half, me[0], me[1])
+        for half in range(self.halves):
+            if self.cut[1]:
+                self.last(1, 1, 1, 0, half, me[0], me[1])
+            if self.cut[0]:
+                self.last(0, 1, 0, 0, half, me[0], me[1])
+
+
+def scatter_scratch(sizes, halves, rows, cols, cut):
+    bufs, sems = [], []
+    for kind, stages in ((0, (1, 0)), (1, (0, 1))):
+        for stage, axis in enumerate(stages):
+            lead = (sizes[1 - axis] if stage == 0 else 1, scatter_slots(sizes[axis]), halves)
+            width = max(cut[kind], 128)
+            bufs.append(pltpu.VMEM(lead + (rows // halves, width), jnp.bfloat16))
+            sems.append(pltpu.SemaphoreType.DMA(lead))
+    return bufs, sems
+
+
+def scatter_sends(sizes, halves):
+    return halves * 2 * (sizes[0] * sizes[1] + sizes[0] + sizes[1])
+
+
+def lines_of(seq):
+    fast = 2 if seq <= 8 else 4
+    return (seq // fast, fast)
+
+VMEM_LIMIT = 60 * 2**20
+
+
+def gather_cut(sizes):
+    if sizes[0] == 4 and sizes[1] == 2:
+        return (1664, 384)
+    return (D // 2, D // 2)
+
+
+def columns_of(cut, kind):
+    return pl.ds(0, cut[0]) if kind == 0 else pl.ds(cut[0], cut[1])
+
+
+def gather_rows(rows_own, sizes, collective):
+    rows = rows_own.shape[0]
+    shards = sizes[0] * sizes[1]
+    cut, halves = gather_cut(sizes), 2
+
+    def kernel(own_ref, out_ref, full, send_sems, recv_sems, local_sems):
+        grid = Grid2(sizes)
+        grid.barrier()
+        full[grid.index(*grid.me)] = own_ref[...]
+        sender = Sender(send_sems)
+        step = rows // halves
+
+        def piece(slot, half, kind):
+            return full.at[slot, pl.ds(half * step, step), columns_of(cut, kind)]
+
+        copies = []
+
+        def ready(slow, fast, order):
+            slot = grid.index(slow, fast)
+            copy = pltpu.make_async_copy(full.at[slot], out_ref.at[slot], local_sems.at[order])
+            copy.start()
+            copies.append(copy)
+
+        gather_rounds(grid, sender, piece, recv_sems, halves, cut, ready)
+        for copy in copies:
+            copy.wait()
+        sender.finish()
+
+    gathered = pl.pallas_call(
+        kernel,
+        out_shape=jax.ShapeDtypeStruct((shards, rows, D), jnp.bfloat16),
+        in_specs=[pl.BlockSpec(memory_space=pltpu.VMEM)],
+        out_specs=pl.BlockSpec(memory_space=pl.ANY),
+        scratch_shapes=[
+            pltpu.VMEM((shards, rows, D), jnp.bfloat16),
+            pltpu.SemaphoreType.DMA((gather_sends(sizes, halves),)),
+            pltpu.SemaphoreType.DMA((2, halves, shards)),
+            pltpu.SemaphoreType.DMA((shards,)),
+        ],
+        compiler_params=pltpu.CompilerParams(
+            collective_id=collective, has_side_effects=True, vmem_limit_bytes=VMEM_LIMIT
+        ),
+    )(rows_own)
+    return gathered.reshape(shards * rows, D)
+
+
+def scatter_rows(partial, sizes, collective):
+    shards = sizes[0] * sizes[1]
+    rows = partial.shape[0] // shards
+    cut, halves = gather_cut(sizes), 2
+    bufs, sems = scatter_scratch(sizes, halves, rows, D, cut)
+
+    def kernel(in_ref, out_ref, part_ref, in_sem, b0, b1, b2, b3, s0, s1, s2, s3, send_sems):
+        grid = Grid2(sizes)
+        copy = pltpu.make_async_copy(in_ref, part_ref, in_sem)
+        copy.start()
+        grid.barrier()
+        copy.wait()
+        sender = Sender(send_sems)
+        step = rows // halves
+
+        def part(slot, half, kind):
+            return part_ref.at[slot, pl.ds(half * step, step), columns_of(cut, kind)]
+
+        scatter = Scatter(
+            grid, sender, part, ((b0, b1), (b2, b3)), ((s0, s1), (s2, s3)), halves, cut
+        )
+        scatter.run(lambda slow, fast: None)
+        sender.finish()
+        out_ref[...] = part_ref[grid.index(*grid.me)].astype(jnp.float32)
+
+    return pl.pallas_call(
+        kernel,
+        out_shape=jax.ShapeDtypeStruct((rows, D), jnp.float32),
+        in_specs=[pl.BlockSpec(memory_space=pl.ANY)],
+        out_specs=pl.BlockSpec(memory_space=pltpu.VMEM),
+        scratch_shapes=[pltpu.VMEM((shards, rows, D), jnp.bfloat16), pltpu.SemaphoreType.DMA]
+        + bufs
+        + sems
+        + [pltpu.SemaphoreType.DMA((scatter_sends(sizes, halves),))],
+        compiler_params=pltpu.CompilerParams(
+            collective_id=collective, has_side_effects=True, vmem_limit_bytes=VMEM_LIMIT
+        ),
+    )(partial.reshape(shards, rows, D))
+
+
 def joined(value, axis, join):
-    pieces = jax.tree.map(lambda part: lax.all_gather(part, axis), value)
-    head = jax.tree.map(lambda part: part[0], pieces)
-    tail = jax.tree.map(lambda part: part[1:], pieces)
+    gathered = lax.all_gather(jnp.stack(value), axis)
+    pieces = tuple(gathered[:, i] for i in range(len(value)))
+    head = tuple(part[0] for part in pieces)
+    tail = tuple(part[1:] for part in pieces)
     so_far, _ = lax.scan(lambda so_far, piece: (join(so_far, piece), None), head, tail)
     return so_far
 
@@ -171,6 +560,7 @@
     head_weight,
 ):
     num_blocks = hidden.shape[0]
+    sizes = lines_of(lax.axis_size("seq"))
     shard_rows = hidden.shape[1]
     local_heads = qkv_weight.shape[1]
     local_vocab = head_weight.shape[1]
@@ -194,7 +584,7 @@
     block_num = 0
     own_rows = hidden[block_num].astype(jnp.float32)
     segment, position = segment_rows(lengths[block_num])
-    gathered = lax.all_gather(hidden[block_num], "seq", axis=0, tiled=True).astype(jnp.float32)
+    gathered = gather_rows(hidden[block_num], sizes, 0).astype(jnp.float32)
     first_norm, normed_one, inverse_one = norm_parts(gathered, gain_one, shift_one)
     second_norm, normed_two, inverse_two = norm_parts(gathered, gain_two, shift_two)
     first_full = first_norm.astype(jnp.bfloat16)
@@ -223,16 +613,13 @@
 
     stream = (
         own_rows
-        + lax.psum_scatter(
-            branch_term(jnp.int32(0), shard_rows * lax.axis_size("seq")),
-            "seq",
-            scatter_dimension=0,
-            tiled=True,
+        + scatter_rows(
+            branch_term(jnp.int32(0), BLOCK).astype(jnp.bfloat16), sizes, 1
         )
         + branch_float
     )
     final_norm, normed_final, inverse_final = norm_parts(stream, gain_final, shift_final)
-    final_full = lax.all_gather(final_norm.astype(jnp.bfloat16), "seq", axis=0, tiled=True)
+    final_full = gather_rows(final_norm.astype(jnp.bfloat16), sizes, 2)
     block_targets = targets[block_num]
 
     def logit_stats(row_block, final_full=final_full, block_targets=block_targets):
@@ -320,17 +707,12 @@
     def final_term(first_row, row_count, grad_logits=grad_logits):
         return jnp.einsum("nv,dv->nd", grad_logits, head_weight, preferred_element_type=jnp.float32)
 
-    grad_final = lax.psum_scatter(
-        final_term(jnp.int32(0), shard_rows * lax.axis_size("seq")),
-        "seq",
-        scatter_dimension=0,
-        tiled=True,
-    )
+    grad_final = scatter_rows(final_term(jnp.int32(0), BLOCK).astype(jnp.bfloat16), sizes, 3)
     grad_stream, part_gain, part_shift = norm_back(
         grad_final, kept["normed_final"], kept["inverse_final"], gain_final
     )
     branch_grad = jnp.sum(grad_stream, axis=0)
-    grad_full = lax.all_gather(grad_stream.astype(jnp.bfloat16), "seq", axis=0, tiled=True)
+    grad_full = gather_rows(grad_stream.astype(jnp.bfloat16), sizes, 4)
     out_grad = jnp.einsum(
         "nc,nd->cd", kept["context"], grad_full, preferred_element_type=jnp.float32
     )
@@ -380,9 +762,9 @@
     part_two, gain_part_two, shift_part_two = norm_back(
         grad_second, kept["normed_two"], kept["inverse_two"], gain_two
     )
-    grad_input = grad_stream + lax.psum_scatter(
-        (part_one + part_two).astype(jnp.bfloat16), "seq", scatter_dimension=0, tiled=True
-    ).astype(jnp.float32)
+    grad_input = grad_stream + scatter_rows(
+        (part_one + part_two).astype(jnp.bfloat16), sizes, 5
+    )
     outputs = [kept["stream"].astype(jnp.bfloat16)]
     input_grads = [grad_input]
     small_sums = lax.psum(

time: 2220 us -> 1630 us (0.73)
  waiting for transfers between devices: 1350 us -> 300 us
  Pallas kernels: 0 us -> 522 us
  blocking collectives: 146 us -> 90.2 us
    reduce_scatter x3 -> x0, waiting for transfers between devices: 683 us -> none  [the longest x1 281 us: per_device(): lax.psum_scatter(final_term(jnp.int32(0), shard_rows * lax.axis_size('seq...]
    pallas_call x0 -> x6, Pallas kernels: none -> 522 us  [the longest x3 261 us: scatter_rows(): pl.pallas_call(kernel, out_shape=jax.ShapeDtypeStruct((rows, D), jnp.floa...]
    all_gather x3 -> x0, waiting for transfers between devices: 326 us -> none  [the longest x1 124 us: per_device(): lax.all_gather(final_norm.astype(jnp.bfloat16), 'seq', axis=0, tiled=True)]
    all_gather x3 -> x1, blocking collectives: 91.5 us -> 32.3 us  [joined(): gathered = lax.all_gather(jnp.stack(value), axis)]
    psum x1, waiting for transfers between devices: 337 us -> 300 us  [per_device(): lax.psum(qkv_grad.astype(jnp.bfloat16), 'dp').astype(jnp.float32)]
  transfers between devices with their start and end apart: 7 -> 1, of which waited for: 7 -> 1; matrix products, arithmetic and copies ran while one was open for 6% -> 0% of each run, Pallas kernels for 0% -> 5%
where the time goes in v1:
time: 1630 us
  Pallas kernels  522 us (32%)
  matrix products  425 us (26%)
  waiting for transfers between devices  300 us (18%)
  other arithmetic  132 us (8%)
  local copies, waits for them, and re-layouts  121 us (7%)
  blocking collectives  90.2 us (6%)
  loops' own time  19.4 us (1%)
  between operations  16.3 us (1%)
    psum x1, waiting for transfers between devices, per_device(): lax.psum(qkv_grad.astype(jnp.bfloat16), 'dp').astype(jnp.float32)  300 us
    pallas_call x3, Pallas kernels, scatter_rows(): pl.pallas_call(kernel, out_shape=jax.ShapeDtypeStruct((rows, D), jnp.floa...  261 us
    pallas_call x3, Pallas kernels, gather_rows(): pl.pallas_call(kernel, out_shape=jax.ShapeDtypeStruct((shards, rows, D),...  260 us
    dot_general x4, matrix products, logit_grads(): logits = jnp.dot(rows_in, head_weight, preferred_element_type=jnp.float32)  56.1 us
    dot_general x4, matrix products, logit_stats(): logits = jnp.dot(rows_in, head_weight, preferred_element_type=jnp.float32)  46.9 us
    dynamic_update_slice x8, local copies, waits for them, and re-layouts, attention_forward(): lax.map(one_block, jnp.arange(BLOCK // ATT_BLK, dtype=jnp.int32))  45.8 us
    psum x1, blocking collectives, per_device(): lax.psum((gain_part_one, shift_part_one, gain_part_two, shift_part_two, p...  45.4 us
    dot_general x1, matrix products, per_device(): jnp.einsum('nd,nv->dv', kept['final_full'], grad_logits, preferred_elemen...  36.8 us
  transfers between devices with their start and end apart: 1, of which 1 were waited for; matrix products, arithmetic and copies ran while one was open for 0% of the time, Pallas kernels for 5%

profile of v1, /device:TPU:0, one launch (start us, length us, event | category | flops | bytes accessed | tf_op | source)
XLA Modules:
  0.0 1625.8 jit_solution(5675409215627851169)
XLA Ops:
  18.3 89.5 %shard_map.314 = bf16[8,256,2048]{2,1,0:T(8,128)(2,1)} custom-call(bf16[256,2048]{1,0:T(8,128)(2,1)} %bitcast.246), custom_call_target="tpu_custom_call" | custom-call | tf_op jit(solution)/shard_map/pallas_call | solution.py:349
  139.7 53.2 %while.67 = (s32[]{:T(128)}, bf16[4,512,2,128]{3,1,2,0:T(8,128)(2,1)}, f32[4,2,512]{2,1,0:T(2,128)}, s32[4]{0:T(128)S(1)}, s32[2048]{0:T(1024)S(1)}, /*index=5*/...) while((s32[]{:T(128)}, ...), condition=%wide.region_8.9_spmd, body=%wide.region_5.0_spmd.sunk | while | flops 1102052864 | bytes 40683776 | solution.py:491
  202.0 28.8 %multiply_convert_fusion.3 = (bf16[2048,1024]{1,0:T(8,128)(2,1)S(1)}, f32[2048,1024]{1,0:T(8,128)}, f32[2048,1024]{1,0:T(8,128)}) fusion(f32[1024]{0:T(1024)S(1)} %convert_element_type.182, bf16[2048,2048]{1,0:T(8,128)(2,1)S(1)} %add_convert_fusion.2, bf16[2048,1024]{1,0:T(8,128)(2,1)S(1)} %copy-done.69), kind=kOutput, calls=%fused_computation.88 | convolution fusion | flops 8728346624 | bytes 33558528 | tf_op jit(solution)/shard_map/dot_general | solution.py:606
  230.9 11.8 fusion.85
  242.7 11.4 add_convert_fusion.1
  254.0 85.1 %shard_map.315 = f32[256,2048]{1,0:T(8,128)} custom-call(bf16[8,256,2048]{2,1,0:T(8,128)(2,1)} %bitcast.236), custom_call_target="tpu_custom_call" | custom-call | tf_op jit(solution)/shard_map/pallas_call | solution.py:392
  345.3 85.8 %shard_map.316 = bf16[8,256,2048]{2,1,0:T(8,128)(2,1)} custom-call(bf16[256,2048]{1,0:T(8,128)(2,1)} %add_convert_fusion.5.own_ref), custom_call_target="tpu_custom_call" | custom-call | tf_op jit(solution)/shard_map/pallas_call | solution.py:349
  431.1 61.9 %while.69 = (s32[]{:T(128)}, f32[4,512]{1,0:T(4,128)S(1)}, f32[4,512]{1,0:T(4,128)S(1)}, f32[4,512]{1,0:T(4,128)S(1)}, s32[4]{0:T(128)S(1)}, /*index=5*/bf16[204...) while((s32[]{:T(128)}, f32[4,512]{1,0:T(4,128)S(1)}, ...), condition=%wide.region_15.16_spmd.clone, body=%wide.region_11.15_spmd.clone.sunk | while | flops 6989547520 | bytes 29413592 | solution.py:637
  432.5 11.7 fusion.152
  448.0 11.7 fusion.152
  463.5 11.7 fusion.152
  479.0 11.7 fusion.152
  493.2 32.3 %all-gather.1 = f32[8,3,2048]{2,1,0:T(4,128)S(1)} all-gather(f32[1,3,2048]{2,1,0:T(4,128)S(1)} %maximum_bitcast_fusion), channel_id=2, replica_groups=mesh['dp'=4,'seq'=8] {'seq'}, dimensions={0}, use_global_device_ids=true | all-gather | bytes 221184 | tf_op jit(solution)/shard_map/all_gather | solution.py:408
  535.2 62.0 %while.70 = (s32[]{:T(128)}, bf16[4,512,3328]{2,1,0:T(8,128)(2,1)}, s32[4]{0:T(128)S(1)}, f32[2048]{0:T(1024)S(1)}, s32[2048]{0:T(1024)S(1)}, /*index=5*/bf16[20...) while((s32[]{:T(128)}, bf16[4,512,3328]{2,1,0:T(8,128)(2,1)}, ...), condition=%wide.region_23.24_spmd.clone, body=%wide.region_22.23_spmd.clone.sunk | while | flops 6989549056 | bytes 19181784 | solution.py:700
  536.7 14.0 fusion.155
  552.2 14.0 fusion.155
  567.7 14.0 fusion.155
  583.2 14.0 fusion.155
  597.2 36.8 %convolution_convert_fusion = bf16[2048,3328]{1,0:T(8,128)(2,1)} fusion(bf16[2048,2048]{1,0:T(8,128)(2,1)} %get-tuple-element.1166, bf16[2048,3328]{1,0:T(8,128)(2,1)} %bitcast.277), kind=kOutput, calls=%fused_computation.80 | convolution fusion | flops 27924103168 | bytes 35651584 | tf_op jit(solution)/shard_map/nd,nv->dv/dot_general | solution.py:703
  634.0 32.3 %convolution_convert_fusion.1 = bf16[2048,2048]{1,0:T(8,128)(2,1)} fusion(bf16[2048,3328]{1,0:T(8,128)(2,1)} %bitcast.278, bf16[2048,3328]{1,0:T(8,128)(2,1)S(1)} %copy-done.67), kind=kOutput, calls=%fused_computation.102 | convolution fusion | flops 27921481728 | bytes 35651584 | tf_op jit(solution)/shard_map/nv,dv->nd/dot_general | solution.py:708
  666.4 88.3 %shard_map.317 = f32[256,2048]{1,0:T(8,128)} custom-call(bf16[8,256,2048]{2,1,0:T(8,128)(2,1)} %bitcast.242), custom_call_target="tpu_custom_call" | custom-call | tf_op jit(solution)/shard_map/pallas_call | solution.py:392
  763.2 85.3 %shard_map.318 = bf16[8,256,2048]{2,1,0:T(8,128)(2,1)} custom-call(bf16[256,2048]{1,0:T(8,128)(2,1)} %convert_element_type.192.own_ref), custom_call_target="tpu_custom_call" | custom-call | tf_op jit(solution)/shard_map/pallas_call | solution.py:349
  848.4 14.4 convolution_convert_fusion.2
  869.6 17.6 %fusion.72 = (bf16[1024]{0:T(1024)(128)(2,1)}, bf16[2048,1024]{1,0:T(8,128)(2,1)}) fusion(f32[2048,1024]{1,0:T(8,128)} %get-tuple-element.625, f32[2048,1024]{1,0:T(8,128)} %get-tuple-element.665, f32[1024]{0:T(1024)S(1)} %copy-done.62, bf16[2048,2048]{1,0:T(8,128)(2,1)S(1)} %bitcast.234, bf16[1024,2048]{1,0:T(8,128)(2,1)} %param.43), kind=kOutput, calls=%fused_computation.174 | convolution fusion | flops 8623488000 | bytes 33560576 | tf_op jit(solution)/shard_map/nd,fd->nf/dot_general | solution.py:727
  887.2 14.5 convolution_convert_fusion.3
  901.8 11.8 fusion.86
  913.6 144.7 %while.71 = (s32[]{:T(128)}, f32[2048,2,128]{0,2,1:T(8,128)}, f32[2048,2,128]{0,2,1:T(8,128)}, f32[4,512,2,128]{1,0,3,2:T(4,128)}, s32[4]{0:T(128)S(1)}, /*index...) while((s32[]{:T(128)}, f32[2048,2,128]{0,2,1:T(8,128)}, ...), condition=%wide.region_28.29_spmd.clone, body=%wide.region_26.28_spmd.clone.sunk | while | flops 2721709568 | bytes 82360616 | solution.py:525
  1088.9 20.1 %fusion.48 = (f32[2048]{0:T(1024)}, f32[2048]{0:T(1024)S(1)}, f32[2048]{0:T(1024)S(1)}, f32[2048]{0:T(1024)}, f32[2048]{0:T(1024)}, /*index=5*/f32[2048]{0:T(102...) fusion(bf16[8,256,2048]{2,1,0:T(8,128)(2,1)} %shard_map.314, f32[2048]{0:T(1024)S(1)} %bitcast.265, ...), kind=kOutput, calls=%fused_computation.67 | convolution fusion | flops 6513737728 | bytes 48332800 | tf_op jit(solution)/shard_map/nhe,dhe->nd/dot_general | solution.py:757
  1111.4 18.6 %add_convert_fusion = (bf16[2048,2048]{1,0:T(8,128)(2,1)}, bf16[2048,2048]{1,0:T(8,128)(2,1)}) fusion(bf16[8,256,2048]{2,1,0:T(8,128)(2,1)} %shard_map.314, f32[2048]{0:T(1024)S(1)} %copy-done.28, f32[2048]{0:T(1024)S(1)} %copy-done.26, f32[2048]{0:T(1024)S(1)} %bitcast.266, f32[2048]{0:T(1024)S(1)} %bitcast.263, f32[2048]{0:T(1024)} %broadcast_multiply_fusion.1, ...), kind=kLoop, calls=%fused_computation.71 | loop fusion | flops 71303168 | bytes 58793984 | tf_op jit(solution)/shard_map/convert_element_type | solution.py:590
  1150.5 87.7 %shard_map.319 = f32[256,2048]{1,0:T(8,128)} custom-call(bf16[8,256,2048]{2,1,0:T(8,128)(2,1)} %bitcast.235), custom_call_target="tpu_custom_call" | custom-call | tf_op jit(solution)/shard_map/pallas_call | solution.py:392
  1238.3 45.4 %all-reduce = (f32[2048]{0:T(1024)}, f32[2048]{0:T(1024)}, f32[2048]{0:T(1024)}, f32[2048]{0:T(1024)}, f32[2048]{0:T(1024)}, /*index=5*/f32[2048]{0:T(1024)}, f32[2048]{0:T(1024)}) all-reduce(f32[2048]{0:T(1024)S(1)} %copy-done.47, f32[2048]{0:T(1024)S(1)} %copy-done.48, ...), channel_id=1, replica_groups=mesh['dp'=4,'seq'=8] {'dp','seq'}, use_global_device_ids=true, to_apply=%region_34.35 | all-reduce | flops 14336 | bytes 114688 | tf_op jit(solution)/shard_map/psum | solution.py:770
  1286.8 299.6 %all-reduce.5.cloned.1.call-done = (bf16[2048,2,384]{2,0,1:T(8,128)(2,1)}, bf16[2,128,2048]{2,1,0:T(8,128)(2,1)}, bf16[2048,1024]{1,0:T(8,128)(2,1)}, bf16[1024,2048]{1,0:T(8,128)(2,1)}, bf16[2048,3328]{1,0:T(8,128)(2,1)}) async-done(((bf16[2048,2,384]{2,0,1:T(8,128)(2,1)}, bf16[2,128,2048]{2,1,0:T(8,128)(2,1)}, bf16[2048,1024]{1,0:T(8,128)(2,1)}, bf16[1024,2048]{1,0:T(8,128)(2,1)}, ...) | async-done | bytes 26214416 | tf_op jit(solution)/shard_map/psum | solution.py:783
  (436 shorter events, 370.6 us)
Async XLA Ops:
  7.2 235.5 %copy-start = (bf16[2,128,2048]{2,1,0:T(8,128)(2,1)S(1)}, bf16[2,128,2048]{2,1,0:T(8,128)(2,1)}, u32[]{:S(2)}) copy-start(bf16[2,128,2048]{2,1,0:T(8,128)(2,1)} %param.40) | copy-start | bytes 3145732
  7.2 1579.3 %all-reduce.5.cloned.1.call-start = ((), (), s32[]{:S(2)}) async-start(), calls=%async_computation | async-start | bytes 52428800 | tf_op jit(solution)/shard_map/psum | solution.py:783
  8.8 107.2 %copy-start.25 = (f32[2048]{0:T(1024)}, f32[2048]{0:T(1024)S(1)}, u32[]{:S(2)}) copy-start(f32[2048]{0:T(1024)S(1)} %convert_element_type.169) | copy-start | bytes 24580
  9.5 106.5 %copy-start.27 = (f32[2048]{0:T(1024)}, f32[2048]{0:T(1024)S(1)}, u32[]{:S(2)}) copy-start(f32[2048]{0:T(1024)S(1)} %convert_element_type.170) | copy-start | bytes 24580
  130.3 71.7 %copy-start.61 = (f32[1024]{0:T(1024)}, f32[1024]{0:T(1024)S(1)}, u32[]{:S(2)}) copy-start(f32[1024]{0:T(1024)S(1)} %convert_element_type.182) | copy-start | bytes 12292
  130.3 65.3 %copy-start.29 = (f32[2048]{0:T(1024)}, f32[2048]{0:T(1024)S(1)}, u32[]{:S(2)}) copy-start(f32[2048]{0:T(1024)S(1)} %convert_element_type.179) | copy-start | bytes 24580
  132.2 63.4 %copy-start.31 = (f32[1,2,8,128]{3,1,2,0:T(2,128)}, f32[1,2,8,128]{3,1,2,0:T(2,128)S(1)}, u32[]{:S(2)}) copy-start(f32[1,2,8,128]{3,1,2,0:T(2,128)S(1)} %copy.155) | copy-start | bytes 24580
  132.3 63.4 %copy-start.34 = (f32[1,2,8,128]{3,1,2,0:T(2,128)}, f32[1,2,8,128]{3,1,2,0:T(2,128)S(1)}, u32[]{:S(2)}) copy-start(f32[1,2,8,128]{3,1,2,0:T(2,128)S(1)} %copy.156) | copy-start | bytes 24580
  254.0 85.1 %copy-start.42 = (f32[2048]{0:T(1024)S(1)}, f32[2048]{0:T(1024)}, u32[]{:S(2)}) copy-start(f32[2048]{0:T(1024)} %convert_element_type.185) | copy-start | bytes 24580
  254.0 89.8 %copy-start.23 = (f32[2048]{0:T(1024)S(1)}, f32[2048]{0:T(1024)}, u32[]{:S(2)}) copy-start(f32[2048]{0:T(1024)} %convert_element_type.186) | copy-start | bytes 24580
  254.0 89.8 %copy-start.41 = (f32[2048]{0:T(1024)S(1)}, f32[2048]{0:T(1024)}, u32[]{:S(2)}) copy-start(f32[2048]{0:T(1024)} %convert_element_type.187) | copy-start | bytes 24580
  342.3 88.7 %copy-start.4 = (f32[256,2048]{1,0:T(8,128)}, f32[256,2048]{1,0:T(8,128)S(1)}, u32[]{:S(2)}) copy-start(f32[256,2048]{1,0:T(8,128)S(1)} %get-tuple-element.619) | copy-start | bytes 6291460
  342.3 88.7 %copy-start.37 = (s32[1,2048]{1,0:T(1,128)S(1)}, s32[1,2048]{1,0:T(1,128)}, u32[]{:S(2)}) copy-start(s32[1,2048]{1,0:T(1,128)} %param.30) | copy-start | bytes 24580
  342.3 88.7 %copy-start.51 = (f32[4,512]{1,0:T(4,128)S(1)}, f32[4,512]{1,0:T(4,128)}, u32[]{:S(2)}) copy-start(f32[4,512]{1,0:T(4,128)} %custom-call.6) | copy-start | bytes 24580
  342.3 88.7 %copy-start.52 = (f32[4,512]{1,0:T(4,128)S(1)}, f32[4,512]{1,0:T(4,128)}, u32[]{:S(2)}) copy-start(f32[4,512]{1,0:T(4,128)} %custom-call.5) | copy-start | bytes 24580
  342.4 88.7 %copy-start.53 = (f32[4,512]{1,0:T(4,128)S(1)}, f32[4,512]{1,0:T(4,128)}, u32[]{:S(2)}) copy-start(f32[4,512]{1,0:T(4,128)} %custom-call.4) | copy-start | bytes 24580
  431.1 95.3 %copy-start.17 = (s32[2048]{0:T(1024)S(1)}, s32[2048]{0:T(1024)}, u32[]{:S(2)}) copy-start(s32[2048]{0:T(1024)} %copy-done.16) | copy-start | bytes 24580
  431.1 95.5 %copy-start.55 = (s32[1,8]{1,0:T(1,128)S(1)}, s32[1,8]{1,0:T(1,128)}, u32[]{:S(2)}) copy-start(s32[1,8]{1,0:T(1,128)} %param.31) | copy-start | bytes 100
  431.1 95.5 %copy-start.65 = (f32[1,8]{1,0:T(1,128)S(1)}, f32[1,8]{1,0:T(1,128)}, u32[]{:S(2)}) copy-start(f32[1,8]{1,0:T(1,128)} %param.33) | copy-start | bytes 100
  431.1 103.4 %copy-start.66 = (s32[1,8]{1,0:T(1,128)S(1)}, s32[1,8]{1,0:T(1,128)}, u32[]{:S(2)}) copy-start(s32[1,8]{1,0:T(1,128)} %param.32) | copy-start | bytes 100
  666.4 88.3 %copy-start.5 = (f32[256,2048]{1,0:T(8,128)S(1)}, f32[256,2048]{1,0:T(8,128)}, u32[]{:S(2)}) copy-start(f32[256,2048]{1,0:T(8,128)} %copy-done.4) | copy-start | bytes 6291460
  666.4 88.3 %copy-start.24 = (f32[2048]{0:T(1024)S(1)}, f32[2048]{0:T(1024)}, u32[]{:S(2)}) copy-start(f32[2048]{0:T(1024)} %convert_element_type.186) | copy-start | bytes 24580
  666.4 88.3 %copy-start.44 = (f32[256]{0:T(256)S(1)}, f32[256]{0:T(256)}, u32[]{:S(2)}) copy-start(f32[256]{0:T(256)} %copy-done.43) | copy-start | bytes 3076
  666.4 88.3 %copy-start.46 = (f32[256]{0:T(256)S(1)}, f32[256]{0:T(256)}, u32[]{:S(2)}) copy-start(f32[256]{0:T(256)} %copy-done.45) | copy-start | bytes 3076
  1140.8 97.4 %copy-start.38 = (f32[2048]{0:T(1024)S(1)}, f32[2048]{0:T(1024)}, u32[]{:S(2)}) copy-start(f32[2048]{0:T(1024)} %get-tuple-element.502) | copy-start | bytes 24580
  1140.8 97.4 %copy-start.39 = (f32[2048]{0:T(1024)S(1)}, f32[2048]{0:T(1024)}, u32[]{:S(2)}) copy-start(f32[2048]{0:T(1024)} %get-tuple-element.505) | copy-start | bytes 24580
  1140.8 97.4 %copy-start.40 = (f32[2048]{0:T(1024)S(1)}, f32[2048]{0:T(1024)}, u32[]{:S(2)}) copy-start(f32[2048]{0:T(1024)} %get-tuple-element.614) | copy-start | bytes 24580
  1140.9 97.4 %copy-start.47 = (f32[2048]{0:T(1024)S(1)}, f32[2048]{0:T(1024)}, u32[]{:S(2)}) copy-start(f32[2048]{0:T(1024)} %get-tuple-element.492) | copy-start | bytes 24580
  1140.9 97.4 %copy-start.48 = (f32[2048]{0:T(1024)S(1)}, f32[2048]{0:T(1024)}, u32[]{:S(2)}) copy-start(f32[2048]{0:T(1024)} %get-tuple-element.497) | copy-start | bytes 24580
  1140.9 97.4 %copy-start.49 = (f32[2048]{0:T(1024)S(1)}, f32[2048]{0:T(1024)}, u32[]{:S(2)}) copy-start(f32[2048]{0:T(1024)} %get-tuple-element.498) | copy-start | bytes 24580
  1140.9 97.4 %copy-start.50 = (f32[2048]{0:T(1024)S(1)}, f32[2048]{0:T(1024)}, u32[]{:S(2)}) copy-start(f32[2048]{0:T(1024)} %get-tuple-element.501) | copy-start | bytes 24580
  1140.9 142.8 %copy-start.8 = (f32[256,2048]{1,0:T(8,128)S(1)}, f32[256,2048]{1,0:T(8,128)}, u32[]{:S(2)}) copy-start(f32[256,2048]{1,0:T(8,128)} %copy-done.7) | copy-start | bytes 6291460
  (52 other events, 606.6 us)
Sparse Core Ops, SparseCore 0:
  1140.9 445.4 all-reduce.4

commit v2 on v1

v2 whole, which is shorter than its diff:
```python
import jax
import jax.numpy as jnp
from jax import lax
from jax.experimental import pallas as pl
from jax.experimental.pallas import tpu as pltpu
from jax.sharding import PartitionSpec as P

D = 2048
HEAD_DIM = 128
ROT = 32
BLOCK = 2048
EXB = 8
EPSILON = 1e-05
BETA = 0.25
LOSS_SCALE = 65536.0
HALVES = 2
VMEM_LIMIT = 62 * 2**20

MESH = pl.DeviceIdType.MESH


class Grid2:
    def __init__(self, sizes):
        self.n = sizes
        place = lax.axis_index("seq")
        self.me = (place // sizes[1], lax.rem(place, sizes[1]))

    def index(self, slow, fast):
        return slow * self.n[1] + fast

    def device(self, axis, spot):
        here = list(self.me)
        here[axis] = spot
        return {"seq": self.index(*here)}

    def nearest(self, axis, rank):
        n, m = self.n[axis], self.me[axis]
        if rank == 0:
            return m
        if n == 2:
            return 1 - m
        after = n - 1 - m
        both = jnp.minimum(m, after)
        dist = (rank + 1) // 2
        near = m - dist if rank % 2 else m + dist
        far = jnp.where(m < after, m + (rank - both), m - (rank - both))
        return jnp.where(rank <= 2 * both, near, far)

    def neighbours(self):
        found = []
        for axis in (0, 1):
            m, n = self.me[axis], self.n[axis]
            if n == 2:
                found.append((None, self.device(axis, 1 - m)))
            elif n > 2:
                found.append((m > 0, self.device(axis, m - 1)))
                found.append((m < n - 1, self.device(axis, m + 1)))
        return found

    def barrier(self):
        sem = pltpu.get_barrier_semaphore()
        amount = jnp.int32(0)
        for there, device in self.neighbours():
            def tell(device=device):
                pl.semaphore_signal(sem, inc=1, device_id=device, device_id_type=MESH)
            if there is None:
                tell()
                amount = amount + 1
            else:
                pl.when(there)(tell)
                amount = amount + there.astype(jnp.int32)
        pl.semaphore_wait(sem, amount)


class Sender:
    def __init__(self, send_sems):
        self.sems = send_sems
        self.used = 0
        self.open = []

    def send(self, src, dst, recv_sem, device, when=None):
        copy = pltpu.make_async_remote_copy(
            src_ref=src, dst_ref=dst, send_sem=self.sems.at[self.used], recv_sem=recv_sem,
            device_id=device, device_id_type=MESH)
        self.used += 1
        if when is None:
            copy.start()
        else:
            pl.when(when)(copy.start)
        self.open.append((when, copy))

    def finish(self):
        for when, copy in self.open:
            if when is None:
                copy.wait_send()
            else:
                pl.when(when)(copy.wait_send)
        self.open = []


def gather_sends(sizes, halves):
    return halves * 2 * (sizes[0] * sizes[1] * 2 + 8)


def gather_rounds(grid, sender, piece, recv_sems, halves, cut, ready):
    n, me = grid.n, grid.me

    def arrived(slow, fast, half, kind):
        ref = piece(grid.index(slow, fast), half, kind)
        sem = recv_sems.at[kind, half, grid.index(slow, fast)]
        pltpu.make_async_copy(ref, ref, sem).wait()

    def push(slow, fast, half, kind, axis, spot, when):
        ref = piece(grid.index(slow, fast), half, kind)
        sem = recv_sems.at[kind, half, grid.index(slow, fast)]
        sender.send(ref, ref, sem, grid.device(axis, spot), when)

    def spread(slow, fast, half, kind, axis):
        m, size = me[axis], n[axis]
        if size == 2:
            push(slow, fast, half, kind, axis, 1 - m, None)
        elif size > 2:
            push(slow, fast, half, kind, axis, m + 1, m < size - 1)
            push(slow, fast, half, kind, axis, m - 1, m > 0)

    def onward(slow, fast, half, kind, axis):
        m, size = me[axis], n[axis]
        if size <= 2:
            return
        source = (slow, fast)[axis]
        below = source < m
        when = (below & (m < size - 1)) | (jnp.logical_not(below) & (m > 0))
        push(slow, fast, half, kind, axis, jnp.where(below, m + 1, m - 1), when)

    todo = []

    def work(count=1):
        for _ in range(count):
            if todo:
                ready(*todo.pop(0))

    def settle(k):
        slow = grid.nearest(0, k)
        for half in range(halves):
            for l in range(n[1]):
                fast = grid.nearest(1, l)
                if k > 0:
                    arrived(slow, fast, half, 1)
                    onward(slow, fast, half, 1, 0)
                else:
                    spread(slow, fast, half, 1, 0)

    def complete(k):
        slow = grid.nearest(0, k)
        if k > 0:
            todo.append((slow, me[1], k * n[1]))
        for l in range(1, n[1]):
            fast = grid.nearest(1, l)
            if cut[0]:
                for half in range(halves):
                    arrived(slow, fast, half, 0)
                    onward(slow, fast, half, 0, 1)
            todo.append((slow, fast, k * n[1] + l))

    for half in range(halves):
        for kind in (1, 0):
            if cut[kind]:
                spread(me[0], me[1], half, kind, kind)
        if cut[0]:
            spread(me[0], me[1], half, 0, 1)
    todo.append((me[0], me[1], 0))
    work()
    if cut[1]:
        for half in range(halves):
            for l in range(1, n[1]):
                fast = grid.nearest(1, l)
                arrived(me[0], fast, half, 1)
                onward(me[0], fast, half, 1, 1)
    for k in range(1, n[0]):
        slow = grid.nearest(0, k)
        for half in range(halves):
            if cut[0]:
                arrived(slow, me[1], half, 0)
                onward(slow, me[1], half, 0, 0)
                spread(slow, me[1], half, 0, 1)
            if half < halves - 1:
                work()
        if cut[1]:
            settle(k - 1)
        complete(k - 1)
        work()
    if cut[1]:
        settle(n[0] - 1)
    work(len(todo))
    complete(n[0] - 1)
    work(len(todo))


def scatter_slots(n):
    return 1 if n == 2 else n + 1


class Scatter:
    def __init__(self, grid, sender, part, bufs, sems, halves, cut):
        self.grid, self.sender, self.part = grid, sender, part
        self.bufs, self.sems, self.halves, self.cut = bufs, sems, halves, cut

    def slot(self, axis, target, from_below):
        if self.grid.n[axis] == 2:
            return 0
        return target + jnp.where(from_below, 1, 0)

    def take(self, kind, stage, axis, other, target, from_below, half, when, slot_index):
        buf, sem = self.bufs[kind][stage], self.sems[kind][stage]
        slot = self.slot(axis, target, from_below)

        def add():
            ref = buf.at[other, slot, half]
            pltpu.make_async_copy(ref, ref, sem.at[other, slot, half]).wait()
            mine = self.part(slot_index, half, kind)
            mine[...] = (mine[...].astype(jnp.float32) + ref[...].astype(jnp.float32)).astype(mine.dtype)

        if when is None:
            add()
        else:
            pl.when(when)(add)

    def toward(self, kind, stage, axis, other, target, half, slow, fast):
        grid = self.grid
        m, n = grid.me[axis], grid.n[axis]
        up = target > m
        index = grid.index(slow, fast)
        if n > 2:
            incoming = (up & (m > 0)) | (jnp.logical_not(up) & (m < n - 1))
            self.take(kind, stage, axis, other, target, up, half, incoming, index)
        buf, sem = self.bufs[kind][stage], self.sems[kind][stage]
        slot = self.slot(axis, target, up)
        spot = 1 - m if n == 2 else jnp.where(up, m + 1, m - 1)
        self.sender.send(
            self.part(index, half, kind), buf.at[other, slot, half], sem.at[other, slot, half],
            grid.device(axis, spot))

    def last(self, kind, stage, axis, other, half, slow, fast):
        grid = self.grid
        m, n = grid.me[axis], grid.n[axis]
        index = grid.index(slow, fast)
        if n == 2:
            self.take(kind, stage, axis, other, m, m > 0, half, None, index)
        elif n > 2:
            self.take(kind, stage, axis, other, m, jnp.bool_(True), half, m > 0, index)
            self.take(kind, stage, axis, other, m, jnp.bool_(False), half, m < n - 1, index)

    def run(self, produce):
        grid, n, me = self.grid, self.grid.n, self.grid.me
        for k in reversed(range(n[0])):
            slow = grid.nearest(0, k)
            for l in reversed(range(n[1])):
                fast = grid.nearest(1, l)
                produce(slow, fast)
                for half in range(self.halves):
                    if self.cut[0] and l > 0:
                        self.toward(0, 0, 1, slow, fast, half, slow, fast)
                    if self.cut[1] and k > 0:
                        self.toward(1, 0, 0, fast, slow, half, slow, fast)
        if self.cut[1]:
            for half in range(self.halves):
                for l in reversed(range(n[1])):
                    fast = grid.nearest(1, l)
                    self.last(1, 0, 0, fast, half, me[0], fast)
                    if l > 0:
                        self.toward(1, 1, 1, 0, fast, half, me[0], fast)
        if self.cut[0]:
            for k in reversed(range(1, n[0])):
                slow = grid.nearest(0, k)
                for half in range(self.halves):
                    self.last(0, 0, 1, slow, half, slow, me[1])
                    self.toward(0, 1, 0, 0, slow, half, slow, me[1])
            for half in range(self.halves):
                self.last(0, 0, 1, me[0], half, me[0], me[1])
        for half in range(self.halves):
            if self.cut[1]:
                self.last(1, 1, 1, 0, half, me[0], me[1])
            if self.cut[0]:
                self.last(0, 1, 0, 0, half, me[0], me[1])


def scatter_scratch(sizes, halves, rows, cols, cut):
    bufs, sems = [], []
    for kind, stages in ((0, (1, 0)), (1, (0, 1))):
        for stage, axis in enumerate(stages):
            lead = (sizes[1 - axis] if stage == 0 else 1, scatter_slots(sizes[axis]), halves)
            width = max(cut[kind], 128)
            bufs.append(pltpu.VMEM(lead + (rows // halves, width), jnp.bfloat16))
            sems.append(pltpu.SemaphoreType.DMA(lead))
    return bufs, sems


def scatter_sends(sizes, halves):
    return halves * 2 * (sizes[0] * sizes[1] + sizes[0] + sizes[1])


def lines_of(seq):
    fast = 2 if seq <= 8 else 4
    return (seq // fast, fast)


ATT_TILE = 256
SCALE = HEAD_DIM ** (-0.5)


def dot_nt(left, right):
    return lax.dot_general(left, right, (((1,), (1,)), ((), ())), preferred_element_type=jnp.float32)


def dot_tn(left, right):
    return lax.dot_general(left, right, (((0,), (0,)), ((), ())), preferred_element_type=jnp.float32)


def rotary_planes(position):
    half_rot = ROT // 2
    frequency = 10000.0 ** (-2.0 * jnp.arange(half_rot, dtype=jnp.float32) / ROT)
    angles = position.astype(jnp.float32)[:, None] * frequency[None, :]
    cos, sin = jnp.cos(angles), jnp.sin(angles)
    rows = position.shape[0]
    rest = jnp.zeros((rows, HEAD_DIM - ROT), jnp.float32)
    none = jnp.zeros_like(sin)
    return (
        jnp.concatenate([cos, cos, rest + 1.0], axis=1),
        jnp.concatenate([none, sin, rest], axis=1),
        jnp.concatenate([-sin, none, rest], axis=1),
    )


def turn(vector, cos, from_below, from_above):
    half_rot = ROT // 2
    return (
        vector * cos
        + pltpu.roll(vector, half_rot, 1) * from_below
        + pltpu.roll(vector, HEAD_DIM - half_rot, 1) * from_above
    )


def tile_mask(start_col, query_tile, key_tile):
    shape = (ATT_TILE, ATT_TILE)
    query_ids = query_tile * ATT_TILE + lax.broadcasted_iota(jnp.int32, shape, 0)
    key_ids = key_tile * ATT_TILE + lax.broadcasted_iota(jnp.int32, shape, 1)
    return (key_ids >= start_col) & (key_ids <= query_ids)


def attention_forward(qkv, start_col, first_tile, heads):
    tiles = BLOCK // ATT_TILE

    def kernel(first_ref, q_ref, k_ref, v_ref, start_ref, ctx_ref, lse_ref):
        tile = pl.program_id(1)
        queries = q_ref[...]
        start = start_ref[...]

        def step(key_tile, carry):
            top, total, acc = carry
            rows = pl.ds(pl.multiple_of(key_tile * ATT_TILE, ATT_TILE), ATT_TILE)
            scores = dot_nt(queries, k_ref[rows, :]) * SCALE
            scores = jnp.where(tile_mask(start, tile, key_tile), scores, -1e30)
            new_top = jnp.maximum(top, jnp.max(scores, axis=1, keepdims=True))
            shrink = jnp.exp(top - new_top)
            weights = jnp.exp(scores - new_top)
            total = total * shrink + jnp.sum(weights, axis=1, keepdims=True)
            acc = acc * shrink + jnp.dot(
                weights.astype(jnp.bfloat16), v_ref[rows, :], preferred_element_type=jnp.float32
            )
            return (new_top, total, acc)

        begin = (
            jnp.full((ATT_TILE, 1), -1e30, jnp.float32),
            jnp.zeros((ATT_TILE, 1), jnp.float32),
            jnp.zeros((ATT_TILE, HEAD_DIM), jnp.float32),
        )
        begin = step(tile, begin)
        top, total, acc = lax.fori_loop(first_ref[tile], tile, step, begin)
        ctx_ref[...] = (acc / total).astype(jnp.bfloat16)
        lse_ref[...] = top + jnp.log(total)

    return pl.pallas_call(
        kernel,
        grid_spec=pltpu.PrefetchScalarGridSpec(
            num_scalar_prefetch=1,
            grid=(heads, tiles),
            in_specs=[
                pl.BlockSpec((ATT_TILE, HEAD_DIM), lambda h, i, first: (i, 3 * h)),
                pl.BlockSpec((BLOCK, HEAD_DIM), lambda h, i, first: (0, 3 * h + 1)),
                pl.BlockSpec((BLOCK, HEAD_DIM), lambda h, i, first: (0, 3 * h + 2)),
                pl.BlockSpec((ATT_TILE, 1), lambda h, i, first: (i, 0)),
            ],
            out_specs=[
                pl.BlockSpec((ATT_TILE, HEAD_DIM), lambda h, i, first: (i, h)),
                pl.BlockSpec((pl.squeezed, ATT_TILE, 1), lambda h, i, first: (h, i, 0)),
            ],
        ),
        out_shape=[
            jax.ShapeDtypeStruct((BLOCK, heads * HEAD_DIM), jnp.bfloat16),
            jax.ShapeDtypeStruct((heads, BLOCK, 1), jnp.float32),
        ],
        compiler_params=pltpu.CompilerParams(vmem_limit_bytes=VMEM_LIMIT),
    )(first_tile, qkv, qkv, qkv, start_col)


def attention_backward(qkv, start_col, first_tile, heads, ctx, lse, grad_ctx, planes):
    tiles = BLOCK // ATT_TILE

    def kernel(
        first_ref, q_ref, k_ref, v_ref, start_ref, ctx_ref, lse_ref, do_ref, cos_ref, below_ref,
        above_ref, out_ref, sums_ref, dk_ref, dv_ref,
    ):
        tile = pl.program_id(1)

        @pl.when(tile == 0)
        def _():
            dk_ref[...] = jnp.zeros_like(dk_ref)
            dv_ref[...] = jnp.zeros_like(dv_ref)

        queries = q_ref[...]
        start = start_ref[...]
        grads = do_ref[...]
        lse_rows = lse_ref[...]
        inner = jnp.sum(
            grads.astype(jnp.float32) * ctx_ref[...].astype(jnp.float32), axis=1, keepdims=True
        )

        def step(key_tile, dq):
            rows = pl.ds(pl.multiple_of(key_tile * ATT_TILE, ATT_TILE), ATT_TILE)
            keys = k_ref[rows, :]
            scores = dot_nt(queries, keys) * SCALE
            probs = jnp.where(
                tile_mask(start, tile, key_tile), jnp.exp(scores - lse_rows), 0.0
            )
            grad_probs = dot_nt(grads, v_ref[rows, :])
            grad_scores = (probs * (grad_probs - inner)).astype(jnp.bfloat16)
            dv_ref[rows, :] += dot_tn(probs.astype(jnp.bfloat16), grads)
            dk_ref[rows, :] += dot_tn(grad_scores, queries)
            return dq + jnp.dot(grad_scores, keys, preferred_element_type=jnp.float32)

        dq = lax.fori_loop(
            first_ref[tile], tile + 1, step, jnp.zeros((ATT_TILE, HEAD_DIM), jnp.float32)
        )
        here = pl.ds(pl.multiple_of(tile * ATT_TILE, ATT_TILE), ATT_TILE)
        out_ref[here, :HEAD_DIM] = turn(
            dq * SCALE, cos_ref[here, :], -below_ref[here, :], -above_ref[here, :]
        ).astype(jnp.bfloat16)

        @pl.when(tile == tiles - 1)
        def _():
            def finish(index, sums):
                rows = pl.ds(pl.multiple_of(index * ATT_TILE, ATT_TILE), ATT_TILE)
                out_ref[rows, HEAD_DIM : 2 * HEAD_DIM] = turn(
                    dk_ref[rows, :] * SCALE, cos_ref[rows, :], -below_ref[rows, :], -above_ref[rows, :]
                ).astype(jnp.bfloat16)
                out_ref[rows, 2 * HEAD_DIM :] = dv_ref[rows, :].astype(jnp.bfloat16)
                return sums + jnp.sum(out_ref[rows, :].astype(jnp.float32), axis=0, keepdims=True)

            sums_ref[...] = lax.fori_loop(
                0, tiles, finish, jnp.zeros((1, 3 * HEAD_DIM), jnp.float32)
            )

    whole = pl.BlockSpec((BLOCK, HEAD_DIM), lambda h, i, first: (0, 0))
    return pl.pallas_call(
        kernel,
        grid_spec=pltpu.PrefetchScalarGridSpec(
            num_scalar_prefetch=1,
            grid=(heads, tiles),
            in_specs=[
                pl.BlockSpec((ATT_TILE, HEAD_DIM), lambda h, i, first: (i, 3 * h)),
                pl.BlockSpec((BLOCK, HEAD_DIM), lambda h, i, first: (0, 3 * h + 1)),
                pl.BlockSpec((BLOCK, HEAD_DIM), lambda h, i, first: (0, 3 * h + 2)),
                pl.BlockSpec((ATT_TILE, 1), lambda h, i, first: (i, 0)),
                pl.BlockSpec((ATT_TILE, HEAD_DIM), lambda h, i, first: (i, h)),
                pl.BlockSpec((pl.squeezed, ATT_TILE, 1), lambda h, i, first: (h, i, 0)),
                pl.BlockSpec((ATT_TILE, HEAD_DIM), lambda h, i, first: (i, h)),
                whole,
                whole,
                whole,
            ],
            out_specs=[
                pl.BlockSpec((BLOCK, 3 * HEAD_DIM), lambda h, i, first: (0, h)),
                pl.BlockSpec((pl.squeezed, 1, 3 * HEAD_DIM), lambda h, i, first: (h, 0, 0)),
            ],
            scratch_shapes=[
                pltpu.VMEM((BLOCK, HEAD_DIM), jnp.float32),
                pltpu.VMEM((BLOCK, HEAD_DIM), jnp.float32),
            ],
        ),
        out_shape=[
            jax.ShapeDtypeStruct((BLOCK, heads * 3 * HEAD_DIM), jnp.bfloat16),
            jax.ShapeDtypeStruct((heads, 1, 3 * HEAD_DIM), jnp.float32),
        ],
        compiler_params=pltpu.CompilerParams(vmem_limit_bytes=VMEM_LIMIT),
    )(first_tile, qkv, qkv, qkv, start_col, ctx, lse, grad_ctx, *planes)


def gather_cut(sizes):
    if sizes[0] == 4 and sizes[1] == 2:
        return (1664, 384)
    return (D // 2, D // 2)


def columns_of(cut, kind):
    return pl.ds(0, cut[0]) if kind == 0 else pl.ds(cut[0], cut[1])


def tile_of(width):
    return 256 if width % 256 == 0 else 128


def span(index, size):
    return pl.ds(pl.multiple_of(index * size, size), size)


ANY = pl.BlockSpec(memory_space=pl.ANY)
VMEM = pl.BlockSpec(memory_space=pltpu.VMEM)


def row_kernel(kernel, collective, out_shape, in_specs, out_specs, scratch, cost):
    return pl.pallas_call(
        kernel,
        out_shape=out_shape,
        in_specs=in_specs,
        out_specs=out_specs,
        scratch_shapes=scratch,
        cost_estimate=pl.CostEstimate(flops=cost, bytes_accessed=2**25, transcendentals=0),
        compiler_params=pltpu.CompilerParams(
            collective_id=collective, has_side_effects=True, vmem_limit_bytes=VMEM_LIMIT
        ),
    )


def gather_scratch(sizes, rows):
    shards = sizes[0] * sizes[1]
    return [
        pltpu.VMEM((shards, rows, D), jnp.bfloat16),
        pltpu.SemaphoreType.DMA((gather_sends(sizes, HALVES),)),
        pltpu.SemaphoreType.DMA((2, HALVES, shards)),
    ]


def run_gather(grid, sizes, rows, full, send_sems, recv_sems, ready):
    cut = gather_cut(sizes)
    step = rows // HALVES
    sender = Sender(send_sems)

    def piece(slot, half, kind):
        return full.at[slot, pl.ds(half * step, step), columns_of(cut, kind)]

    gather_rounds(grid, sender, piece, recv_sems, HALVES, cut, ready)
    sender.finish()


def sum_scratch(sizes, rows):
    shards = sizes[0] * sizes[1]
    bufs, sems = scatter_scratch(sizes, HALVES, rows, D, gather_cut(sizes))
    return (
        [pltpu.VMEM((shards, rows, D), jnp.bfloat16)]
        + bufs
        + sems
        + [pltpu.SemaphoreType.DMA((scatter_sends(sizes, HALVES),))]
    )


def run_scatter(grid, sizes, rows, scratch, produce):
    cut = gather_cut(sizes)
    step = rows // HALVES
    parts, b0, b1, b2, b3, s0, s1, s2, s3, send_sems = scratch
    sender = Sender(send_sems)

    def part(slot, half, kind):
        return parts.at[slot, pl.ds(half * step, step), columns_of(cut, kind)]

    scatter = Scatter(
        grid, sender, part, ((b0, b1), (b2, b3)), ((s0, s1), (s2, s3)), HALVES, cut
    )
    scatter.run(produce)
    sender.finish()


def production_order(grid):
    return [
        grid.index(grid.nearest(0, k), grid.nearest(1, l))
        for k in reversed(range(grid.n[0]))
        for l in reversed(range(grid.n[1]))
    ]


ROW_TILE = 32


def tile_stats(values):
    centered = values - jnp.mean(values, axis=1, keepdims=True)
    inverse = lax.rsqrt(jnp.mean(centered * centered, axis=1, keepdims=True) + EPSILON)
    return centered, inverse


def open_rows(own, sizes, collective, norms, qkv_flat, qkv_bias, up_weight, up_bias, planes):
    rows = own.shape[0]
    shards = sizes[0] * sizes[1]
    width, hidden = qkv_flat.shape[1], up_weight.shape[1]
    heads = width // (3 * HEAD_DIM)

    def kernel(
        own_ref, norms_ref, qkvw_any, qkvb_ref, upw_any, upb_ref, cos_ref, below_ref, above_ref,
        hid_any, one_any, two_any, qkv_any, act_any, slope_any,
        full, send_sems, recv_sems, qkvw, upw, load_sems, one, two, qkv, act, slope, out_sems, row_sems,
    ):
        grid = Grid2(sizes)
        loads = [
            pltpu.make_async_copy(qkvw_any, qkvw, load_sems.at[0]),
            pltpu.make_async_copy(upw_any, upw, load_sems.at[1]),
        ]
        for copy in loads:
            copy.start()
        full[grid.index(*grid.me)] = own_ref[...]
        grid.barrier()
        open_copies = []

        def outs(place, slot):
            pairs = ((one, one_any), (two, two_any), (qkv, qkv_any), (act, act_any), (slope, slope_any))
            return [
                pltpu.make_async_copy(here.at[slot], there.at[place], out_sems.at[slot, i])
                for i, (here, there) in enumerate(pairs)
            ]

        def ready(slow, fast, order):
            place = grid.index(slow, fast)
            slot = order % 2
            if order == 0:
                for copy in loads:
                    copy.wait()
            if order >= 2:
                for copy in open_copies.pop(0):
                    copy.wait()

            def norm_tile(index, _):
                here = span(index, ROW_TILE)
                centered, inverse = tile_stats(full[place, here].astype(jnp.float32))
                normed = centered * inverse
                one[slot, here] = (normed * norms_ref[0:1] + norms_ref[1:2]).astype(jnp.bfloat16)
                two[slot, here] = (normed * norms_ref[2:3] + norms_ref[3:4]).astype(jnp.bfloat16)
                return _

            lax.fori_loop(0, rows // ROW_TILE, norm_tile, 0)
            places = pl.ds(pl.multiple_of(place * rows, rows), rows)
            cos, below, above = cos_ref[places, :], below_ref[places, :], above_ref[places, :]
            for head in range(heads):
                first = head * 3 * HEAD_DIM
                found = jnp.dot(
                    one[slot], qkvw[:, first : first + 3 * HEAD_DIM], preferred_element_type=jnp.float32
                ) + qkvb_ref[:, first : first + 3 * HEAD_DIM]
                qkv[slot, :, first : first + HEAD_DIM] = turn(
                    found[:, :HEAD_DIM], cos, below, above
                ).astype(jnp.bfloat16)
                qkv[slot, :, first + HEAD_DIM : first + 2 * HEAD_DIM] = turn(
                    found[:, HEAD_DIM : 2 * HEAD_DIM], cos, below, above
                ).astype(jnp.bfloat16)
                qkv[slot, :, first + 2 * HEAD_DIM : first + 3 * HEAD_DIM] = found[
                    :, 2 * HEAD_DIM :
                ].astype(jnp.bfloat16)
            tile = tile_of(hidden)

            def up_tile(index, _):
                here = span(index, tile)
                pre = jnp.dot(two[slot], upw[:, here], preferred_element_type=jnp.float32) + upb_ref[:, here]
                share = 0.5 * (1.0 + lax.erf(pre * 0.7071067811865476))
                act[slot, :, here] = (pre * share).astype(jnp.bfloat16)
                slope[slot, :, here] = (
                    share + pre * (jnp.exp(-0.5 * pre * pre) * 0.3989422804014327)
                ).astype(jnp.bfloat16)
                return _

            lax.fori_loop(0, hidden // tile, up_tile, 0)
            copies = outs(place, slot)
            for copy in copies:
                copy.start()
            open_copies.append(copies)
            raw = pltpu.make_async_copy(full.at[place], hid_any.at[place], row_sems.at[order])
            raw.start()
            raw_copies.append(raw)

        raw_copies = []
        run_gather(grid, sizes, rows, full, send_sems, recv_sems, ready)
        for copies in open_copies:
            for copy in copies:
                copy.wait()
        for copy in raw_copies:
            copy.wait()

    def out(columns):
        return jax.ShapeDtypeStruct((shards, rows, columns), jnp.bfloat16)

    def staged(columns):
        return pltpu.VMEM((2, rows, columns), jnp.bfloat16)

    return row_kernel(
        kernel, collective,
        [out(D), out(D), out(D), out(width), out(hidden), out(hidden)],
        [VMEM, VMEM, ANY, VMEM, ANY, VMEM, VMEM, VMEM, VMEM],
        [ANY] * 6,
        gather_scratch(sizes, rows)
        + [
            pltpu.VMEM(qkv_flat.shape, jnp.bfloat16),
            pltpu.VMEM(up_weight.shape, jnp.bfloat16),
            pltpu.SemaphoreType.DMA((2,)),
            staged(D), staged(D), staged(width), staged(hidden), staged(hidden),
            pltpu.SemaphoreType.DMA((2, 5)),
            pltpu.SemaphoreType.DMA((shards,)),
        ],
        2 * BLOCK * D * (width + hidden),
    )(own, norms, qkv_flat, qkv_bias, up_weight, up_bias, *planes)


def branch_rows(own, ctx, act, out_flat, down_weight, norms, sizes, collective):
    rows = own.shape[0]
    shards = sizes[0] * sizes[1]
    inner, hidden = out_flat.shape[0], down_weight.shape[0]

    def kernel(
        own_ref, ctx_any, act_any, outw_any, downw_any, norms_ref, out_ref, final_ref, normed_ref, inverse_ref,
        ctx, act, outw, downw, load_sems, *scratch,
    ):
        grid = Grid2(sizes)
        parts = scratch[0]
        weights = [
            pltpu.make_async_copy(outw_any, outw, load_sems.at[0, 0]),
            pltpu.make_async_copy(downw_any, downw, load_sems.at[0, 1]),
        ]
        order = production_order(grid)
        loads = [
            [
                pltpu.make_async_copy(ctx_any.at[place], ctx.at[place], load_sems.at[1 + i, 0]),
                pltpu.make_async_copy(act_any.at[place], act.at[place], load_sems.at[1 + i, 1]),
            ]
            for i, place in enumerate(order)
        ]
        for copy in loads[0] + weights:
            copy.start()
        for copies in loads[1:]:
            for copy in copies:
                copy.start()
        grid.barrier()
        for copy in weights:
            copy.wait()

        def produce(slow, fast):
            place = grid.index(slow, fast)
            for copy in loads.pop(0):
                copy.wait()

            def columns(index, _):
                here = span(index, 512)
                parts[place, :, here] = (
                    jnp.dot(ctx[place], outw[:, here], preferred_element_type=jnp.float32)
                    + jnp.dot(act[place], downw[:, here], preferred_element_type=jnp.float32)
                ).astype(jnp.bfloat16)
                return _

            lax.fori_loop(0, D // 512, columns, 0)

        run_scatter(grid, sizes, rows, scratch, produce)
        mine = grid.index(*grid.me)

        def norm_tile(index, _):
            here = span(index, ROW_TILE)
            stream = own_ref[here].astype(jnp.float32) + parts[mine, here].astype(jnp.float32) + norms_ref[2:3]
            out_ref[here] = stream.astype(jnp.bfloat16)
            centered, inverse = tile_stats(stream)
            normed = centered * inverse
            final_ref[here] = (normed * norms_ref[0:1] + norms_ref[1:2]).astype(jnp.bfloat16)
            normed_ref[here] = normed
            inverse_ref[here] = inverse
            return _

        lax.fori_loop(0, rows // ROW_TILE, norm_tile, 0)

    return row_kernel(
        kernel, collective,
        [
            jax.ShapeDtypeStruct((rows, D), jnp.bfloat16),
            jax.ShapeDtypeStruct((rows, D), jnp.bfloat16),
            jax.ShapeDtypeStruct((rows, D), jnp.float32),
            jax.ShapeDtypeStruct((rows, 1), jnp.float32),
        ],
        [VMEM, ANY, ANY, ANY, ANY, VMEM],
        [VMEM] * 4,
        [
            pltpu.VMEM(ctx.shape, jnp.bfloat16),
            pltpu.VMEM(act.shape, jnp.bfloat16),
            pltpu.VMEM(out_flat.shape, jnp.bfloat16),
            pltpu.VMEM(down_weight.shape, jnp.bfloat16),
            pltpu.SemaphoreType.DMA((1 + shards, 2)),
        ]
        + sum_scratch(sizes, rows),
        2 * BLOCK * D * (inner + hidden),
    )(own, ctx, act, out_flat, down_weight, norms)


def logit_rows(final, head_weight, targets_col, sizes, collective):
    rows = final.shape[0]
    shards = sizes[0] * sizes[1]
    vocab = head_weight.shape[1]
    tile = tile_of(vocab)
    tiles = vocab // tile

    def kernel(
        own_ref, headw_any, target_ref, final_any, weights_any, stats_ref,
        full, send_sems, recv_sems, headw, load_sem, logits, weights, out_sems, row_sems,
    ):
        grid = Grid2(sizes)
        load = pltpu.make_async_copy(headw_any, headw, load_sem)
        load.start()
        full[grid.index(*grid.me)] = own_ref[...]
        grid.barrier()
        base = lax.axis_index("seq") * vocab
        open_copies, raw_copies = [], []

        def ready(slow, fast, order):
            place = grid.index(slow, fast)
            slot = order % 2
            if order == 0:
                load.wait()
            if order >= 2:
                open_copies.pop(0).wait()
            places = pl.ds(pl.multiple_of(place * rows, rows), rows)
            target = target_ref[places, :] - base

            def fold(values, join):
                while values.shape[1] > 128:
                    half = values.shape[1] // 2
                    values = join(values[:, :half], values[:, half:])
                return values

            def logit_tile(index, carry):
                top, pick = carry
                here = span(index, tile)
                found = jnp.dot(full[place], headw[:, here], preferred_element_type=jnp.float32)
                logits[:, here] = found
                ids = index * tile + lax.broadcasted_iota(jnp.int32, (rows, tile), 1)
                top = jnp.maximum(top, fold(found, jnp.maximum))
                pick = pick + fold(jnp.where(ids == target, found, 0.0), jnp.add)
                return (top, pick)

            top, pick = lax.fori_loop(
                0, tiles, logit_tile,
                (jnp.full((rows, 128), -jnp.inf, jnp.float32), jnp.zeros((rows, 128), jnp.float32)),
            )
            top = jnp.max(top, axis=1, keepdims=True)
            pick = jnp.sum(pick, axis=1, keepdims=True)

            def weight_tile(index, total):
                here = span(index, tile)
                found = jnp.exp(logits[:, here] - top)
                weights[slot, :, here] = found.astype(jnp.bfloat16)
                return total + fold(found, jnp.add)

            total = lax.fori_loop(0, tiles, weight_tile, jnp.zeros((rows, 128), jnp.float32))
            total = jnp.sum(total, axis=1, keepdims=True)
            lane = lax.broadcasted_iota(jnp.int32, (rows, 128), 1)
            stats_ref[places, :] = jnp.where(lane == 0, top, jnp.where(lane == 1, total, pick))
            copy = pltpu.make_async_copy(weights.at[slot], weights_any.at[place], out_sems.at[slot])
            copy.start()
            open_copies.append(copy)
            raw = pltpu.make_async_copy(full.at[place], final_any.at[place], row_sems.at[order])
            raw.start()
            raw_copies.append(raw)

        run_gather(grid, sizes, rows, full, send_sems, recv_sems, ready)
        for copy in open_copies + raw_copies:
            copy.wait()

    return row_kernel(
        kernel, collective,
        [
            jax.ShapeDtypeStruct((shards, rows, D), jnp.bfloat16),
            jax.ShapeDtypeStruct((shards, rows, vocab), jnp.bfloat16),
            jax.ShapeDtypeStruct((shards * rows, 128), jnp.float32),
        ],
        [VMEM, ANY, VMEM],
        [ANY, ANY, VMEM],
        gather_scratch(sizes, rows)
        + [
            pltpu.VMEM(head_weight.shape, jnp.bfloat16),
            pltpu.SemaphoreType.DMA,
            pltpu.VMEM((rows, vocab), jnp.float32),
            pltpu.VMEM((2, rows, vocab), jnp.bfloat16),
            pltpu.SemaphoreType.DMA((2,)),
            pltpu.SemaphoreType.DMA((shards,)),
        ],
        2 * BLOCK * D * vocab,
    )(final, head_weight, targets_col)


def final_grad_rows(grad_logits, head_weight, normed, inverse, gain, sizes, collective):
    shards, rows, vocab = grad_logits.shape

    def kernel(
        grads_any, headw_any, normed_ref, inverse_ref, gain_ref, stream_ref, down_ref, sums_ref,
        headw, grads, load_sems, *scratch,
    ):
        grid = Grid2(sizes)
        parts = scratch[0]
        order = production_order(grid)
        loads = [
            pltpu.make_async_copy(grads_any.at[place], grads.at[i % 2], load_sems.at[1 + i])
            for i, place in enumerate(order)
        ]
        weights = pltpu.make_async_copy(headw_any, headw, load_sems.at[0])
        loads[0].start()
        weights.start()
        grid.barrier()
        weights.wait()
        count = [0]

        def produce(slow, fast):
            place = grid.index(slow, fast)
            i = count[0]
            count[0] += 1
            if i + 1 < shards:
                loads[i + 1].start()
            loads[i].wait()

            def columns(index, _):
                here = span(index, 256)
                parts[place, :, here] = dot_nt(grads[i % 2], headw[here, :]).astype(jnp.bfloat16)
                return _

            lax.fori_loop(0, D // 256, columns, 0)

        run_scatter(grid, sizes, rows, scratch, produce)
        mine = grid.index(*grid.me)
        sums_ref[...] = jnp.zeros_like(sums_ref)

        def norm_tile(index, _):
            here = span(index, ROW_TILE)
            grad = parts[mine, here].astype(jnp.float32)
            norm = normed_ref[here]
            scaled = grad * gain_ref[...]
            stream = inverse_ref[here] * (
                scaled
                - jnp.mean(scaled, axis=1, keepdims=True)
                - norm * jnp.mean(scaled * norm, axis=1, keepdims=True)
            )
            stream_ref[here] = stream
            down_ref[here] = stream.astype(jnp.bfloat16)
            sums_ref[0:1] += jnp.sum(grad * norm, axis=0, keepdims=True)
            sums_ref[1:2] += jnp.sum(grad, axis=0, keepdims=True)
            sums_ref[2:3] += jnp.sum(stream, axis=0, keepdims=True)
            return _

        lax.fori_loop(0, rows // ROW_TILE, norm_tile, 0)

    return row_kernel(
        kernel, collective,
        [
            jax.ShapeDtypeStruct((rows, D), jnp.float32),
            jax.ShapeDtypeStruct((rows, D), jnp.bfloat16),
            jax.ShapeDtypeStruct((8, D), jnp.float32),
        ],
        [ANY, ANY, VMEM, VMEM, VMEM],
        [VMEM] * 3,
        [
            pltpu.VMEM(head_weight.shape, jnp.bfloat16),
            pltpu.VMEM((2, rows, vocab), jnp.bfloat16),
            pltpu.SemaphoreType.DMA((1 + shards,)),
        ]
        + sum_scratch(sizes, rows),
        2 * BLOCK * D * vocab,
    )(grad_logits, head_weight, normed, inverse, gain)


def branch_grad_rows(own, out_flat, down_weight, slope, sizes, collective):
    rows = own.shape[0]
    shards = sizes[0] * sizes[1]
    inner, hidden = out_flat.shape[0], down_weight.shape[0]

    def kernel(
        own_ref, outw_any, downw_any, slope_any, rows_any, ctx_any, up_any, sums_ref,
        full, send_sems, recv_sems, outw, downw, load_sems, slope, slope_sems, ctx, up, out_sems, row_sems,
    ):
        grid = Grid2(sizes)
        loads = [
            pltpu.make_async_copy(outw_any, outw, load_sems.at[0]),
            pltpu.make_async_copy(downw_any, downw, load_sems.at[1]),
        ]
        for copy in loads:
            copy.start()
        slopes = pltpu.make_async_copy(slope_any, slope, slope_sems)
        slopes.start()
        full[grid.index(*grid.me)] = own_ref[...]
        sums_ref[...] = jnp.zeros_like(sums_ref)
        grid.barrier()
        open_copies, raw_copies = [], []

        def ready(slow, fast, order):
            place = grid.index(slow, fast)
            slot = order % 2
            if order == 0:
                for copy in loads + [slopes]:
                    copy.wait()
            if order >= 2:
                for copy in open_copies.pop(0):
                    copy.wait()
            ctx[slot] = dot_nt(full[place], outw[...]).astype(jnp.bfloat16)
            tile = tile_of(hidden)

            def up_tile(index, _):
                here = span(index, tile)
                found = dot_nt(full[place], downw[here, :]) * slope[place, :, here].astype(jnp.float32)
                rounded = found.astype(jnp.bfloat16)
                up[slot, :, here] = rounded
                sums_ref[0:1, here] += jnp.sum(rounded.astype(jnp.float32), axis=0, keepdims=True)
                return _

            lax.fori_loop(0, hidden // tile, up_tile, 0)
            copies = [
                pltpu.make_async_copy(ctx.at[slot], ctx_any.at[place], out_sems.at[slot, 0]),
                pltpu.make_async_copy(up.at[slot], up_any.at[place], out_sems.at[slot, 1]),
            ]
            for copy in copies:
                copy.start()
            open_copies.append(copies)
            raw = pltpu.make_async_copy(full.at[place], rows_any.at[place], row_sems.at[order])
            raw.start()
            raw_copies.append(raw)

        run_gather(grid, sizes, rows, full, send_sems, recv_sems, ready)
        for copies in open_copies:
            for copy in copies:
                copy.wait()
        for copy in raw_copies:
            copy.wait()

    def out(columns):
        return jax.ShapeDtypeStruct((shards, rows, columns), jnp.bfloat16)

    return row_kernel(
        kernel, collective,
        [out(D), out(inner), out(hidden), jax.ShapeDtypeStruct((8, hidden), jnp.float32)],
        [VMEM, ANY, ANY, ANY],
        [ANY, ANY, ANY, VMEM],
        gather_scratch(sizes, rows)
        + [
            pltpu.VMEM(out_flat.shape, jnp.bfloat16),
            pltpu.VMEM(down_weight.shape, jnp.bfloat16),
            pltpu.SemaphoreType.DMA((2,)),
            pltpu.VMEM((shards, rows, hidden), jnp.bfloat16),
            pltpu.SemaphoreType.DMA,
            pltpu.VMEM((2, rows, inner), jnp.bfloat16),
            pltpu.VMEM((2, rows, hidden), jnp.bfloat16),
            pltpu.SemaphoreType.DMA((2, 2)),
            pltpu.SemaphoreType.DMA((shards,)),
        ],
        2 * BLOCK * D * (inner + hidden),
    )(own, out_flat, down_weight, slope)


def input_grad_rows(
    own, grad_stream, hid, grad_qkv, grad_up, qkv_flat, up_weight, gains, sizes, collective
):
    shards, rows, width = grad_qkv.shape
    hidden = grad_up.shape[2]

    def kernel(
        own_ref, stream_ref, hid_any, qkv_any, up_any, qkvw_any, upw_any, gains_ref, out_ref, sums_ref,
        qkvw, upw, weight_sems, hid, qkv, up, load_sems, stats, *scratch,
    ):
        grid = Grid2(sizes)
        parts = scratch[0]
        order = production_order(grid)

        def loads(i):
            place = order[i]
            return [
                pltpu.make_async_copy(hid_any.at[place], hid.at[i % 2], load_sems.at[i, 0]),
                pltpu.make_async_copy(qkv_any.at[place], qkv.at[i % 2], load_sems.at[i, 1]),
                pltpu.make_async_copy(up_any.at[place], up.at[i % 2], load_sems.at[i, 2]),
            ]

        copies = [loads(i) for i in range(shards)]
        weights = [
            pltpu.make_async_copy(qkvw_any, qkvw, weight_sems.at[0]),
            pltpu.make_async_copy(upw_any, upw, weight_sems.at[1]),
        ]
        for copy in copies[0] + weights:
            copy.start()
        sums_ref[...] = jnp.zeros_like(sums_ref)
        grid.barrier()
        for copy in weights:
            copy.wait()
        count = [0]

        def produce(slow, fast):
            place = grid.index(slow, fast)
            i = count[0]
            count[0] += 1
            if i + 1 < shards:
                for copy in copies[i + 1]:
                    copy.start()
            for copy in copies[i]:
                copy.wait()
            slot = i % 2

            def stats_tile(index, _):
                here = span(index, ROW_TILE)
                values = hid[slot, here].astype(jnp.float32)
                mean = jnp.mean(values, axis=1, keepdims=True)
                centered = values - mean
                stats[0, here] = mean
                stats[1, here] = lax.rsqrt(jnp.mean(centered * centered, axis=1, keepdims=True) + EPSILON)
                return _

            lax.fori_loop(0, rows // ROW_TILE, stats_tile, 0)

            def columns(index, _):
                here = span(index, 256)
                one = dot_nt(qkv[slot], qkvw[here, :])
                two = dot_nt(up[slot], upw[here, :])
                normed = (hid[slot, :, here].astype(jnp.float32) - stats[0]) * stats[1]
                parts[place, :, here] = (one * gains_ref[0:1, here] + two * gains_ref[1:2, here]).astype(
                    jnp.bfloat16
                )
                sums_ref[0:1, here] += jnp.sum(one * normed, axis=0, keepdims=True)
                sums_ref[1:2, here] += jnp.sum(one, axis=0, keepdims=True)
                sums_ref[2:3, here] += jnp.sum(two * normed, axis=0, keepdims=True)
                sums_ref[3:4, here] += jnp.sum(two, axis=0, keepdims=True)
                return _

            lax.fori_loop(0, D // 256, columns, 0)

        run_scatter(grid, sizes, rows, scratch, produce)
        mine = grid.index(*grid.me)

        def norm_tile(index, _):
            here = span(index, ROW_TILE)
            grad = parts[mine, here].astype(jnp.float32)
            centered, inverse = tile_stats(own_ref[here].astype(jnp.float32))
            normed = centered * inverse
            out_ref[here] = stream_ref[here] + inverse * (
                grad
                - jnp.mean(grad, axis=1, keepdims=True)
                - normed * jnp.mean(grad * normed, axis=1, keepdims=True)
            )
            return _

        lax.fori_loop(0, rows // ROW_TILE, norm_tile, 0)

    return row_kernel(
        kernel, collective,
        [jax.ShapeDtypeStruct((rows, D), jnp.float32), jax.ShapeDtypeStruct((8, D), jnp.float32)],
        [VMEM, VMEM, ANY, ANY, ANY, ANY, ANY, VMEM],
        [VMEM, VMEM],
        [
            pltpu.VMEM(qkv_flat.shape, jnp.bfloat16),
            pltpu.VMEM(up_weight.shape, jnp.bfloat16),
            pltpu.SemaphoreType.DMA((2,)),
            pltpu.VMEM((2, rows, D), jnp.bfloat16),
            pltpu.VMEM((2, rows, width), jnp.bfloat16),
            pltpu.VMEM((2, rows, hidden), jnp.bfloat16),
            pltpu.SemaphoreType.DMA((shards, 3)),
            pltpu.VMEM((2, rows, 1), jnp.float32),
        ]
        + sum_scratch(sizes, rows),
        2 * BLOCK * D * (width + hidden),
    )(own, grad_stream, hid, grad_qkv, grad_up, qkv_flat, up_weight, gains)


def segment_rows(block_lengths):
    row_ends = jnp.cumsum(block_lengths)
    row_ids = jnp.arange(BLOCK, dtype=jnp.int32)
    passed = (row_ids[:, None] >= row_ends[None, :]).astype(jnp.int32)
    segment = jnp.sum(passed, axis=1)
    position = row_ids - jnp.sum(passed * block_lengths[None, :], axis=1)
    return (segment, position)


def merge_stats(left_stats, right_stats):
    left_top, left_sum, left_pick = left_stats
    right_top, right_sum, right_pick = right_stats
    joint_top = jnp.maximum(left_top, right_top)
    joint_sum = left_sum * jnp.exp(left_top - joint_top) + right_sum * jnp.exp(
        right_top - joint_top
    )
    return (joint_top, joint_sum, left_pick + right_pick)


def row_of(vector):
    return vector.astype(jnp.float32)[None, :]


def rounded_sum(values):
    return lax.psum(values.astype(jnp.bfloat16), "dp")


def after(values, earlier):
    flat, tree = jax.tree.flatten(values)

    def kernel(*refs):
        del refs

    held = pl.pallas_call(
        kernel,
        out_shape=[jax.ShapeDtypeStruct(v.shape, v.dtype) for v in flat],
        in_specs=[ANY] * (len(flat) + 1),
        out_specs=[ANY] * len(flat),
        input_output_aliases={i: i for i in range(len(flat))},
    )(*flat, earlier)
    return jax.tree.unflatten(tree, held)


def per_device(
    hidden, targets, lengths, labels, ref_logps, ln1_gain, ln1_bias, ln2_gain, ln2_bias, qkv_weight, qv_bias,
    out_weight, up_weight, up_bias, down_weight, branch_bias, lnf_gain, lnf_bias, head_weight,
):
    sizes = lines_of(lax.axis_size("seq"))
    own = hidden[0]
    local_heads = qkv_weight.shape[1]
    local_vocab = head_weight.shape[1]
    local_hidden = up_weight.shape[1]
    width = local_heads * 3 * HEAD_DIM
    inner = local_heads * HEAD_DIM
    qv_float = qv_bias.astype(jnp.float32)
    full_bias = jnp.concatenate(
        [qv_float[:, :HEAD_DIM], jnp.zeros_like(qv_float[:, :HEAD_DIM]), qv_float[:, HEAD_DIM:]], axis=-1
    ).reshape(1, width)
    qkv_flat = qkv_weight.reshape(D, width)
    out_flat = out_weight.reshape(inner, D)
    block_lengths = lengths[0]
    segment, position = segment_rows(block_lengths)
    start = jnp.arange(BLOCK, dtype=jnp.int32) - position
    start_col = start[:, None]
    first_tile = start[::ATT_TILE] // ATT_TILE
    planes = rotary_planes(position)

    norms = jnp.concatenate([row_of(v) for v in (ln1_gain, ln1_bias, ln2_gain, ln2_bias)], axis=0)
    hid, first_full, second_full, qkv, act, slope = open_rows(
        own, sizes, 0, norms, qkv_flat, full_bias, up_weight, row_of(up_bias), planes
    )
    flat_qkv = qkv.reshape(BLOCK, width)
    ctx, lse = attention_forward(flat_qkv, start_col, first_tile, local_heads)
    shards, rows = hid.shape[0], hid.shape[1]
    end_norms = jnp.concatenate([row_of(v) for v in (lnf_gain, lnf_bias, branch_bias)], axis=0)
    output, final, normed, inverse = branch_rows(
        own, ctx.reshape(shards, rows, inner), act, out_flat, down_weight, end_norms, sizes, 1
    )
    final_full, weights, stats = logit_rows(final, head_weight, targets[0][:, None], sizes, 2)

    local_top = stats[:, 0]
    gathered = lax.all_gather(stats[:, :3].T, "seq")
    merged = tuple(gathered[0, i] for i in range(3))
    for other in range(1, gathered.shape[0]):
        merged = merge_stats(merged, tuple(gathered[other, i] for i in range(3)))
    log_total = merged[0] + jnp.log(merged[1])
    token_logp = merged[2] - log_total
    member = (jnp.arange(EXB, dtype=jnp.int32)[:, None] == segment[None, :]).astype(jnp.float32)
    float_lengths = block_lengths.astype(jnp.float32)
    mean_logp = jnp.sum(member * token_logp[None, :], axis=1) / float_lengths
    log_ratio = mean_logp - ref_logps[0]
    center = lax.psum(jnp.sum(log_ratio), "dp") / (lax.axis_size("dp") * EXB)
    label_sign = (2 * labels[0] - 1).astype(jnp.float32)
    squashed = jax.nn.sigmoid(BETA * label_sign * (log_ratio - center))
    losses = 1.0 - squashed
    grad_ratio = -LOSS_SCALE * BETA * label_sign * squashed * (1.0 - squashed)
    token_grad = jnp.sum(member * (grad_ratio / float_lengths)[:, None], axis=0)

    vocab_ids = lax.axis_index("seq") * local_vocab + jnp.arange(local_vocab, dtype=jnp.int32)
    onehot = (vocab_ids[None, :] == targets[0][:, None]).astype(jnp.float32)
    share = jnp.exp(local_top - log_total)
    grad_logits = (
        token_grad[:, None] * (onehot - weights.reshape(BLOCK, local_vocab).astype(jnp.float32) * share[:, None])
    ).astype(jnp.bfloat16)
    head_sum = rounded_sum(dot_tn(final_full.reshape(BLOCK, D), grad_logits))

    grad_stream, grad_own, end_sums = final_grad_rows(
        grad_logits.reshape(shards, rows, local_vocab), head_weight, normed, inverse, row_of(lnf_gain), sizes, 3
    )
    grad_full, grad_ctx, grad_up, up_sums = branch_grad_rows(
        grad_own, out_flat, down_weight, slope, sizes, 4
    )
    grad_rows = grad_full.reshape(BLOCK, D)
    out_grad = dot_tn(ctx, grad_rows).astype(jnp.bfloat16)
    down_grad = dot_tn(act.reshape(BLOCK, local_hidden), grad_rows).astype(jnp.bfloat16)
    up_grad = dot_tn(second_full.reshape(BLOCK, D), grad_up.reshape(BLOCK, local_hidden)).astype(jnp.bfloat16)
    middle = lax.psum(after((out_grad, down_grad, up_grad, up_sums[0].astype(jnp.bfloat16)), head_sum[:8, :128]), "dp")
    grad_qkv, qkv_sums = attention_backward(
        flat_qkv, start_col, first_tile, local_heads, ctx, lse, grad_ctx.reshape(BLOCK, inner), planes
    )
    qkv_grad = dot_tn(first_full.reshape(BLOCK, D), grad_qkv).astype(jnp.bfloat16)
    qkv_sums = qkv_sums[:, 0]
    qv_grad = jnp.concatenate([qkv_sums[:, :HEAD_DIM], qkv_sums[:, 2 * HEAD_DIM :]], axis=-1)
    last = lax.psum(after((qkv_grad, qv_grad.astype(jnp.bfloat16)), jnp.concatenate([v[:8, :128] for v in middle[:3]] + [jnp.broadcast_to(middle[3][None, :128], (8, 128))])), "dp")
    gains = jnp.concatenate([row_of(ln1_gain), row_of(ln2_gain)], axis=0)
    grad_input, start_sums = input_grad_rows(
        own, grad_stream, hid, grad_qkv.reshape(shards, rows, width), grad_up, qkv_flat, up_weight, gains,
        sizes, 5,
    )
    small = lax.psum(jnp.concatenate([start_sums[:4], end_sums[:3]], axis=0), ("dp", "seq"))
    wide = lambda values: values.astype(jnp.float32)
    return (
        losses[None],
        output[None],
        grad_input[None],
        small[0],
        small[1],
        small[2],
        small[3],
        wide(last[0]).reshape(qkv_weight.shape),
        wide(last[1]),
        wide(middle[0]).reshape(out_weight.shape),
        wide(middle[2]),
        wide(middle[3]),
        wide(middle[1]),
        small[6],
        small[4],
        small[5],
        wide(head_sum),
    )


def solution(mesh):
    return jax.shard_map(
        per_device,
        mesh=mesh,
        in_specs=(
            P("dp", "seq", None),
            P("dp", None),
            P("dp", None),
            P("dp", None),
            P("dp", None),
            P(),
            P(),
            P(),
            P(),
            P(None, "seq", None),
            P("seq", None),
            P("seq", None, None),
            P(None, "seq"),
            P("seq"),
            P("seq", None),
            P(),
            P(),
            P(),
            P(None, "seq"),
        ),
        out_specs=(
            P("dp", None),
            P("dp", "seq", None),
            P("dp", "seq", None),
            P(),
            P(),
            P(),
            P(),
            P(None, "seq", None),
            P("seq", None),
            P("seq", None, None),
            P(None, "seq"),
            P("seq"),
            P("seq", None),
            P(),
            P(),
            P(),
            P(None, "seq"),
        ),
        check_vma=False,
    )
```

time: 1630 us -> 1120 us (0.69)
  matrix products: 425 us -> 78.4 us
  waiting for transfers between devices: 300 us -> 115 us
  Pallas kernels: 522 us -> 694 us
  local copies, waits for them, and re-layouts: 121 us -> 52.4 us
  other arithmetic: 132 us -> 70 us
  loops' own time: 19.4 us -> 0 us
    dot_general x50 -> x5, matrix products: 425 us -> 78.4 us  [dot_tn(): lax.dot_general(left, right, (((0,), (0,)), ((), ())), preferred_element_...]
    psum x1 -> x3, waiting for transfers between devices: 300 us -> 115 us  [the longest x1 115 us: per_device(): lax.psum(after((out_grad, down_grad, up_grad, up_sums[0].astype(jnp.bfloa...]
    pallas_call x6 -> x10, Pallas kernels: 522 us -> 694 us  [the longest x1 114 us: logit_rows(): row_kernel(kernel, collective, [jax.ShapeDtypeStruct((shards, rows, D), j...]
    dynamic_update_slice x20 -> x0, local copies, waits for them, and re-layouts: 46.4 us -> none  [the longest x8 45.8 us: attention_forward(): lax.map(one_block, jnp.arange(BLOCK // ATT_BLK, dtype=jnp.int32))]
    reduce_sum x19 -> x4, other arithmetic: 36 us -> 1.6 us  [the longest x1 0.76 us: segment_rows(): segment = jnp.sum(passed, axis=1)]
    convert_element_type x23 -> x7, other arithmetic: 65.3 us -> 35.8 us  [the longest x5 25.7 us: per_device(): wide = lambda values: values.astype(jnp.float32)]
    squeeze x0 -> x17, local copies, waits for them, and re-layouts: none -> 19.8 us  [the longest x14 17 us: per_device(): merged = merge_stats(merged, tuple((gathered[other, i] for i in range(3))))]
    another operation x5 -> x0, loops' own time: 19.4 us -> none  [the longest x1 10.7 us: attention_backward(): lax.scan(one_block, (empty, empty), jnp.arange(BLOCK // ATT_BLK, dtype=jn...]
  transfers between devices with their start and end apart: 1 -> 3, of which waited for: 1 -> 1; matrix products, arithmetic and copies ran while one was open for 0% -> 7% of each run, Pallas kernels for 5% -> 32%
where the time goes in v2:
time: 1120 us; the launch traced here: 1110 us
  Pallas kernels  694 us (62%)
  waiting for transfers between devices  115 us (10%)
  blocking collectives  88.8 us (8%)
  matrix products  78.4 us (7%)
  other arithmetic  70 us (6%)
  local copies, waits for them, and re-layouts  52.4 us (5%)
  between operations  15.4 us (1%)
    psum x1, waiting for transfers between devices, per_device(): lax.psum(after((out_grad, down_grad, up_grad, up_sums[0].astype(jnp.bfloa...  115 us
    pallas_call x1, Pallas kernels, logit_rows(): row_kernel(kernel, collective, [jax.ShapeDtypeStruct((shards, rows, D), j...  114 us
    pallas_call x1, Pallas kernels, input_grad_rows(): row_kernel(kernel, collective, [jax.ShapeDtypeStruct((rows, D), jnp.float...  113 us
    pallas_call x1, Pallas kernels, final_grad_rows(): row_kernel(kernel, collective, [jax.ShapeDtypeStruct((rows, D), jnp.float...  112 us
    pallas_call x1, Pallas kernels, open_rows(): row_kernel(kernel, collective, [out(D), out(D), out(D), out(width), out(h...  111 us
    pallas_call x1, Pallas kernels, branch_grad_rows(): row_kernel(kernel, collective, [out(D), out(inner), out(hidden), jax.Shap...  92.6 us
    pallas_call x1, Pallas kernels, branch_rows(): row_kernel(kernel, collective, [jax.ShapeDtypeStruct((rows, D), jnp.bfloa...  90.9 us
    dot_general x5, matrix products, dot_tn(): lax.dot_general(left, right, (((0,), (0,)), ((), ())), preferred_element_...  78.4 us
  transfers between devices with their start and end apart: 3, of which 1 were waited for; matrix products, arithmetic and copies ran while one was open for 7% of the time, Pallas kernels for 32%

profile of v2, /device:TPU:0, one launch (start us, length us, event | category | flops | bytes accessed | tf_op | source)
XLA Modules:
  0.0 1113.5 jit_solution(8607037113904520322)
XLA Ops:
  12.3 4.2 copy.158
  22.1 3.7 fusion.12
  26.5 2.6 maximum_maximum_fusion.2
  29.1 110.8 %shard_map.314 = (bf16[8,256,2048]{2,1,0:T(8,128)(2,1)}, bf16[8,256,2048]{2,1,0:T(8,128)(2,1)}, bf16[8,256,2048]{2,1,0:T(8,128)(2,1)}, bf16[8,256,768]{2,1,0:T(8...) custom-call(bf16[256,2048]{1,0:T(8,128)(2,1)} %bitcast.200, ...), custom_call_target="tpu_custom_call" | custom-call | flops 15032385536 | bytes 33554432 | tf_op jit(solution)/shard_map/pallas_call | solution.py:698
  139.9 24.7 %shard_map.315 = (bf16[2048,256]{1,0:T(8,128)(2,1)}, f32[2,2048,1]{2,1,0:T(8,128)}) custom-call(s32[8]{0:T(128)} %and_select_fusion.first_ref, bf16[2048,768]{1,0:T(8,128)(2,1)} %bitcast.138, bf16[2048,768]{1,0:T(8,128)(2,1)} %bitcast.139, bf16[2048,768]{1,0:T(8,128)(2,1)} %bitcast.140, s32[2048,1]{1,0:T(8,128)} %subtract_subtract_fusion.start_ref), custom_call_target="tpu_custom_call" | custom-call | tf_op jit(solution)/shard_map/pallas_call | solution.py:382
  165.2 90.9 %shard_map.316 = (bf16[256,2048]{1,0:T(8,128)(2,1)}, bf16[256,2048]{1,0:T(8,128)(2,1)}, f32[256,2048]{1,0:T(8,128)}, f32[256,1]{1,0:T(8,128)}) custom-call(bf16[256,2048]{1,0:T(8,128)(2,1)} %bitcast.201, bf16[8,256,256]{2,1,0:T(8,128)(2,1)} %bitcast.147, bf16[8,256,1024]{2,1,0:T(8,128)(2,1)} %get-tuple-element.51.act_any, bf16[256,2048]{1,0:T(8,128)(2,1)} %bitcast.198, ...), custom_call_target="tpu_custom_call" | custom-call | flops 10737418240 | bytes 33554432 | tf_op jit(solution)/shard_map/pallas_call | solution.py:779
  256.1 113.5 %shard_map.317 = (bf16[8,256,2048]{2,1,0:T(8,128)(2,1)}, bf16[8,256,3328]{2,1,0:T(8,128)(2,1)}, f32[2048,128]{1,0:T(8,128)}) custom-call(bf16[256,2048]{1,0:T(8,128)(2,1)} %get-tuple-element.52.own_ref, bf16[2048,3328]{1,0:T(8,128)(2,1)} %headw_any.3, s32[2048,1]{1,0:T(8,128)} %copy.123.target_ref), custom_call_target="tpu_custom_call" | custom-call | flops 27917287424 | bytes 33554432 | tf_op jit(solution)/shard_map/pallas_call | solution.py:874
  371.3 30.7 %all-gather.1 = f32[8,3,2048]{2,1,0:T(4,128)S(1)} all-gather(f32[1,3,2048]{2,1,0:T(4,128)S(1)} %copy.124), channel_id=2, replica_groups=mesh['dp'=4,'seq'=8] {'seq'}, dimensions={0}, use_global_device_ids=true | all-gather | bytes 221184 | tf_op jit(solution)/shard_map/all_gather | solution.py:1251
  403.1 6.4 psum.63
  430.6 7.0 exponential_reduce_fusion
  439.6 10.1 multiply_convert_fusion.grads_any
  449.8 5.1 copy-done
  454.9 35.5 %bitcast_convert_fusion = bf16[2048,3328]{1,0:T(8,128)(2,1)} fusion(bf16[8,256,2048]{2,1,0:T(8,128)(2,1)} %get-tuple-element.74, bf16[8,256,3328]{2,1,0:T(8,128)(2,1)S(1)} %multiply_convert_fusion.grads_any), kind=kOutput, calls=%fused_computation | convolution fusion | flops 27924103168 | bytes 35651584 | tf_op jit(solution)/shard_map/dot_general | solution.py:316
  490.5 112.5 %shard_map.318 = (f32[256,2048]{1,0:T(8,128)}, bf16[256,2048]{1,0:T(8,128)(2,1)}, f32[8,2048]{1,0:T(8,128)}) custom-call(bf16[8,256,3328]{2,1,0:T(8,128)(2,1)} %copy-done, bf16[2048,3328]{1,0:T(8,128)(2,1)} %headw_any.3, f32[256,2048]{1,0:T(8,128)} %get-tuple-element.56.normed_ref, f32[256,1]{1,0:T(8,128)} %get-tuple-element.57.inverse_ref, f32[1,2048]{1,0:T(1,128)} %bitcast.177), custom_call_target="tpu_custom_call" | custom-call | flops 27917287424 | bytes 33554432 | tf_op jit(solution)/shard_map/pallas_call | solution.py:955
  603.0 92.6 %shard_map.319 = (bf16[8,256,2048]{2,1,0:T(8,128)(2,1)}, bf16[8,256,256]{2,1,0:T(8,128)(2,1)}, bf16[8,256,1024]{2,1,0:T(8,128)(2,1)}, f32[8,1024]{1,0:T(8,128)}) custom-call(bf16[256,2048]{1,0:T(8,128)(2,1)} %get-tuple-element.61.own_ref, bf16[256,2048]{1,0:T(8,128)(2,1)} %bitcast.199, bf16[1024,2048]{1,0:T(8,128)(2,1)} %downw_any.3, ...), custom_call_target="tpu_custom_call" | custom-call | flops 10737418240 | bytes 33554432 | tf_op jit(solution)/shard_map/pallas_call | solution.py:1039
  695.6 1.5 fusion.28.refs_3_
  697.1 7.0 convolution_convert_fusion.1.refs_0_
  704.1 13.0 %bitcast_convert_fusion.1.refs_2_ = bf16[2048,1024]{1,0:T(8,128)(2,1)} fusion(bf16[8,256,2048]{2,1,0:T(8,128)(2,1)} %get-tuple-element.72, bf16[8,256,1024]{2,1,0:T(8,128)(2,1)S(1)} %copy-done.29), kind=kOutput, calls=%fused_computation.2 | convolution fusion | flops 8592031744 | bytes 16777216 | tf_op jit(solution)/shard_map/dot_general | solution.py:316
  717.1 11.2 %bitcast_convert_fusion.2.refs_1_ = bf16[1024,2048]{1,0:T(8,128)(2,1)} fusion(bf16[8,256,1024]{2,1,0:T(8,128)(2,1)S(1)} %copy-done.28, bf16[8,256,2048]{2,1,0:T(8,128)(2,1)S(1)} %bitcast.146), kind=kOutput, calls=%fused_computation.3 | convolution fusion | flops 8592031744 | bytes 16777216 | tf_op jit(solution)/shard_map/dot_general | solution.py:316
  729.6 35.5 %shard_map.320 = (bf16[2048,768]{1,0:T(8,128)(2,1)}, f32[2,1,384]{2,1,0:T(1,128)}) custom-call(s32[8]{0:T(128)} %and_select_fusion.first_ref, bf16[2048,768]{1,0:T(8,128)(2,1)} %bitcast.141, bf16[2048,768]{1,0:T(8,128)(2,1)} %bitcast.142, bf16[2048,768]{1,0:T(8,128)(2,1)} %bitcast.143, s32[2048,1]{1,0:T(8,128)} %subtract_subtract_fusion.start_ref, ...), custom_call_target="tpu_custom_call" | custom-call | tf_op jit(solution)/shard_map/pallas_call | solution.py:464
  767.0 11.7 %convolution_convert_fusion.refs_0_ = bf16[2048,768]{1,0:T(8,128)(2,1)} fusion(bf16[2048,2048]{1,0:T(8,128)(2,1)} %bitcast.203, bf16[2048,768]{1,0:T(8,128)(2,1)} %get-tuple-element.64), kind=kOutput, calls=%fused_computation.4 | convolution fusion | flops 6444023808 | bytes 14680064 | tf_op jit(solution)/shard_map/dot_general | solution.py:316
  778.7 6.2 psum.69
  784.9 114.6 %all-reduce.9.cloned.1.call-done = (bf16[2048,1024]{1,0:T(8,128)(2,1)}, bf16[1024,2048]{1,0:T(8,128)(2,1)}, bf16[256,2048]{1,0:T(8,128)(2,1)}) async-done(((bf16[2048,1024]{1,0:T(8,128)(2,1)}, bf16[1024,2048]{1,0:T(8,128)(2,1)}, bf16[256,2048]{1,0:T(8,128)(2,1)}), (bf16[2048,1024]{1,0:T(8,128)(2,1)}, bf16[1024,2048]{1,0:T(8,128)(2,1)}, bf16[256,2048]{1,0:T(8,128)(2,1)})) %all-reduce.9.cloned.1.call-update) | async-done | bytes 9437200 | tf_op jit(solution)/shard_map/psum | solution.py:1286
  902.1 7.0 reshape.757
  909.2 113.4 %shard_map.321 = (f32[256,2048]{1,0:T(8,128)}, f32[8,2048]{1,0:T(8,128)}) custom-call(bf16[256,2048]{1,0:T(8,128)(2,1)} %bitcast.202, f32[256,2048]{1,0:T(8,128)} %get-tuple-element.58.stream_ref, bf16[8,256,2048]{2,1,0:T(8,128)(2,1)} %get-tuple-element.59.hid_any, bf16[8,256,768]{2,1,0:T(8,128)(2,1)} %bitcast.197, ...), custom_call_target="tpu_custom_call" | custom-call | flops 15032385536 | bytes 33554432 | tf_op jit(solution)/shard_map/pallas_call | solution.py:1150
  1023.5 39.4 %psum.64 = f32[7,2048]{1,0:T(8,128)S(1)} all-reduce(f32[7,2048]{1,0:T(8,128)S(1)} %pad_maximum_fusion), channel_id=1, replica_groups=mesh['dp'=4,'seq'=8] {'dp','seq'}, use_global_device_ids=true, to_apply=%region_7.8 | all-reduce | flops 14336 | bytes 114688 | tf_op jit(solution)/shard_map/psum | solution.py:1299
  1064.7 15.6 %convert_element_type.114 = f32[2048,3328]{1,0:T(8,128)} convert(bf16[2048,3328]{1,0:T(8,128)(2,1)} %all-reduce.5.cloned.1.call-done) | non-fusion elementwise | flops 6815744 | bytes 40894464 | tf_op jit(solution)/shard_map/convert_element_type | solution.py:1300
  1080.3 4.4 convert_element_type.111
  1084.8 4.4 convert_element_type.113
  1089.2 6.2 psum.71
  1096.0 1.6 convert.22
  1097.6 6.7 reshape.758
  (157 shorter events, 48.6 us)
Async XLA Ops:
  7.2 13.5 %copy-start.21 = (bf16[2048]{0:T(1024)(128)(2,1)S(1)}, bf16[2048]{0:T(1024)(128)(2,1)}, u32[]{:S(2)}) copy-start(bf16[2048]{0:T(1024)(128)(2,1)} %param.34) | copy-start | bytes 12292
  7.2 13.5 %copy-start.22 = (bf16[2048]{0:T(1024)(128)(2,1)S(1)}, bf16[2048]{0:T(1024)(128)(2,1)}, u32[]{:S(2)}) copy-start(bf16[2048]{0:T(1024)(128)(2,1)} %param.36) | copy-start | bytes 12292
  7.2 13.5 %copy-start.23 = (bf16[2048]{0:T(1024)(128)(2,1)S(1)}, bf16[2048]{0:T(1024)(128)(2,1)}, u32[]{:S(2)}) copy-start(bf16[2048]{0:T(1024)(128)(2,1)} %param.35) | copy-start | bytes 12292
  7.2 13.5 %copy-start.12 = (s32[1,2048]{1,0:T(1,128)S(1)}, s32[1,2048]{1,0:T(1,128)}, u32[]{:S(2)}) copy-start(s32[1,2048]{1,0:T(1,128)} %param.20) | copy-start | bytes 24580
  7.2 721.0 %all-reduce.5.cloned.1.call-start = ((), (), s32[]{:S(2)}) async-start(), calls=%async_computation | async-start | bytes 27262976 | tf_op jit(solution)/shard_map/psum | solution.py:1194
  10.9 18.2 %copy-start.8 = (f32[2048]{0:T(1024)}, f32[2048]{0:T(1024)S(1)}, u32[]{:S(2)}) copy-start(f32[2048]{0:T(1024)S(1)} %broadcast_in_dim.107) | copy-start | bytes 24580
  12.3 16.8 %copy-start.10 = (f32[2048]{0:T(1024)}, f32[2048]{0:T(1024)S(1)}, u32[]{:S(2)}) copy-start(f32[2048]{0:T(1024)S(1)} %broadcast_in_dim.105) | copy-start | bytes 24580
  20.7 143.9 %copy-start.13 = (f32[2048]{0:T(1024)}, f32[2048]{0:T(1024)S(1)}, u32[]{:S(2)}) copy-start(f32[2048]{0:T(1024)S(1)} %broadcast_in_dim.110) | copy-start | bytes 24580
  256.1 146.4 %copy-start.17 = (s32[1,8]{1,0:T(1,128)S(1)}, s32[1,8]{1,0:T(1,128)}, u32[]{:S(2)}) copy-start(s32[1,8]{1,0:T(1,128)} %param.21) | copy-start | bytes 100
  256.1 146.4 %copy-start.24 = (f32[1,8]{1,0:T(1,128)S(1)}, f32[1,8]{1,0:T(1,128)}, u32[]{:S(2)}) copy-start(f32[1,8]{1,0:T(1,128)} %param.23) | copy-start | bytes 100
  402.5 7.4 copy-start.19
  409.9 20.8 %copy-start.4 = (f32[2048,128]{1,0:T(8,128)S(1)}, f32[2048,128]{1,0:T(8,128)}, u32[]{:S(2)}) copy-start(f32[2048,128]{1,0:T(8,128)} %get-tuple-element.53) | copy-start | bytes 3145732
  430.6 8.9 copy-start.26
  490.5 409.0 %all-reduce.9.cloned.1.call-start = ((), (), s32[]{:S(2)}) async-start(), calls=%async_computation.2 | async-start | bytes 18874368 | tf_op jit(solution)/shard_map/psum | solution.py:1286
  603.0 94.1 %copy-start.1 = (bf16[2048,256]{1,0:T(8,128)(2,1)S(1)}, bf16[2048,256]{1,0:T(8,128)(2,1)}, u32[]{:S(2)}) copy-start(bf16[2048,256]{1,0:T(8,128)(2,1)} %get-tuple-element.50.ctx_ref) | copy-start | bytes 3145732
  695.6 8.5 copy-start.29
  697.1 20.0 %slice-start = ((s8[8388608]{0:T(1024)(128)(4,1)}), s8[4194304]{0:T(1024)(128)(4,1)S(1)}, s32[]{:S(2)}) async-start(s8[8388608]{0:T(1024)(128)(4,1)} %bitcast.145), calls=%async_computation.3 | async-start | bytes 8388608
  704.1 13.0 %slice-start.1 = ((s8[8388608]{0:T(1024)(128)(4,1)}), s8[4194304]{0:T(1024)(128)(4,1)S(1)}, s32[]{:S(2)}) async-start(s8[8388608]{0:T(1024)(128)(4,1)} %bitcast.145), calls=%async_computation.4 | async-start | bytes 8388608
  704.1 13.0 %copy-start.28 = (bf16[8,256,1024]{2,1,0:T(8,128)(2,1)S(1)}, bf16[8,256,1024]{2,1,0:T(8,128)(2,1)}, u32[]{:S(2)}) copy-start(bf16[8,256,1024]{2,1,0:T(8,128)(2,1)} %get-tuple-element.51.act_any) | copy-start | bytes 12582916
  729.6 368.0 %all-reduce.7.cloned.1.call-start = ((), (), s32[]{:S(2)}) async-start(), calls=%async_computation.1 | async-start | bytes 6291456 | tf_op jit(solution)/shard_map/psum | solution.py:1293
  729.6 36.8 %copy-start.9 = (f32[2048]{0:T(1024)S(1)}, f32[2048]{0:T(1024)}, u32[]{:S(2)}) copy-start(f32[2048]{0:T(1024)} %copy-done.8) | copy-start | bytes 24580
  729.6 36.8 %copy-start.11 = (f32[2048]{0:T(1024)S(1)}, f32[2048]{0:T(1024)}, u32[]{:S(2)}) copy-start(f32[2048]{0:T(1024)} %copy-done.10) | copy-start | bytes 24580
  767.0 11.7 %copy-start.14 = (bf16[1024]{0:T(1024)(128)(2,1)S(1)}, bf16[1024]{0:T(1024)(128)(2,1)}, u32[]{:S(2)}) copy-start(bf16[1024]{0:T(1024)(128)(2,1)} %get-tuple-element.78) | copy-start | bytes 6148
  909.1 113.5 %copy-start.15 = (f32[8,2048]{1,0:T(8,128)S(1)}, f32[8,2048]{1,0:T(8,128)}, u32[]{:S(2)}) copy-start(f32[8,2048]{1,0:T(8,128)} %get-tuple-element.68) | copy-start | bytes 196612
  909.1 153.7 %copy-start.18 = (s32[1,8]{1,0:T(1,128)S(1)}, s32[1,8]{1,0:T(1,128)}, u32[]{:S(2)}) copy-start(s32[1,8]{1,0:T(1,128)} %param.21) | copy-start | bytes 100
  909.2 153.7 %copy-start.20 = (f32[8]{0:T(128)S(1)}, f32[8]{0:T(128)}, u32[]{:S(2)}) copy-start(f32[8]{0:T(128)} %copy-done.19) | copy-start | bytes 100
  909.2 153.7 %copy-start.25 = (f32[1,8]{1,0:T(1,128)S(1)}, f32[1,8]{1,0:T(1,128)}, u32[]{:S(2)}) copy-start(f32[1,8]{1,0:T(1,128)} %param.23) | copy-start | bytes 100
  909.2 153.7 %copy-start.27 = (s32[1,8]{1,0:T(1,128)S(1)}, s32[1,8]{1,0:T(1,128)}, u32[]{:S(2)}) copy-start(s32[1,8]{1,0:T(1,128)} %param.22) | copy-start | bytes 100
  1064.7 15.6 %copy-start.3 = (bf16[2048,1024]{1,0:T(8,128)(2,1)S(1)}, bf16[2048,1024]{1,0:T(8,128)(2,1)}, u32[]{:S(2)}) copy-start(bf16[2048,1024]{1,0:T(8,128)(2,1)} %get-tuple-element.83) | copy-start | bytes 12582916
  1084.8 11.2 %copy-start.6 = (bf16[256,2048]{1,0:T(8,128)(2,1)S(1)}, bf16[256,2048]{1,0:T(8,128)(2,1)}, u32[]{:S(2)}) copy-start(bf16[256,2048]{1,0:T(8,128)(2,1)} %get-tuple-element.85) | copy-start | bytes 3145732
  1089.2 16.0 %copy-start.5 = (f32[256,2048]{1,0:T(8,128)S(1)}, f32[256,2048]{1,0:T(8,128)}, u32[]{:S(2)}) copy-start(f32[256,2048]{1,0:T(8,128)} %get-tuple-element.66) | copy-start | bytes 6291460
  1097.6 6.7 copy-start.7
  (3 other events, 14.0 us)
Sparse Core Ops, SparseCore 0:
  490.6 233.9 all-reduce.4
  729.7 169.7 all-reduce.8
  909.3 68.6 all-reduce.6

commit v3 on v2

--- a/solution.py
+++ b/solution.py
@@ -250,8 +250,15 @@
             self.take(kind, stage, axis, other, m, jnp.bool_(True), half, m > 0, index)
             self.take(kind, stage, axis, other, m, jnp.bool_(False), half, m < n - 1, index)
 
-    def run(self, produce):
+    def run(self, produce, made=lambda: None, between=lambda: None):
         grid, n, me = self.grid, self.grid.n, self.grid.me
+
+        def chain(k):
+            slow = grid.nearest(0, k)
+            for half in range(self.halves):
+                self.last(0, 0, 1, slow, half, slow, me[1])
+                self.toward(0, 1, 0, 0, slow, half, slow, me[1])
+
         for k in reversed(range(n[0])):
             slow = grid.nearest(0, k)
             for l in reversed(range(n[1])):
@@ -262,6 +269,11 @@
                         self.toward(0, 0, 1, slow, fast, half, slow, fast)
                     if self.cut[1] and k > 0:
                         self.toward(1, 0, 0, fast, slow, half, slow, fast)
+            if k == 0:
+                made()
+            if self.cut[0] and k < n[0] - 1:
+                chain(k + 1)
+        between()
         if self.cut[1]:
             for half in range(self.halves):
                 for l in reversed(range(n[1])):
@@ -270,11 +282,6 @@
                     if l > 0:
                         self.toward(1, 1, 1, 0, fast, half, me[0], fast)
         if self.cut[0]:
-            for k in reversed(range(1, n[0])):
-                slow = grid.nearest(0, k)
-                for half in range(self.halves):
-                    self.last(0, 0, 1, slow, half, slow, me[1])
-                    self.toward(0, 1, 0, 0, slow, half, slow, me[1])
             for half in range(self.halves):
                 self.last(0, 0, 1, me[0], half, me[0], me[1])
         for half in range(self.halves):
@@ -403,13 +410,14 @@
     )(first_tile, qkv, qkv, qkv, start_col)
 
 
-def attention_backward(qkv, start_col, first_tile, heads, ctx, lse, grad_ctx, planes):
+def attention_backward(qkv, start_col, first_tile, heads, ctx, lse, grad_ctx, planes, before):
     tiles = BLOCK // ATT_TILE
 
     def kernel(
         first_ref, q_ref, k_ref, v_ref, start_ref, ctx_ref, lse_ref, do_ref, cos_ref, below_ref,
-        above_ref, out_ref, sums_ref, dk_ref, dv_ref,
+        above_ref, *rest,
     ):
+        out_ref, sums_ref, dk_ref, dv_ref = rest[len(before) :]
         tile = pl.program_id(1)
 
         @pl.when(tile == 0)
@@ -477,7 +485,8 @@
                 whole,
                 whole,
                 whole,
-            ],
+            ]
+            + [pl.BlockSpec(memory_space=pl.ANY)] * len(before),
             out_specs=[
                 pl.BlockSpec((BLOCK, 3 * HEAD_DIM), lambda h, i, first: (0, h)),
                 pl.BlockSpec((pl.squeezed, 1, 3 * HEAD_DIM), lambda h, i, first: (h, 0, 0)),
@@ -492,7 +501,7 @@
             jax.ShapeDtypeStruct((heads, 1, 3 * HEAD_DIM), jnp.float32),
         ],
         compiler_params=pltpu.CompilerParams(vmem_limit_bytes=VMEM_LIMIT),
-    )(first_tile, qkv, qkv, qkv, start_col, ctx, lse, grad_ctx, *planes)
+    )(first_tile, qkv, qkv, qkv, start_col, ctx, lse, grad_ctx, *planes, *before)
 
 
 def gather_cut(sizes):
@@ -517,18 +526,24 @@
 VMEM = pl.BlockSpec(memory_space=pltpu.VMEM)
 
 
-def row_kernel(kernel, collective, out_shape, in_specs, out_specs, scratch, cost):
-    return pl.pallas_call(
-        kernel,
-        out_shape=out_shape,
-        in_specs=in_specs,
-        out_specs=out_specs,
-        scratch_shapes=scratch,
-        cost_estimate=pl.CostEstimate(flops=cost, bytes_accessed=2**25, transcendentals=0),
-        compiler_params=pltpu.CompilerParams(
-            collective_id=collective, has_side_effects=True, vmem_limit_bytes=VMEM_LIMIT
-        ),
-    )
+def row_kernel(kernel, collective, out_shape, in_specs, out_specs, scratch, cost, before=()):
+    def body(*refs):
+        kernel(*refs[len(before):])
+
+    def call(*args):
+        return pl.pallas_call(
+            body,
+            out_shape=out_shape,
+            in_specs=[ANY] * len(before) + in_specs,
+            out_specs=out_specs,
+            scratch_shapes=scratch,
+            cost_estimate=pl.CostEstimate(flops=cost, bytes_accessed=2**28, transcendentals=0),
+            compiler_params=pltpu.CompilerParams(
+                collective_id=collective, has_side_effects=True, vmem_limit_bytes=VMEM_LIMIT
+            ),
+        )(*before, *args)
+
+    return call
 
 
 def gather_scratch(sizes, rows):
@@ -563,7 +578,7 @@
     )
 
 
-def run_scatter(grid, sizes, rows, scratch, produce):
+def run_scatter(grid, sizes, rows, scratch, produce, *hooks):
     cut = gather_cut(sizes)
     step = rows // HALVES
     parts, b0, b1, b2, b3, s0, s1, s2, s3, send_sems = scratch
@@ -575,7 +590,7 @@
     scatter = Scatter(
         grid, sender, part, ((b0, b1), (b2, b3)), ((s0, s1), (s2, s3)), HALVES, cut
     )
-    scatter.run(produce)
+    scatter.run(produce, *hooks)
     sender.finish()
 
 
@@ -893,7 +908,7 @@
     )(final, head_weight, targets_col)
 
 
-def final_grad_rows(grad_logits, head_weight, normed, inverse, gain, sizes, collective):
+def final_grad_rows(grad_logits, head_weight, normed, inverse, gain, sizes, collective, before):
     shards, rows, vocab = grad_logits.shape
 
     def kernel(
@@ -968,6 +983,7 @@
         ]
         + sum_scratch(sizes, rows),
         2 * BLOCK * D * vocab,
+        before,
     )(grad_logits, head_weight, normed, inverse, gain)
 
 
@@ -1057,17 +1073,129 @@
     )(own, out_flat, down_weight, slope)
 
 
+class SmallSum:
+    def __init__(self, shards, replicas, sums, bias, total, bias_total, scratch):
+        self.shards, self.replicas = shards, replicas
+        self.sums, self.bias, self.total, self.bias_total = sums, bias, total, bias_total
+        (
+            self.came, self.block, self.blocks, self.biases, self.spread_send, self.spread_recv, self.cross_send,
+            self.cross_recv, self.back_send, self.back_recv,
+        ) = scratch
+        self.seq, self.dp = lax.axis_index("seq"), lax.axis_index("dp")
+        self.width = D // shards
+
+    @staticmethod
+    def scratch(shards, replicas):
+        width = D // shards
+        dma = pltpu.SemaphoreType.DMA
+        return [
+            pltpu.VMEM((shards, 8, width), jnp.float32),
+            pltpu.VMEM((8, width), jnp.float32),
+            pltpu.VMEM((replicas, 8, width), jnp.float32),
+            pltpu.VMEM((replicas, 8, D), jnp.float32),
+            dma((shards,)), dma((shards,)), dma((2, replicas)), dma((2, replicas)), dma((shards,)), dma((shards,)),
+        ]
+
+    def others(self, axis):
+        count, here = (self.shards, self.seq) if axis == "seq" else (self.replicas, self.dp)
+        return [(step, lax.rem(here + step, count)) for step in range(1, count)]
+
+    def barrier(self):
+        sem = pltpu.get_barrier_semaphore()
+        amount = 0
+        for axis in ("seq", "dp"):
+            for _, place in self.others(axis):
+                pl.semaphore_signal(sem, inc=1, device_id={axis: place}, device_id_type=MESH)
+                amount += 1
+        pl.semaphore_wait(sem, amount)
+
+    def copy(self, axis, place, src, dst, send, recv):
+        return pltpu.make_async_remote_copy(
+            src_ref=src, dst_ref=dst, send_sem=send, recv_sem=recv, device_id={axis: place}, device_id_type=MESH
+        )
+
+    def columns(self, place):
+        return pl.ds(pl.multiple_of(place * self.width, self.width), self.width)
+
+    def spread(self):
+        self.first = [
+            self.copy(
+                "seq", place, self.sums.at[:, self.columns(place)], self.came.at[step], self.spread_send.at[step],
+                self.spread_recv.at[step],
+            )
+            for step, place in self.others("seq")
+        ]
+        self.second = [
+            self.copy(
+                "dp", place, self.bias, self.biases.at[self.dp], self.cross_send.at[1, step],
+                self.cross_recv.at[1, step],
+            )
+            for step, place in self.others("dp")
+        ]
+        for copy in self.first + self.second:
+            copy.start()
+
+    def cross(self):
+        total = self.sums[:, self.columns(self.seq)]
+        for (step, _), copy in zip(self.others("seq"), self.first):
+            copy.wait_recv()
+            total = total + self.came[step]
+        self.block[...] = total
+        self.blocks[self.dp] = total
+        self.third = [
+            self.copy(
+                "dp", place, self.block, self.blocks.at[self.dp], self.cross_send.at[0, step],
+                self.cross_recv.at[0, step],
+            )
+            for step, place in self.others("dp")
+        ]
+        for copy in self.third:
+            copy.start()
+
+    def collect(self):
+        for copy in self.third + self.second:
+            copy.wait_recv()
+        self.biases[self.dp] = self.bias[...]
+        total, bias = self.blocks[0], self.biases[0]
+        for place in range(1, self.replicas):
+            total, bias = total + self.blocks[place], bias + self.biases[place]
+        self.bias_total[...] = bias
+        here = self.columns(self.seq)
+        self.total[:, here] = total
+        self.fourth = [
+            self.copy(
+                "seq", place, self.total.at[:, here], self.total.at[:, here], self.back_send.at[step],
+                self.back_recv.at[step],
+            )
+            for step, place in self.others("seq")
+        ]
+        for copy in self.fourth:
+            copy.start()
+
+    def finish(self):
+        for (step, _), copy in zip(self.others("seq"), self.fourth):
+            source = lax.rem(self.seq + self.shards - step, self.shards)
+            there = self.total.at[:, self.columns(source)]
+            self.copy("seq", source, there, there, self.back_send.at[step], self.back_recv.at[step]).wait_recv()
+        for copy in self.first + self.second + self.third + self.fourth:
+            copy.wait_send()
+
+
 def input_grad_rows(
-    own, grad_stream, hid, grad_qkv, grad_up, qkv_flat, up_weight, gains, sizes, collective
+    own, grad_stream, hid, grad_qkv, grad_up, qkv_flat, up_weight, gains, end_sums, biases, sizes, replicas,
+    collective, before,
 ):
     shards, rows, width = grad_qkv.shape
     hidden = grad_up.shape[2]
 
     def kernel(
-        own_ref, stream_ref, hid_any, qkv_any, up_any, qkvw_any, upw_any, gains_ref, out_ref, sums_ref,
-        qkvw, upw, weight_sems, hid, qkv, up, load_sems, stats, *scratch,
+        own_ref, stream_ref, hid_any, qkv_any, up_any, qkvw_any, upw_any, gains_ref, end_ref,
+        bias_ref, out_ref, total_ref, bias_total_ref,
+        qkvw, upw, weight_sems, hid, qkv, up, load_sems, stats, sums_ref, *scratch,
     ):
         grid = Grid2(sizes)
+        small = SmallSum(shards, replicas, sums_ref, bias_ref, total_ref, bias_total_ref, scratch[:10])
+        scratch = scratch[10:]
         parts = scratch[0]
         order = production_order(grid)
 
@@ -1087,7 +1215,7 @@
         for copy in copies[0] + weights:
             copy.start()
         sums_ref[...] = jnp.zeros_like(sums_ref)
-        grid.barrier()
+        small.barrier()
         for copy in weights:
             copy.wait()
         count = [0]
@@ -1130,7 +1258,12 @@
 
             lax.fori_loop(0, D // 256, columns, 0)
 
-        run_scatter(grid, sizes, rows, scratch, produce)
+        def made():
+            sums_ref[4:8] = end_ref[0:4]
+            small.spread()
+
+        run_scatter(grid, sizes, rows, scratch, produce, made, small.cross)
+        small.collect()
         mine = grid.index(*grid.me)
 
         def norm_tile(index, _):
@@ -1146,12 +1279,13 @@
             return _
 
         lax.fori_loop(0, rows // ROW_TILE, norm_tile, 0)
+        small.finish()
 
     return row_kernel(
         kernel, collective,
-        [jax.ShapeDtypeStruct((rows, D), jnp.float32), jax.ShapeDtypeStruct((8, D), jnp.float32)],
-        [VMEM, VMEM, ANY, ANY, ANY, ANY, ANY, VMEM],
-        [VMEM, VMEM],
+        [jax.ShapeDtypeStruct((rows, D), jnp.float32), jax.ShapeDtypeStruct((8, D), jnp.float32), jax.ShapeDtypeStruct((8, D), jnp.float32)],
+        [VMEM, VMEM, ANY, ANY, ANY, ANY, ANY, VMEM, VMEM, VMEM],
+        [VMEM, VMEM, VMEM],
         [
             pltpu.VMEM(qkv_flat.shape, jnp.bfloat16),
             pltpu.VMEM(up_weight.shape, jnp.bfloat16),
@@ -1161,10 +1295,13 @@
             pltpu.VMEM((2, rows, hidden), jnp.bfloat16),
             pltpu.SemaphoreType.DMA((shards, 3)),
             pltpu.VMEM((2, rows, 1), jnp.float32),
+            pltpu.VMEM((8, D), jnp.float32),
         ]
+        + SmallSum.scratch(shards, replicas)
         + sum_scratch(sizes, rows),
         2 * BLOCK * D * (width + hidden),
-    )(own, grad_stream, hid, grad_qkv, grad_up, qkv_flat, up_weight, gains)
+        before,
+    )(own, grad_stream, hid, grad_qkv, grad_up, qkv_flat, up_weight, gains, end_sums, biases)
 
 
 def segment_rows(block_lengths):
@@ -1190,24 +1327,63 @@
     return vector.astype(jnp.float32)[None, :]
 
 
-def rounded_sum(values):
-    return lax.psum(values.astype(jnp.bfloat16), "dp")
+PAIR = [(0, 1), (1, 0), (2, 3), (3, 2)]
+CROSS = [(0, 2), (2, 0), (1, 3), (3, 1)]
+
+
+def held(values):
+    return lax.optimization_barrier(values)
+
+
+def half_of(values, which):
+    half = values.shape[1] // 2
+    return lax.dynamic_slice_in_dim(values, which * half, half, 1)
+
+
+class PairSum:
+    def __init__(self, product):
+        self.plain = lax.axis_size("dp") != 4
+        if self.plain:
+            self.sum = jnp.stack([product(0), product(1)]).astype(jnp.bfloat16)
+            return
+        self.core = lax.rem(lax.axis_index("dp"), 2)
+        away = product(1 - self.core).astype(jnp.bfloat16)
+        came = lax.ppermute(away, "dp", PAIR)
+        mine = held(product(self.core))
+        self.sum = (mine + came.astype(jnp.float32)).astype(jnp.bfloat16)
+
+    def cross(self):
+        self.other = lax.psum(self.sum, "dp") if self.plain else lax.ppermute(self.sum, "dp", CROSS)
+        return self
+
+    def join(self):
+        if self.plain:
+            self.total = self.other
+        else:
+            self.total = (self.sum.astype(jnp.float32) + self.other.astype(jnp.float32)).astype(jnp.bfloat16)
+        return self
+
+    def settle(self):
+        if self.plain:
+            first, second = self.total[0], self.total[1]
+        else:
+            back = lax.ppermute(self.total, "dp", PAIR)
+            first = jnp.where(self.core == 0, self.total, back)
+            second = jnp.where(self.core == 0, back, self.total)
+        return first.astype(jnp.float32), second.astype(jnp.float32)
 
 
 def after(values, earlier):
-    flat, tree = jax.tree.flatten(values)
-
     def kernel(*refs):
         del refs
 
-    held = pl.pallas_call(
+    return pl.pallas_call(
         kernel,
-        out_shape=[jax.ShapeDtypeStruct(v.shape, v.dtype) for v in flat],
-        in_specs=[ANY] * (len(flat) + 1),
-        out_specs=[ANY] * len(flat),
-        input_output_aliases={i: i for i in range(len(flat))},
-    )(*flat, earlier)
-    return jax.tree.unflatten(tree, held)
+        out_shape=[jax.ShapeDtypeStruct(v.shape, v.dtype) for v in values],
+        in_specs=[ANY] * (len(values) + 1),
+        out_specs=[ANY] * len(values),
+        input_output_aliases={i: i for i in range(len(values))},
+    )(*values, earlier)
 
 
 def per_device(
@@ -1271,33 +1447,50 @@
     grad_logits = (
         token_grad[:, None] * (onehot - weights.reshape(BLOCK, local_vocab).astype(jnp.float32) * share[:, None])
     ).astype(jnp.bfloat16)
-    head_sum = rounded_sum(dot_tn(final_full.reshape(BLOCK, D), grad_logits))
+    final_rows = final_full.reshape(BLOCK, D)
+    head_sum = PairSum(lambda which: dot_tn(half_of(final_rows, which), grad_logits)).cross()
 
     grad_stream, grad_own, end_sums = final_grad_rows(
-        grad_logits.reshape(shards, rows, local_vocab), head_weight, normed, inverse, row_of(lnf_gain), sizes, 3
+        grad_logits.reshape(shards, rows, local_vocab), head_weight, normed, inverse, row_of(lnf_gain), sizes, 3,
+        (head_sum.sum,),
     )
     grad_full, grad_ctx, grad_up, up_sums = branch_grad_rows(
         grad_own, out_flat, down_weight, slope, sizes, 4
     )
     grad_rows = grad_full.reshape(BLOCK, D)
-    out_grad = dot_tn(ctx, grad_rows).astype(jnp.bfloat16)
-    down_grad = dot_tn(act.reshape(BLOCK, local_hidden), grad_rows).astype(jnp.bfloat16)
-    up_grad = dot_tn(second_full.reshape(BLOCK, D), grad_up.reshape(BLOCK, local_hidden)).astype(jnp.bfloat16)
-    middle = lax.psum(after((out_grad, down_grad, up_grad, up_sums[0].astype(jnp.bfloat16)), head_sum[:8, :128]), "dp")
+    act_rows = act.reshape(BLOCK, local_hidden)
+    second_rows = second_full.reshape(BLOCK, D)
+    up_rows = grad_up.reshape(BLOCK, local_hidden)
+    sums = [
+        PairSum(lambda which: dot_tn(ctx, half_of(grad_rows, which))),
+        PairSum(lambda which: dot_tn(act_rows, half_of(grad_rows, which))),
+        PairSum(lambda which: dot_tn(half_of(second_rows, which), up_rows)),
+    ]
+    for one in sums:
+        one.cross()
+    made = [one.sum for one in sums]
     grad_qkv, qkv_sums = attention_backward(
-        flat_qkv, start_col, first_tile, local_heads, ctx, lse, grad_ctx.reshape(BLOCK, inner), planes
+        flat_qkv, start_col, first_tile, local_heads, ctx, lse, grad_ctx.reshape(BLOCK, inner), planes,
+        made,
     )
-    qkv_grad = dot_tn(first_full.reshape(BLOCK, D), grad_qkv).astype(jnp.bfloat16)
+    first_rows = first_full.reshape(BLOCK, D)
+    sums.append(PairSum(lambda which: dot_tn(half_of(first_rows, which), grad_qkv)))
+    sums[-1].cross()
     qkv_sums = qkv_sums[:, 0]
     qv_grad = jnp.concatenate([qkv_sums[:, :HEAD_DIM], qkv_sums[:, 2 * HEAD_DIM :]], axis=-1)
-    last = lax.psum(after((qkv_grad, qv_grad.astype(jnp.bfloat16)), jnp.concatenate([v[:8, :128] for v in middle[:3]] + [jnp.broadcast_to(middle[3][None, :128], (8, 128))])), "dp")
+    split = local_heads * 2 * HEAD_DIM
+    biases = jnp.concatenate([qv_grad.reshape(-1), up_sums[0]])
+    biases = jnp.pad(biases[None, :], ((0, 7), (0, D - biases.shape[0])))
     gains = jnp.concatenate([row_of(ln1_gain), row_of(ln2_gain)], axis=0)
-    grad_input, start_sums = input_grad_rows(
+    grad_input, small, biases = input_grad_rows(
         own, grad_stream, hid, grad_qkv.reshape(shards, rows, width), grad_up, qkv_flat, up_weight, gains,
-        sizes, 5,
+        end_sums, biases, sizes, lax.axis_size("dp"), 5, (sums[-1].sum, head_sum.join().total),
     )
-    small = lax.psum(jnp.concatenate([start_sums[:4], end_sums[:3]], axis=0), ("dp", "seq"))
-    wide = lambda values: values.astype(jnp.float32)
+    for one, other in zip(sums, after([one.other for one in sums], small)):
+        one.other = other
+        one.join()
+    out_grad, down_grad, up_grad, qkv_grad = [one.settle() for one in sums]
+    head_grad = head_sum.settle()
     return (
         losses[None],
         output[None],
@@ -1306,16 +1499,16 @@
         small[1],
         small[2],
         small[3],
-        wide(last[0]).reshape(qkv_weight.shape),
-        wide(last[1]),
-        wide(middle[0]).reshape(out_weight.shape),
-        wide(middle[2]),
-        wide(middle[3]),
-        wide(middle[1]),
+        jnp.concatenate(qkv_grad, axis=0).reshape(qkv_weight.shape),
+        biases[0, :split].reshape(local_heads, 2 * HEAD_DIM),
+        jnp.concatenate(out_grad, axis=1).reshape(out_weight.shape),
+        jnp.concatenate(up_grad, axis=0),
+        biases[0, split : split + local_hidden],
+        jnp.concatenate(down_grad, axis=1),
         small[6],
         small[4],
         small[5],
-        wide(head_sum),
+        jnp.concatenate(head_grad, axis=0),
     )
 
 

time: 1120 us -> 1010 us (0.902)
  waiting for transfers between devices: 115 us -> 0.04 us
  other arithmetic: 70 us -> 122 us
  blocking collectives: 88.8 us -> 37.1 us
  between operations: 15.4 us -> 2.27 us
  starting transfers between devices: 0.12 us -> 11.5 us
    psum x3 -> x0, waiting for transfers between devices: 115 us -> none  [the longest x1 115 us: per_device(): lax.psum(after((out_grad, down_grad, up_grad, up_sums[0].astype(jnp.bfloa...]
    psum x3 -> x0, blocking collectives: 51.7 us -> none  [the longest x1 39.4 us: per_device(): lax.psum(jnp.concatenate([start_sums[:4], end_sums[:3]], axis=0), ('dp',...]
    concatenate x3 -> x5, other arithmetic: 1.19 us -> 22.6 us  [the longest x1 13.2 us: per_device(): jnp.concatenate(head_grad, axis=0)]
    pallas_call x6, Pallas kernels: 634 us -> 649 us  [call(): pl.pallas_call(body, out_shape=out_shape, in_specs=[ANY] * len(before) +...]
    convert_element_type x5 -> x10, other arithmetic: 25.7 us -> 37.6 us  [the longest x5 21.9 us: join(): (self.sum.astype(jnp.float32) + self.other.astype(jnp.float32)).astype(jn...]
    ppermute x0 -> x15, starting transfers between devices: none -> 11.5 us  [the longest x5 6.36 us: cross(): lax.ppermute(self.sum, 'dp', CROSS)]
    dot_general x5 -> x10, matrix products: 78.4 us -> 85.4 us  [dot_tn(): lax.dot_general(left, right, (((0,), (0,)), ((), ())), preferred_element_...]
  transfers between devices with their start and end apart: 3 -> 15, of which waited for: 1 -> 0; matrix products, arithmetic and copies ran while one was open for 7% -> 14% of each run, Pallas kernels for 32% -> 35%
where the time goes in v3:
time: 1010 us
  Pallas kernels  702 us (70%)
  other arithmetic  122 us (12%)
  matrix products  85.4 us (8%)
  local copies, waits for them, and re-layouts  49.1 us (5%)
  blocking collectives  37.1 us (4%)
  starting transfers between devices  11.5 us (1%)
    pallas_call x6, Pallas kernels, call(): pl.pallas_call(body, out_shape=out_shape, in_specs=[ANY] * len(before) +...  649 us
    dot_general x10, matrix products, dot_tn(): lax.dot_general(left, right, (((0,), (0,)), ((), ())), preferred_element_...  85.4 us
    pallas_call x1, Pallas kernels, attention_backward(): pl.pallas_call(kernel, grid_spec=pltpu.PrefetchScalarGridSpec(num_scalar_...  31.6 us
    all_gather x1, blocking collectives, per_device(): gathered = lax.all_gather(stats[:, :3].T, 'seq')  30.8 us
    convert_element_type x5, other arithmetic, join(): (self.sum.astype(jnp.float32) + self.other.astype(jnp.float32)).astype(jn...  21.9 us
    pallas_call x1, Pallas kernels, attention_forward(): pl.pallas_call(kernel, grid_spec=pltpu.PrefetchScalarGridSpec(num_scalar_...  21.7 us
    convert_element_type x2, other arithmetic, per_device(): grad_logits = (token_grad[:, None] * (onehot - weights.reshape(BLOCK, loc...  20.6 us
  transfers between devices with their start and end apart: 15, of which 0 were waited for; matrix products, arithmetic and copies ran while one was open for 14% of the time, Pallas kernels for 35%

profile of v3, /device:TPU:0, one launch (start us, length us, event | category | flops | bytes accessed | tf_op | source)
XLA Modules:
  0.0 1009.6 jit_solution(14511566137956722594)
XLA Ops:
  14.0 4.2 copy.130
  18.2 3.7 fusion.46
  25.8 110.7 %shard_map.314 = (bf16[8,256,2048]{2,1,0:T(8,128)(2,1)}, bf16[8,256,2048]{2,1,0:T(8,128)(2,1)}, bf16[8,256,2048]{2,1,0:T(8,128)(2,1)}, bf16[8,256,768]{2,1,0:T(8...) custom-call(bf16[256,2048]{1,0:T(8,128)(2,1)} %bitcast.217, ...), custom_call_target="tpu_custom_call" | custom-call | flops 15032385536 | bytes 268435456 | tf_op jit(solution)/shard_map/pallas_call | solution.py:534
  136.5 21.7 %shard_map.315 = (bf16[2048,256]{1,0:T(8,128)(2,1)}, f32[2,2048,1]{2,1,0:T(8,128)}) custom-call(s32[8]{0:T(128)} %and_select_fusion.first_ref, bf16[2048,768]{1,0:T(8,128)(2,1)} %bitcast.150, bf16[2048,768]{1,0:T(8,128)(2,1)} %bitcast.151, bf16[2048,768]{1,0:T(8,128)(2,1)} %bitcast.152, s32[2048,1]{1,0:T(8,128)} %subtract_subtract_fusion.start_ref), custom_call_target="tpu_custom_call" | custom-call | tf_op jit(solution)/shard_map/pallas_call | solution.py:389
  158.2 98.9 %shard_map.316 = (bf16[256,2048]{1,0:T(8,128)(2,1)}, bf16[256,2048]{1,0:T(8,128)(2,1)}, f32[256,2048]{1,0:T(8,128)}, f32[256,1]{1,0:T(8,128)}) custom-call(bf16[256,2048]{1,0:T(8,128)(2,1)} %bitcast.218, bf16[8,256,256]{2,1,0:T(8,128)(2,1)} %bitcast.165, bf16[8,256,1024]{2,1,0:T(8,128)(2,1)} %get-tuple-element.50.refs_2_, bf16[256,2048]{1,0:T(8,128)(2,1)} %bitcast.215, ...), custom_call_target="tpu_custom_call" | custom-call | flops 10737418240 | bytes 268435456 | tf_op jit(solution)/shard_map/pallas_call | solution.py:534
  257.1 115.3 %shard_map.317 = (bf16[8,256,2048]{2,1,0:T(8,128)(2,1)}, bf16[8,256,3328]{2,1,0:T(8,128)(2,1)}, f32[2048,128]{1,0:T(8,128)}) custom-call(bf16[256,2048]{1,0:T(8,128)(2,1)} %get-tuple-element.51.refs_0_, bf16[2048,3328]{1,0:T(8,128)(2,1)} %refs_2_.2, s32[2048,1]{1,0:T(8,128)} %copy.101.refs_2_), custom_call_target="tpu_custom_call" | custom-call | flops 27917287424 | bytes 268435456 | tf_op jit(solution)/shard_map/pallas_call | solution.py:534
  374.1 30.8 %all-gather.1 = f32[8,3,2048]{2,1,0:T(4,128)S(1)} all-gather(f32[1,3,2048]{2,1,0:T(4,128)S(1)} %copy.102), channel_id=2, replica_groups=mesh['dp'=4,'seq'=8] {'seq'}, dimensions={0}, use_global_device_ids=true | all-gather | bytes 221184 | tf_op jit(solution)/shard_map/all_gather | solution.py:1427
  405.9 6.4 psum.7
  434.2 7.0 exponential_reduce_fusion
  441.3 10.8 %fusion.2 = bf16[2048,3328]{1,0:T(8,128)(2,1)S(1)} fusion(f32[2048]{0:T(1024)S(1)} %exponential_reduce_fusion, s32[3328]{0:T(1024)S(1)} %iota_add_fusion, f32[2048]{0:T(1024)S(1)} %select_reduce_fusion, s32[2048]{0:T(1024)S(1)} %bitcast.169, bf16[8,256,3328]{2,1,0:T(8,128)(2,1)} %get-tuple-element.57), kind=kLoop, calls=%fused_computation.3 | loop fusion | flops 47710208 | bytes 27300864 | tf_op jit(solution)/shard_map/convert_element_type | solution.py:1449
  452.1 17.0 %convolution_convert_fusion = bf16[1024,3328]{1,0:T(8,128)(2,1)} fusion(bf16[2048,3328]{1,0:T(8,128)(2,1)S(1)} %fusion.2, bf16[2048,2048]{1,0:T(8,128)(2,1)S(1)} %bitcast.229, s32[]{:T(128)S(6)} %select_n.77), kind=kOutput, calls=%fused_computation.8 | convolution fusion | flops 13962051584 | bytes 24641540 | tf_op jit(solution)/shard_map/dot_general | solution.py:323
  470.4 23.4 %fusion.10 = f32[1024,3328]{1,0:T(8,128)} fusion(bf16[2048,3328]{1,0:T(8,128)(2,1)} %copy-done, bf16[2048,2048]{1,0:T(8,128)(2,1)} %bitcast.226, s32[]{:T(128)S(6)} %select_n.76), kind=kOutput, calls=%fused_computation.24 | convolution fusion | flops 13958643712 | bytes 31457284 | tf_op jit(solution)/shard_map/dot_general | solution.py:323
  494.9 9.8 multiply_convert_fusion.refs_1_
  504.8 7.5 add_convert_fusion.1.refs_0_
  512.4 114.0 %shard_map.318 = (f32[256,2048]{1,0:T(8,128)}, bf16[256,2048]{1,0:T(8,128)(2,1)}, f32[8,2048]{1,0:T(8,128)}) custom-call(bf16[1024,3328]{1,0:T(8,128)(2,1)} %add_convert_fusion.1.refs_0_, bf16[8,256,3328]{2,1,0:T(8,128)(2,1)} %multiply_convert_fusion.refs_1_, bf16[2048,3328]{1,0:T(8,128)(2,1)} %refs_2_.2, f32[256,2048]{1,0:T(8,128)} %get-tuple-element.58.refs_3_, ...), custom_call_target="tpu_custom_call" | custom-call | flops 27917287424 | bytes 268435456 | tf_op jit(solution)/shard_map/pallas_call | solution.py:534
  626.5 93.1 %shard_map.319 = (bf16[8,256,2048]{2,1,0:T(8,128)(2,1)}, bf16[8,256,256]{2,1,0:T(8,128)(2,1)}, bf16[8,256,1024]{2,1,0:T(8,128)(2,1)}, f32[8,1024]{1,0:T(8,128)}) custom-call(bf16[256,2048]{1,0:T(8,128)(2,1)} %get-tuple-element.60.refs_0_, bf16[256,2048]{1,0:T(8,128)(2,1)} %bitcast.216, bf16[1024,2048]{1,0:T(8,128)(2,1)} %refs_2_.3, ...), custom_call_target="tpu_custom_call" | custom-call | flops 10737418240 | bytes 268435456 | tf_op jit(solution)/shard_map/pallas_call | solution.py:534
  719.6 8.2 fusion.25
  727.9 4.8 fusion.22
  732.7 7.0 fusion.18
  744.6 3.7 fusion.20
  748.4 4.6 fusion.7
  761.9 31.6 %shard_map.320 = (bf16[2048,768]{1,0:T(8,128)(2,1)}, f32[2,1,384]{2,1,0:T(1,128)}) custom-call(s32[8]{0:T(128)} %and_select_fusion.first_ref, bf16[2048,768]{1,0:T(8,128)(2,1)} %bitcast.153, bf16[2048,768]{1,0:T(8,128)(2,1)} %bitcast.154, bf16[2048,768]{1,0:T(8,128)(2,1)} %bitcast.155, s32[2048,1]{1,0:T(8,128)} %subtract_subtract_fusion.start_ref, ...), custom_call_target="tpu_custom_call" | custom-call | tf_op jit(solution)/shard_map/pallas_call | solution.py:472
  794.2 8.0 fusion.28
  805.6 5.3 fusion.12
  810.9 9.4 add_convert_fusion.refs_1_
  826.5 116.7 %shard_map.321 = (f32[256,2048]{1,0:T(8,128)}, f32[8,2048]{1,0:T(8,128)}, f32[8,2048]{1,0:T(8,128)}) custom-call(bf16[1024,768]{1,0:T(8,128)(2,1)} %add_convert_fusion.7.refs_0_, bf16[1024,3328]{1,0:T(8,128)(2,1)} %add_convert_fusion.refs_1_, bf16[256,2048]{1,0:T(8,128)(2,1)} %bitcast.219, f32[256,2048]{1,0:T(8,128)} %get-tuple-element.67.refs_3_, ...), custom_call_target="tpu_custom_call" | custom-call | flops 15032385536 | bytes 268435456 | tf_op jit(solution)/shard_map/pallas_call | solution.py:534
  954.4 4.5 add_convert_fusion.3
  968.4 8.2 reshape.767
  978.5 4.4 maximum_convert_fusion.2
  984.8 4.9 maximum_convert_fusion.1
  989.9 4.0 broadcast_select_fusion.1
  993.9 13.2 %maximum_convert_fusion = f32[2048,3328]{1,0:T(8,128)} fusion(bf16[1024,3328]{1,0:T(8,128)(2,1)S(1)} %get-tuple-element.84, bf16[1024,3328]{1,0:T(8,128)(2,1)S(1)} %get-tuple-element.83), kind=kLoop, calls=%fused_computation.5 | loop fusion | flops 27262976 | bytes 40894464 | tf_op jit(solution)/shard_map/concatenate | solution.py:1511
  (186 shorter events, 94.6 us)
Async XLA Ops:
  8.4 13.5 %copy-start.10 = (f32[2048]{0:T(1024)}, f32[2048]{0:T(1024)S(1)}, u32[]{:S(2)}) copy-start(f32[2048]{0:T(1024)S(1)} %broadcast_in_dim.107) | copy-start | bytes 24580
  372.4 32.9 %copy-start.11 = (s32[1,8]{1,0:T(1,128)S(1)}, s32[1,8]{1,0:T(1,128)}, u32[]{:S(2)}) copy-start(s32[1,8]{1,0:T(1,128)} %param.21) | copy-start | bytes 100
  372.4 32.9 %copy-start.12 = (f32[1,8]{1,0:T(1,128)S(1)}, f32[1,8]{1,0:T(1,128)}, u32[]{:S(2)}) copy-start(f32[1,8]{1,0:T(1,128)} %param.23) | copy-start | bytes 100
  372.4 40.5 %copy-start.13 = (s32[1,8]{1,0:T(1,128)S(1)}, s32[1,8]{1,0:T(1,128)}, u32[]{:S(2)}) copy-start(s32[1,8]{1,0:T(1,128)} %param.22) | copy-start | bytes 100
  423.4 10.9 %copy-start.4 = (f32[2048,128]{1,0:T(8,128)S(1)}, f32[2048,128]{1,0:T(8,128)}, u32[]{:S(2)}) copy-start(f32[2048,128]{1,0:T(8,128)} %get-tuple-element.52) | copy-start | bytes 3145732
  434.2 17.8 %slice-start.8 = ((s8[8388608]{0:T(1024)(128)(4,1)}), s8[4194304]{0:T(1024)(128)(4,1)S(1)}, s32[]{:S(2)}) async-start(s8[8388608]{0:T(1024)(128)(4,1)} %bitcast.227), calls=%async_computation.8 | async-start | bytes 8388608
  441.3 10.8 %slice-start.9 = ((s8[8388608]{0:T(1024)(128)(4,1)}), s8[4194304]{0:T(1024)(128)(4,1)S(1)}, s32[]{:S(2)}) async-start(s8[8388608]{0:T(1024)(128)(4,1)} %bitcast.227), calls=%async_computation.9 | async-start | bytes 8388608
  452.1 17.1 %copy-start = (bf16[2048,3328]{1,0:T(8,128)(2,1)}, bf16[2048,3328]{1,0:T(8,128)(2,1)S(1)}, u32[]{:S(2)}) copy-start(bf16[2048,3328]{1,0:T(8,128)(2,1)S(1)} %fusion.2) | copy-start | bytes 40894468
  469.1 35.7 %collective-permute-start = (bf16[1024,3328]{1,0:T(8,128)(2,1)}, bf16[1024,3328]{1,0:T(8,128)(2,1)}, u32[]{:S(2)}, u32[]{:S(2)}) collective-permute-start(bf16[1024,3328]{1,0:T(8,128)(2,1)} %convolution_convert_fusion), channel_id=1, source_target_pairs={{0,8},{8,0},{16,24},{24,16},{1,9},{9,1},{17,25},{25,17},{2,10},{10... | collective-permute-start | bytes 20447240 | tf_op jit(solution)/shard_map/ppermute | solution.py:1351
  470.3 24.6 %slice-start = ((s8[13631488]{0:T(1024)(128)(4,1)}), s8[1048576]{0:T(1024)(128)(4,1)S(1)}, s32[]{:S(2)}) async-start(s8[13631488]{0:T(1024)(128)(4,1)} %bitcast.156), calls=%async_computation | async-start | bytes 2097152
  470.4 24.6 %slice-start.1 = ((s8[13631488]{0:T(1024)(128)(4,1)}), s8[4194304]{0:T(1024)(128)(4,1)S(1)}, s32[]{:S(2)}) async-start(s8[13631488]{0:T(1024)(128)(4,1)} %bitcast.156), calls=%async_computation.1 | async-start | bytes 8388608
  470.4 24.6 %slice-start.2 = ((s8[13631488]{0:T(1024)(128)(4,1)}), s8[4194304]{0:T(1024)(128)(4,1)S(1)}, s32[]{:S(2)}) async-start(s8[13631488]{0:T(1024)(128)(4,1)} %bitcast.156), calls=%async_computation.2 | async-start | bytes 8388608
  470.4 24.6 %slice-start.3 = ((s8[13631488]{0:T(1024)(128)(4,1)}), s8[4194304]{0:T(1024)(128)(4,1)S(1)}, s32[]{:S(2)}) async-start(s8[13631488]{0:T(1024)(128)(4,1)} %bitcast.156), calls=%async_computation.3 | async-start | bytes 8388608
  512.3 298.6 %collective-permute-start.5 = (bf16[1024,3328]{1,0:T(8,128)(2,1)}, bf16[1024,3328]{1,0:T(8,128)(2,1)}, u32[]{:S(2)}, u32[]{:S(2)}) collective-permute-start(bf16[1024,3328]{1,0:T(8,128)(2,1)} %add_convert_fusion.1.refs_0_), channel_id=1, source_target_pairs={{0,16},{16,0},{8,24},{24,8},{1,17},{17,1},{9,25},{25,9},{2,18},{18... | collective-permute-start | bytes 20447240 | tf_op jit(solution)/shard_map/ppermute | solution.py:1356
  727.8 27.8 %collective-permute-start.3 = (bf16[1024,1024]{1,0:T(8,128)(2,1)S(1)}, bf16[1024,1024]{1,0:T(8,128)(2,1)S(1)}, u32[]{:S(2)}, u32[]{:S(2)}) collective-permute-start(bf16[1024,1024]{1,0:T(8,128)(2,1)S(1)} %fusion.25), channel_id=1, source_target_pairs={{0,8},{8,0},{16,24},{24,16},{1,9},{9,1},{17,25},{25,17},{2,10},{10... | collective-permute-start | bytes 6291464 | tf_op jit(solution)/shard_map/ppermute | solution.py:1351
  727.9 20.5 %slice-start.6 = ((s8[8388608]{0:T(1024)(128)(4,1)}), s8[4194304]{0:T(1024)(128)(4,1)S(1)}, s32[]{:S(2)}) async-start(s8[8388608]{0:T(1024)(128)(4,1)} %bitcast.223), calls=%async_computation.6 | async-start | bytes 8388608
  732.7 15.7 %slice-start.7 = ((s8[8388608]{0:T(1024)(128)(4,1)}), s8[4194304]{0:T(1024)(128)(4,1)S(1)}, s32[]{:S(2)}) async-start(s8[8388608]{0:T(1024)(128)(4,1)} %bitcast.223), calls=%async_computation.7 | async-start | bytes 8388608
  739.7 18.5 %collective-permute-start.2 = (bf16[1024,1024]{1,0:T(8,128)(2,1)S(1)}, bf16[1024,1024]{1,0:T(8,128)(2,1)S(1)}, u32[]{:S(2)}, u32[]{:S(2)}) collective-permute-start(bf16[1024,1024]{1,0:T(8,128)(2,1)S(1)} %fusion.22), channel_id=1, source_target_pairs={{0,8},{8,0},{16,24},{24,16},{1,9},{9,1},{17,25},{25,17},{2,10},{10... | collective-permute-start | bytes 6291464 | tf_op jit(solution)/shard_map/ppermute | solution.py:1351
  744.6 8.5 collective-permute-start.1
  754.0 189.3 %collective-permute-start.6 = (bf16[256,1024]{1,0:T(8,128)(2,1)}, bf16[256,1024]{1,0:T(8,128)(2,1)}, u32[]{:S(2)}, u32[]{:S(2)}) collective-permute-start(bf16[256,1024]{1,0:T(8,128)(2,1)} %add_convert_fusion.9.rest_0_), channel_id=1, source_target_pairs={{0,16},{16,0},{8,24},{24,8},{1,17},{17,1},{9,25},{25,9},{2,18},{18... | collective-permute-start | bytes 1572872 | tf_op jit(solution)/shard_map/ppermute | solution.py:1356
  757.7 185.6 %collective-permute-start.8 = (bf16[1024,1024]{1,0:T(8,128)(2,1)}, bf16[1024,1024]{1,0:T(8,128)(2,1)}, u32[]{:S(2)}, u32[]{:S(2)}) collective-permute-start(bf16[1024,1024]{1,0:T(8,128)(2,1)} %add_convert_fusion.4.rest_2_), channel_id=1, source_target_pairs={{0,16},{16,0},{8,24},{24,8},{1,17},{17,1},{9,25},{25,9},{2,18},{18... | collective-permute-start | bytes 6291464 | tf_op jit(solution)/shard_map/ppermute | solution.py:1356
  760.3 182.9 %collective-permute-start.7 = (bf16[1024,1024]{1,0:T(8,128)(2,1)}, bf16[1024,1024]{1,0:T(8,128)(2,1)}, u32[]{:S(2)}, u32[]{:S(2)}) collective-permute-start(bf16[1024,1024]{1,0:T(8,128)(2,1)} %add_convert_fusion.5.rest_1_), channel_id=1, source_target_pairs={{0,16},{16,0},{8,24},{24,8},{1,17},{17,1},{9,25},{25,9},{2,18},{18... | collective-permute-start | bytes 6291464 | tf_op jit(solution)/shard_map/ppermute | solution.py:1356
  794.2 11.4 %copy-start.14 = (bf16[2048,768]{1,0:T(8,128)(2,1)S(1)}, bf16[2048,768]{1,0:T(8,128)(2,1)}, u32[]{:S(2)}) copy-start(bf16[2048,768]{1,0:T(8,128)(2,1)} %get-tuple-element.66) | copy-start | bytes 9437188
  802.1 18.2 %collective-permute-start.4 = (bf16[1024,768]{1,0:T(8,128)(2,1)}, bf16[1024,768]{1,0:T(8,128)(2,1)}, u32[]{:S(2)}, u32[]{:S(2)}) collective-permute-start(bf16[1024,768]{1,0:T(8,128)(2,1)} %fusion.28), channel_id=1, source_target_pairs={{0,8},{8,0},{16,24},{24,16},{1,9},{9,1},{17,25},{25,17},{2,10},{10... | collective-permute-start | bytes 4718600 | tf_op jit(solution)/shard_map/ppermute | solution.py:1351
  820.3 169.5 %collective-permute-start.14 = (bf16[1024,3328]{1,0:T(8,128)(2,1)}, bf16[1024,3328]{1,0:T(8,128)(2,1)}, u32[]{:S(2)}, u32[]{:S(2)}) collective-permute-start(bf16[1024,3328]{1,0:T(8,128)(2,1)} %add_convert_fusion.refs_1_), channel_id=1, source_target_pairs={{0,8},{8,0},{16,24},{24,16},{1,9},{9,1},{17,25},{25,17},{2,10},{10... | collective-permute-start | bytes 20447240 | tf_op jit(solution)/shard_map/ppermute | solution.py:1370
  823.2 120.1 %collective-permute-start.9 = (bf16[1024,768]{1,0:T(8,128)(2,1)}, bf16[1024,768]{1,0:T(8,128)(2,1)S(1)}, u32[]{:S(2)}, u32[]{:S(2)}) collective-permute-start(bf16[1024,768]{1,0:T(8,128)(2,1)} %add_convert_fusion.7.refs_0_), channel_id=1, source_target_pairs={{0,16},{16,0},{8,24},{24,8},{1,17},{17,1},{9,25},{25,9},{2,18},{18... | collective-permute-start | bytes 4718600 | tf_op jit(solution)/shard_map/ppermute | solution.py:1356
  947.9 15.2 %collective-permute-start.10 = (bf16[1024,768]{1,0:T(8,128)(2,1)}, bf16[1024,768]{1,0:T(8,128)(2,1)}, u32[]{:S(2)}, u32[]{:S(2)}) collective-permute-start(bf16[1024,768]{1,0:T(8,128)(2,1)} %add_convert_fusion.6), channel_id=1, source_target_pairs={{0,8},{8,0},{16,24},{24,16},{1,9},{9,1},{17,25},{25,17},{2,10},{10... | collective-permute-start | bytes 4718600 | tf_op jit(solution)/shard_map/ppermute | solution.py:1370
  953.9 7.5 collective-permute-start.11
  954.4 22.3 %collective-permute-start.13 = (bf16[1024,1024]{1,0:T(8,128)(2,1)S(1)}, bf16[1024,1024]{1,0:T(8,128)(2,1)}, u32[]{:S(2)}, u32[]{:S(2)}) collective-permute-start(bf16[1024,1024]{1,0:T(8,128)(2,1)S(1)} %add_convert_fusion.2), channel_id=1, source_target_pairs={{0,8},{8,0},{16,24},{24,16},{1,9},{9,1},{17,25},{25,17},{2,10},{10... | collective-permute-start | bytes 6291464 | tf_op jit(solution)/shard_map/ppermute | solution.py:1370
  960.2 22.8 %collective-permute-start.12 = (bf16[1024,1024]{1,0:T(8,128)(2,1)}, bf16[1024,1024]{1,0:T(8,128)(2,1)}, u32[]{:S(2)}, u32[]{:S(2)}) collective-permute-start(bf16[1024,1024]{1,0:T(8,128)(2,1)} %add_convert_fusion.3), channel_id=1, source_target_pairs={{0,8},{8,0},{16,24},{24,16},{1,9},{9,1},{17,25},{25,17},{2,10},{10... | collective-permute-start | bytes 6291464 | tf_op jit(solution)/shard_map/ppermute | solution.py:1370
  993.9 13.2 %copy-start.7 = (bf16[256,2048]{1,0:T(8,128)(2,1)S(1)}, bf16[256,2048]{1,0:T(8,128)(2,1)}, u32[]{:S(2)}) copy-start(bf16[256,2048]{1,0:T(8,128)(2,1)} %get-tuple-element.53) | copy-start | bytes 3145732
  993.9 14.2 %copy-start.5 = (f32[256,2048]{1,0:T(8,128)S(1)}, f32[256,2048]{1,0:T(8,128)}, u32[]{:S(2)}) copy-start(f32[256,2048]{1,0:T(8,128)} %get-tuple-element.72) | copy-start | bytes 6291460
  (11 other events, 71.0 us)

commit v4 on v3

--- a/solution.py
+++ b/solution.py
@@ -152,8 +152,6 @@
 
     def complete(k):
         slow = grid.nearest(0, k)
-        if k > 0:
-            todo.append((slow, me[1], k * n[1]))
         for l in range(1, n[1]):
             fast = grid.nearest(1, l)
             if cut[0]:
@@ -176,28 +174,40 @@
                 fast = grid.nearest(1, l)
                 arrived(me[0], fast, half, 1)
                 onward(me[0], fast, half, 1, 1)
+    if cut[1]:
+        settle(0)
     for k in range(1, n[0]):
         slow = grid.nearest(0, k)
-        for half in range(halves):
-            if cut[0]:
+        if cut[0]:
+            for half in range(halves):
                 arrived(slow, me[1], half, 0)
                 onward(slow, me[1], half, 0, 0)
                 spread(slow, me[1], half, 0, 1)
-            if half < halves - 1:
-                work()
+        complete(k - 1)
+        work(len(todo))
         if cut[1]:
-            settle(k - 1)
-        complete(k - 1)
+            settle(k)
+        todo.append((slow, me[1], k * n[1]))
         work()
-    if cut[1]:
-        settle(n[0] - 1)
-    work(len(todo))
     complete(n[0] - 1)
     work(len(todo))
 
 
 def scatter_slots(n):
     return 1 if n == 2 else n + 1
+
+
+def scatter_plan(n):
+    plan = []
+    far = n[0] - 1
+    for k in range(far, -2, -1):
+        near = [("make", k + 1, 0)] if k + 1 <= far else []
+        back = [("chain", k + 2, 0)] if k + 2 <= far else []
+        if k >= 0:
+            plan += [("make", k, l) for l in range(n[1] - 1, 0, -1)] + back + near
+        else:
+            plan += near + back
+    return plan
 
 
 class Scatter:
@@ -259,20 +269,21 @@
                 self.last(0, 0, 1, slow, half, slow, me[1])
                 self.toward(0, 1, 0, 0, slow, half, slow, me[1])
 
-        for k in reversed(range(n[0])):
-            slow = grid.nearest(0, k)
-            for l in reversed(range(n[1])):
-                fast = grid.nearest(1, l)
-                produce(slow, fast)
-                for half in range(self.halves):
-                    if self.cut[0] and l > 0:
-                        self.toward(0, 0, 1, slow, fast, half, slow, fast)
-                    if self.cut[1] and k > 0:
-                        self.toward(1, 0, 0, fast, slow, half, slow, fast)
-            if k == 0:
-                made()
-            if self.cut[0] and k < n[0] - 1:
-                chain(k + 1)
+        def make(k, l):
+            slow, fast = grid.nearest(0, k), grid.nearest(1, l)
+            produce(slow, fast)
+            for half in range(self.halves):
+                if self.cut[0] and l > 0:
+                    self.toward(0, 0, 1, slow, fast, half, slow, fast)
+                if self.cut[1] and k > 0:
+                    self.toward(1, 0, 0, fast, slow, half, slow, fast)
+
+        for action, k, l in scatter_plan(n):
+            if action == "make":
+                make(k, l)
+            elif self.cut[0]:
+                chain(k)
+        made()
         between()
         if self.cut[1]:
             for half in range(self.halves):
@@ -505,9 +516,11 @@
 
 
 def gather_cut(sizes):
-    if sizes[0] == 4 and sizes[1] == 2:
-        return (1664, 384)
-    return (D // 2, D // 2)
+    return (1792, 256) if sizes == (4, 2) else (D // 2, D // 2)
+
+
+def scatter_cut(sizes):
+    return (1664, 384) if sizes == (4, 2) else (D // 2, D // 2)
 
 
 def columns_of(cut, kind):
@@ -569,7 +582,7 @@
 
 def sum_scratch(sizes, rows):
     shards = sizes[0] * sizes[1]
-    bufs, sems = scatter_scratch(sizes, HALVES, rows, D, gather_cut(sizes))
+    bufs, sems = scatter_scratch(sizes, HALVES, rows, D, scatter_cut(sizes))
     return (
         [pltpu.VMEM((shards, rows, D), jnp.bfloat16)]
         + bufs
@@ -579,7 +592,7 @@
 
 
 def run_scatter(grid, sizes, rows, scratch, produce, *hooks):
-    cut = gather_cut(sizes)
+    cut = scatter_cut(sizes)
     step = rows // HALVES
     parts, b0, b1, b2, b3, s0, s1, s2, s3, send_sems = scratch
     sender = Sender(send_sems)
@@ -597,12 +610,12 @@
 def production_order(grid):
     return [
         grid.index(grid.nearest(0, k), grid.nearest(1, l))
-        for k in reversed(range(grid.n[0]))
-        for l in reversed(range(grid.n[1]))
+        for action, k, l in scatter_plan(grid.n)
+        if action == "make"
     ]
 
 
-ROW_TILE = 32
+ROW_TILE = 64
 
 
 def tile_stats(values):
@@ -619,8 +632,8 @@
 
     def kernel(
         own_ref, norms_ref, qkvw_any, qkvb_ref, upw_any, upb_ref, cos_ref, below_ref, above_ref,
-        hid_any, one_any, two_any, qkv_any, act_any, slope_any,
-        full, send_sems, recv_sems, qkvw, upw, load_sems, one, two, qkv, act, slope, out_sems, row_sems,
+        plain_any, one_any, two_any, qkv_any, act_any, slope_any,
+        full, send_sems, recv_sems, qkvw, upw, load_sems, plain, one, two, qkv, act, slope, out_sems,
     ):
         grid = Grid2(sizes)
         loads = [
@@ -634,7 +647,7 @@
         open_copies = []
 
         def outs(place, slot):
-            pairs = ((one, one_any), (two, two_any), (qkv, qkv_any), (act, act_any), (slope, slope_any))
+            pairs = ((plain, plain_any), (one, one_any), (two, two_any), (qkv, qkv_any), (act, act_any), (slope, slope_any))
             return [
                 pltpu.make_async_copy(here.at[slot], there.at[place], out_sems.at[slot, i])
                 for i, (here, there) in enumerate(pairs)
@@ -654,6 +667,7 @@
                 here = span(index, ROW_TILE)
                 centered, inverse = tile_stats(full[place, here].astype(jnp.float32))
                 normed = centered * inverse
+                plain[slot, here] = normed.astype(jnp.bfloat16)
                 one[slot, here] = (normed * norms_ref[0:1] + norms_ref[1:2]).astype(jnp.bfloat16)
                 two[slot, here] = (normed * norms_ref[2:3] + norms_ref[3:4]).astype(jnp.bfloat16)
                 return _
@@ -692,17 +706,11 @@
             for copy in copies:
                 copy.start()
             open_copies.append(copies)
-            raw = pltpu.make_async_copy(full.at[place], hid_any.at[place], row_sems.at[order])
-            raw.start()
-            raw_copies.append(raw)
-
-        raw_copies = []
+
         run_gather(grid, sizes, rows, full, send_sems, recv_sems, ready)
         for copies in open_copies:
             for copy in copies:
                 copy.wait()
-        for copy in raw_copies:
-            copy.wait()
 
     def out(columns):
         return jax.ShapeDtypeStruct((shards, rows, columns), jnp.bfloat16)
@@ -720,9 +728,8 @@
             pltpu.VMEM(qkv_flat.shape, jnp.bfloat16),
             pltpu.VMEM(up_weight.shape, jnp.bfloat16),
             pltpu.SemaphoreType.DMA((2,)),
-            staged(D), staged(D), staged(width), staged(hidden), staged(hidden),
-            pltpu.SemaphoreType.DMA((2, 5)),
-            pltpu.SemaphoreType.DMA((shards,)),
+            staged(D), staged(D), staged(D), staged(width), staged(hidden), staged(hidden),
+            pltpu.SemaphoreType.DMA((2, 6)),
         ],
         2 * BLOCK * D * (width + hidden),
     )(own, norms, qkv_flat, qkv_bias, up_weight, up_bias, *planes)
@@ -874,7 +881,8 @@
             total = lax.fori_loop(0, tiles, weight_tile, jnp.zeros((rows, 128), jnp.float32))
             total = jnp.sum(total, axis=1, keepdims=True)
             lane = lax.broadcasted_iota(jnp.int32, (rows, 128), 1)
-            stats_ref[places, :] = jnp.where(lane == 0, top, jnp.where(lane == 1, total, pick))
+            found = jnp.where(lane == 0, top, jnp.where(lane == 1, total, pick))
+            stats_ref[:, places] = found.T[0:8]
             copy = pltpu.make_async_copy(weights.at[slot], weights_any.at[place], out_sems.at[slot])
             copy.start()
             open_copies.append(copy)
@@ -891,7 +899,7 @@
         [
             jax.ShapeDtypeStruct((shards, rows, D), jnp.bfloat16),
             jax.ShapeDtypeStruct((shards, rows, vocab), jnp.bfloat16),
-            jax.ShapeDtypeStruct((shards * rows, 128), jnp.float32),
+            jax.ShapeDtypeStruct((8, shards * rows), jnp.float32),
         ],
         [VMEM, ANY, VMEM],
         [ANY, ANY, VMEM],
@@ -1181,17 +1189,121 @@
             copy.wait_send()
 
 
+def score_rows(stats, seg_row, examples, sizes, replicas, collective):
+    shards = sizes[0] * sizes[1]
+    width = BLOCK // shards
+
+    def kernel(
+        stats_ref, seg_ref, examples_ref, coef_ref, losses_ref,
+        came, full, ratio, ratios, spread_send, spread_recv, back_send, back_recv, cross_send, cross_recv,
+    ):
+        seq, dp = lax.axis_index("seq"), lax.axis_index("dp")
+        peers = {
+            "seq": [(step, lax.rem(seq + step, shards)) for step in range(1, shards)],
+            "dp": [(step, lax.rem(dp + step, replicas)) for step in range(1, replicas)],
+        }
+        barrier = pltpu.get_barrier_semaphore()
+        for axis in peers:
+            for _, place in peers[axis]:
+                pl.semaphore_signal(barrier, inc=1, device_id={axis: place}, device_id_type=MESH)
+        pl.semaphore_wait(barrier, shards + replicas - 2)
+
+        def columns(place):
+            return pl.ds(pl.multiple_of(place * width, width), width)
+
+        def copy(axis, place, src, dst, send, recv):
+            return pltpu.make_async_remote_copy(
+                src_ref=src, dst_ref=dst, send_sem=send, recv_sem=recv, device_id={axis: place}, device_id_type=MESH
+            )
+
+        sent = [
+            copy("seq", place, stats_ref.at[:, columns(place)], came.at[step], spread_send.at[step], spread_recv.at[step])
+            for step, place in peers["seq"]
+        ]
+        for one in sent:
+            one.start()
+        mine = stats_ref[:, columns(seq)]
+        top, total, pick = mine[0:1], mine[1:2], mine[2:3]
+        for (step, _), one in zip(peers["seq"], sent):
+            one.wait_recv()
+            other = came[step]
+            joint = jnp.maximum(top, other[0:1])
+            total = total * jnp.exp(top - joint) + other[1:2] * jnp.exp(other[0:1] - joint)
+            pick = pick + other[2:3]
+            top = joint
+        log_total = top + jnp.log(total)
+        here = columns(seq)
+        full[0:1, here] = log_total
+        full[1:2, here] = pick - log_total
+        back = [
+            copy("seq", place, full.at[:, here], full.at[:, here], back_send.at[step], back_recv.at[step])
+            for step, place in peers["seq"]
+        ]
+        for one in back:
+            one.start()
+        for step, _ in peers["seq"]:
+            source = lax.rem(seq + shards - step, shards)
+            there = full.at[:, columns(source)]
+            copy("seq", source, there, there, back_send.at[step], back_recv.at[step]).wait_recv()
+        member = lax.broadcasted_iota(jnp.int32, (EXB, BLOCK), 0) == seg_ref[...]
+        counts, reference, sign = examples_ref[:, 0:1], examples_ref[:, 1:2], examples_ref[:, 2:3]
+        mean = jnp.sum(jnp.where(member, full[1:2, :], 0.0), axis=1, keepdims=True) / counts
+        log_ratio = mean - reference
+        ratio[...] = jnp.broadcast_to(jnp.sum(log_ratio, axis=0, keepdims=True), ratio.shape)
+        crossed = [
+            copy("dp", place, ratio, ratios.at[dp], cross_send.at[step], cross_recv.at[step])
+            for step, place in peers["dp"]
+        ]
+        for one in crossed:
+            one.start()
+        for one in crossed:
+            one.wait_recv()
+        ratios[dp] = ratio[...]
+        whole = ratios[0]
+        for place in range(1, replicas):
+            whole = whole + ratios[place]
+        center = whole[:, 0:1] / (replicas * EXB)
+        squashed = jax.nn.sigmoid(BETA * sign * (log_ratio - center))
+        losses_ref[...] = jnp.broadcast_to(1.0 - squashed, losses_ref.shape)
+        grad = -LOSS_SCALE * BETA * sign * squashed * (1.0 - squashed) / counts
+        token = jnp.sum(jnp.where(member, grad, 0.0), axis=0, keepdims=True)
+        coef_ref[...] = jnp.zeros_like(coef_ref)
+        coef_ref[0:1, :] = token
+        coef_ref[1:2, :] = token * jnp.exp(stats_ref[0:1, :] - full[0:1, :])
+        for one in sent + back + crossed:
+            one.wait_send()
+
+    dma = pltpu.SemaphoreType.DMA
+    return pl.pallas_call(
+        kernel,
+        out_shape=[
+            jax.ShapeDtypeStruct((8, BLOCK), jnp.float32),
+            jax.ShapeDtypeStruct((EXB, 128), jnp.float32),
+        ],
+        in_specs=[VMEM] * 3,
+        out_specs=[VMEM] * 2,
+        scratch_shapes=[
+            pltpu.VMEM((shards, 8, width), jnp.float32),
+            pltpu.VMEM((8, BLOCK), jnp.float32),
+            pltpu.VMEM((EXB, 128), jnp.float32),
+            pltpu.VMEM((replicas, EXB, 128), jnp.float32),
+            dma((shards,)), dma((shards,)), dma((shards,)), dma((shards,)), dma((replicas,)), dma((replicas,)),
+        ],
+        compiler_params=pltpu.CompilerParams(collective_id=collective, has_side_effects=True),
+    )(stats, seg_row, examples)
+
+
 def input_grad_rows(
-    own, grad_stream, hid, grad_qkv, grad_up, qkv_flat, up_weight, gains, end_sums, biases, sizes, replicas,
+    own, grad_stream, plain, grad_qkv, grad_up, qkv_flat, up_weight, gains, end_sums, biases, sizes, replicas,
     collective, before,
 ):
     shards, rows, width = grad_qkv.shape
     hidden = grad_up.shape[2]
 
     def kernel(
-        own_ref, stream_ref, hid_any, qkv_any, up_any, qkvw_any, upw_any, gains_ref, end_ref,
+        own_ref, stream_ref, normed_any, qkv_any, up_any, qkvw_any, upw_any, gains_ref, end_ref,
         bias_ref, out_ref, total_ref, bias_total_ref,
-        qkvw, upw, weight_sems, hid, qkv, up, load_sems, stats, sums_ref, *scratch,
+        qkvw, upw, weight_sems, normed, qkv, up, load_sems, sums_ref, *scratch,
     ):
         grid = Grid2(sizes)
         small = SmallSum(shards, replicas, sums_ref, bias_ref, total_ref, bias_total_ref, scratch[:10])
@@ -1202,7 +1314,7 @@
         def loads(i):
             place = order[i]
             return [
-                pltpu.make_async_copy(hid_any.at[place], hid.at[i % 2], load_sems.at[i, 0]),
+                pltpu.make_async_copy(normed_any.at[place], normed.at[i % 2], load_sems.at[i, 0]),
                 pltpu.make_async_copy(qkv_any.at[place], qkv.at[i % 2], load_sems.at[i, 1]),
                 pltpu.make_async_copy(up_any.at[place], up.at[i % 2], load_sems.at[i, 2]),
             ]
@@ -1231,28 +1343,17 @@
                 copy.wait()
             slot = i % 2
 
-            def stats_tile(index, _):
-                here = span(index, ROW_TILE)
-                values = hid[slot, here].astype(jnp.float32)
-                mean = jnp.mean(values, axis=1, keepdims=True)
-                centered = values - mean
-                stats[0, here] = mean
-                stats[1, here] = lax.rsqrt(jnp.mean(centered * centered, axis=1, keepdims=True) + EPSILON)
-                return _
-
-            lax.fori_loop(0, rows // ROW_TILE, stats_tile, 0)
-
             def columns(index, _):
                 here = span(index, 256)
                 one = dot_nt(qkv[slot], qkvw[here, :])
                 two = dot_nt(up[slot], upw[here, :])
-                normed = (hid[slot, :, here].astype(jnp.float32) - stats[0]) * stats[1]
+                norm = normed[slot, :, here].astype(jnp.float32)
                 parts[place, :, here] = (one * gains_ref[0:1, here] + two * gains_ref[1:2, here]).astype(
                     jnp.bfloat16
                 )
-                sums_ref[0:1, here] += jnp.sum(one * normed, axis=0, keepdims=True)
+                sums_ref[0:1, here] += jnp.sum(one * norm, axis=0, keepdims=True)
                 sums_ref[1:2, here] += jnp.sum(one, axis=0, keepdims=True)
-                sums_ref[2:3, here] += jnp.sum(two * normed, axis=0, keepdims=True)
+                sums_ref[2:3, here] += jnp.sum(two * norm, axis=0, keepdims=True)
                 sums_ref[3:4, here] += jnp.sum(two, axis=0, keepdims=True)
                 return _
 
@@ -1294,14 +1395,13 @@
             pltpu.VMEM((2, rows, width), jnp.bfloat16),
             pltpu.VMEM((2, rows, hidden), jnp.bfloat16),
             pltpu.SemaphoreType.DMA((shards, 3)),
-            pltpu.VMEM((2, rows, 1), jnp.float32),
             pltpu.VMEM((8, D), jnp.float32),
         ]
         + SmallSum.scratch(shards, replicas)
         + sum_scratch(sizes, rows),
         2 * BLOCK * D * (width + hidden),
         before,
-    )(own, grad_stream, hid, grad_qkv, grad_up, qkv_flat, up_weight, gains, end_sums, biases)
+    )(own, grad_stream, plain, grad_qkv, grad_up, qkv_flat, up_weight, gains, end_sums, biases)
 
 
 def segment_rows(block_lengths):
@@ -1311,16 +1411,6 @@
     segment = jnp.sum(passed, axis=1)
     position = row_ids - jnp.sum(passed * block_lengths[None, :], axis=1)
     return (segment, position)
-
-
-def merge_stats(left_stats, right_stats):
-    left_top, left_sum, left_pick = left_stats
-    right_top, right_sum, right_pick = right_stats
-    joint_top = jnp.maximum(left_top, right_top)
-    joint_sum = left_sum * jnp.exp(left_top - joint_top) + right_sum * jnp.exp(
-        right_top - joint_top
-    )
-    return (joint_top, joint_sum, left_pick + right_pick)
 
 
 def row_of(vector):
@@ -1411,41 +1501,28 @@
     planes = rotary_planes(position)
 
     norms = jnp.concatenate([row_of(v) for v in (ln1_gain, ln1_bias, ln2_gain, ln2_bias)], axis=0)
-    hid, first_full, second_full, qkv, act, slope = open_rows(
+    plain, first_full, second_full, qkv, act, slope = open_rows(
         own, sizes, 0, norms, qkv_flat, full_bias, up_weight, row_of(up_bias), planes
     )
     flat_qkv = qkv.reshape(BLOCK, width)
     ctx, lse = attention_forward(flat_qkv, start_col, first_tile, local_heads)
-    shards, rows = hid.shape[0], hid.shape[1]
+    shards, rows = plain.shape[0], plain.shape[1]
     end_norms = jnp.concatenate([row_of(v) for v in (lnf_gain, lnf_bias, branch_bias)], axis=0)
     output, final, normed, inverse = branch_rows(
         own, ctx.reshape(shards, rows, inner), act, out_flat, down_weight, end_norms, sizes, 1
     )
     final_full, weights, stats = logit_rows(final, head_weight, targets[0][:, None], sizes, 2)
 
-    local_top = stats[:, 0]
-    gathered = lax.all_gather(stats[:, :3].T, "seq")
-    merged = tuple(gathered[0, i] for i in range(3))
-    for other in range(1, gathered.shape[0]):
-        merged = merge_stats(merged, tuple(gathered[other, i] for i in range(3)))
-    log_total = merged[0] + jnp.log(merged[1])
-    token_logp = merged[2] - log_total
-    member = (jnp.arange(EXB, dtype=jnp.int32)[:, None] == segment[None, :]).astype(jnp.float32)
-    float_lengths = block_lengths.astype(jnp.float32)
-    mean_logp = jnp.sum(member * token_logp[None, :], axis=1) / float_lengths
-    log_ratio = mean_logp - ref_logps[0]
-    center = lax.psum(jnp.sum(log_ratio), "dp") / (lax.axis_size("dp") * EXB)
-    label_sign = (2 * labels[0] - 1).astype(jnp.float32)
-    squashed = jax.nn.sigmoid(BETA * label_sign * (log_ratio - center))
-    losses = 1.0 - squashed
-    grad_ratio = -LOSS_SCALE * BETA * label_sign * squashed * (1.0 - squashed)
-    token_grad = jnp.sum(member * (grad_ratio / float_lengths)[:, None], axis=0)
-
+    examples = jnp.stack(
+        [block_lengths.astype(jnp.float32), ref_logps[0], (2 * labels[0] - 1).astype(jnp.float32)], axis=1
+    )
+    coef, losses = score_rows(
+        stats, segment[None, :], jnp.pad(examples, ((0, 0), (0, 125))), sizes, lax.axis_size("dp"), 6
+    )
     vocab_ids = lax.axis_index("seq") * local_vocab + jnp.arange(local_vocab, dtype=jnp.int32)
-    onehot = (vocab_ids[None, :] == targets[0][:, None]).astype(jnp.float32)
-    share = jnp.exp(local_top - log_total)
     grad_logits = (
-        token_grad[:, None] * (onehot - weights.reshape(BLOCK, local_vocab).astype(jnp.float32) * share[:, None])
+        jnp.where(vocab_ids[None, :] == targets[0][:, None], coef[0][:, None], 0.0)
+        - weights.reshape(BLOCK, local_vocab).astype(jnp.float32) * coef[1][:, None]
     ).astype(jnp.bfloat16)
     final_rows = final_full.reshape(BLOCK, D)
     head_sum = PairSum(lambda which: dot_tn(half_of(final_rows, which), grad_logits)).cross()
@@ -1483,7 +1560,7 @@
     biases = jnp.pad(biases[None, :], ((0, 7), (0, D - biases.shape[0])))
     gains = jnp.concatenate([row_of(ln1_gain), row_of(ln2_gain)], axis=0)
     grad_input, small, biases = input_grad_rows(
-        own, grad_stream, hid, grad_qkv.reshape(shards, rows, width), grad_up, qkv_flat, up_weight, gains,
+        own, grad_stream, plain, grad_qkv.reshape(shards, rows, width), grad_up, qkv_flat, up_weight, gains,
         end_sums, biases, sizes, lax.axis_size("dp"), 5, (sums[-1].sum, head_sum.join().total),
     )
     for one, other in zip(sums, after([one.other for one in sums], small)):
@@ -1492,7 +1569,7 @@
     out_grad, down_grad, up_grad, qkv_grad = [one.settle() for one in sums]
     head_grad = head_sum.settle()
     return (
-        losses[None],
+        losses[:, 0][None],
         output[None],
         grad_input[None],
         small[0],

time: 1010 us -> 928 us (0.919)
  blocking collectives: 37.1 us -> 0 us
  local copies, waits for them, and re-layouts: 49.1 us -> 29.3 us
  Pallas kernels: 702 us -> 683 us
    pallas_call x6, Pallas kernels: 649 us -> 607 us  [call(): pl.pallas_call(body, out_shape=out_shape, in_specs=[ANY] * len(before) +...]
    all_gather x1 -> x0, blocking collectives: 30.8 us -> none  [per_device(): gathered = lax.all_gather(stats[:, :3].T, 'seq')]
    squeeze x17 -> x0, local copies, waits for them, and re-layouts: 20.9 us -> none  [the longest x14 19.1 us: per_device(): merged = merge_stats(merged, tuple((gathered[other, i] for i in range(3))))]
    pallas_call x0 -> x1, Pallas kernels: none -> 14.8 us  [score_rows(): pl.pallas_call(kernel, out_shape=[jax.ShapeDtypeStruct((8, BLOCK), jnp.fl...]
    convert_element_type x2 -> x4, other arithmetic: 20.6 us -> 20 us  [the longest x2 19.4 us: per_device(): grad_logits = (jnp.where(vocab_ids[None, :] == targets[0][:, None], coef[...]
  transfers between devices with their start and end apart: 15 -> 15, of which waited for: 0 -> 0; matrix products, arithmetic and copies ran while one was open for 14% -> 16% of each run, Pallas kernels for 35% -> 37%
where the time goes in v4:
time: 928 us; the launch traced here: 921 us
  Pallas kernels  683 us (74%)
  other arithmetic  114 us (12%)
  matrix products  85.2 us (9%)
  local copies, waits for them, and re-layouts  29.3 us (3%)
    pallas_call x6, Pallas kernels, call(): pl.pallas_call(body, out_shape=out_shape, in_specs=[ANY] * len(before) +...  607 us
    dot_general x10, matrix products, dot_tn(): lax.dot_general(left, right, (((0,), (0,)), ((), ())), preferred_element_...  85.2 us
    pallas_call x1, Pallas kernels, attention_backward(): pl.pallas_call(kernel, grid_spec=pltpu.PrefetchScalarGridSpec(num_scalar_...  35.9 us
    pallas_call x1, Pallas kernels, attention_forward(): pl.pallas_call(kernel, grid_spec=pltpu.PrefetchScalarGridSpec(num_scalar_...  24.7 us
    convert_element_type x5, other arithmetic, join(): (self.sum.astype(jnp.float32) + self.other.astype(jnp.float32)).astype(jn...  21.9 us
    convert_element_type x2, other arithmetic, per_device(): grad_logits = (jnp.where(vocab_ids[None, :] == targets[0][:, None], coef[...  19.4 us
  transfers between devices with their start and end apart: 15, of which 0 were waited for; matrix products, arithmetic and copies ran while one was open for 16% of the time, Pallas kernels for 37%

profile of v4, /device:TPU:0, one launch (start us, length us, event | category | flops | bytes accessed | tf_op | source)
XLA Modules:
  0.0 920.6 jit_solution(14483342771443797483)
XLA Ops:
  16.8 4.2 copy.60
  21.0 3.7 fusion.33
  29.3 106.7 %shard_map.314 = (bf16[8,256,2048]{2,1,0:T(8,128)(2,1)}, bf16[8,256,2048]{2,1,0:T(8,128)(2,1)}, bf16[8,256,2048]{2,1,0:T(8,128)(2,1)}, bf16[8,256,768]{2,1,0:T(8...) custom-call(bf16[256,2048]{1,0:T(8,128)(2,1)} %bitcast.130, ...), custom_call_target="tpu_custom_call" | custom-call | flops 15032385536 | bytes 268435456 | tf_op jit(solution)/shard_map/pallas_call | solution.py:547
  135.9 24.7 %shard_map.315 = (bf16[2048,256]{1,0:T(8,128)(2,1)}, f32[2,2048,1]{2,1,0:T(8,128)}) custom-call(s32[8]{0:T(128)} %and_select_fusion.first_ref, bf16[2048,768]{1,0:T(8,128)(2,1)} %bitcast.74, bf16[2048,768]{1,0:T(8,128)(2,1)} %bitcast.75, bf16[2048,768]{1,0:T(8,128)(2,1)} %bitcast.76, s32[2048,1]{1,0:T(8,128)} %subtract_subtract_fusion.start_ref), custom_call_target="tpu_custom_call" | custom-call | tf_op jit(solution)/shard_map/pallas_call | solution.py:400
  160.6 86.7 %shard_map.316 = (bf16[256,2048]{1,0:T(8,128)(2,1)}, bf16[256,2048]{1,0:T(8,128)(2,1)}, f32[256,2048]{1,0:T(8,128)}, f32[256,1]{1,0:T(8,128)}) custom-call(bf16[256,2048]{1,0:T(8,128)(2,1)} %bitcast.131, bf16[8,256,256]{2,1,0:T(8,128)(2,1)} %bitcast.89, bf16[8,256,1024]{2,1,0:T(8,128)(2,1)} %get-tuple-element.52.refs_2_, bf16[256,2048]{1,0:T(8,128)(2,1)} %bitcast.128, ...), custom_call_target="tpu_custom_call" | custom-call | flops 10737418240 | bytes 268435456 | tf_op jit(solution)/shard_map/pallas_call | solution.py:547
  247.3 105.3 %shard_map.317 = (bf16[8,256,2048]{2,1,0:T(8,128)(2,1)}, bf16[8,256,3328]{2,1,0:T(8,128)(2,1)}, f32[8,2048]{1,0:T(8,128)}) custom-call(bf16[256,2048]{1,0:T(8,128)(2,1)} %get-tuple-element.53.refs_0_, bf16[2048,3328]{1,0:T(8,128)(2,1)} %refs_2_.2, s32[2048,1]{1,0:T(8,128)} %copy.55.refs_2_), custom_call_target="tpu_custom_call" | custom-call | flops 27917287424 | bytes 268435456 | tf_op jit(solution)/shard_map/pallas_call | solution.py:547
  352.6 14.8 %shard_map.318 = (f32[8,2048]{1,0:T(8,128)}, f32[8,128]{1,0:T(8,128)}) custom-call(f32[8,2048]{1,0:T(8,128)} %get-tuple-element.54.stats_ref, s32[1,2048]{1,0:T(1,128)} %bitcast.103, f32[8,128]{1,0:T(8,128)} %select_maximum_fusion.examples_ref), custom_call_target="tpu_custom_call" | custom-call | tf_op jit(solution)/shard_map/pallas_call | solution.py:1277
  368.4 9.9 %fusion.1 = bf16[2048,3328]{1,0:T(8,128)(2,1)S(1)} fusion(f32[2048]{0:T(1024)S(1)} %bitcast.99, f32[2048]{0:T(1024)S(1)} %bitcast.100, s32[3328]{0:T(1024)S(1)} %iota_add_fusion, s32[2048]{0:T(1024)S(1)} %bitcast.93, bf16[8,256,3328]{2,1,0:T(8,128)(2,1)} %get-tuple-element.61), kind=kLoop, calls=%fused_computation.2 | loop fusion | flops 40894464 | bytes 27300864 | tf_op jit(solution)/shard_map/convert_element_type | solution.py:1526
  378.4 17.0 %convolution_convert_fusion = bf16[1024,3328]{1,0:T(8,128)(2,1)} fusion(bf16[2048,3328]{1,0:T(8,128)(2,1)S(1)} %fusion.1, bf16[2048,2048]{1,0:T(8,128)(2,1)S(1)} %bitcast.140, s32[]{:T(128)S(6)} %select_n.85), kind=kOutput, calls=%fused_computation.7 | convolution fusion | flops 13962051584 | bytes 24641540 | tf_op jit(solution)/shard_map/dot_general | solution.py:334
  396.8 23.4 %fusion.9 = f32[1024,3328]{1,0:T(8,128)} fusion(bf16[2048,3328]{1,0:T(8,128)(2,1)} %copy-done, bf16[2048,2048]{1,0:T(8,128)(2,1)} %bitcast.139, s32[]{:T(128)S(6)} %select_n.83), kind=kOutput, calls=%fused_computation.23 | convolution fusion | flops 13958643712 | bytes 31457284 | tf_op jit(solution)/shard_map/dot_general | solution.py:334
  421.4 9.5 %subtract_convert_fusion.refs_1_ = bf16[8,256,3328]{2,1,0:T(8,128)(2,1)} fusion(f32[8,256]{1,0:T(8,128)S(1)} %mul.83, f32[8,256]{1,0:T(8,128)S(1)} %broadcast_in_dim.120, s32[8,256]{1,0:T(8,128)S(1)} %eq.41, s32[3328]{0:T(1024)S(1)} %iota_add_fusion, bf16[8,256,3328]{2,1,0:T(8,128)(2,1)S(1)} %bitcast.81), kind=kLoop, calls=%fused_computation.3 | loop fusion | flops 40894464 | bytes 27300864 | tf_op jit(solution)/shard_map/convert_element_type | solution.py:1526
  430.9 7.5 add_convert_fusion.1.refs_0_
  439.5 109.4 %shard_map.319 = (f32[256,2048]{1,0:T(8,128)}, bf16[256,2048]{1,0:T(8,128)(2,1)}, f32[8,2048]{1,0:T(8,128)}) custom-call(bf16[1024,3328]{1,0:T(8,128)(2,1)} %add_convert_fusion.1.refs_0_, bf16[8,256,3328]{2,1,0:T(8,128)(2,1)} %subtract_convert_fusion.refs_1_, bf16[2048,3328]{1,0:T(8,128)(2,1)} %refs_2_.2, f32[256,2048]{1,0:T(8,128)} %get-tuple-element.62.refs_3_, ...), custom_call_target="tpu_custom_call" | custom-call | flops 27917287424 | bytes 268435456 | tf_op jit(solution)/shard_map/pallas_call | solution.py:547
  548.8 90.6 %shard_map.320 = (bf16[8,256,2048]{2,1,0:T(8,128)(2,1)}, bf16[8,256,256]{2,1,0:T(8,128)(2,1)}, bf16[8,256,1024]{2,1,0:T(8,128)(2,1)}, f32[8,1024]{1,0:T(8,128)}) custom-call(bf16[256,2048]{1,0:T(8,128)(2,1)} %get-tuple-element.64.refs_0_, bf16[256,2048]{1,0:T(8,128)(2,1)} %bitcast.129, bf16[1024,2048]{1,0:T(8,128)(2,1)} %refs_2_.3, ...), custom_call_target="tpu_custom_call" | custom-call | flops 10737418240 | bytes 268435456 | tf_op jit(solution)/shard_map/pallas_call | solution.py:547
  639.5 8.2 fusion.24
  647.8 4.8 fusion.21
  652.6 6.8 fusion.17
  659.9 3.5 fusion.30
  664.4 3.7 fusion.19
  668.1 4.6 fusion.6
  681.0 35.9 %shard_map.321 = (bf16[2048,768]{1,0:T(8,128)(2,1)}, f32[2,1,384]{2,1,0:T(1,128)}) custom-call(s32[8]{0:T(128)} %and_select_fusion.first_ref, bf16[2048,768]{1,0:T(8,128)(2,1)} %bitcast.77, bf16[2048,768]{1,0:T(8,128)(2,1)} %bitcast.78, bf16[2048,768]{1,0:T(8,128)(2,1)} %bitcast.79, s32[2048,1]{1,0:T(8,128)} %subtract_subtract_fusion.start_ref, ...), custom_call_target="tpu_custom_call" | custom-call | tf_op jit(solution)/shard_map/pallas_call | solution.py:483
  717.5 8.0 fusion.27
  725.5 5.3 fusion.11
  730.9 9.4 %add_convert_fusion.refs_1_ = bf16[1024,3328]{1,0:T(8,128)(2,1)} fusion(bf16[1024,3328]{1,0:T(8,128)(2,1)} %collective-permute-done.5, bf16[1024,3328]{1,0:T(8,128)(2,1)} %add_convert_fusion.1.refs_0_), kind=kLoop, calls=%fused_computation.5 | loop fusion | flops 13631488 | bytes 20447232 | tf_op jit(solution)/shard_map/convert_element_type | solution.py:1453
  745.5 108.8 %shard_map.322 = (f32[256,2048]{1,0:T(8,128)}, f32[8,2048]{1,0:T(8,128)}, f32[8,2048]{1,0:T(8,128)}) custom-call(bf16[1024,768]{1,0:T(8,128)(2,1)} %add_convert_fusion.7.refs_0_, bf16[1024,3328]{1,0:T(8,128)(2,1)} %add_convert_fusion.refs_1_, bf16[256,2048]{1,0:T(8,128)(2,1)} %bitcast.132, f32[256,2048]{1,0:T(8,128)} %get-tuple-element.71.refs_3_, ...), custom_call_target="tpu_custom_call" | custom-call | flops 15032385536 | bytes 268435456 | tf_op jit(solution)/shard_map/pallas_call | solution.py:547
  855.5 3.4 add_convert_fusion.6
  865.4 4.5 add_convert_fusion.3
  879.4 8.2 reshape.232
  889.5 4.4 maximum_convert_fusion.2
  895.8 4.9 maximum_convert_fusion.1
  900.9 4.0 broadcast_select_fusion.1
  904.9 13.2 %maximum_convert_fusion = f32[2048,3328]{1,0:T(8,128)} fusion(bf16[1024,3328]{1,0:T(8,128)(2,1)S(1)} %get-tuple-element.88, bf16[1024,3328]{1,0:T(8,128)(2,1)S(1)} %get-tuple-element.87), kind=kLoop, calls=%fused_computation.4 | loop fusion | flops 27262976 | bytes 40894464 | tf_op jit(solution)/shard_map/concatenate | solution.py:1588
  (154 shorter events, 64.3 us)
Async XLA Ops:
  10.6 14.8 %copy-start.9 = (f32[2048]{0:T(1024)}, f32[2048]{0:T(1024)S(1)}, u32[]{:S(2)}) copy-start(f32[2048]{0:T(1024)S(1)} %broadcast_in_dim.130) | copy-start | bytes 24580
  247.3 121.1 %copy-start.8 = (s32[1,2048]{1,0:T(1,128)S(1)}, s32[1,2048]{1,0:T(1,128)}, u32[]{:S(2)}) copy-start(s32[1,2048]{1,0:T(1,128)} %param.20) | copy-start | bytes 24580
  368.4 9.9 %copy-start.12 = (bf16[8,256,2048]{2,1,0:T(8,128)(2,1)S(1)}, bf16[8,256,2048]{2,1,0:T(8,128)(2,1)}, u32[]{:S(2)}) copy-start(bf16[8,256,2048]{2,1,0:T(8,128)(2,1)} %get-tuple-element.59) | copy-start | bytes 25165828
  378.3 17.0 %copy-start = (bf16[2048,3328]{1,0:T(8,128)(2,1)}, bf16[2048,3328]{1,0:T(8,128)(2,1)S(1)}, u32[]{:S(2)}) copy-start(bf16[2048,3328]{1,0:T(8,128)(2,1)S(1)} %fusion.1) | copy-start | bytes 40894468
  395.4 35.5 %collective-permute-start = (bf16[1024,3328]{1,0:T(8,128)(2,1)}, bf16[1024,3328]{1,0:T(8,128)(2,1)}, u32[]{:S(2)}, u32[]{:S(2)}) collective-permute-start(bf16[1024,3328]{1,0:T(8,128)(2,1)} %convolution_convert_fusion), channel_id=1, source_target_pairs={{0,8},{8,0},{16,24},{24,16},{1,9},{9,1},{17,25},{25,17},{2,10},{10... | collective-permute-start | bytes 20447240 | tf_op jit(solution)/shard_map/ppermute | solution.py:1441
  396.7 24.7 %slice-start = ((s8[13631488]{0:T(1024)(128)(4,1)}), s8[1048576]{0:T(1024)(128)(4,1)S(1)}, s32[]{:S(2)}) async-start(s8[13631488]{0:T(1024)(128)(4,1)} %bitcast.80), calls=%async_computation | async-start | bytes 2097152
  396.7 23.4 %copy-start.10 = (f32[8,128]{1,0:T(8,128)S(1)}, f32[8,128]{1,0:T(8,128)}, u32[]{:S(2)}) copy-start(f32[8,128]{1,0:T(8,128)} %get-tuple-element.55) | copy-start | bytes 12292
  396.7 24.7 %slice-start.1 = ((s8[13631488]{0:T(1024)(128)(4,1)}), s8[4194304]{0:T(1024)(128)(4,1)S(1)}, s32[]{:S(2)}) async-start(s8[13631488]{0:T(1024)(128)(4,1)} %bitcast.80), calls=%async_computation.1 | async-start | bytes 8388608
  396.7 24.6 %slice-start.2 = ((s8[13631488]{0:T(1024)(128)(4,1)}), s8[4194304]{0:T(1024)(128)(4,1)S(1)}, s32[]{:S(2)}) async-start(s8[13631488]{0:T(1024)(128)(4,1)} %bitcast.80), calls=%async_computation.2 | async-start | bytes 8388608
  396.8 24.6 %slice-start.3 = ((s8[13631488]{0:T(1024)(128)(4,1)}), s8[4194304]{0:T(1024)(128)(4,1)S(1)}, s32[]{:S(2)}) async-start(s8[13631488]{0:T(1024)(128)(4,1)} %bitcast.80), calls=%async_computation.3 | async-start | bytes 8388608
  421.4 9.5 %copy-start.1 = (f32[1024,3328]{1,0:T(8,128)S(1)}, f32[1024,3328]{1,0:T(8,128)}, u32[]{:S(2)}) copy-start(f32[1024,3328]{1,0:T(8,128)} %fusion.9) | copy-start | bytes 40894468
  438.4 292.5 %collective-permute-start.5 = (bf16[1024,3328]{1,0:T(8,128)(2,1)}, bf16[1024,3328]{1,0:T(8,128)(2,1)}, u32[]{:S(2)}, u32[]{:S(2)}) collective-permute-start(bf16[1024,3328]{1,0:T(8,128)(2,1)} %add_convert_fusion.1.refs_0_), channel_id=1, source_target_pairs={{0,16},{16,0},{8,24},{24,8},{1,17},{17,1},{9,25},{25,9},{2,18},{18... | collective-permute-start | bytes 20447240 | tf_op jit(solution)/shard_map/ppermute | solution.py:1446
  639.5 8.3 copy-start.13
  639.5 8.3 copy-start.15
  647.7 26.9 %collective-permute-start.3 = (bf16[1024,1024]{1,0:T(8,128)(2,1)S(1)}, bf16[1024,1024]{1,0:T(8,128)(2,1)S(1)}, u32[]{:S(2)}, u32[]{:S(2)}) collective-permute-start(bf16[1024,1024]{1,0:T(8,128)(2,1)S(1)} %fusion.24), channel_id=1, source_target_pairs={{0,8},{8,0},{16,24},{24,16},{1,9},{9,1},{17,25},{25,17},{2,10},{10... | collective-permute-start | bytes 6291464 | tf_op jit(solution)/shard_map/ppermute | solution.py:1441
  647.8 20.3 %slice-start.6 = ((s8[8388608]{0:T(1024)(128)(4,1)}), s8[4194304]{0:T(1024)(128)(4,1)S(1)}, s32[]{:S(2)}) async-start(s8[8388608]{0:T(1024)(128)(4,1)} %bitcast.136), calls=%async_computation.6 | async-start | bytes 8388608
  652.6 15.5 %slice-start.7 = ((s8[8388608]{0:T(1024)(128)(4,1)}), s8[4194304]{0:T(1024)(128)(4,1)S(1)}, s32[]{:S(2)}) async-start(s8[8388608]{0:T(1024)(128)(4,1)} %bitcast.136), calls=%async_computation.7 | async-start | bytes 8388608
  659.4 18.6 %collective-permute-start.2 = (bf16[1024,1024]{1,0:T(8,128)(2,1)S(1)}, bf16[1024,1024]{1,0:T(8,128)(2,1)S(1)}, u32[]{:S(2)}, u32[]{:S(2)}) collective-permute-start(bf16[1024,1024]{1,0:T(8,128)(2,1)S(1)} %fusion.21), channel_id=1, source_target_pairs={{0,8},{8,0},{16,24},{24,16},{1,9},{9,1},{17,25},{25,17},{2,10},{10... | collective-permute-start | bytes 6291464 | tf_op jit(solution)/shard_map/ppermute | solution.py:1441
  664.3 8.5 collective-permute-start.1
  673.7 180.5 %collective-permute-start.6 = (bf16[256,1024]{1,0:T(8,128)(2,1)}, bf16[256,1024]{1,0:T(8,128)(2,1)}, u32[]{:S(2)}, u32[]{:S(2)}) collective-permute-start(bf16[256,1024]{1,0:T(8,128)(2,1)} %add_convert_fusion.9.rest_0_), channel_id=1, source_target_pairs={{0,16},{16,0},{8,24},{24,8},{1,17},{17,1},{9,25},{25,9},{2,18},{18... | collective-permute-start | bytes 1572872 | tf_op jit(solution)/shard_map/ppermute | solution.py:1446
  676.8 177.5 %collective-permute-start.8 = (bf16[1024,1024]{1,0:T(8,128)(2,1)}, bf16[1024,1024]{1,0:T(8,128)(2,1)}, u32[]{:S(2)}, u32[]{:S(2)}) collective-permute-start(bf16[1024,1024]{1,0:T(8,128)(2,1)} %add_convert_fusion.4.rest_2_), channel_id=1, source_target_pairs={{0,16},{16,0},{8,24},{24,8},{1,17},{17,1},{9,25},{25,9},{2,18},{18... | collective-permute-start | bytes 6291464 | tf_op jit(solution)/shard_map/ppermute | solution.py:1446
  680.1 174.2 %collective-permute-start.7 = (bf16[1024,1024]{1,0:T(8,128)(2,1)}, bf16[1024,1024]{1,0:T(8,128)(2,1)}, u32[]{:S(2)}, u32[]{:S(2)}) collective-permute-start(bf16[1024,1024]{1,0:T(8,128)(2,1)} %add_convert_fusion.5.rest_1_), channel_id=1, source_target_pairs={{0,16},{16,0},{8,24},{24,8},{1,17},{17,1},{9,25},{25,9},{2,18},{18... | collective-permute-start | bytes 6291464 | tf_op jit(solution)/shard_map/ppermute | solution.py:1446
  725.5 15.3 %collective-permute-start.4 = (bf16[1024,768]{1,0:T(8,128)(2,1)}, bf16[1024,768]{1,0:T(8,128)(2,1)}, u32[]{:S(2)}, u32[]{:S(2)}) collective-permute-start(bf16[1024,768]{1,0:T(8,128)(2,1)} %fusion.27), channel_id=1, source_target_pairs={{0,8},{8,0},{16,24},{24,16},{1,9},{9,1},{17,25},{25,17},{2,10},{10... | collective-permute-start | bytes 4718600 | tf_op jit(solution)/shard_map/ppermute | solution.py:1441
  740.3 160.5 %collective-permute-start.14 = (bf16[1024,3328]{1,0:T(8,128)(2,1)}, bf16[1024,3328]{1,0:T(8,128)(2,1)}, u32[]{:S(2)}, u32[]{:S(2)}) collective-permute-start(bf16[1024,3328]{1,0:T(8,128)(2,1)} %add_convert_fusion.refs_1_), channel_id=1, source_target_pairs={{0,8},{8,0},{16,24},{24,16},{1,9},{9,1},{17,25},{25,17},{2,10},{10... | collective-permute-start | bytes 20447240 | tf_op jit(solution)/shard_map/ppermute | solution.py:1460
  743.7 110.7 %collective-permute-start.9 = (bf16[1024,768]{1,0:T(8,128)(2,1)}, bf16[1024,768]{1,0:T(8,128)(2,1)S(1)}, u32[]{:S(2)}, u32[]{:S(2)}) collective-permute-start(bf16[1024,768]{1,0:T(8,128)(2,1)} %add_convert_fusion.7.refs_0_), channel_id=1, source_target_pairs={{0,16},{16,0},{8,24},{24,8},{1,17},{17,1},{9,25},{25,9},{2,18},{18... | collective-permute-start | bytes 4718600 | tf_op jit(solution)/shard_map/ppermute | solution.py:1446
  858.9 15.2 %collective-permute-start.10 = (bf16[1024,768]{1,0:T(8,128)(2,1)}, bf16[1024,768]{1,0:T(8,128)(2,1)}, u32[]{:S(2)}, u32[]{:S(2)}) collective-permute-start(bf16[1024,768]{1,0:T(8,128)(2,1)} %add_convert_fusion.6), channel_id=1, source_target_pairs={{0,8},{8,0},{16,24},{24,16},{1,9},{9,1},{17,25},{25,17},{2,10},{10... | collective-permute-start | bytes 4718600 | tf_op jit(solution)/shard_map/ppermute | solution.py:1460
  862.1 9.6 %copy-start.7 = (f32[8,2048]{1,0:T(8,128)S(1)}, f32[8,2048]{1,0:T(8,128)}, u32[]{:S(2)}) copy-start(f32[8,2048]{1,0:T(8,128)} %get-tuple-element.77.refs_4_) | copy-start | bytes 196612
  864.9 7.5 collective-permute-start.11
  865.4 22.3 %collective-permute-start.13 = (bf16[1024,1024]{1,0:T(8,128)(2,1)S(1)}, bf16[1024,1024]{1,0:T(8,128)(2,1)}, u32[]{:S(2)}, u32[]{:S(2)}) collective-permute-start(bf16[1024,1024]{1,0:T(8,128)(2,1)S(1)} %add_convert_fusion.2), channel_id=1, source_target_pairs={{0,8},{8,0},{16,24},{24,16},{1,9},{9,1},{17,25},{25,17},{2,10},{10... | collective-permute-start | bytes 6291464 | tf_op jit(solution)/shard_map/ppermute | solution.py:1460
  871.2 22.7 %collective-permute-start.12 = (bf16[1024,1024]{1,0:T(8,128)(2,1)}, bf16[1024,1024]{1,0:T(8,128)(2,1)}, u32[]{:S(2)}, u32[]{:S(2)}) collective-permute-start(bf16[1024,1024]{1,0:T(8,128)(2,1)} %add_convert_fusion.3), channel_id=1, source_target_pairs={{0,8},{8,0},{16,24},{24,16},{1,9},{9,1},{17,25},{25,17},{2,10},{10... | collective-permute-start | bytes 6291464 | tf_op jit(solution)/shard_map/ppermute | solution.py:1460
  904.9 13.2 %copy-start.6 = (bf16[256,2048]{1,0:T(8,128)(2,1)S(1)}, bf16[256,2048]{1,0:T(8,128)(2,1)}, u32[]{:S(2)}) copy-start(bf16[256,2048]{1,0:T(8,128)(2,1)} %get-tuple-element.56) | copy-start | bytes 3145732
  904.9 14.2 %copy-start.4 = (f32[256,2048]{1,0:T(8,128)S(1)}, f32[256,2048]{1,0:T(8,128)}, u32[]{:S(2)}) copy-start(f32[256,2048]{1,0:T(8,128)} %get-tuple-element.76) | copy-start | bytes 6291460
  (7 other events, 35.6 us)

commit v5 on v4

--- a/solution.py
+++ b/solution.py
@@ -99,98 +99,106 @@
 
 
 def gather_sends(sizes, halves):
-    return halves * 2 * (sizes[0] * sizes[1] * 2 + 8)
+    return halves * 2 * (sizes[0] * sizes[1] * 5 + 8)
 
 
 def gather_rounds(grid, sender, piece, recv_sems, halves, cut, ready):
     n, me = grid.n, grid.me
 
-    def arrived(slow, fast, half, kind):
+    def arrived(slow, fast, half, kind, when):
         ref = piece(grid.index(slow, fast), half, kind)
         sem = recv_sems.at[kind, half, grid.index(slow, fast)]
-        pltpu.make_async_copy(ref, ref, sem).wait()
-
-    def push(slow, fast, half, kind, axis, spot, when):
+        wait = pltpu.make_async_copy(ref, ref, sem).wait
+        if when is None:
+            wait()
+        else:
+            pl.when(when)(wait)
+
+    def push(slow, fast, half, kind, axis, spot, *conditions):
         ref = piece(grid.index(slow, fast), half, kind)
         sem = recv_sems.at[kind, half, grid.index(slow, fast)]
+        when = None
+        for condition in conditions:
+            if condition is not None:
+                when = condition if when is None else when & condition
         sender.send(ref, ref, sem, grid.device(axis, spot), when)
 
-    def spread(slow, fast, half, kind, axis):
+    def spread(slow, fast, half, kind, axis, when):
         m, size = me[axis], n[axis]
         if size == 2:
-            push(slow, fast, half, kind, axis, 1 - m, None)
+            push(slow, fast, half, kind, axis, 1 - m, when)
         elif size > 2:
-            push(slow, fast, half, kind, axis, m + 1, m < size - 1)
-            push(slow, fast, half, kind, axis, m - 1, m > 0)
-
-    def onward(slow, fast, half, kind, axis):
+            push(slow, fast, half, kind, axis, m + 1, when, m < size - 1)
+            push(slow, fast, half, kind, axis, m - 1, when, m > 0)
+
+    def onward(slow, fast, half, kind, axis, when):
         m, size = me[axis], n[axis]
         if size <= 2:
             return
-        source = (slow, fast)[axis]
-        below = source < m
-        when = (below & (m < size - 1)) | (jnp.logical_not(below) & (m > 0))
-        push(slow, fast, half, kind, axis, jnp.where(below, m + 1, m - 1), when)
-
-    todo = []
-
-    def work(count=1):
-        for _ in range(count):
-            if todo:
-                ready(*todo.pop(0))
-
-    def settle(k):
-        slow = grid.nearest(0, k)
+        below = (slow, fast)[axis] < m
+        more = (below & (m < size - 1)) | (jnp.logical_not(below) & (m > 0))
+        push(slow, fast, half, kind, axis, jnp.where(below, m + 1, m - 1), when, more)
+
+    def sides(d):
+        if d == 0:
+            return [(me[0], None)]
+        if n[0] == 2:
+            return [(1 - me[0], None)]
+        return [(me[0] - d, me[0] >= d), (me[0] + d, me[0] + d < n[0])]
+
+    def settle(d):
         for half in range(halves):
-            for l in range(n[1]):
-                fast = grid.nearest(1, l)
-                if k > 0:
-                    arrived(slow, fast, half, 1)
-                    onward(slow, fast, half, 1, 0)
-                else:
-                    spread(slow, fast, half, 1, 0)
-
-    def complete(k):
-        slow = grid.nearest(0, k)
+            for slow, when in sides(d):
+                for l in range(n[1]):
+                    fast = grid.nearest(1, l)
+                    if d > 0:
+                        arrived(slow, fast, half, 1, when)
+                        onward(slow, fast, half, 1, 0, when)
+                    else:
+                        spread(slow, fast, half, 1, 0, when)
+
+    def complete(d):
         for l in range(1, n[1]):
             fast = grid.nearest(1, l)
-            if cut[0]:
-                for half in range(halves):
-                    arrived(slow, fast, half, 0)
-                    onward(slow, fast, half, 0, 1)
-            todo.append((slow, fast, k * n[1] + l))
+            for half in range(halves):
+                for slow, when in sides(d):
+                    arrived(slow, fast, half, 0, when)
+                    onward(slow, fast, half, 0, 1, when)
+
+    def work(k, l):
+        ready(grid.nearest(0, k), grid.nearest(1, l), k * n[1] + l)
 
     for half in range(halves):
         for kind in (1, 0):
             if cut[kind]:
-                spread(me[0], me[1], half, kind, kind)
+                spread(me[0], me[1], half, kind, kind, None)
         if cut[0]:
-            spread(me[0], me[1], half, 0, 1)
-    todo.append((me[0], me[1], 0))
-    work()
+            spread(me[0], me[1], half, 0, 1, None)
+    work(0, 0)
     if cut[1]:
         for half in range(halves):
             for l in range(1, n[1]):
                 fast = grid.nearest(1, l)
-                arrived(me[0], fast, half, 1)
-                onward(me[0], fast, half, 1, 1)
-    if cut[1]:
+                arrived(me[0], fast, half, 1, None)
+                onward(me[0], fast, half, 1, 1, None)
         settle(0)
-    for k in range(1, n[0]):
-        slow = grid.nearest(0, k)
+    for d in range(1, n[0]):
         if cut[0]:
             for half in range(halves):
-                arrived(slow, me[1], half, 0)
-                onward(slow, me[1], half, 0, 0)
-                spread(slow, me[1], half, 0, 1)
-        complete(k - 1)
-        work(len(todo))
+                for slow, when in sides(d):
+                    arrived(slow, me[1], half, 0, when)
+                    onward(slow, me[1], half, 0, 0, when)
+                    spread(slow, me[1], half, 0, 1, when)
+            complete(d - 1)
+        for l in range(1, n[1]):
+            work(d - 1, l)
         if cut[1]:
-            settle(k)
-        todo.append((slow, me[1], k * n[1]))
-        work()
-    complete(n[0] - 1)
-    work(len(todo))
+            settle(d)
+        work(d, 0)
+    if cut[0]:
+        complete(n[0] - 1)
+    for l in range(1, n[1]):
+        work(n[0] - 1, l)
 
 
 def scatter_slots(n):
@@ -198,15 +206,16 @@
 
 
 def scatter_plan(n):
-    plan = []
+    if n == (4, 2):
+        return [
+            ("make", 3, 1), ("make", 2, 1), ("make", 3, 0), ("make", 1, 1), ("first", 3), ("make", 2, 0),
+            ("make", 0, 1), ("later", 3, 0), ("make", 1, 0), ("later", 3, 1), ("first", 2), ("make", 0, 0), ("made",),
+            ("later", 2, 0), ("later", 2, 1), ("first", 1), ("later", 1, 0), ("later", 1, 1),
+        ]
     far = n[0] - 1
-    for k in range(far, -2, -1):
-        near = [("make", k + 1, 0)] if k + 1 <= far else []
-        back = [("chain", k + 2, 0)] if k + 2 <= far else []
-        if k >= 0:
-            plan += [("make", k, l) for l in range(n[1] - 1, 0, -1)] + back + near
-        else:
-            plan += near + back
+    plan = [("make", k, l) for k in range(far, -1, -1) for l in range(n[1] - 1, -1, -1)] + [("made",)]
+    for k in range(far, 0, -1):
+        plan += [("first", k), ("later", k, 0), ("later", k, 1)]
     return plan
 
 
@@ -235,20 +244,27 @@
         else:
             pl.when(when)(add)
 
-    def toward(self, kind, stage, axis, other, target, half, slow, fast):
+    def incoming(self, axis, target):
+        m, n = self.grid.me[axis], self.grid.n[axis]
+        if n == 2:
+            return None
+        up = target > m
+        return (up & (m > 0)) | (jnp.logical_not(up) & (m < n - 1))
+
+    def toward(self, kind, stage, axis, other, target, half, slow, fast, when=None):
         grid = self.grid
         m, n = grid.me[axis], grid.n[axis]
         up = target > m
         index = grid.index(slow, fast)
         if n > 2:
-            incoming = (up & (m > 0)) | (jnp.logical_not(up) & (m < n - 1))
-            self.take(kind, stage, axis, other, target, up, half, incoming, index)
+            incoming = self.incoming(axis, target)
+            self.take(kind, stage, axis, other, target, up, half, incoming if when is None else incoming & when, index)
         buf, sem = self.bufs[kind][stage], self.sems[kind][stage]
         slot = self.slot(axis, target, up)
         spot = 1 - m if n == 2 else jnp.where(up, m + 1, m - 1)
         self.sender.send(
             self.part(index, half, kind), buf.at[other, slot, half], sem.at[other, slot, half],
-            grid.device(axis, spot))
+            grid.device(axis, spot), when)
 
     def last(self, kind, stage, axis, other, half, slow, fast):
         grid = self.grid
@@ -260,30 +276,49 @@
             self.take(kind, stage, axis, other, m, jnp.bool_(True), half, m > 0, index)
             self.take(kind, stage, axis, other, m, jnp.bool_(False), half, m < n - 1, index)
 
-    def run(self, produce, made=lambda: None, between=lambda: None):
+    def run(self, produce, made=lambda: None, between=lambda: None, late=lambda: None):
         grid, n, me = self.grid, self.grid.n, self.grid.me
-
-        def chain(k):
+        lagging = []
+
+        def chain(k, half, begins):
             slow = grid.nearest(0, k)
-            for half in range(self.halves):
-                self.last(0, 0, 1, slow, half, slow, me[1])
-                self.toward(0, 1, 0, 0, slow, half, slow, me[1])
+            incoming = self.incoming(0, slow)
+            if incoming is None:
+                if begins:
+                    self.last(0, 0, 1, slow, half, slow, me[1])
+                    self.toward(0, 1, 0, 0, slow, half, slow, me[1])
+                return
+            when = jnp.logical_not(incoming) if begins else incoming
+            pl.when(when)(lambda: self.last(0, 0, 1, slow, half, slow, me[1]))
+            self.toward(0, 1, 0, 0, slow, half, slow, me[1], when)
+
+        def catch_up():
+            for step in lagging:
+                self.toward(*step)
+            lagging.clear()
 
         def make(k, l):
             slow, fast = grid.nearest(0, k), grid.nearest(1, l)
             produce(slow, fast)
-            for half in range(self.halves):
-                if self.cut[0] and l > 0:
+            if self.cut[0] and l > 0:
+                for half in range(self.halves):
                     self.toward(0, 0, 1, slow, fast, half, slow, fast)
-                if self.cut[1] and k > 0:
-                    self.toward(1, 0, 0, fast, slow, half, slow, fast)
-
-        for action, k, l in scatter_plan(n):
-            if action == "make":
-                make(k, l)
+            catch_up()
+            if self.cut[1] and k > 0:
+                for half in range(self.halves):
+                    lagging.append((1, 0, 0, fast, slow, half, slow, fast))
+
+        for step in scatter_plan(n):
+            if step[0] == "make":
+                make(*step[1:])
+            elif step[0] == "made":
+                catch_up()
+                made()
+            elif step[0] == "first" and self.cut[0]:
+                for half in range(self.halves):
+                    chain(step[1], half, True)
             elif self.cut[0]:
-                chain(k)
-        made()
+                chain(step[1], step[2], False)
         between()
         if self.cut[1]:
             for half in range(self.halves):
@@ -292,6 +327,7 @@
                     self.last(1, 0, 0, fast, half, me[0], fast)
                     if l > 0:
                         self.toward(1, 1, 1, 0, fast, half, me[0], fast)
+        late()
         if self.cut[0]:
             for half in range(self.halves):
                 self.last(0, 0, 1, me[0], half, me[0], me[1])
@@ -528,7 +564,7 @@
 
 
 def tile_of(width):
-    return 256 if width % 256 == 0 else 128
+    return 512 if width % 512 == 0 else 256 if width % 256 == 0 else 128
 
 
 def span(index, size):
@@ -610,8 +646,7 @@
 def production_order(grid):
     return [
         grid.index(grid.nearest(0, k), grid.nearest(1, l))
-        for action, k, l in scatter_plan(grid.n)
-        if action == "make"
+        for action, k, l in [step for step in scatter_plan(grid.n) if step[0] == "make"]
     ]
 
 
@@ -675,11 +710,10 @@
             lax.fori_loop(0, rows // ROW_TILE, norm_tile, 0)
             places = pl.ds(pl.multiple_of(place * rows, rows), rows)
             cos, below, above = cos_ref[places, :], below_ref[places, :], above_ref[places, :]
+            whole = jnp.dot(one[slot], qkvw[...], preferred_element_type=jnp.float32) + qkvb_ref[...]
             for head in range(heads):
                 first = head * 3 * HEAD_DIM
-                found = jnp.dot(
-                    one[slot], qkvw[:, first : first + 3 * HEAD_DIM], preferred_element_type=jnp.float32
-                ) + qkvb_ref[:, first : first + 3 * HEAD_DIM]
+                found = whole[:, first : first + 3 * HEAD_DIM]
                 qkv[slot, :, first : first + HEAD_DIM] = turn(
                     found[:, :HEAD_DIM], cos, below, above
                 ).astype(jnp.bfloat16)
@@ -824,8 +858,6 @@
     rows = final.shape[0]
     shards = sizes[0] * sizes[1]
     vocab = head_weight.shape[1]
-    tile = tile_of(vocab)
-    tiles = vocab // tile
 
     def kernel(
         own_ref, headw_any, target_ref, final_any, weights_any, stats_ref,
@@ -850,35 +882,44 @@
             target = target_ref[places, :] - base
 
             def fold(values, join):
-                while values.shape[1] > 128:
-                    half = values.shape[1] // 2
-                    values = join(values[:, :half], values[:, half:])
-                return values
-
-            def logit_tile(index, carry):
+                total = values[:, :128]
+                for first in range(128, values.shape[1], 128):
+                    total = join(total, values[:, first : first + 128])
+                return total
+
+            def logit_tile(start, size, carry):
                 top, pick = carry
-                here = span(index, tile)
+                here = pl.ds(start, size)
                 found = jnp.dot(full[place], headw[:, here], preferred_element_type=jnp.float32)
                 logits[:, here] = found
-                ids = index * tile + lax.broadcasted_iota(jnp.int32, (rows, tile), 1)
+                ids = start + lax.broadcasted_iota(jnp.int32, (rows, size), 1)
                 top = jnp.maximum(top, fold(found, jnp.maximum))
                 pick = pick + fold(jnp.where(ids == target, found, 0.0), jnp.add)
                 return (top, pick)
 
-            top, pick = lax.fori_loop(
-                0, tiles, logit_tile,
+            def tiled(step, carry):
+                count = vocab // 512
+                carry = lax.fori_loop(
+                    0, count, lambda i, c: step(pl.multiple_of(i * 512, 512), 512, c), carry
+                )
+                if vocab % 512:
+                    carry = step(count * 512, vocab % 512, carry)
+                return carry
+
+            top, pick = tiled(
+                logit_tile,
                 (jnp.full((rows, 128), -jnp.inf, jnp.float32), jnp.zeros((rows, 128), jnp.float32)),
             )
             top = jnp.max(top, axis=1, keepdims=True)
             pick = jnp.sum(pick, axis=1, keepdims=True)
 
-            def weight_tile(index, total):
-                here = span(index, tile)
+            def weight_tile(start, size, total):
+                here = pl.ds(start, size)
                 found = jnp.exp(logits[:, here] - top)
                 weights[slot, :, here] = found.astype(jnp.bfloat16)
                 return total + fold(found, jnp.add)
 
-            total = lax.fori_loop(0, tiles, weight_tile, jnp.zeros((rows, 128), jnp.float32))
+            total = tiled(weight_tile, jnp.zeros((rows, 128), jnp.float32))
             total = jnp.sum(total, axis=1, keepdims=True)
             lane = lax.broadcasted_iota(jnp.int32, (rows, 128), 1)
             found = jnp.where(lane == 0, top, jnp.where(lane == 1, total, pick))
@@ -927,14 +968,20 @@
         parts = scratch[0]
         order = production_order(grid)
         loads = [
-            pltpu.make_async_copy(grads_any.at[place], grads.at[i % 2], load_sems.at[1 + i])
+            pltpu.make_async_copy(grads_any.at[place], grads.at[i % 2], load_sems.at[i])
             for i, place in enumerate(order)
         ]
-        weights = pltpu.make_async_copy(headw_any, headw, load_sems.at[0])
+        tile = 512
+        weights = [
+            pltpu.make_async_copy(
+                headw_any.at[pl.ds(i * tile, tile)], headw.at[pl.ds(i * tile, tile)], load_sems.at[1 + shards + i]
+            )
+            for i in range(D // tile)
+        ]
         loads[0].start()
-        weights.start()
+        for copy in weights:
+            copy.start()
         grid.barrier()
-        weights.wait()
         count = [0]
 
         def produce(slow, fast):
@@ -946,11 +993,16 @@
             loads[i].wait()
 
             def columns(index, _):
-                here = span(index, 256)
+                here = span(index, tile)
                 parts[place, :, here] = dot_nt(grads[i % 2], headw[here, :]).astype(jnp.bfloat16)
                 return _
 
-            lax.fori_loop(0, D // 256, columns, 0)
+            if i == 0:
+                for index, copy in enumerate(weights):
+                    copy.wait()
+                    columns(index, 0)
+            else:
+                lax.fori_loop(0, D // tile, columns, 0)
 
         run_scatter(grid, sizes, rows, scratch, produce)
         mine = grid.index(*grid.me)
@@ -987,7 +1039,7 @@
         [
             pltpu.VMEM(head_weight.shape, jnp.bfloat16),
             pltpu.VMEM((2, rows, vocab), jnp.bfloat16),
-            pltpu.SemaphoreType.DMA((1 + shards,)),
+            pltpu.SemaphoreType.DMA((1 + shards + D // 512,)),
         ]
         + sum_scratch(sizes, rows),
         2 * BLOCK * D * vocab,
@@ -1344,7 +1396,7 @@
             slot = i % 2
 
             def columns(index, _):
-                here = span(index, 256)
+                here = span(index, 512)
                 one = dot_nt(qkv[slot], qkvw[here, :])
                 two = dot_nt(up[slot], upw[here, :])
                 norm = normed[slot, :, here].astype(jnp.float32)
@@ -1357,14 +1409,13 @@
                 sums_ref[3:4, here] += jnp.sum(two, axis=0, keepdims=True)
                 return _
 
-            lax.fori_loop(0, D // 256, columns, 0)
+            lax.fori_loop(0, D // 512, columns, 0)
 
         def made():
             sums_ref[4:8] = end_ref[0:4]
             small.spread()
 
-        run_scatter(grid, sizes, rows, scratch, produce, made, small.cross)
-        small.collect()
+        run_scatter(grid, sizes, rows, scratch, produce, made, small.cross, small.collect)
         mine = grid.index(*grid.me)
 
         def norm_tile(index, _):
@@ -1520,10 +1571,10 @@
         stats, segment[None, :], jnp.pad(examples, ((0, 0), (0, 125))), sizes, lax.axis_size("dp"), 6
     )
     vocab_ids = lax.axis_index("seq") * local_vocab + jnp.arange(local_vocab, dtype=jnp.int32)
-    grad_logits = (
+    grad_logits = held((
         jnp.where(vocab_ids[None, :] == targets[0][:, None], coef[0][:, None], 0.0)
         - weights.reshape(BLOCK, local_vocab).astype(jnp.float32) * coef[1][:, None]
-    ).astype(jnp.bfloat16)
+    ).astype(jnp.bfloat16))
     final_rows = final_full.reshape(BLOCK, D)
     head_sum = PairSum(lambda which: dot_tn(half_of(final_rows, which), grad_logits)).cross()
 

time: 928 us -> 909 us (0.980)
  Pallas kernels: 683 us -> 670 us
    pallas_call x6, Pallas kernels: 607 us -> 586 us  [call(): pl.pallas_call(body, out_shape=out_shape, in_specs=[ANY] * len(before) +...]
    convert_element_type x2 -> x1, other arithmetic: 19.4 us -> 14.7 us  [per_device(): grad_logits = held((jnp.where(vocab_ids[None, :] == targets[0][:, None],...]
  transfers between devices with their start and end apart: 15 -> 15, of which waited for: 0 -> 0; matrix products, arithmetic and copies ran while one was open for 16% -> 14% of each run, Pallas kernels for 37% -> 36%
where the time goes in v5:
time: 909 us; the launch traced here: 905 us
  Pallas kernels  670 us (74%)
  other arithmetic  109 us (12%)
  matrix products  87.2 us (10%)
  local copies, waits for them, and re-layouts  28.7 us (3%)
    pallas_call x6, Pallas kernels, call(): pl.pallas_call(body, out_shape=out_shape, in_specs=[ANY] * len(before) +...  586 us
    dot_general x10, matrix products, dot_tn(): lax.dot_general(left, right, (((0,), (0,)), ((), ())), preferred_element_...  87.2 us
    pallas_call x1, Pallas kernels, attention_backward(): pl.pallas_call(kernel, grid_spec=pltpu.PrefetchScalarGridSpec(num_scalar_...  36.7 us
    pallas_call x1, Pallas kernels, attention_forward(): pl.pallas_call(kernel, grid_spec=pltpu.PrefetchScalarGridSpec(num_scalar_...  25.6 us
    pallas_call x1, Pallas kernels, score_rows(): pl.pallas_call(kernel, out_shape=[jax.ShapeDtypeStruct((8, BLOCK), jnp.fl...  22.1 us
    convert_element_type x5, other arithmetic, join(): (self.sum.astype(jnp.float32) + self.other.astype(jnp.float32)).astype(jn...  21.9 us
  transfers between devices with their start and end apart: 15, of which 0 were waited for; matrix products, arithmetic and copies ran while one was open for 14% of the time, Pallas kernels for 36%

profile of v5, /device:TPU:0, one launch (start us, length us, event | category | flops | bytes accessed | tf_op | source)
XLA Modules:
  0.0 905.3 jit_solution(18018362996750207974)
XLA Ops:
  16.7 4.2 copy.60
  20.9 3.7 fusion.33
  29.2 96.3 %shard_map.314 = (bf16[8,256,2048]{2,1,0:T(8,128)(2,1)}, bf16[8,256,2048]{2,1,0:T(8,128)(2,1)}, bf16[8,256,2048]{2,1,0:T(8,128)(2,1)}, bf16[8,256,768]{2,1,0:T(8...) custom-call(bf16[256,2048]{1,0:T(8,128)(2,1)} %bitcast.127, ...), custom_call_target="tpu_custom_call" | custom-call | flops 15032385536 | bytes 268435456 | tf_op jit(solution)/shard_map/pallas_call | solution.py:583
  125.5 25.6 %shard_map.315 = (bf16[2048,256]{1,0:T(8,128)(2,1)}, f32[2,2048,1]{2,1,0:T(8,128)}) custom-call(s32[8]{0:T(128)} %and_select_fusion.first_ref, bf16[2048,768]{1,0:T(8,128)(2,1)} %bitcast.72, bf16[2048,768]{1,0:T(8,128)(2,1)} %bitcast.73, bf16[2048,768]{1,0:T(8,128)(2,1)} %bitcast.74, s32[2048,1]{1,0:T(8,128)} %subtract_subtract_fusion.start_ref), custom_call_target="tpu_custom_call" | custom-call | tf_op jit(solution)/shard_map/pallas_call | solution.py:436
  151.0 99.0 %shard_map.316 = (bf16[256,2048]{1,0:T(8,128)(2,1)}, bf16[256,2048]{1,0:T(8,128)(2,1)}, f32[256,2048]{1,0:T(8,128)}, f32[256,1]{1,0:T(8,128)}) custom-call(bf16[256,2048]{1,0:T(8,128)(2,1)} %bitcast.128, bf16[8,256,256]{2,1,0:T(8,128)(2,1)} %bitcast.86, bf16[8,256,1024]{2,1,0:T(8,128)(2,1)} %get-tuple-element.52.refs_2_, bf16[256,2048]{1,0:T(8,128)(2,1)} %bitcast.125, ...), custom_call_target="tpu_custom_call" | custom-call | flops 10737418240 | bytes 268435456 | tf_op jit(solution)/shard_map/pallas_call | solution.py:583
  250.1 98.7 %shard_map.317 = (bf16[8,256,2048]{2,1,0:T(8,128)(2,1)}, bf16[8,256,3328]{2,1,0:T(8,128)(2,1)}, f32[8,2048]{1,0:T(8,128)}) custom-call(bf16[256,2048]{1,0:T(8,128)(2,1)} %get-tuple-element.53.refs_0_, bf16[2048,3328]{1,0:T(8,128)(2,1)} %refs_2_.2, s32[2048,1]{1,0:T(8,128)} %copy.55.refs_2_), custom_call_target="tpu_custom_call" | custom-call | flops 27917287424 | bytes 268435456 | tf_op jit(solution)/shard_map/pallas_call | solution.py:583
  348.8 22.1 %shard_map.318 = (f32[8,2048]{1,0:T(8,128)}, f32[8,128]{1,0:T(8,128)}) custom-call(f32[8,2048]{1,0:T(8,128)} %get-tuple-element.54.stats_ref, s32[1,2048]{1,0:T(1,128)} %bitcast.100, f32[8,128]{1,0:T(8,128)} %select_maximum_fusion.examples_ref), custom_call_target="tpu_custom_call" | custom-call | tf_op jit(solution)/shard_map/pallas_call | solution.py:1329
  371.9 14.7 %fusion.1 = bf16[2048,3328]{1,0:T(8,128)(2,1)} fusion(bf16[8,256,3328]{2,1,0:T(8,128)(2,1)} %get-tuple-element.61, f32[2048]{0:T(1024)S(1)} %bitcast.97, f32[2048]{0:T(1024)S(1)} %bitcast.96, s32[3328]{0:T(1024)S(1)} %iota_add_fusion, s32[2048]{0:T(1024)S(1)} %bitcast.95), kind=kLoop, calls=%fused_computation.2 | loop fusion | flops 40894464 | bytes 27300864 | tf_op jit(solution)/shard_map/convert_element_type | solution.py:1577
  386.6 21.8 %convolution_convert_fusion = bf16[1024,3328]{1,0:T(8,128)(2,1)} fusion(bf16[2048,3328]{1,0:T(8,128)(2,1)} %fusion.1, bf16[2048,2048]{1,0:T(8,128)(2,1)} %bitcast.136, s32[]{:T(128)S(6)} %select_n.82), kind=kOutput, calls=%fused_computation.6 | convolution fusion | flops 13962051584 | bytes 24641540 | tf_op jit(solution)/shard_map/dot_general | solution.py:370
  408.4 20.6 %fusion.9 = f32[1024,3328]{1,0:T(8,128)S(1)} fusion(bf16[2048,3328]{1,0:T(8,128)(2,1)} %fusion.1, bf16[2048,2048]{1,0:T(8,128)(2,1)} %bitcast.137, s32[]{:T(128)S(6)} %select_n.80), kind=kOutput, calls=%fused_computation.22 | convolution fusion | flops 13958643712 | bytes 31457284 | tf_op jit(solution)/shard_map/dot_general | solution.py:370
  430.2 7.7 add_convert_fusion.1.refs_0_
  440.4 98.0 %shard_map.319 = (f32[256,2048]{1,0:T(8,128)}, bf16[256,2048]{1,0:T(8,128)(2,1)}, f32[8,2048]{1,0:T(8,128)}) custom-call(bf16[1024,3328]{1,0:T(8,128)(2,1)} %add_convert_fusion.1.refs_0_, bf16[8,256,3328]{2,1,0:T(8,128)(2,1)} %bitcast.80, bf16[2048,3328]{1,0:T(8,128)(2,1)} %refs_2_.2, f32[256,2048]{1,0:T(8,128)} %get-tuple-element.62.refs_3_, ...), custom_call_target="tpu_custom_call" | custom-call | flops 27917287424 | bytes 268435456 | tf_op jit(solution)/shard_map/pallas_call | solution.py:583
  538.4 92.6 %shard_map.320 = (bf16[8,256,2048]{2,1,0:T(8,128)(2,1)}, bf16[8,256,256]{2,1,0:T(8,128)(2,1)}, bf16[8,256,1024]{2,1,0:T(8,128)(2,1)}, f32[8,1024]{1,0:T(8,128)}) custom-call(bf16[256,2048]{1,0:T(8,128)(2,1)} %get-tuple-element.64.refs_0_, bf16[256,2048]{1,0:T(8,128)(2,1)} %bitcast.126, bf16[1024,2048]{1,0:T(8,128)(2,1)} %refs_2_.3, ...), custom_call_target="tpu_custom_call" | custom-call | flops 10737418240 | bytes 268435456 | tf_op jit(solution)/shard_map/pallas_call | solution.py:583
  631.0 8.2 fusion.24
  639.3 4.8 fusion.21
  644.1 6.7 fusion.17
  651.4 3.5 fusion.30
  655.9 3.7 fusion.19
  659.6 4.6 fusion.6
  672.0 36.7 %shard_map.321 = (bf16[2048,768]{1,0:T(8,128)(2,1)}, f32[2,1,384]{2,1,0:T(1,128)}) custom-call(s32[8]{0:T(128)} %and_select_fusion.first_ref, bf16[2048,768]{1,0:T(8,128)(2,1)} %bitcast.75, bf16[2048,768]{1,0:T(8,128)(2,1)} %bitcast.76, bf16[2048,768]{1,0:T(8,128)(2,1)} %bitcast.77, s32[2048,1]{1,0:T(8,128)} %subtract_subtract_fusion.start_ref, ...), custom_call_target="tpu_custom_call" | custom-call | tf_op jit(solution)/shard_map/pallas_call | solution.py:519
  709.4 8.0 fusion.27
  717.3 5.3 fusion.11
  722.7 9.4 %add_convert_fusion.refs_1_ = bf16[1024,3328]{1,0:T(8,128)(2,1)} fusion(bf16[1024,3328]{1,0:T(8,128)(2,1)} %collective-permute-done.5, bf16[1024,3328]{1,0:T(8,128)(2,1)} %add_convert_fusion.1.refs_0_), kind=kLoop, calls=%fused_computation.4 | loop fusion | flops 13631488 | bytes 20447232 | tf_op jit(solution)/shard_map/convert_element_type | solution.py:1504
  737.8 101.0 %shard_map.322 = (f32[256,2048]{1,0:T(8,128)}, f32[8,2048]{1,0:T(8,128)}, f32[8,2048]{1,0:T(8,128)}) custom-call(bf16[1024,768]{1,0:T(8,128)(2,1)} %add_convert_fusion.7.refs_0_, bf16[1024,3328]{1,0:T(8,128)(2,1)} %add_convert_fusion.refs_1_, bf16[256,2048]{1,0:T(8,128)(2,1)} %bitcast.129, f32[256,2048]{1,0:T(8,128)} %get-tuple-element.71.refs_3_, ...), custom_call_target="tpu_custom_call" | custom-call | flops 15032385536 | bytes 268435456 | tf_op jit(solution)/shard_map/pallas_call | solution.py:583
  840.0 3.4 add_convert_fusion.6
  849.9 4.5 add_convert_fusion.3
  860.7 3.2 maximum_convert_fusion.3
  863.9 8.2 reshape.215
  874.0 4.4 maximum_convert_fusion.2
  880.3 4.9 maximum_convert_fusion.1
  885.4 4.0 broadcast_select_fusion.1
  889.4 13.2 %maximum_convert_fusion = f32[2048,3328]{1,0:T(8,128)} fusion(bf16[1024,3328]{1,0:T(8,128)(2,1)S(1)} %get-tuple-element.86, bf16[1024,3328]{1,0:T(8,128)(2,1)S(1)} %get-tuple-element.85), kind=kLoop, calls=%fused_computation.3 | loop fusion | flops 27262976 | bytes 40894464 | tf_op jit(solution)/shard_map/concatenate | solution.py:1639
  (133 shorter events, 61.1 us)
Async XLA Ops:
  10.6 14.8 %copy-start.7 = (f32[2048]{0:T(1024)}, f32[2048]{0:T(1024)S(1)}, u32[]{:S(2)}) copy-start(f32[2048]{0:T(1024)S(1)} %broadcast_in_dim.121) | copy-start | bytes 24580
  250.0 121.8 %copy-start.6 = (s32[1,2048]{1,0:T(1,128)S(1)}, s32[1,2048]{1,0:T(1,128)}, u32[]{:S(2)}) copy-start(s32[1,2048]{1,0:T(1,128)} %param.20) | copy-start | bytes 24580
  408.3 21.9 %collective-permute-start = (bf16[1024,3328]{1,0:T(8,128)(2,1)}, bf16[1024,3328]{1,0:T(8,128)(2,1)}, u32[]{:S(2)}, u32[]{:S(2)}) collective-permute-start(bf16[1024,3328]{1,0:T(8,128)(2,1)} %convolution_convert_fusion), channel_id=1, source_target_pairs={{0,8},{8,0},{16,24},{24,16},{1,9},{9,1},{17,25},{25,17},{2,10},{10... | collective-permute-start | bytes 20447240 | tf_op jit(solution)/shard_map/ppermute | solution.py:1492
  408.4 20.6 %copy-start.8 = (f32[8,128]{1,0:T(8,128)S(1)}, f32[8,128]{1,0:T(8,128)}, u32[]{:S(2)}) copy-start(f32[8,128]{1,0:T(8,128)} %get-tuple-element.55) | copy-start | bytes 12292
  437.9 284.8 %collective-permute-start.5 = (bf16[1024,3328]{1,0:T(8,128)(2,1)}, bf16[1024,3328]{1,0:T(8,128)(2,1)}, u32[]{:S(2)}, u32[]{:S(2)}) collective-permute-start(bf16[1024,3328]{1,0:T(8,128)(2,1)} %add_convert_fusion.1.refs_0_), channel_id=1, source_target_pairs={{0,16},{16,0},{8,24},{24,8},{1,17},{17,1},{9,25},{25,9},{2,18},{18... | collective-permute-start | bytes 20447240 | tf_op jit(solution)/shard_map/ppermute | solution.py:1497
  631.0 8.3 copy-start.10
  631.0 8.3 copy-start.12
  639.2 26.4 %collective-permute-start.3 = (bf16[1024,1024]{1,0:T(8,128)(2,1)S(1)}, bf16[1024,1024]{1,0:T(8,128)(2,1)S(1)}, u32[]{:S(2)}, u32[]{:S(2)}) collective-permute-start(bf16[1024,1024]{1,0:T(8,128)(2,1)S(1)} %fusion.24), channel_id=1, source_target_pairs={{0,8},{8,0},{16,24},{24,16},{1,9},{9,1},{17,25},{25,17},{2,10},{10... | collective-permute-start | bytes 6291464 | tf_op jit(solution)/shard_map/ppermute | solution.py:1492
  639.3 20.3 %slice-start.2 = ((s8[8388608]{0:T(1024)(128)(4,1)}), s8[4194304]{0:T(1024)(128)(4,1)S(1)}, s32[]{:S(2)}) async-start(s8[8388608]{0:T(1024)(128)(4,1)} %bitcast.133), calls=%async_computation.2 | async-start | bytes 8388608
  644.1 7.3 copy-start.3
  644.1 15.5 %slice-start.3 = ((s8[8388608]{0:T(1024)(128)(4,1)}), s8[4194304]{0:T(1024)(128)(4,1)S(1)}, s32[]{:S(2)}) async-start(s8[8388608]{0:T(1024)(128)(4,1)} %bitcast.133), calls=%async_computation.3 | async-start | bytes 8388608
  650.9 18.5 %collective-permute-start.2 = (bf16[1024,1024]{1,0:T(8,128)(2,1)S(1)}, bf16[1024,1024]{1,0:T(8,128)(2,1)S(1)}, u32[]{:S(2)}, u32[]{:S(2)}) collective-permute-start(bf16[1024,1024]{1,0:T(8,128)(2,1)S(1)} %fusion.21), channel_id=1, source_target_pairs={{0,8},{8,0},{16,24},{24,16},{1,9},{9,1},{17,25},{25,17},{2,10},{10... | collective-permute-start | bytes 6291464 | tf_op jit(solution)/shard_map/ppermute | solution.py:1492
  654.9 4.7 copy-start.11
  655.8 8.5 collective-permute-start.1
  665.2 173.5 %collective-permute-start.6 = (bf16[256,1024]{1,0:T(8,128)(2,1)}, bf16[256,1024]{1,0:T(8,128)(2,1)}, u32[]{:S(2)}, u32[]{:S(2)}) collective-permute-start(bf16[256,1024]{1,0:T(8,128)(2,1)} %add_convert_fusion.9.rest_0_), channel_id=1, source_target_pairs={{0,16},{16,0},{8,24},{24,8},{1,17},{17,1},{9,25},{25,9},{2,18},{18... | collective-permute-start | bytes 1572872 | tf_op jit(solution)/shard_map/ppermute | solution.py:1497
  667.8 171.0 %collective-permute-start.8 = (bf16[1024,1024]{1,0:T(8,128)(2,1)}, bf16[1024,1024]{1,0:T(8,128)(2,1)}, u32[]{:S(2)}, u32[]{:S(2)}) collective-permute-start(bf16[1024,1024]{1,0:T(8,128)(2,1)} %add_convert_fusion.4.rest_2_), channel_id=1, source_target_pairs={{0,16},{16,0},{8,24},{24,8},{1,17},{17,1},{9,25},{25,9},{2,18},{18... | collective-permute-start | bytes 6291464 | tf_op jit(solution)/shard_map/ppermute | solution.py:1497
  671.5 167.2 %collective-permute-start.7 = (bf16[1024,1024]{1,0:T(8,128)(2,1)}, bf16[1024,1024]{1,0:T(8,128)(2,1)}, u32[]{:S(2)}, u32[]{:S(2)}) collective-permute-start(bf16[1024,1024]{1,0:T(8,128)(2,1)} %add_convert_fusion.5.rest_1_), channel_id=1, source_target_pairs={{0,16},{16,0},{8,24},{24,8},{1,17},{17,1},{9,25},{25,9},{2,18},{18... | collective-permute-start | bytes 6291464 | tf_op jit(solution)/shard_map/ppermute | solution.py:1497
  709.4 8.0 copy-start.9
  717.3 15.3 %collective-permute-start.4 = (bf16[1024,768]{1,0:T(8,128)(2,1)}, bf16[1024,768]{1,0:T(8,128)(2,1)}, u32[]{:S(2)}, u32[]{:S(2)}) collective-permute-start(bf16[1024,768]{1,0:T(8,128)(2,1)} %fusion.27), channel_id=1, source_target_pairs={{0,8},{8,0},{16,24},{24,16},{1,9},{9,1},{17,25},{25,17},{2,10},{10... | collective-permute-start | bytes 4718600 | tf_op jit(solution)/shard_map/ppermute | solution.py:1492
  732.1 153.1 %collective-permute-start.14 = (bf16[1024,3328]{1,0:T(8,128)(2,1)}, bf16[1024,3328]{1,0:T(8,128)(2,1)}, u32[]{:S(2)}, u32[]{:S(2)}) collective-permute-start(bf16[1024,3328]{1,0:T(8,128)(2,1)} %add_convert_fusion.refs_1_), channel_id=1, source_target_pairs={{0,8},{8,0},{16,24},{24,16},{1,9},{9,1},{17,25},{25,17},{2,10},{10... | collective-permute-start | bytes 20447240 | tf_op jit(solution)/shard_map/ppermute | solution.py:1511
  735.5 103.3 %collective-permute-start.9 = (bf16[1024,768]{1,0:T(8,128)(2,1)}, bf16[1024,768]{1,0:T(8,128)(2,1)S(1)}, u32[]{:S(2)}, u32[]{:S(2)}) collective-permute-start(bf16[1024,768]{1,0:T(8,128)(2,1)} %add_convert_fusion.7.refs_0_), channel_id=1, source_target_pairs={{0,16},{16,0},{8,24},{24,8},{1,17},{17,1},{9,25},{25,9},{2,18},{18... | collective-permute-start | bytes 4718600 | tf_op jit(solution)/shard_map/ppermute | solution.py:1497
  838.8 1.1 copy-start.1
  843.4 15.2 %collective-permute-start.10 = (bf16[1024,768]{1,0:T(8,128)(2,1)}, bf16[1024,768]{1,0:T(8,128)(2,1)}, u32[]{:S(2)}, u32[]{:S(2)}) collective-permute-start(bf16[1024,768]{1,0:T(8,128)(2,1)} %add_convert_fusion.6), channel_id=1, source_target_pairs={{0,8},{8,0},{16,24},{24,16},{1,9},{9,1},{17,25},{25,17},{2,10},{10... | collective-permute-start | bytes 4718600 | tf_op jit(solution)/shard_map/ppermute | solution.py:1511
  846.6 9.6 %copy-start.5 = (f32[8,2048]{1,0:T(8,128)S(1)}, f32[8,2048]{1,0:T(8,128)}, u32[]{:S(2)}) copy-start(f32[8,2048]{1,0:T(8,128)} %get-tuple-element.77.refs_4_) | copy-start | bytes 196612
  849.4 7.5 collective-permute-start.11
  849.9 22.3 %collective-permute-start.13 = (bf16[1024,1024]{1,0:T(8,128)(2,1)S(1)}, bf16[1024,1024]{1,0:T(8,128)(2,1)}, u32[]{:S(2)}, u32[]{:S(2)}) collective-permute-start(bf16[1024,1024]{1,0:T(8,128)(2,1)S(1)} %add_convert_fusion.2), channel_id=1, source_target_pairs={{0,8},{8,0},{16,24},{24,16},{1,9},{9,1},{17,25},{25,17},{2,10},{10... | collective-permute-start | bytes 6291464 | tf_op jit(solution)/shard_map/ppermute | solution.py:1511
  855.7 22.7 %collective-permute-start.12 = (bf16[1024,1024]{1,0:T(8,128)(2,1)}, bf16[1024,1024]{1,0:T(8,128)(2,1)}, u32[]{:S(2)}, u32[]{:S(2)}) collective-permute-start(bf16[1024,1024]{1,0:T(8,128)(2,1)} %add_convert_fusion.3), channel_id=1, source_target_pairs={{0,8},{8,0},{16,24},{24,16},{1,9},{9,1},{17,25},{25,17},{2,10},{10... | collective-permute-start | bytes 6291464 | tf_op jit(solution)/shard_map/ppermute | solution.py:1511
  874.0 4.4 copy-start
  880.3 5.0 slice-start
  880.3 5.1 slice-start.1
  889.4 13.2 %copy-start.4 = (bf16[256,2048]{1,0:T(8,128)(2,1)S(1)}, bf16[256,2048]{1,0:T(8,128)(2,1)}, u32[]{:S(2)}) copy-start(bf16[256,2048]{1,0:T(8,128)(2,1)} %get-tuple-element.56) | copy-start | bytes 3145732
  889.4 14.2 %copy-start.2 = (f32[256,2048]{1,0:T(8,128)S(1)}, f32[256,2048]{1,0:T(8,128)}, u32[]{:S(2)}) copy-start(f32[256,2048]{1,0:T(8,128)} %get-tuple-element.76) | copy-start | bytes 6291460

commit v6 on v5

--- a/solution.py
+++ b/solution.py
@@ -370,18 +370,29 @@
     return lax.dot_general(left, right, (((0,), (0,)), ((), ())), preferred_element_type=jnp.float32)
 
 
-def rotary_planes(position):
+def rotary_frequencies():
     half_rot = ROT // 2
     frequency = 10000.0 ** (-2.0 * jnp.arange(half_rot, dtype=jnp.float32) / ROT)
-    angles = position.astype(jnp.float32)[:, None] * frequency[None, :]
+    return jnp.tile(frequency, HEAD_DIM // half_rot)[None, :]
+
+
+def first_rows(lengths, row):
+    start, end = jnp.zeros_like(row), jnp.int32(0)
+    for example in range(EXB):
+        end = end + lengths[example]
+        start = jnp.where(row >= end, end, start)
+    return start
+
+
+def rotary_planes(position, frequencies):
+    half_rot = ROT // 2
+    angles = position.astype(jnp.float32) * frequencies
     cos, sin = jnp.cos(angles), jnp.sin(angles)
-    rows = position.shape[0]
-    rest = jnp.zeros((rows, HEAD_DIM - ROT), jnp.float32)
-    none = jnp.zeros_like(sin)
+    lane = lax.broadcasted_iota(jnp.int32, angles.shape, 1)
     return (
-        jnp.concatenate([cos, cos, rest + 1.0], axis=1),
-        jnp.concatenate([none, sin, rest], axis=1),
-        jnp.concatenate([-sin, none, rest], axis=1),
+        jnp.where(lane < ROT, cos, 1.0),
+        jnp.where((lane >= half_rot) & (lane < ROT), sin, 0.0),
+        jnp.where(lane < half_rot, -sin, 0.0),
     )
 
 
@@ -401,13 +412,18 @@
     return (key_ids >= start_col) & (key_ids <= query_ids)
 
 
-def attention_forward(qkv, start_col, first_tile, heads):
+def tile_starts(lengths, tile):
+    rows = tile * ATT_TILE + lax.broadcasted_iota(jnp.int32, (ATT_TILE, 1), 0)
+    return first_rows(lengths, rows), first_rows(lengths, tile * ATT_TILE) // ATT_TILE
+
+
+def attention_forward(qkv, lengths, heads):
     tiles = BLOCK // ATT_TILE
 
-    def kernel(first_ref, q_ref, k_ref, v_ref, start_ref, ctx_ref, lse_ref):
+    def kernel(lengths_ref, q_ref, k_ref, v_ref, ctx_ref, lse_ref):
         tile = pl.program_id(1)
         queries = q_ref[...]
-        start = start_ref[...]
+        start, first = tile_starts(lengths_ref, tile)
 
         def step(key_tile, carry):
             top, total, acc = carry
@@ -429,7 +445,7 @@
             jnp.zeros((ATT_TILE, HEAD_DIM), jnp.float32),
         )
         begin = step(tile, begin)
-        top, total, acc = lax.fori_loop(first_ref[tile], tile, step, begin)
+        top, total, acc = lax.fori_loop(first, tile, step, begin)
         ctx_ref[...] = (acc / total).astype(jnp.bfloat16)
         lse_ref[...] = top + jnp.log(total)
 
@@ -442,7 +458,6 @@
                 pl.BlockSpec((ATT_TILE, HEAD_DIM), lambda h, i, first: (i, 3 * h)),
                 pl.BlockSpec((BLOCK, HEAD_DIM), lambda h, i, first: (0, 3 * h + 1)),
                 pl.BlockSpec((BLOCK, HEAD_DIM), lambda h, i, first: (0, 3 * h + 2)),
-                pl.BlockSpec((ATT_TILE, 1), lambda h, i, first: (i, 0)),
             ],
             out_specs=[
                 pl.BlockSpec((ATT_TILE, HEAD_DIM), lambda h, i, first: (i, h)),
@@ -454,14 +469,14 @@
             jax.ShapeDtypeStruct((heads, BLOCK, 1), jnp.float32),
         ],
         compiler_params=pltpu.CompilerParams(vmem_limit_bytes=VMEM_LIMIT),
-    )(first_tile, qkv, qkv, qkv, start_col)
-
-
-def attention_backward(qkv, start_col, first_tile, heads, ctx, lse, grad_ctx, planes, before):
+    )(lengths, qkv, qkv, qkv)
+
+
+def attention_backward(qkv, lengths, heads, ctx, lse, grad_ctx, planes, before):
     tiles = BLOCK // ATT_TILE
 
     def kernel(
-        first_ref, q_ref, k_ref, v_ref, start_ref, ctx_ref, lse_ref, do_ref, cos_ref, below_ref,
+        lengths_ref, q_ref, k_ref, v_ref, ctx_ref, lse_ref, do_ref, cos_ref, below_ref,
         above_ref, *rest,
     ):
         out_ref, sums_ref, dk_ref, dv_ref = rest[len(before) :]
@@ -473,7 +488,7 @@
             dv_ref[...] = jnp.zeros_like(dv_ref)
 
         queries = q_ref[...]
-        start = start_ref[...]
+        start, first = tile_starts(lengths_ref, tile)
         grads = do_ref[...]
         lse_rows = lse_ref[...]
         inner = jnp.sum(
@@ -494,7 +509,7 @@
             return dq + jnp.dot(grad_scores, keys, preferred_element_type=jnp.float32)
 
         dq = lax.fori_loop(
-            first_ref[tile], tile + 1, step, jnp.zeros((ATT_TILE, HEAD_DIM), jnp.float32)
+            first, tile + 1, step, jnp.zeros((ATT_TILE, HEAD_DIM), jnp.float32)
         )
         here = pl.ds(pl.multiple_of(tile * ATT_TILE, ATT_TILE), ATT_TILE)
         out_ref[here, :HEAD_DIM] = turn(
@@ -525,7 +540,6 @@
                 pl.BlockSpec((ATT_TILE, HEAD_DIM), lambda h, i, first: (i, 3 * h)),
                 pl.BlockSpec((BLOCK, HEAD_DIM), lambda h, i, first: (0, 3 * h + 1)),
                 pl.BlockSpec((BLOCK, HEAD_DIM), lambda h, i, first: (0, 3 * h + 2)),
-                pl.BlockSpec((ATT_TILE, 1), lambda h, i, first: (i, 0)),
                 pl.BlockSpec((ATT_TILE, HEAD_DIM), lambda h, i, first: (i, h)),
                 pl.BlockSpec((pl.squeezed, ATT_TILE, 1), lambda h, i, first: (h, i, 0)),
                 pl.BlockSpec((ATT_TILE, HEAD_DIM), lambda h, i, first: (i, h)),
@@ -548,7 +562,7 @@
             jax.ShapeDtypeStruct((heads, 1, 3 * HEAD_DIM), jnp.float32),
         ],
         compiler_params=pltpu.CompilerParams(vmem_limit_bytes=VMEM_LIMIT),
-    )(first_tile, qkv, qkv, qkv, start_col, ctx, lse, grad_ctx, *planes, *before)
+    )(lengths, qkv, qkv, qkv, ctx, lse, grad_ctx, *planes, *before)
 
 
 def gather_cut(sizes):
@@ -573,6 +587,7 @@
 
 ANY = pl.BlockSpec(memory_space=pl.ANY)
 VMEM = pl.BlockSpec(memory_space=pltpu.VMEM)
+SMEM = pl.BlockSpec(memory_space=pltpu.SMEM)
 
 
 def row_kernel(kernel, collective, out_shape, in_specs, out_specs, scratch, cost, before=()):
@@ -659,15 +674,15 @@
     return centered, inverse
 
 
-def open_rows(own, sizes, collective, norms, qkv_flat, qkv_bias, up_weight, up_bias, planes):
+def open_rows(own, sizes, collective, norms, qkv_flat, qkv_bias, up_weight, up_bias, lengths):
     rows = own.shape[0]
     shards = sizes[0] * sizes[1]
     width, hidden = qkv_flat.shape[1], up_weight.shape[1]
     heads = width // (3 * HEAD_DIM)
 
     def kernel(
-        own_ref, norms_ref, qkvw_any, qkvb_ref, upw_any, upb_ref, cos_ref, below_ref, above_ref,
-        plain_any, one_any, two_any, qkv_any, act_any, slope_any,
+        own_ref, norms_ref, qkvw_any, qkvb_ref, upw_any, upb_ref, lengths_ref, freq_ref,
+        plain_any, one_any, two_any, qkv_any, act_any, slope_any, cos_ref, below_ref, above_ref,
         full, send_sems, recv_sems, qkvw, upw, load_sems, plain, one, two, qkv, act, slope, out_sems,
     ):
         grid = Grid2(sizes)
@@ -709,7 +724,9 @@
 
             lax.fori_loop(0, rows // ROW_TILE, norm_tile, 0)
             places = pl.ds(pl.multiple_of(place * rows, rows), rows)
-            cos, below, above = cos_ref[places, :], below_ref[places, :], above_ref[places, :]
+            row = place * rows + lax.broadcasted_iota(jnp.int32, (rows, 1), 0)
+            cos, below, above = rotary_planes(row - first_rows(lengths_ref, row), freq_ref[...])
+            cos_ref[places, :], below_ref[places, :], above_ref[places, :] = cos, below, above
             whole = jnp.dot(one[slot], qkvw[...], preferred_element_type=jnp.float32) + qkvb_ref[...]
             for head in range(heads):
                 first = head * 3 * HEAD_DIM
@@ -754,9 +771,10 @@
 
     return row_kernel(
         kernel, collective,
-        [out(D), out(D), out(D), out(width), out(hidden), out(hidden)],
-        [VMEM, VMEM, ANY, VMEM, ANY, VMEM, VMEM, VMEM, VMEM],
-        [ANY] * 6,
+        [out(D), out(D), out(D), out(width), out(hidden), out(hidden)]
+        + [jax.ShapeDtypeStruct((shards * rows, HEAD_DIM), jnp.float32)] * 3,
+        [VMEM, VMEM, ANY, VMEM, ANY, VMEM, SMEM, VMEM],
+        [ANY] * 6 + [VMEM] * 3,
         gather_scratch(sizes, rows)
         + [
             pltpu.VMEM(qkv_flat.shape, jnp.bfloat16),
@@ -766,7 +784,7 @@
             pltpu.SemaphoreType.DMA((2, 6)),
         ],
         2 * BLOCK * D * (width + hidden),
-    )(own, norms, qkv_flat, qkv_bias, up_weight, up_bias, *planes)
+    )(own, norms, qkv_flat, qkv_bias, up_weight, up_bias, lengths, rotary_frequencies())
 
 
 def branch_rows(own, ctx, act, out_flat, down_weight, norms, sizes, collective):
@@ -1241,12 +1259,12 @@
             copy.wait_send()
 
 
-def score_rows(stats, seg_row, examples, sizes, replicas, collective):
+def score_rows(stats, lengths, labels, reference, sizes, replicas, collective):
     shards = sizes[0] * sizes[1]
     width = BLOCK // shards
 
     def kernel(
-        stats_ref, seg_ref, examples_ref, coef_ref, losses_ref,
+        stats_ref, lengths_ref, labels_ref, reference_ref, coef_ref, losses_ref,
         came, full, ratio, ratios, spread_send, spread_recv, back_send, back_recv, cross_send, cross_recv,
     ):
         seq, dp = lax.axis_index("seq"), lax.axis_index("dp")
@@ -1297,8 +1315,19 @@
             source = lax.rem(seq + shards - step, shards)
             there = full.at[:, columns(source)]
             copy("seq", source, there, there, back_send.at[step], back_recv.at[step]).wait_recv()
-        member = lax.broadcasted_iota(jnp.int32, (EXB, BLOCK), 0) == seg_ref[...]
-        counts, reference, sign = examples_ref[:, 0:1], examples_ref[:, 1:2], examples_ref[:, 2:3]
+        example = lax.broadcasted_iota(jnp.int32, (EXB, 1), 0)
+        start, end = jnp.zeros_like(example), jnp.zeros_like(example)
+        sign, reference = jnp.zeros((EXB, 1), jnp.float32), jnp.zeros((EXB, 1), jnp.float32)
+        reached = jnp.int32(0)
+        for index in range(EXB):
+            start = jnp.where(example == index, reached, start)
+            reached = reached + lengths_ref[index]
+            end = jnp.where(example == index, reached, end)
+            sign = jnp.where(example == index, (2 * labels_ref[index] - 1).astype(jnp.float32), sign)
+            reference = jnp.where(example == index, reference_ref[index], reference)
+        counts = (end - start).astype(jnp.float32)
+        row = lax.broadcasted_iota(jnp.int32, (EXB, BLOCK), 1)
+        member = (row >= start) & (row < end)
         mean = jnp.sum(jnp.where(member, full[1:2, :], 0.0), axis=1, keepdims=True) / counts
         log_ratio = mean - reference
         ratio[...] = jnp.broadcast_to(jnp.sum(log_ratio, axis=0, keepdims=True), ratio.shape)
@@ -1332,7 +1361,7 @@
             jax.ShapeDtypeStruct((8, BLOCK), jnp.float32),
             jax.ShapeDtypeStruct((EXB, 128), jnp.float32),
         ],
-        in_specs=[VMEM] * 3,
+        in_specs=[VMEM] + [SMEM] * 3,
         out_specs=[VMEM] * 2,
         scratch_shapes=[
             pltpu.VMEM((shards, 8, width), jnp.float32),
@@ -1342,7 +1371,7 @@
             dma((shards,)), dma((shards,)), dma((shards,)), dma((shards,)), dma((replicas,)), dma((replicas,)),
         ],
         compiler_params=pltpu.CompilerParams(collective_id=collective, has_side_effects=True),
-    )(stats, seg_row, examples)
+    )(stats, lengths, labels, reference)
 
 
 def input_grad_rows(
@@ -1455,13 +1484,73 @@
     )(own, grad_stream, plain, grad_qkv, grad_up, qkv_flat, up_weight, gains, end_sums, biases)
 
 
-def segment_rows(block_lengths):
-    row_ends = jnp.cumsum(block_lengths)
-    row_ids = jnp.arange(BLOCK, dtype=jnp.int32)
-    passed = (row_ids[:, None] >= row_ends[None, :]).astype(jnp.int32)
-    segment = jnp.sum(passed, axis=1)
-    position = row_ids - jnp.sum(passed * block_lengths[None, :], axis=1)
-    return (segment, position)
+def join_halves(sums, others, earlier):
+    steps, count = 8, len(sums)
+
+    def kernel(*refs):
+        for i in range(count):
+            refs[2 * count + 1 + i][...] = (
+                refs[i][...].astype(jnp.float32) + refs[count + i][...].astype(jnp.float32)
+            ).astype(jnp.bfloat16)
+
+    specs = [pl.BlockSpec((v.shape[0] // steps, v.shape[1]), lambda i: (i, 0)) for v in sums]
+    return pl.pallas_call(
+        kernel,
+        grid=(steps,),
+        out_shape=[jax.ShapeDtypeStruct(v.shape, jnp.bfloat16) for v in sums],
+        in_specs=specs + specs + [ANY],
+        out_specs=specs,
+        compiler_params=pltpu.CompilerParams(vmem_limit_bytes=VMEM_LIMIT),
+    )(*sums, *others, earlier)
+
+
+def settle_halves(core, totals, backs, shapes, before=()):
+    steps = 8
+
+    def kernel(core_ref, *refs):
+        count = len(totals)
+        mine = pl.program_id(0) == 0
+        for i in range(count):
+            found = jnp.where(mine, refs[i][...].astype(jnp.float32), refs[count + i][...].astype(jnp.float32))
+            out = refs[2 * count + len(before) + i]
+            if len(out.shape) == 3:
+                for head in range(out.shape[1]):
+                    out[:, head, :] = found[:, head * out.shape[2] : (head + 1) * out.shape[2]]
+            else:
+                out[...] = found
+
+    def place(half, core_ref):
+        return jnp.where(half == 0, core_ref[0], 1 - core_ref[0])
+
+    ins, outs = [], []
+    for which in (0, 1):
+        for value in totals:
+            ins.append(
+                pl.BlockSpec(
+                    (value.shape[0] // steps, value.shape[1]),
+                    (lambda h, i, core_ref: (jnp.where(h == 0, i, steps - 1), 0))
+                    if which == 0
+                    else (lambda h, i, core_ref: (jnp.where(h == 0, 0, i), 0)),
+                )
+            )
+    for value, shape in zip(totals, shapes):
+        rows = value.shape[0] // steps
+        if len(shape) == 3:
+            outs.append(
+                pl.BlockSpec((rows,) + shape[1:], lambda h, i, core_ref: (place(h, core_ref) * steps + i, 0, 0))
+            )
+        elif shape[0] == value.shape[0]:
+            outs.append(pl.BlockSpec((rows, value.shape[1]), lambda h, i, core_ref: (i, place(h, core_ref))))
+        else:
+            outs.append(pl.BlockSpec((rows, shape[1]), lambda h, i, core_ref: (place(h, core_ref) * steps + i, 0)))
+    return pl.pallas_call(
+        kernel,
+        grid_spec=pltpu.PrefetchScalarGridSpec(
+            num_scalar_prefetch=1, grid=(2, steps), in_specs=ins + [ANY] * len(before), out_specs=outs
+        ),
+        out_shape=[jax.ShapeDtypeStruct(shape, jnp.float32) for shape in shapes],
+        compiler_params=pltpu.CompilerParams(vmem_limit_bytes=VMEM_LIMIT),
+    )(core, *totals, *backs, *before)
 
 
 def row_of(vector):
@@ -1498,33 +1587,23 @@
         return self
 
     def join(self):
-        if self.plain:
-            self.total = self.other
-        else:
-            self.total = (self.sum.astype(jnp.float32) + self.other.astype(jnp.float32)).astype(jnp.bfloat16)
+        self.total = self.other if self.plain else join_halves([self.sum], [self.other], self.other)[0]
         return self
 
-    def settle(self):
-        if self.plain:
-            first, second = self.total[0], self.total[1]
-        else:
-            back = lax.ppermute(self.total, "dp", PAIR)
-            first = jnp.where(self.core == 0, self.total, back)
-            second = jnp.where(self.core == 0, back, self.total)
-        return first.astype(jnp.float32), second.astype(jnp.float32)
-
-
-def after(values, earlier):
-    def kernel(*refs):
-        del refs
-
-    return pl.pallas_call(
-        kernel,
-        out_shape=[jax.ShapeDtypeStruct(v.shape, v.dtype) for v in values],
-        in_specs=[ANY] * (len(values) + 1),
-        out_specs=[ANY] * len(values),
-        input_output_aliases={i: i for i in range(len(values))},
-    )(*values, earlier)
+
+def join_all(sums, earlier):
+    if not sums[0].plain:
+        totals = join_halves([one.sum for one in sums], [one.other for one in sums], earlier)
+        for one, total in zip(sums, totals):
+            one.total = total
+
+
+def settle_all(sums, shapes, before=()):
+    if sums[0].plain:
+        core = jnp.zeros((1,), jnp.int32)
+        return settle_halves(core, [s.other[0] for s in sums], [s.other[1] for s in sums], shapes, before)
+    backs = [lax.ppermute(one.total, "dp", PAIR) for one in sums]
+    return settle_halves(sums[0].core[None], [one.total for one in sums], backs, shapes, before)
 
 
 def per_device(
@@ -1545,18 +1624,12 @@
     qkv_flat = qkv_weight.reshape(D, width)
     out_flat = out_weight.reshape(inner, D)
     block_lengths = lengths[0]
-    segment, position = segment_rows(block_lengths)
-    start = jnp.arange(BLOCK, dtype=jnp.int32) - position
-    start_col = start[:, None]
-    first_tile = start[::ATT_TILE] // ATT_TILE
-    planes = rotary_planes(position)
-
     norms = jnp.concatenate([row_of(v) for v in (ln1_gain, ln1_bias, ln2_gain, ln2_bias)], axis=0)
-    plain, first_full, second_full, qkv, act, slope = open_rows(
-        own, sizes, 0, norms, qkv_flat, full_bias, up_weight, row_of(up_bias), planes
+    plain, first_full, second_full, qkv, act, slope, *planes = open_rows(
+        own, sizes, 0, norms, qkv_flat, full_bias, up_weight, row_of(up_bias), block_lengths
     )
     flat_qkv = qkv.reshape(BLOCK, width)
-    ctx, lse = attention_forward(flat_qkv, start_col, first_tile, local_heads)
+    ctx, lse = attention_forward(flat_qkv, block_lengths, local_heads)
     shards, rows = plain.shape[0], plain.shape[1]
     end_norms = jnp.concatenate([row_of(v) for v in (lnf_gain, lnf_bias, branch_bias)], axis=0)
     output, final, normed, inverse = branch_rows(
@@ -1564,11 +1637,8 @@
     )
     final_full, weights, stats = logit_rows(final, head_weight, targets[0][:, None], sizes, 2)
 
-    examples = jnp.stack(
-        [block_lengths.astype(jnp.float32), ref_logps[0], (2 * labels[0] - 1).astype(jnp.float32)], axis=1
-    )
     coef, losses = score_rows(
-        stats, segment[None, :], jnp.pad(examples, ((0, 0), (0, 125))), sizes, lax.axis_size("dp"), 6
+        stats, block_lengths, labels[0], ref_logps[0], sizes, lax.axis_size("dp"), 6
     )
     vocab_ids = lax.axis_index("seq") * local_vocab + jnp.arange(local_vocab, dtype=jnp.int32)
     grad_logits = held((
@@ -1598,7 +1668,7 @@
         one.cross()
     made = [one.sum for one in sums]
     grad_qkv, qkv_sums = attention_backward(
-        flat_qkv, start_col, first_tile, local_heads, ctx, lse, grad_ctx.reshape(BLOCK, inner), planes,
+        flat_qkv, block_lengths, local_heads, ctx, lse, grad_ctx.reshape(BLOCK, inner), planes,
         made,
     )
     first_rows = first_full.reshape(BLOCK, D)
@@ -1614,11 +1684,11 @@
         own, grad_stream, plain, grad_qkv.reshape(shards, rows, width), grad_up, qkv_flat, up_weight, gains,
         end_sums, biases, sizes, lax.axis_size("dp"), 5, (sums[-1].sum, head_sum.join().total),
     )
-    for one, other in zip(sums, after([one.other for one in sums], small)):
-        one.other = other
-        one.join()
-    out_grad, down_grad, up_grad, qkv_grad = [one.settle() for one in sums]
-    head_grad = head_sum.settle()
+    join_all(sums, small)
+    (head_grad,) = settle_all([head_sum], [(D, local_vocab)])
+    out_grad, down_grad, up_grad, qkv_grad = settle_all(
+        sums, [(inner, D), (local_hidden, D), (D, local_hidden), qkv_weight.shape], (head_grad,)
+    )
     return (
         losses[:, 0][None],
         output[None],
@@ -1627,16 +1697,16 @@
         small[1],
         small[2],
         small[3],
-        jnp.concatenate(qkv_grad, axis=0).reshape(qkv_weight.shape),
+        qkv_grad,
         biases[0, :split].reshape(local_heads, 2 * HEAD_DIM),
-        jnp.concatenate(out_grad, axis=1).reshape(out_weight.shape),
-        jnp.concatenate(up_grad, axis=0),
+        out_grad.reshape(out_weight.shape),
+        up_grad,
         biases[0, split : split + local_hidden],
-        jnp.concatenate(down_grad, axis=1),
+        down_grad,
         small[6],
         small[4],
         small[5],
-        jnp.concatenate(head_grad, axis=0),
+        head_grad,
     )
 
 

time: 909 us -> 938 us (1.032)
  Pallas kernels: 670 us -> 770 us
  other arithmetic: 109 us -> 38.8 us
    pallas_call x1 -> x4, Pallas kernels: 0.01 us -> 54.9 us  [the longest x2 35.9 us: settle_halves(): pl.pallas_call(kernel, grid_spec=pltpu.PrefetchScalarGridSpec(num_scalar_...]
    pallas_call x6, Pallas kernels: 586 us -> 639 us  [call(): pl.pallas_call(body, out_shape=out_shape, in_specs=[ANY] * len(before) +...]
    concatenate x5 -> x0, other arithmetic: 25.2 us -> none  [the longest x1 13.2 us: per_device(): jnp.concatenate(head_grad, axis=0)]
    convert_element_type x8 -> x0, other arithmetic: 22.6 us -> none  [the longest x5 21.9 us: join(): (self.sum.astype(jnp.float32) + self.other.astype(jnp.float32)).astype(jn...]
    select_n x6 -> x0, other arithmetic: 10.4 us -> none  [the longest x5 9.89 us: settle(): first = jnp.where(self.core == 0, self.total, back)]
  transfers between devices with their start and end apart: 15 -> 15, of which waited for: 0 -> 0; matrix products, arithmetic and copies ran while one was open for 14% -> 8% of each run, Pallas kernels for 36% -> 43%
where the time goes in v6:
time: 938 us; the launch traced here: 927 us
  Pallas kernels  770 us (82%)
  matrix products  81.9 us (9%)
  other arithmetic  38.8 us (4%)
  local copies, waits for them, and re-layouts  21.8 us (2%)
  starting transfers between devices  13.2 us (1%)
    pallas_call x6, Pallas kernels, call(): pl.pallas_call(body, out_shape=out_shape, in_specs=[ANY] * len(before) +...  639 us
    dot_general x10, matrix products, dot_tn(): lax.dot_general(left, right, (((0,), (0,)), ((), ())), preferred_element_...  81.9 us
    pallas_call x2, Pallas kernels, settle_halves(): pl.pallas_call(kernel, grid_spec=pltpu.PrefetchScalarGridSpec(num_scalar_...  35.9 us
    pallas_call x1, Pallas kernels, attention_backward(): pl.pallas_call(kernel, grid_spec=pltpu.PrefetchScalarGridSpec(num_scalar_...  31.2 us
    pallas_call x1, Pallas kernels, score_rows(): pl.pallas_call(kernel, out_shape=[jax.ShapeDtypeStruct((8, BLOCK), jnp.fl...  24.4 us
    pallas_call x1, Pallas kernels, attention_forward(): pl.pallas_call(kernel, grid_spec=pltpu.PrefetchScalarGridSpec(num_scalar_...  20.7 us
    pallas_call x2, Pallas kernels, join_halves(): pl.pallas_call(kernel, grid=(steps,), out_shape=[jax.ShapeDtypeStruct(v.s...  19 us
  transfers between devices with their start and end apart: 15, of which 0 were waited for; matrix products, arithmetic and copies ran while one was open for 8% of the time, Pallas kernels for 43%

profile of v6, /device:TPU:0, one launch (start us, length us, event | category | flops | bytes accessed | tf_op | source)
XLA Modules:
  0.0 927.5 jit_solution(16433707781039623915)
XLA Ops:
  8.7 2.0 copy.36.refs_2_
  10.7 4.2 copy.38
  15.6 97.3 %shard_map.314 = (bf16[8,256,2048]{2,1,0:T(8,128)(2,1)}, bf16[8,256,2048]{2,1,0:T(8,128)(2,1)}, bf16[8,256,2048]{2,1,0:T(8,128)(2,1)}, bf16[8,256,768]{2,1,0:T(8...) custom-call(bf16[256,2048]{1,0:T(8,128)(2,1)} %bitcast.119, ...), custom_call_target="tpu_custom_call" | custom-call | flops 15032385536 | bytes 268435456 | tf_op jit(solution)/shard_map/pallas_call | solution.py:598
  112.9 20.7 %shard_map.315 = (bf16[2048,256]{1,0:T(8,128)(2,1)}, f32[2,2048,1]{2,1,0:T(8,128)}) custom-call(s32[8]{0:T(128)} %bitcast.106, bf16[2048,768]{1,0:T(8,128)(2,1)} %bitcast.67, bf16[2048,768]{1,0:T(8,128)(2,1)} %bitcast.68, bf16[2048,768]{1,0:T(8,128)(2,1)} %bitcast.69), custom_call_target="tpu_custom_call" | custom-call | tf_op jit(solution)/shard_map/pallas_call | solution.py:452
  134.3 109.5 %shard_map.316 = (bf16[256,2048]{1,0:T(8,128)(2,1)}, bf16[256,2048]{1,0:T(8,128)(2,1)}, f32[256,2048]{1,0:T(8,128)}, f32[256,1]{1,0:T(8,128)}) custom-call(bf16[256,2048]{1,0:T(8,128)(2,1)} %bitcast.120, bf16[8,256,256]{2,1,0:T(8,128)(2,1)} %bitcast.78, bf16[8,256,1024]{2,1,0:T(8,128)(2,1)} %get-tuple-element.59.refs_2_, bf16[256,2048]{1,0:T(8,128)(2,1)} %bitcast.117, ...), custom_call_target="tpu_custom_call" | custom-call | flops 10737418240 | bytes 268435456 | tf_op jit(solution)/shard_map/pallas_call | solution.py:598
  243.8 100.7 %shard_map.317 = (bf16[8,256,2048]{2,1,0:T(8,128)(2,1)}, bf16[8,256,3328]{2,1,0:T(8,128)(2,1)}, f32[8,2048]{1,0:T(8,128)}) custom-call(bf16[256,2048]{1,0:T(8,128)(2,1)} %get-tuple-element.60.refs_0_, bf16[2048,3328]{1,0:T(8,128)(2,1)} %refs_2_.2, s32[2048,1]{1,0:T(8,128)} %copy.36.refs_2_), custom_call_target="tpu_custom_call" | custom-call | flops 27917287424 | bytes 268435456 | tf_op jit(solution)/shard_map/pallas_call | solution.py:598
  344.6 24.4 %shard_map.318 = (f32[8,2048]{1,0:T(8,128)}, f32[8,128]{1,0:T(8,128)}) custom-call(f32[8,2048]{1,0:T(8,128)} %get-tuple-element.61.stats_ref, s32[8]{0:T(128)} %bitcast.107, s32[8]{0:T(128)} %bitcast.112, f32[8]{0:T(128)} %bitcast.113), custom_call_target="tpu_custom_call" | custom-call | tf_op jit(solution)/shard_map/pallas_call | solution.py:1358
  369.9 14.7 %fusion.1 = bf16[2048,3328]{1,0:T(8,128)(2,1)} fusion(bf16[8,256,3328]{2,1,0:T(8,128)(2,1)} %get-tuple-element.68, f32[2048]{0:T(1024)S(1)} %bitcast.88, f32[2048]{0:T(1024)S(1)} %bitcast.87, s32[3328]{0:T(1024)S(1)} %iota_add_fusion, s32[2048]{0:T(1024)S(1)} %bitcast.86), kind=kLoop, calls=%fused_computation.2 | loop fusion | flops 40894464 | bytes 27300864 | tf_op jit(solution)/shard_map/convert_element_type | solution.py:1647
  384.5 21.8 %convolution_convert_fusion = bf16[1024,3328]{1,0:T(8,128)(2,1)} fusion(bf16[2048,3328]{1,0:T(8,128)(2,1)} %fusion.1, bf16[2048,2048]{1,0:T(8,128)(2,1)} %bitcast.128, s32[]{:T(128)S(6)} %select_n.10), kind=kOutput, calls=%fused_computation.4 | convolution fusion | flops 13962051584 | bytes 24641540 | tf_op jit(solution)/shard_map/dot_general | solution.py:370
  406.4 20.6 %fusion.9 = f32[1024,3328]{1,0:T(8,128)S(1)} fusion(bf16[2048,3328]{1,0:T(8,128)(2,1)} %fusion.1, bf16[2048,2048]{1,0:T(8,128)(2,1)} %bitcast.129, s32[]{:T(128)S(6)} %select_n.8), kind=kOutput, calls=%fused_computation.14 | convolution fusion | flops 13958643712 | bytes 31457284 | tf_op jit(solution)/shard_map/dot_general | solution.py:370
  427.0 7.7 add_convert_fusion.refs_0_
  434.7 2.5 collective-permute-start.5
  437.2 97.9 %shard_map.319 = (f32[256,2048]{1,0:T(8,128)}, bf16[256,2048]{1,0:T(8,128)(2,1)}, f32[8,2048]{1,0:T(8,128)}) custom-call(bf16[1024,3328]{1,0:T(8,128)(2,1)} %add_convert_fusion.refs_0_, bf16[8,256,3328]{2,1,0:T(8,128)(2,1)} %bitcast.73, bf16[2048,3328]{1,0:T(8,128)(2,1)} %refs_2_.2, f32[256,2048]{1,0:T(8,128)} %get-tuple-element.69.refs_3_, ...), custom_call_target="tpu_custom_call" | custom-call | flops 27917287424 | bytes 268435456 | tf_op jit(solution)/shard_map/pallas_call | solution.py:598
  535.1 91.9 %shard_map.320 = (bf16[8,256,2048]{2,1,0:T(8,128)(2,1)}, bf16[8,256,256]{2,1,0:T(8,128)(2,1)}, bf16[8,256,1024]{2,1,0:T(8,128)(2,1)}, f32[8,1024]{1,0:T(8,128)}) custom-call(bf16[256,2048]{1,0:T(8,128)(2,1)} %get-tuple-element.71.refs_0_, bf16[256,2048]{1,0:T(8,128)(2,1)} %bitcast.118, bf16[1024,2048]{1,0:T(8,128)(2,1)} %refs_2_.3, ...), custom_call_target="tpu_custom_call" | custom-call | flops 10737418240 | bytes 268435456 | tf_op jit(solution)/shard_map/pallas_call | solution.py:598
  627.1 8.2 fusion.24
  635.4 5.8 fusion.21
  641.1 6.2 fusion.17
  651.4 4.6 fusion.6
  657.0 2.1 add_convert_fusion.1.rest_2_.refs_2_
  659.1 9.9 %shard_map.322.refs_1_.refs_0_ = bf16[1024,3328]{1,0:T(8,128)(2,1)} custom-call(bf16[1024,3328]{1,0:T(8,128)(2,1)} %add_convert_fusion.refs_0_, bf16[1024,3328]{1,0:T(8,128)(2,1)} %collective-permute-done.5.refs_1_.refs_2_, bf16[1024,3328]{1,0:T(8,128)(2,1)} %collective-permute-done.5.refs_1_.refs_2_), custom_call_target="tpu_custom_call" | custom-call | tf_op jit(solution)/shard_map/pallas_call | solution.py:1497
  669.1 5.0 add_convert_fusion.2.rest_1_.refs_1_
  674.1 31.2 %shard_map.321 = (bf16[2048,768]{1,0:T(8,128)(2,1)}, f32[2,1,384]{2,1,0:T(1,128)}) custom-call(s32[8]{0:T(128)} %bitcast.108, bf16[2048,768]{1,0:T(8,128)(2,1)} %bitcast.70, bf16[2048,768]{1,0:T(8,128)(2,1)} %bitcast.71, bf16[2048,768]{1,0:T(8,128)(2,1)} %bitcast.72, bf16[2048,256]{1,0:T(8,128)(2,1)} %get-tuple-element.58.ctx_ref, ...), custom_call_target="tpu_custom_call" | custom-call | tf_op jit(solution)/shard_map/pallas_call | solution.py:534
  705.4 6.8 fusion.27
  712.2 4.7 collective-permute-start.4
  720.4 5.3 fusion.11
  726.2 1.9 collective-permute-start.9
  728.8 141.5 %shard_map.323 = (f32[256,2048]{1,0:T(8,128)}, f32[8,2048]{1,0:T(8,128)}, f32[8,2048]{1,0:T(8,128)}) custom-call(bf16[1024,768]{1,0:T(8,128)(2,1)} %copy-done, bf16[1024,3328]{1,0:T(8,128)(2,1)} %shard_map.322.refs_1_.refs_0_, bf16[256,2048]{1,0:T(8,128)(2,1)} %bitcast.121, f32[256,2048]{1,0:T(8,128)} %get-tuple-element.81.refs_3_, ...), custom_call_target="tpu_custom_call" | custom-call | flops 15032385536 | bytes 268435456 | tf_op jit(solution)/shard_map/pallas_call | solution.py:598
  870.4 9.1 shard_map.324
  884.6 18.1 %shard_map.325.refs_8_ = f32[2048,3328]{1,0:T(8,128)} custom-call(s32[1]{0:T(128)} %bitcast.36.core_ref, bf16[1024,3328]{1,0:T(8,128)(2,1)} %shard_map.322.refs_1_.refs_0_, bf16[1024,3328]{1,0:T(8,128)(2,1)} %collective-permute-done.14.refs_1_), custom_call_target="tpu_custom_call" | custom-call | tf_op jit(solution)/shard_map/pallas_call | solution.py:1546
  903.9 17.7 %shard_map.326 = (f32[256,2048]{1,0:T(8,128)}, f32[1024,2048]{1,0:T(8,128)}, f32[2048,1024]{1,0:T(8,128)}, f32[2048,2,384]{2,1,0:T(2,128)}) custom-call(s32[1]{0:T(128)} %bitcast.36.core_ref, bf16[256,1024]{1,0:T(8,128)(2,1)} %get-tuple-element.88.refs_0_, bf16[1024,1024]{1,0:T(8,128)(2,1)} %get-tuple-element.89.refs_1_, ...), custom_call_target="tpu_custom_call" | custom-call | tf_op jit(solution)/shard_map/pallas_call | solution.py:1546
  921.6 2.3 copy.45
  923.9 3.1 copy.46
  (102 shorter events, 26.2 us)
Async XLA Ops:
  4.5 10.4 %copy-start.4 = (f32[2048]{0:T(1024)}, f32[2048]{0:T(1024)S(1)}, u32[]{:S(2)}) copy-start(f32[2048]{0:T(1024)S(1)} %broadcast_in_dim.104) | copy-start | bytes 24580
  5.9 9.7 %copy-start.6 = (f32[2048]{0:T(1024)}, f32[2048]{0:T(1024)S(1)}, u32[]{:S(2)}) copy-start(f32[2048]{0:T(1024)S(1)} %broadcast_in_dim.106) | copy-start | bytes 24580
  8.0 125.7 %copy-start.9 = (f32[2048]{0:T(1024)}, f32[2048]{0:T(1024)S(1)}, u32[]{:S(2)}) copy-start(f32[2048]{0:T(1024)S(1)} %broadcast_in_dim.109) | copy-start | bytes 24580
  243.8 126.1 %copy-start.8 = (s32[1,2048]{1,0:T(1,128)S(1)}, s32[1,2048]{1,0:T(1,128)}, u32[]{:S(2)}) copy-start(s32[1,2048]{1,0:T(1,128)} %param.20) | copy-start | bytes 24580
  406.3 20.7 %collective-permute-start = (bf16[1024,3328]{1,0:T(8,128)(2,1)}, bf16[1024,3328]{1,0:T(8,128)(2,1)}, u32[]{:S(2)}, u32[]{:S(2)}) collective-permute-start(bf16[1024,3328]{1,0:T(8,128)(2,1)} %convolution_convert_fusion), channel_id=1, source_target_pairs={{0,8},{8,0},{16,24},{24,16},{1,9},{9,1},{17,25},{25,17},{2,10},{10... | collective-permute-start | bytes 20447240 | tf_op jit(solution)/shard_map/ppermute | solution.py:1581
  434.7 224.5 %collective-permute-start.5 = (bf16[1024,3328]{1,0:T(8,128)(2,1)}, bf16[1024,3328]{1,0:T(8,128)(2,1)}, u32[]{:S(2)}, u32[]{:S(2)}) collective-permute-start(bf16[1024,3328]{1,0:T(8,128)(2,1)} %add_convert_fusion.refs_0_), channel_id=1, source_target_pairs={{0,16},{16,0},{8,24},{24,8},{1,17},{17,1},{9,25},{25,9},{2,18},{18... | collective-permute-start | bytes 20447240 | tf_op jit(solution)/shard_map/ppermute | solution.py:1586
  627.0 8.3 copy-start.13
  627.0 8.3 copy-start.15
  635.3 21.7 %collective-permute-start.3 = (bf16[1024,1024]{1,0:T(8,128)(2,1)S(1)}, bf16[1024,1024]{1,0:T(8,128)(2,1)S(1)}, u32[]{:S(2)}, u32[]{:S(2)}) collective-permute-start(bf16[1024,1024]{1,0:T(8,128)(2,1)S(1)} %fusion.24), channel_id=1, source_target_pairs={{0,8},{8,0},{16,24},{24,16},{1,9},{9,1},{17,25},{25,17},{2,10},{10... | collective-permute-start | bytes 6291464 | tf_op jit(solution)/shard_map/ppermute | solution.py:1581
  635.4 15.2 %slice-start = ((s8[8388608]{0:T(1024)(128)(4,1)}), s8[4194304]{0:T(1024)(128)(4,1)S(1)}, s32[]{:S(2)}) async-start(s8[8388608]{0:T(1024)(128)(4,1)} %bitcast.125), calls=%async_computation | async-start | bytes 8388608
  641.1 6.8 copy-start.2
  641.1 9.5 %slice-start.1 = ((s8[8388608]{0:T(1024)(128)(4,1)}), s8[4194304]{0:T(1024)(128)(4,1)S(1)}, s32[]{:S(2)}) async-start(s8[8388608]{0:T(1024)(128)(4,1)} %bitcast.125), calls=%async_computation.1 | async-start | bytes 8388608
  647.4 21.7 %collective-permute-start.2 = (bf16[1024,1024]{1,0:T(8,128)(2,1)}, bf16[1024,1024]{1,0:T(8,128)(2,1)}, u32[]{:S(2)}, u32[]{:S(2)}) collective-permute-start(bf16[1024,1024]{1,0:T(8,128)(2,1)} %fusion.21), channel_id=1, source_target_pairs={{0,8},{8,0},{16,24},{24,16},{1,9},{9,1},{17,25},{25,17},{2,10},{10... | collective-permute-start | bytes 6291464 | tf_op jit(solution)/shard_map/ppermute | solution.py:1581
  649.2 2.2 copy-start.14
  649.2 6.8 collective-permute-start.1
  669.0 215.5 %collective-permute-start.14 = (bf16[1024,3328]{1,0:T(8,128)(2,1)}, bf16[1024,3328]{1,0:T(8,128)(2,1)}, u32[]{:S(2)}, u32[]{:S(2)}) collective-permute-start(bf16[1024,3328]{1,0:T(8,128)(2,1)} %shard_map.322.refs_1_.refs_0_), channel_id=1, source_target_pairs={{0,8},{8,0},{16,24},{24,16},{1,9},{9,1},{17,25},{25,17},{2,10},{10... | collective-permute-start | bytes 20447240 | tf_op jit(solution)/shard_map/ppermute | solution.py:1605
  705.3 11.5 %copy-start.5 = (f32[2048]{0:T(1024)S(1)}, f32[2048]{0:T(1024)}, u32[]{:S(2)}) copy-start(f32[2048]{0:T(1024)} %copy-done.4) | copy-start | bytes 24580
  705.3 11.5 %copy-start.7 = (f32[2048]{0:T(1024)S(1)}, f32[2048]{0:T(1024)}, u32[]{:S(2)}) copy-start(f32[2048]{0:T(1024)} %copy-done.6) | copy-start | bytes 24580
  705.3 15.1 %copy-start.11 = (f32[2,1,384]{2,1,0:T(1,128)S(1)}, f32[2,1,384]{2,1,0:T(1,128)}, u32[]{:S(2)}) copy-start(f32[2,1,384]{2,1,0:T(1,128)} %get-tuple-element.84) | copy-start | bytes 9220
  705.3 15.1 %copy-start.12 = (bf16[2048,768]{1,0:T(8,128)(2,1)S(1)}, bf16[2048,768]{1,0:T(8,128)(2,1)}, u32[]{:S(2)}) copy-start(bf16[2048,768]{1,0:T(8,128)(2,1)} %get-tuple-element.80) | copy-start | bytes 9437188
  712.2 13.6 %collective-permute-start.4 = (bf16[1024,768]{1,0:T(8,128)(2,1)S(1)}, bf16[1024,768]{1,0:T(8,128)(2,1)S(1)}, u32[]{:S(2)}, u32[]{:S(2)}) collective-permute-start(bf16[1024,768]{1,0:T(8,128)(2,1)S(1)} %fusion.27), channel_id=1, source_target_pairs={{0,8},{8,0},{16,24},{24,16},{1,9},{9,1},{17,25},{25,17},{2,10},{10... | collective-permute-start | bytes 4718600 | tf_op jit(solution)/shard_map/ppermute | solution.py:1581
  718.2 152.1 %collective-permute-start.6 = (bf16[256,1024]{1,0:T(8,128)(2,1)}, bf16[256,1024]{1,0:T(8,128)(2,1)}, u32[]{:S(2)}, u32[]{:S(2)}) collective-permute-start(bf16[256,1024]{1,0:T(8,128)(2,1)} %add_convert_fusion.4.rest_0_.refs_0_), channel_id=1, source_target_pairs={{0,16},{16,0},{8,24},{24,8},{1,17},{17,1},{9,25},{25,9},{2,18},{18... | collective-permute-start | bytes 1572872 | tf_op jit(solution)/shard_map/ppermute | solution.py:1586
  718.4 152.0 %collective-permute-start.8 = (bf16[1024,1024]{1,0:T(8,128)(2,1)}, bf16[1024,1024]{1,0:T(8,128)(2,1)}, u32[]{:S(2)}, u32[]{:S(2)}) collective-permute-start(bf16[1024,1024]{1,0:T(8,128)(2,1)} %add_convert_fusion.1.rest_2_.refs_2_), channel_id=1, source_target_pairs={{0,16},{16,0},{8,24},{24,8},{1,17},{17,1},{9,25},{25,9},{2,18},{18... | collective-permute-start | bytes 6291464 | tf_op jit(solution)/shard_map/ppermute | solution.py:1586
  720.3 150.1 %collective-permute-start.7 = (bf16[1024,1024]{1,0:T(8,128)(2,1)}, bf16[1024,1024]{1,0:T(8,128)(2,1)}, u32[]{:S(2)}, u32[]{:S(2)}) collective-permute-start(bf16[1024,1024]{1,0:T(8,128)(2,1)} %add_convert_fusion.2.rest_1_.refs_1_), channel_id=1, source_target_pairs={{0,16},{16,0},{8,24},{24,8},{1,17},{17,1},{9,25},{25,9},{2,18},{18... | collective-permute-start | bytes 6291464 | tf_op jit(solution)/shard_map/ppermute | solution.py:1586
  726.2 2.6 copy-start
  726.2 144.2 %collective-permute-start.9 = (bf16[1024,768]{1,0:T(8,128)(2,1)S(1)}, bf16[1024,768]{1,0:T(8,128)(2,1)}, u32[]{:S(2)}, u32[]{:S(2)}) collective-permute-start(bf16[1024,768]{1,0:T(8,128)(2,1)S(1)} %add_convert_fusion.3.refs_0_.refs_3_), channel_id=1, source_target_pairs={{0,16},{16,0},{8,24},{24,8},{1,17},{17,1},{9,25},{25,9},{2,18},{18... | collective-permute-start | bytes 4718600 | tf_op jit(solution)/shard_map/ppermute | solution.py:1586
  870.4 9.8 %copy-start.10 = (f32[8,128]{1,0:T(8,128)S(1)}, f32[8,128]{1,0:T(8,128)}, u32[]{:S(2)}) copy-start(f32[8,128]{1,0:T(8,128)} %get-tuple-element.62) | copy-start | bytes 12292
  870.4 13.5 %copy-start.3 = (f32[8,2048]{1,0:T(8,128)S(1)}, f32[8,2048]{1,0:T(8,128)}, u32[]{:S(2)}) copy-start(f32[8,2048]{1,0:T(8,128)} %get-tuple-element.87.refs_8_) | copy-start | bytes 196612
  879.5 23.2 %collective-permute-start.11 = (bf16[1024,1024]{1,0:T(8,128)(2,1)}, bf16[1024,1024]{1,0:T(8,128)(2,1)}, u32[]{:S(2)}, u32[]{:S(2)}) collective-permute-start(bf16[1024,1024]{1,0:T(8,128)(2,1)} %get-tuple-element.89.refs_1_), channel_id=1, source_target_pairs={{0,8},{8,0},{16,24},{24,16},{1,9},{9,1},{17,25},{25,17},{2,10},{10... | collective-permute-start | bytes 6291464 | tf_op jit(solution)/shard_map/ppermute | solution.py:1605
  879.6 23.2 %collective-permute-start.12 = (bf16[1024,1024]{1,0:T(8,128)(2,1)}, bf16[1024,1024]{1,0:T(8,128)(2,1)}, u32[]{:S(2)}, u32[]{:S(2)}) collective-permute-start(bf16[1024,1024]{1,0:T(8,128)(2,1)} %get-tuple-element.90.refs_2_), channel_id=1, source_target_pairs={{0,8},{8,0},{16,24},{24,16},{1,9},{9,1},{17,25},{25,17},{2,10},{10... | collective-permute-start | bytes 6291464 | tf_op jit(solution)/shard_map/ppermute | solution.py:1605
  880.1 22.6 %collective-permute-start.13 = (bf16[1024,768]{1,0:T(8,128)(2,1)}, bf16[1024,768]{1,0:T(8,128)(2,1)S(1)}, u32[]{:S(2)}, u32[]{:S(2)}) collective-permute-start(bf16[1024,768]{1,0:T(8,128)(2,1)} %get-tuple-element.91.refs_3_), channel_id=1, source_target_pairs={{0,8},{8,0},{16,24},{24,16},{1,9},{9,1},{17,25},{25,17},{2,10},{10... | collective-permute-start | bytes 4718600 | tf_op jit(solution)/shard_map/ppermute | solution.py:1605
  882.2 20.6 %collective-permute-start.10 = (bf16[256,1024]{1,0:T(8,128)(2,1)}, bf16[256,1024]{1,0:T(8,128)(2,1)}, u32[]{:S(2)}, u32[]{:S(2)}) collective-permute-start(bf16[256,1024]{1,0:T(8,128)(2,1)} %get-tuple-element.88.refs_0_), channel_id=1, source_target_pairs={{0,8},{8,0},{16,24},{24,16},{1,9},{9,1},{17,25},{25,17},{2,10},{10... | collective-permute-start | bytes 1572872 | tf_op jit(solution)/shard_map/ppermute | solution.py:1605
  (1 other events, 1.1 us)

commit v7 on v6

--- a/solution.py
+++ b/solution.py
@@ -57,10 +57,10 @@
                 found.append((m < n - 1, self.device(axis, m + 1)))
         return found
 
-    def barrier(self):
+    def barrier(self, *others):
         sem = pltpu.get_barrier_semaphore()
         amount = jnp.int32(0)
-        for there, device in self.neighbours():
+        for there, device in self.neighbours() + [(None, device) for device in others]:
             def tell(device=device):
                 pl.semaphore_signal(sem, inc=1, device_id=device, device_id_type=MESH)
             if there is None:
@@ -276,9 +276,9 @@
             self.take(kind, stage, axis, other, m, jnp.bool_(True), half, m > 0, index)
             self.take(kind, stage, axis, other, m, jnp.bool_(False), half, m < n - 1, index)
 
-    def run(self, produce, made=lambda: None, between=lambda: None, late=lambda: None):
+    def run(self, produce, made=lambda: None, between=lambda: None, late=lambda: None, fill=lambda: None):
         grid, n, me = self.grid, self.grid.n, self.grid.me
-        lagging = []
+        lagging, filling = [], []
 
         def chain(k, half, begins):
             slow = grid.nearest(0, k)
@@ -314,12 +314,18 @@
             elif step[0] == "made":
                 catch_up()
                 made()
+                filling.append(fill)
             elif step[0] == "first" and self.cut[0]:
+                for more in filling:
+                    more()
                 for half in range(self.halves):
                     chain(step[1], half, True)
             elif self.cut[0]:
+                for more in filling:
+                    more()
                 chain(step[1], step[2], False)
         between()
+        fill()
         if self.cut[1]:
             for half in range(self.halves):
                 for l in reversed(range(n[1])):
@@ -330,6 +336,7 @@
         late()
         if self.cut[0]:
             for half in range(self.halves):
+                fill()
                 self.last(0, 0, 1, me[0], half, me[0], me[1])
         for half in range(self.halves):
             if self.cut[1]:
@@ -601,7 +608,7 @@
             in_specs=[ANY] * len(before) + in_specs,
             out_specs=out_specs,
             scratch_shapes=scratch,
-            cost_estimate=pl.CostEstimate(flops=cost, bytes_accessed=2**28, transcendentals=0),
+            cost_estimate=pl.CostEstimate(flops=cost, bytes_accessed=2**28 if cost > 1 else 1, transcendentals=0),
             compiler_params=pltpu.CompilerParams(
                 collective_id=collective, has_side_effects=True, vmem_limit_bytes=VMEM_LIMIT
             ),
@@ -1152,44 +1159,27 @@
 
 
 class SmallSum:
-    def __init__(self, shards, replicas, sums, bias, total, bias_total, scratch):
-        self.shards, self.replicas = shards, replicas
-        self.sums, self.bias, self.total, self.bias_total = sums, bias, total, bias_total
-        (
-            self.came, self.block, self.blocks, self.biases, self.spread_send, self.spread_recv, self.cross_send,
-            self.cross_recv, self.back_send, self.back_recv,
-        ) = scratch
-        self.seq, self.dp = lax.axis_index("seq"), lax.axis_index("dp")
+    def __init__(self, shards, sums, total, scratch):
+        self.shards, self.sums, self.total = shards, sums, total
+        self.came, self.spread_send, self.spread_recv, self.back_send, self.back_recv = scratch
+        self.here = lax.axis_index("seq")
         self.width = D // shards
+        self.others = [(step, lax.rem(self.here + step, shards)) for step in range(1, shards)]
 
     @staticmethod
-    def scratch(shards, replicas):
-        width = D // shards
+    def scratch(shards):
         dma = pltpu.SemaphoreType.DMA
-        return [
-            pltpu.VMEM((shards, 8, width), jnp.float32),
-            pltpu.VMEM((8, width), jnp.float32),
-            pltpu.VMEM((replicas, 8, width), jnp.float32),
-            pltpu.VMEM((replicas, 8, D), jnp.float32),
-            dma((shards,)), dma((shards,)), dma((2, replicas)), dma((2, replicas)), dma((shards,)), dma((shards,)),
-        ]
-
-    def others(self, axis):
-        count, here = (self.shards, self.seq) if axis == "seq" else (self.replicas, self.dp)
-        return [(step, lax.rem(here + step, count)) for step in range(1, count)]
+        return [pltpu.VMEM((shards, 8, D // shards), jnp.float32)] + [dma((shards,))] * 4
 
     def barrier(self):
         sem = pltpu.get_barrier_semaphore()
-        amount = 0
-        for axis in ("seq", "dp"):
-            for _, place in self.others(axis):
-                pl.semaphore_signal(sem, inc=1, device_id={axis: place}, device_id_type=MESH)
-                amount += 1
-        pl.semaphore_wait(sem, amount)
-
-    def copy(self, axis, place, src, dst, send, recv):
+        for _, place in self.others:
+            pl.semaphore_signal(sem, inc=1, device_id={"seq": place}, device_id_type=MESH)
+        pl.semaphore_wait(sem, self.shards - 1)
+
+    def copy(self, place, src, dst, send, recv):
         return pltpu.make_async_remote_copy(
-            src_ref=src, dst_ref=dst, send_sem=send, recv_sem=recv, device_id={axis: place}, device_id_type=MESH
+            src_ref=src, dst_ref=dst, send_sem=send, recv_sem=recv, device_id={"seq": place}, device_id_type=MESH
         )
 
     def columns(self, place):
@@ -1198,64 +1188,36 @@
     def spread(self):
         self.first = [
             self.copy(
-                "seq", place, self.sums.at[:, self.columns(place)], self.came.at[step], self.spread_send.at[step],
+                place, self.sums.at[:, self.columns(place)], self.came.at[step], self.spread_send.at[step],
                 self.spread_recv.at[step],
             )
-            for step, place in self.others("seq")
+            for step, place in self.others
         ]
+        for copy in self.first:
+            copy.start()
+
+    def collect(self):
+        here = self.columns(self.here)
+        total = self.sums[:, here]
+        for (step, _), copy in zip(self.others, self.first):
+            copy.wait_recv()
+            total = total + self.came[step]
+        self.total[:, here] = total
         self.second = [
             self.copy(
-                "dp", place, self.bias, self.biases.at[self.dp], self.cross_send.at[1, step],
-                self.cross_recv.at[1, step],
+                place, self.total.at[:, here], self.total.at[:, here], self.back_send.at[step], self.back_recv.at[step]
             )
-            for step, place in self.others("dp")
+            for step, place in self.others
         ]
+        for copy in self.second:
+            copy.start()
+
+    def finish(self):
+        for step, _ in self.others:
+            source = lax.rem(self.here + self.shards - step, self.shards)
+            there = self.total.at[:, self.columns(source)]
+            self.copy(source, there, there, self.back_send.at[step], self.back_recv.at[step]).wait_recv()
         for copy in self.first + self.second:
-            copy.start()
-
-    def cross(self):
-        total = self.sums[:, self.columns(self.seq)]
-        for (step, _), copy in zip(self.others("seq"), self.first):
-            copy.wait_recv()
-            total = total + self.came[step]
-        self.block[...] = total
-        self.blocks[self.dp] = total
-        self.third = [
-            self.copy(
-                "dp", place, self.block, self.blocks.at[self.dp], self.cross_send.at[0, step],
-                self.cross_recv.at[0, step],
-            )
-            for step, place in self.others("dp")
-        ]
-        for copy in self.third:
-            copy.start()
-
-    def collect(self):
-        for copy in self.third + self.second:
-            copy.wait_recv()
-        self.biases[self.dp] = self.bias[...]
-        total, bias = self.blocks[0], self.biases[0]
-        for place in range(1, self.replicas):
-            total, bias = total + self.blocks[place], bias + self.biases[place]
-        self.bias_total[...] = bias
-        here = self.columns(self.seq)
-        self.total[:, here] = total
-        self.fourth = [
-            self.copy(
-                "seq", place, self.total.at[:, here], self.total.at[:, here], self.back_send.at[step],
-                self.back_recv.at[step],
-            )
-            for step, place in self.others("seq")
-        ]
-        for copy in self.fourth:
-            copy.start()
-
-    def finish(self):
-        for (step, _), copy in zip(self.others("seq"), self.fourth):
-            source = lax.rem(self.seq + self.shards - step, self.shards)
-            there = self.total.at[:, self.columns(source)]
-            self.copy("seq", source, there, there, self.back_send.at[step], self.back_recv.at[step]).wait_recv()
-        for copy in self.first + self.second + self.third + self.fourth:
             copy.wait_send()
 
 
@@ -1375,20 +1337,20 @@
 
 
 def input_grad_rows(
-    own, grad_stream, plain, grad_qkv, grad_up, qkv_flat, up_weight, gains, end_sums, biases, sizes, replicas,
-    collective, before,
+    own, grad_stream, plain, grad_qkv, grad_up, qkv_flat, up_weight, gains, end_sums, sizes, collective,
+    before,
 ):
     shards, rows, width = grad_qkv.shape
     hidden = grad_up.shape[2]
 
     def kernel(
         own_ref, stream_ref, normed_any, qkv_any, up_any, qkvw_any, upw_any, gains_ref, end_ref,
-        bias_ref, out_ref, total_ref, bias_total_ref,
+        out_ref, total_ref,
         qkvw, upw, weight_sems, normed, qkv, up, load_sems, sums_ref, *scratch,
     ):
         grid = Grid2(sizes)
-        small = SmallSum(shards, replicas, sums_ref, bias_ref, total_ref, bias_total_ref, scratch[:10])
-        scratch = scratch[10:]
+        small = SmallSum(shards, sums_ref, total_ref, scratch[:5])
+        scratch = scratch[5:]
         parts = scratch[0]
         order = production_order(grid)
 
@@ -1444,7 +1406,7 @@
             sums_ref[4:8] = end_ref[0:4]
             small.spread()
 
-        run_scatter(grid, sizes, rows, scratch, produce, made, small.cross, small.collect)
+        run_scatter(grid, sizes, rows, scratch, produce, made, lambda: None, small.collect)
         mine = grid.index(*grid.me)
 
         def norm_tile(index, _):
@@ -1464,9 +1426,9 @@
 
     return row_kernel(
         kernel, collective,
-        [jax.ShapeDtypeStruct((rows, D), jnp.float32), jax.ShapeDtypeStruct((8, D), jnp.float32), jax.ShapeDtypeStruct((8, D), jnp.float32)],
-        [VMEM, VMEM, ANY, ANY, ANY, ANY, ANY, VMEM, VMEM, VMEM],
-        [VMEM, VMEM, VMEM],
+        [jax.ShapeDtypeStruct((rows, D), jnp.float32), jax.ShapeDtypeStruct((8, D), jnp.float32)],
+        [VMEM, VMEM, ANY, ANY, ANY, ANY, ANY, VMEM, VMEM],
+        [VMEM, VMEM],
         [
             pltpu.VMEM(qkv_flat.shape, jnp.bfloat16),
             pltpu.VMEM(up_weight.shape, jnp.bfloat16),
@@ -1477,11 +1439,11 @@
             pltpu.SemaphoreType.DMA((shards, 3)),
             pltpu.VMEM((8, D), jnp.float32),
         ]
-        + SmallSum.scratch(shards, replicas)
+        + SmallSum.scratch(shards)
         + sum_scratch(sizes, rows),
-        2 * BLOCK * D * (width + hidden),
+        1,
         before,
-    )(own, grad_stream, plain, grad_qkv, grad_up, qkv_flat, up_weight, gains, end_sums, biases)
+    )(own, grad_stream, plain, grad_qkv, grad_up, qkv_flat, up_weight, gains, end_sums)
 
 
 def join_halves(sums, others, earlier):
@@ -1557,10 +1519,6 @@
     return vector.astype(jnp.float32)[None, :]
 
 
-PAIR = [(0, 1), (1, 0), (2, 3), (3, 2)]
-CROSS = [(0, 2), (2, 0), (1, 3), (3, 1)]
-
-
 def held(values):
     return lax.optimization_barrier(values)
 
@@ -1570,25 +1528,44 @@
     return lax.dynamic_slice_in_dim(values, which * half, half, 1)
 
 
+def pairs(step):
+    return [(place, place ^ step) for place in range(lax.axis_size("dp"))]
+
+
 class PairSum:
-    def __init__(self, product):
+    def __init__(self, product=None, made=None):
         self.plain = lax.axis_size("dp") != 4
+        self.core = lax.rem(lax.axis_index("dp"), 2)
+        if made is None:
+            away = product(1 - self.core).astype(jnp.bfloat16)
+            came = lax.ppermute(away, "dp", pairs(1))
+            mine = held(product(self.core))
+            made = (mine + came.astype(jnp.float32)).astype(jnp.bfloat16)
+        self.sum = made
+
+    def cross(self):
         if self.plain:
-            self.sum = jnp.stack([product(0), product(1)]).astype(jnp.bfloat16)
-            return
-        self.core = lax.rem(lax.axis_index("dp"), 2)
-        away = product(1 - self.core).astype(jnp.bfloat16)
-        came = lax.ppermute(away, "dp", PAIR)
-        mine = held(product(self.core))
-        self.sum = (mine + came.astype(jnp.float32)).astype(jnp.bfloat16)
-
-    def cross(self):
-        self.other = lax.psum(self.sum, "dp") if self.plain else lax.ppermute(self.sum, "dp", CROSS)
+            none = jnp.zeros_like(self.sum)
+            both = jnp.stack([jnp.where(self.core == which, self.sum, none) for which in (0, 1)])
+            self.other = lax.psum(both, "dp")
+        else:
+            self.other = lax.ppermute(self.sum, "dp", pairs(2))
         return self
 
     def join(self):
-        self.total = self.other if self.plain else join_halves([self.sum], [self.other], self.other)[0]
+        if self.plain:
+            self.total = self.other
+        else:
+            self.total = (self.sum.astype(jnp.float32) + self.other.astype(jnp.float32)).astype(jnp.bfloat16)
         return self
+
+
+def sum_over_dp(values):
+    if lax.axis_size("dp") != 4:
+        return lax.psum(values, "dp")
+    for step in (1, 2):
+        values = values + lax.ppermute(values, "dp", pairs(step))
+    return values
 
 
 def join_all(sums, earlier):
@@ -1602,7 +1579,7 @@
     if sums[0].plain:
         core = jnp.zeros((1,), jnp.int32)
         return settle_halves(core, [s.other[0] for s in sums], [s.other[1] for s in sums], shapes, before)
-    backs = [lax.ppermute(one.total, "dp", PAIR) for one in sums]
+    backs = [lax.ppermute(one.total, "dp", pairs(1)) for one in sums]
     return settle_halves(sums[0].core[None], [one.total for one in sums], backs, shapes, before)
 
 
@@ -1635,7 +1612,8 @@
     output, final, normed, inverse = branch_rows(
         own, ctx.reshape(shards, rows, inner), act, out_flat, down_weight, end_norms, sizes, 1
     )
-    final_full, weights, stats = logit_rows(final, head_weight, targets[0][:, None], sizes, 2)
+    targets_col = targets[0][:, None]
+    final_full, weights, stats = logit_rows(final, head_weight, targets_col, sizes, 2)
 
     coef, losses = score_rows(
         stats, block_lengths, labels[0], ref_logps[0], sizes, lax.axis_size("dp"), 6
@@ -1678,16 +1656,17 @@
     qv_grad = jnp.concatenate([qkv_sums[:, :HEAD_DIM], qkv_sums[:, 2 * HEAD_DIM :]], axis=-1)
     split = local_heads * 2 * HEAD_DIM
     biases = jnp.concatenate([qv_grad.reshape(-1), up_sums[0]])
-    biases = jnp.pad(biases[None, :], ((0, 7), (0, D - biases.shape[0])))
+    biases = jnp.pad(biases[None, :], ((0, 0), (0, D - biases.shape[0])))
     gains = jnp.concatenate([row_of(ln1_gain), row_of(ln2_gain)], axis=0)
-    grad_input, small, biases = input_grad_rows(
+    grad_input, group_sums = input_grad_rows(
         own, grad_stream, plain, grad_qkv.reshape(shards, rows, width), grad_up, qkv_flat, up_weight, gains,
-        end_sums, biases, sizes, lax.axis_size("dp"), 5, (sums[-1].sum, head_sum.join().total),
+        end_sums, sizes, 5, (sums[-1].sum, head_sum.join().total),
     )
-    join_all(sums, small)
-    (head_grad,) = settle_all([head_sum], [(D, local_vocab)])
+    (head_grad,) = settle_all([head_sum], [(D, local_vocab)], (group_sums,))
+    join_all(sums, head_grad)
+    small = sum_over_dp(jnp.concatenate([group_sums[:7], biases], axis=0))
     out_grad, down_grad, up_grad, qkv_grad = settle_all(
-        sums, [(inner, D), (local_hidden, D), (D, local_hidden), qkv_weight.shape], (head_grad,)
+        sums, [(inner, D), (local_hidden, D), (D, local_hidden), qkv_weight.shape]
     )
     return (
         losses[:, 0][None],
@@ -1698,10 +1677,10 @@
         small[2],
         small[3],
         qkv_grad,
-        biases[0, :split].reshape(local_heads, 2 * HEAD_DIM),
+        small[7, :split].reshape(local_heads, 2 * HEAD_DIM),
         out_grad.reshape(out_weight.shape),
         up_grad,
-        biases[0, split : split + local_hidden],
+        small[7, split : split + local_hidden],
         down_grad,
         small[6],
         small[4],

time: 938 us -> 917 us (0.978)
  Pallas kernels: 770 us -> 715 us
  waiting for transfers between devices: 0.04 us -> 14 us
    pallas_call x6, Pallas kernels: 639 us -> 591 us  [call(): pl.pallas_call(body, out_shape=out_shape, in_specs=[ANY] * len(before) +...]
    ppermute x15 -> x17, waiting for transfers between devices: 0.04 us -> 14 us  [the longest x5 8.14 us: cross(): self.other = lax.ppermute(self.sum, 'dp', pairs(2))]
    pallas_call x2 -> x1, Pallas kernels: 19 us -> 9.12 us  [join_halves(): pl.pallas_call(kernel, grid=(steps,), out_shape=[jax.ShapeDtypeStruct(v.s...]
    convert_element_type x5 -> x6, other arithmetic: 16.1 us -> 24.6 us  [the longest x5 15.1 us: __init__(): made = (mine + came.astype(jnp.float32)).astype(jnp.bfloat16)]
  transfers between devices with their start and end apart: 15 -> 17, of which waited for: 0 -> 4; matrix products, arithmetic and copies ran while one was open for 8% -> 10% of each run, Pallas kernels for 43% -> 38%
where the time goes in v7:
time: 917 us; the launch traced here: 901 us
  Pallas kernels  715 us (78%)
  matrix products  89.8 us (10%)
  other arithmetic  47.4 us (5%)
  local copies, waits for them, and re-layouts  19.7 us (2%)
  waiting for transfers between devices  14 us (2%)
  starting transfers between devices  13.3 us (1%)
    pallas_call x6, Pallas kernels, call(): pl.pallas_call(body, out_shape=out_shape, in_specs=[ANY] * len(before) +...  591 us
    dot_general x10, matrix products, dot_tn(): lax.dot_general(left, right, (((0,), (0,)), ((), ())), preferred_element_...  89.8 us
    pallas_call x2, Pallas kernels, settle_halves(): pl.pallas_call(kernel, grid_spec=pltpu.PrefetchScalarGridSpec(num_scalar_...  35.9 us
    pallas_call x1, Pallas kernels, attention_backward(): pl.pallas_call(kernel, grid_spec=pltpu.PrefetchScalarGridSpec(num_scalar_...  31.1 us
    pallas_call x1, Pallas kernels, score_rows(): pl.pallas_call(kernel, out_shape=[jax.ShapeDtypeStruct((8, BLOCK), jnp.fl...  27.6 us
    pallas_call x1, Pallas kernels, attention_forward(): pl.pallas_call(kernel, grid_spec=pltpu.PrefetchScalarGridSpec(num_scalar_...  20.8 us
  transfers between devices with their start and end apart: 17, of which 4 were waited for; matrix products, arithmetic and copies ran while one was open for 10% of the time, Pallas kernels for 38%

profile of v7, /device:TPU:0, one launch (start us, length us, event | category | flops | bytes accessed | tf_op | source)
XLA Modules:
  0.0 900.9 jit_solution(15305754403284973377)
XLA Ops:
  10.7 4.2 copy.38
  15.6 97.3 %shard_map.314 = (bf16[8,256,2048]{2,1,0:T(8,128)(2,1)}, bf16[8,256,2048]{2,1,0:T(8,128)(2,1)}, bf16[8,256,2048]{2,1,0:T(8,128)(2,1)}, bf16[8,256,768]{2,1,0:T(8...) custom-call(bf16[256,2048]{1,0:T(8,128)(2,1)} %bitcast.82, ...), custom_call_target="tpu_custom_call" | custom-call | flops 15032385536 | bytes 268435456 | tf_op jit(solution)/shard_map/pallas_call | solution.py:605
  112.9 20.8 %shard_map.315 = (bf16[2048,256]{1,0:T(8,128)(2,1)}, f32[2,2048,1]{2,1,0:T(8,128)}) custom-call(s32[8]{0:T(128)} %bitcast.115, bf16[2048,768]{1,0:T(8,128)(2,1)} %bitcast.68, bf16[2048,768]{1,0:T(8,128)(2,1)} %bitcast.69, bf16[2048,768]{1,0:T(8,128)(2,1)} %bitcast.70), custom_call_target="tpu_custom_call" | custom-call | tf_op jit(solution)/shard_map/pallas_call | solution.py:459
  134.3 106.9 %shard_map.316 = (bf16[256,2048]{1,0:T(8,128)(2,1)}, bf16[256,2048]{1,0:T(8,128)(2,1)}, f32[256,2048]{1,0:T(8,128)}, f32[256,1]{1,0:T(8,128)}) custom-call(bf16[256,2048]{1,0:T(8,128)(2,1)} %bitcast.83, bf16[8,256,256]{2,1,0:T(8,128)(2,1)} %bitcast.85, bf16[8,256,1024]{2,1,0:T(8,128)(2,1)} %get-tuple-element.58.refs_2_, bf16[256,2048]{1,0:T(8,128)(2,1)} %bitcast.125, ...), custom_call_target="tpu_custom_call" | custom-call | flops 10737418240 | bytes 268435456 | tf_op jit(solution)/shard_map/pallas_call | solution.py:605
  241.2 96.1 %shard_map.317 = (bf16[8,256,2048]{2,1,0:T(8,128)(2,1)}, bf16[8,256,3328]{2,1,0:T(8,128)(2,1)}, f32[8,2048]{1,0:T(8,128)}) custom-call(bf16[256,2048]{1,0:T(8,128)(2,1)} %get-tuple-element.59.refs_0_, bf16[2048,3328]{1,0:T(8,128)(2,1)} %refs_2_.2, s32[2048,1]{1,0:T(8,128)} %copy.36.refs_2_), custom_call_target="tpu_custom_call" | custom-call | flops 27917287424 | bytes 268435456 | tf_op jit(solution)/shard_map/pallas_call | solution.py:605
  337.3 27.6 %shard_map.318 = (f32[8,2048]{1,0:T(8,128)}, f32[8,128]{1,0:T(8,128)}) custom-call(f32[8,2048]{1,0:T(8,128)} %get-tuple-element.60.stats_ref, s32[8]{0:T(128)} %bitcast.116, s32[8]{0:T(128)} %bitcast.121, f32[8]{0:T(128)} %bitcast.122), custom_call_target="tpu_custom_call" | custom-call | tf_op jit(solution)/shard_map/pallas_call | solution.py:1320
  365.8 14.7 %fusion.1 = bf16[2048,3328]{1,0:T(8,128)(2,1)} fusion(bf16[8,256,3328]{2,1,0:T(8,128)(2,1)} %get-tuple-element.67, f32[2048]{0:T(1024)S(1)} %bitcast.97, f32[2048]{0:T(1024)S(1)} %bitcast.96, s32[3328]{0:T(1024)S(1)} %iota_add_fusion, s32[2048]{0:T(1024)S(1)} %bitcast.95), kind=kLoop, calls=%fused_computation.2 | loop fusion | flops 40894464 | bytes 27300864 | tf_op jit(solution)/shard_map/convert_element_type | solution.py:1625
  380.4 21.8 %convolution_convert_fusion = bf16[1024,3328]{1,0:T(8,128)(2,1)} fusion(bf16[2048,3328]{1,0:T(8,128)(2,1)} %fusion.1, bf16[2048,2048]{1,0:T(8,128)(2,1)} %bitcast.131, s32[]{:T(128)S(6)} %select_n.10), kind=kOutput, calls=%fused_computation.5 | convolution fusion | flops 13962051584 | bytes 24641540 | tf_op jit(solution)/shard_map/dot_general | solution.py:377
  402.3 20.6 %fusion.9 = f32[1024,3328]{1,0:T(8,128)S(1)} fusion(bf16[2048,3328]{1,0:T(8,128)(2,1)} %fusion.1, bf16[2048,2048]{1,0:T(8,128)(2,1)} %bitcast.132, s32[]{:T(128)S(6)} %select_n.8), kind=kOutput, calls=%fused_computation.15 | convolution fusion | flops 13958643712 | bytes 31457284 | tf_op jit(solution)/shard_map/dot_general | solution.py:377
  423.0 7.7 add_convert_fusion.1.refs_0_
  431.1 97.8 %shard_map.319 = (f32[256,2048]{1,0:T(8,128)}, bf16[256,2048]{1,0:T(8,128)(2,1)}, f32[8,2048]{1,0:T(8,128)}) custom-call(bf16[1024,3328]{1,0:T(8,128)(2,1)} %add_convert_fusion.1.refs_0_, bf16[8,256,3328]{2,1,0:T(8,128)(2,1)} %bitcast.74, bf16[2048,3328]{1,0:T(8,128)(2,1)} %refs_2_.2, f32[256,2048]{1,0:T(8,128)} %get-tuple-element.68.refs_3_, ...), custom_call_target="tpu_custom_call" | custom-call | flops 27917287424 | bytes 268435456 | tf_op jit(solution)/shard_map/pallas_call | solution.py:605
  529.0 92.1 %shard_map.320 = (bf16[8,256,2048]{2,1,0:T(8,128)(2,1)}, bf16[8,256,256]{2,1,0:T(8,128)(2,1)}, bf16[8,256,1024]{2,1,0:T(8,128)(2,1)}, f32[8,1024]{1,0:T(8,128)}) custom-call(bf16[256,2048]{1,0:T(8,128)(2,1)} %get-tuple-element.70.refs_0_, bf16[256,2048]{1,0:T(8,128)(2,1)} %bitcast.126, bf16[1024,2048]{1,0:T(8,128)(2,1)} %refs_2_.3, ...), custom_call_target="tpu_custom_call" | custom-call | flops 10737418240 | bytes 268435456 | tf_op jit(solution)/shard_map/pallas_call | solution.py:605
  621.1 9.5 %fusion.24 = bf16[1024,1024]{1,0:T(8,128)(2,1)} fusion(bf16[2048,1024]{1,0:T(8,128)(2,1)} %bitcast.77, bf16[2048,2048]{1,0:T(8,128)(2,1)} %bitcast.129, s32[]{:T(128)S(6)} %select_n.10), kind=kOutput, calls=%fused_computation.29 | convolution fusion | flops 4296015872 | bytes 10485764 | tf_op jit(solution)/shard_map/dot_general | solution.py:377
  630.6 5.8 fusion.21
  636.8 6.2 fusion.17
  643.1 9.5 %add_convert_fusion.refs_1_.refs_0_ = bf16[1024,3328]{1,0:T(8,128)(2,1)} fusion(bf16[1024,3328]{1,0:T(8,128)(2,1)} %collective-permute-done.5, bf16[1024,3328]{1,0:T(8,128)(2,1)} %add_convert_fusion.1.refs_0_), kind=kLoop, calls=%fused_computation.3 | loop fusion | flops 13631488 | bytes 20447232 | tf_op jit(solution)/shard_map/convert_element_type | solution.py:1559
  652.6 3.5 fusion.30
  656.6 3.7 fusion.19
  660.4 6.4 fusion.6
  667.7 3.9 add_convert_fusion.2.rest_2_.refs_2_
  673.8 31.1 %shard_map.321 = (bf16[2048,768]{1,0:T(8,128)(2,1)}, f32[2,1,384]{2,1,0:T(1,128)}) custom-call(s32[8]{0:T(128)} %bitcast.117, bf16[2048,768]{1,0:T(8,128)(2,1)} %bitcast.71, bf16[2048,768]{1,0:T(8,128)(2,1)} %bitcast.72, bf16[2048,768]{1,0:T(8,128)(2,1)} %bitcast.73, bf16[2048,256]{1,0:T(8,128)(2,1)} %get-tuple-element.57.ctx_ref, ...), custom_call_target="tpu_custom_call" | custom-call | tf_op jit(solution)/shard_map/pallas_call | solution.py:541
  704.9 6.8 fusion.27
  711.8 5.1 collective-permute-start.4
  718.9 5.5 fusion.11
  727.6 100.8 %shard_map.322 = (f32[256,2048]{1,0:T(8,128)}, f32[8,2048]{1,0:T(8,128)}) custom-call(bf16[1024,768]{1,0:T(8,128)(2,1)} %copy-done, bf16[1024,3328]{1,0:T(8,128)(2,1)} %add_convert_fusion.refs_1_.refs_0_, bf16[256,2048]{1,0:T(8,128)(2,1)} %bitcast.84, f32[256,2048]{1,0:T(8,128)} %get-tuple-element.80.refs_3_, ...), custom_call_target="tpu_custom_call" | custom-call | flops 1 | bytes 1 | tf_op jit(solution)/shard_map/pallas_call | solution.py:605
  828.4 18.2 %shard_map.323.refs_8_ = f32[2048,3328]{1,0:T(8,128)} custom-call(s32[1]{0:T(128)} %bitcast.36.core_ref, bf16[1024,3328]{1,0:T(8,128)(2,1)} %add_convert_fusion.refs_1_.refs_0_, bf16[1024,3328]{1,0:T(8,128)(2,1)} %collective-permute-done.12.refs_1_, f32[8,2048]{1,0:T(8,128)} %get-tuple-element.84.refs_2_), custom_call_target="tpu_custom_call" | custom-call | tf_op jit(solution)/shard_map/pallas_call | solution.py:1508
  846.6 8.1 collective-permute-done.8.refs_4_
  854.7 9.1 %shard_map.324 = (bf16[256,1024]{1,0:T(8,128)(2,1)}, bf16[1024,1024]{1,0:T(8,128)(2,1)}, bf16[1024,1024]{1,0:T(8,128)(2,1)}, bf16[1024,768]{1,0:T(8,128)(2,1)}) custom-call(bf16[256,1024]{1,0:T(8,128)(2,1)} %add_convert_fusion.5.rest_0_.refs_0_, bf16[1024,1024]{1,0:T(8,128)(2,1)} %add_convert_fusion.3.rest_1_.refs_1_, ...), custom_call_target="tpu_custom_call" | custom-call | tf_op jit(solution)/shard_map/pallas_call | solution.py:1459
  865.9 2.5 collective-permute-done.6
  870.1 2.6 collective-permute-done.7
  877.4 17.7 %shard_map.325 = (f32[256,2048]{1,0:T(8,128)}, f32[1024,2048]{1,0:T(8,128)}, f32[2048,1024]{1,0:T(8,128)}, f32[2048,2,384]{2,1,0:T(2,128)}) custom-call(s32[1]{0:T(128)} %bitcast.36.core_ref, bf16[256,1024]{1,0:T(8,128)(2,1)} %get-tuple-element.87.refs_0_, bf16[1024,1024]{1,0:T(8,128)(2,1)} %get-tuple-element.88.refs_1_, ...), custom_call_target="tpu_custom_call" | custom-call | tf_op jit(solution)/shard_map/pallas_call | solution.py:1508
  897.4 3.1 copy.46
  (107 shorter events, 33.0 us)
Async XLA Ops:
  4.5 10.4 %copy-start.8 = (f32[2048]{0:T(1024)}, f32[2048]{0:T(1024)S(1)}, u32[]{:S(2)}) copy-start(f32[2048]{0:T(1024)S(1)} %broadcast_in_dim.104) | copy-start | bytes 24580
  5.9 9.7 %copy-start.10 = (f32[2048]{0:T(1024)}, f32[2048]{0:T(1024)S(1)}, u32[]{:S(2)}) copy-start(f32[2048]{0:T(1024)S(1)} %broadcast_in_dim.106) | copy-start | bytes 24580
  8.0 125.7 %copy-start.13 = (f32[2048]{0:T(1024)}, f32[2048]{0:T(1024)S(1)}, u32[]{:S(2)}) copy-start(f32[2048]{0:T(1024)S(1)} %broadcast_in_dim.109) | copy-start | bytes 24580
  241.2 124.6 %copy-start.12 = (s32[1,2048]{1,0:T(1,128)S(1)}, s32[1,2048]{1,0:T(1,128)}, u32[]{:S(2)}) copy-start(s32[1,2048]{1,0:T(1,128)} %param.20) | copy-start | bytes 24580
  402.2 20.7 %collective-permute-start = (bf16[1024,3328]{1,0:T(8,128)(2,1)}, bf16[1024,3328]{1,0:T(8,128)(2,1)}, u32[]{:S(2)}, u32[]{:S(2)}) collective-permute-start(bf16[1024,3328]{1,0:T(8,128)(2,1)} %convolution_convert_fusion), channel_id=1, source_target_pairs={{0,8},{8,0},{16,24},{24,16},{1,9},{9,1},{17,25},{25,17},{2,10},{10... | collective-permute-start | bytes 20447240 | tf_op jit(solution)/shard_map/ppermute | solution.py:1541
  430.6 212.4 %collective-permute-start.5 = (bf16[1024,3328]{1,0:T(8,128)(2,1)}, bf16[1024,3328]{1,0:T(8,128)(2,1)}, u32[]{:S(2)}, u32[]{:S(2)}) collective-permute-start(bf16[1024,3328]{1,0:T(8,128)(2,1)} %add_convert_fusion.1.refs_0_), channel_id=1, source_target_pairs={{0,16},{8,24},{16,0},{24,8},{1,17},{9,25},{17,1},{25,9},{2,18},{10... | collective-permute-start | bytes 20447240 | tf_op jit(solution)/shard_map/ppermute | solution.py:1552
  621.0 9.5 %copy-start.16 = (bf16[8,256,2048]{2,1,0:T(8,128)(2,1)S(1)}, bf16[8,256,2048]{2,1,0:T(8,128)(2,1)}, u32[]{:S(2)}) copy-start(bf16[8,256,2048]{2,1,0:T(8,128)(2,1)} %get-tuple-element.76) | copy-start | bytes 25165828
  621.0 9.5 %copy-start.17 = (bf16[8,256,1024]{2,1,0:T(8,128)(2,1)S(1)}, bf16[8,256,1024]{2,1,0:T(8,128)(2,1)}, u32[]{:S(2)}) copy-start(bf16[8,256,1024]{2,1,0:T(8,128)(2,1)} %get-tuple-element.58.refs_2_) | copy-start | bytes 12582916
  630.6 37.2 %collective-permute-start.3 = (bf16[1024,1024]{1,0:T(8,128)(2,1)}, bf16[1024,1024]{1,0:T(8,128)(2,1)}, u32[]{:S(2)}, u32[]{:S(2)}) collective-permute-start(bf16[1024,1024]{1,0:T(8,128)(2,1)} %fusion.24), channel_id=1, source_target_pairs={{0,8},{8,0},{16,24},{24,16},{1,9},{9,1},{17,25},{25,17},{2,10},{10... | collective-permute-start | bytes 6291464 | tf_op jit(solution)/shard_map/ppermute | solution.py:1541
  636.3 35.3 %collective-permute-start.2 = (bf16[1024,1024]{1,0:T(8,128)(2,1)}, bf16[1024,1024]{1,0:T(8,128)(2,1)S(1)}, u32[]{:S(2)}, u32[]{:S(2)}) collective-permute-start(bf16[1024,1024]{1,0:T(8,128)(2,1)} %fusion.21), channel_id=1, source_target_pairs={{0,8},{8,0},{16,24},{24,16},{1,9},{9,1},{17,25},{25,17},{2,10},{10... | collective-permute-start | bytes 6291464 | tf_op jit(solution)/shard_map/ppermute | solution.py:1541
  643.0 9.5 %copy-start.5 = (bf16[2048,256]{1,0:T(8,128)(2,1)S(1)}, bf16[2048,256]{1,0:T(8,128)(2,1)}, u32[]{:S(2)}) copy-start(bf16[2048,256]{1,0:T(8,128)(2,1)} %get-tuple-element.57.ctx_ref) | copy-start | bytes 3145732
  652.6 175.8 %collective-permute-start.12 = (bf16[1024,3328]{1,0:T(8,128)(2,1)}, bf16[1024,3328]{1,0:T(8,128)(2,1)}, u32[]{:S(2)}, u32[]{:S(2)}) collective-permute-start(bf16[1024,3328]{1,0:T(8,128)(2,1)} %add_convert_fusion.refs_1_.refs_0_), channel_id=1, source_target_pairs={{0,8},{8,0},{16,24},{24,16},{1,9},{9,1},{17,25},{25,17},{2,10},{10... | collective-permute-start | bytes 20447240 | tf_op jit(solution)/shard_map/ppermute | solution.py:1582
  656.1 4.3 copy-start.2
  656.1 10.7 %collective-permute-start.1 = (bf16[256,1024]{1,0:T(8,128)(2,1)S(1)}, bf16[256,1024]{1,0:T(8,128)(2,1)S(1)}, u32[]{:S(2)}, u32[]{:S(2)}) collective-permute-start(bf16[256,1024]{1,0:T(8,128)(2,1)S(1)} %fusion.30), channel_id=1, source_target_pairs={{0,8},{8,0},{16,24},{24,16},{1,9},{9,1},{17,25},{25,17},{2,10},{10... | collective-permute-start | bytes 1572872 | tf_op jit(solution)/shard_map/ppermute | solution.py:1541
  667.7 3.9 copy-start.1
  704.9 14.0 %copy-start.3 = (bf16[2048,768]{1,0:T(8,128)(2,1)S(1)}, bf16[2048,768]{1,0:T(8,128)(2,1)}, u32[]{:S(2)}) copy-start(bf16[2048,768]{1,0:T(8,128)(2,1)} %get-tuple-element.79) | copy-start | bytes 9437188
  711.8 12.7 %collective-permute-start.4 = (bf16[1024,768]{1,0:T(8,128)(2,1)S(1)}, bf16[1024,768]{1,0:T(8,128)(2,1)S(1)}, u32[]{:S(2)}, u32[]{:S(2)}) collective-permute-start(bf16[1024,768]{1,0:T(8,128)(2,1)S(1)} %fusion.27), channel_id=1, source_target_pairs={{0,8},{8,0},{16,24},{24,16},{1,9},{9,1},{17,25},{25,17},{2,10},{10... | collective-permute-start | bytes 4718600 | tf_op jit(solution)/shard_map/ppermute | solution.py:1541
  716.9 137.8 %collective-permute-start.10 = (bf16[1024,1024]{1,0:T(8,128)(2,1)}, bf16[1024,1024]{1,0:T(8,128)(2,1)}, u32[]{:S(2)}, u32[]{:S(2)}) collective-permute-start(bf16[1024,1024]{1,0:T(8,128)(2,1)} %add_convert_fusion.2.rest_2_.refs_2_), channel_id=1, source_target_pairs={{0,16},{8,24},{16,0},{24,8},{1,17},{9,25},{17,1},{25,9},{2,18},{10... | collective-permute-start | bytes 6291464 | tf_op jit(solution)/shard_map/ppermute | solution.py:1552
  717.6 137.1 %collective-permute-start.9 = (bf16[1024,1024]{1,0:T(8,128)(2,1)}, bf16[1024,1024]{1,0:T(8,128)(2,1)}, u32[]{:S(2)}, u32[]{:S(2)}) collective-permute-start(bf16[1024,1024]{1,0:T(8,128)(2,1)} %add_convert_fusion.3.rest_1_.refs_1_), channel_id=1, source_target_pairs={{0,16},{8,24},{16,0},{24,8},{1,17},{9,25},{17,1},{25,9},{2,18},{10... | collective-permute-start | bytes 6291464 | tf_op jit(solution)/shard_map/ppermute | solution.py:1552
  724.5 2.5 copy-start.9
  724.9 2.7 copy-start
  724.9 129.8 %collective-permute-start.11 = (bf16[1024,768]{1,0:T(8,128)(2,1)S(1)}, bf16[1024,768]{1,0:T(8,128)(2,1)}, u32[]{:S(2)}, u32[]{:S(2)}) collective-permute-start(bf16[1024,768]{1,0:T(8,128)(2,1)S(1)} %add_convert_fusion.4.refs_0_.refs_3_), channel_id=1, source_target_pairs={{0,16},{8,24},{16,0},{24,8},{1,17},{9,25},{17,1},{25,9},{2,18},{10... | collective-permute-start | bytes 4718600 | tf_op jit(solution)/shard_map/ppermute | solution.py:1552
  725.7 129.1 %collective-permute-start.8 = (bf16[256,1024]{1,0:T(8,128)(2,1)}, bf16[256,1024]{1,0:T(8,128)(2,1)}, u32[]{:S(2)}, u32[]{:S(2)}) collective-permute-start(bf16[256,1024]{1,0:T(8,128)(2,1)} %add_convert_fusion.5.rest_0_.refs_0_), channel_id=1, source_target_pairs={{0,16},{8,24},{16,0},{24,8},{1,17},{9,25},{17,1},{25,9},{2,18},{10... | collective-permute-start | bytes 1572872 | tf_op jit(solution)/shard_map/ppermute | solution.py:1552
  846.6 18.6 %copy-start.15 = (f32[2,1,384]{2,1,0:T(1,128)S(1)}, f32[2,1,384]{2,1,0:T(1,128)}, u32[]{:S(2)}) copy-start(f32[2,1,384]{2,1,0:T(1,128)} %get-tuple-element.85) | copy-start | bytes 9220
  846.6 18.8 %copy-start.6 = (f32[8,2048]{1,0:T(8,128)S(1)}, f32[8,2048]{1,0:T(8,128)}, u32[]{:S(2)}) copy-start(f32[8,2048]{1,0:T(8,128)} %get-tuple-element.84.refs_2_) | copy-start | bytes 196612
  846.6 22.9 %copy-start.14 = (f32[8,128]{1,0:T(8,128)S(1)}, f32[8,128]{1,0:T(8,128)}, u32[]{:S(2)}) copy-start(f32[8,128]{1,0:T(8,128)} %get-tuple-element.61) | copy-start | bytes 12292
  863.8 12.4 %collective-permute-start.14 = (bf16[1024,1024]{1,0:T(8,128)(2,1)}, bf16[1024,1024]{1,0:T(8,128)(2,1)}, u32[]{:S(2)}, u32[]{:S(2)}) collective-permute-start(bf16[1024,1024]{1,0:T(8,128)(2,1)} %get-tuple-element.88.refs_1_), channel_id=1, source_target_pairs={{0,8},{8,0},{16,24},{24,16},{1,9},{9,1},{17,25},{25,17},{2,10},{10... | collective-permute-start | bytes 6291464 | tf_op jit(solution)/shard_map/ppermute | solution.py:1582
  863.9 12.3 %collective-permute-start.15 = (bf16[1024,1024]{1,0:T(8,128)(2,1)}, bf16[1024,1024]{1,0:T(8,128)(2,1)}, u32[]{:S(2)}, u32[]{:S(2)}) collective-permute-start(bf16[1024,1024]{1,0:T(8,128)(2,1)} %get-tuple-element.89.refs_2_), channel_id=1, source_target_pairs={{0,8},{8,0},{16,24},{24,16},{1,9},{9,1},{17,25},{25,17},{2,10},{10... | collective-permute-start | bytes 6291464 | tf_op jit(solution)/shard_map/ppermute | solution.py:1582
  865.2 10.2 %collective-permute-start.16 = (bf16[1024,768]{1,0:T(8,128)(2,1)}, bf16[1024,768]{1,0:T(8,128)(2,1)S(1)}, u32[]{:S(2)}, u32[]{:S(2)}) collective-permute-start(bf16[1024,768]{1,0:T(8,128)(2,1)} %get-tuple-element.90.refs_3_), channel_id=1, source_target_pairs={{0,8},{8,0},{16,24},{24,16},{1,9},{9,1},{17,25},{25,17},{2,10},{10... | collective-permute-start | bytes 4718600 | tf_op jit(solution)/shard_map/ppermute | solution.py:1582
  865.4 3.0 collective-permute-start.6
  868.4 4.3 collective-permute-start.7
  873.3 2.1 collective-permute-start.13
  (3 other events, 4.4 us)

commit v8 on v7

--- a/solution.py
+++ b/solution.py
@@ -205,23 +205,23 @@
     return 1 if n == 2 else n + 1
 
 
-def scatter_plan(n):
-    if n == (4, 2):
+def scatter_plan(n, quick):
+    if n == (4, 2) and not quick:
         return [
             ("make", 3, 1), ("make", 2, 1), ("make", 3, 0), ("make", 1, 1), ("first", 3), ("make", 2, 0),
             ("make", 0, 1), ("later", 3, 0), ("make", 1, 0), ("later", 3, 1), ("first", 2), ("make", 0, 0), ("made",),
             ("later", 2, 0), ("later", 2, 1), ("first", 1), ("later", 1, 0), ("later", 1, 1),
         ]
     far = n[0] - 1
-    plan = [("make", k, l) for k in range(far, -1, -1) for l in range(n[1] - 1, -1, -1)] + [("made",)]
+    plan = [("make", k, l) for l in range(n[1] - 1, -1, -1) for k in range(far, -1, -1)] + [("made",)]
     for k in range(far, 0, -1):
         plan += [("first", k), ("later", k, 0), ("later", k, 1)]
     return plan
 
 
 class Scatter:
-    def __init__(self, grid, sender, part, bufs, sems, halves, cut):
-        self.grid, self.sender, self.part = grid, sender, part
+    def __init__(self, grid, sender, part, bufs, sems, halves, cut, quick):
+        self.grid, self.sender, self.part, self.quick = grid, sender, part, quick
         self.bufs, self.sems, self.halves, self.cut = bufs, sems, halves, cut
 
     def slot(self, axis, target, from_below):
@@ -276,9 +276,9 @@
             self.take(kind, stage, axis, other, m, jnp.bool_(True), half, m > 0, index)
             self.take(kind, stage, axis, other, m, jnp.bool_(False), half, m < n - 1, index)
 
-    def run(self, produce, made=lambda: None, between=lambda: None, late=lambda: None, fill=lambda: None):
+    def run(self, produce, made=lambda: None, late=lambda: None):
         grid, n, me = self.grid, self.grid.n, self.grid.me
-        lagging, filling = [], []
+        lagging = []
 
         def chain(k, half, begins):
             slow = grid.nearest(0, k)
@@ -308,24 +308,17 @@
                 for half in range(self.halves):
                     lagging.append((1, 0, 0, fast, slow, half, slow, fast))
 
-        for step in scatter_plan(n):
+        for step in scatter_plan(n, self.quick):
             if step[0] == "make":
                 make(*step[1:])
             elif step[0] == "made":
                 catch_up()
                 made()
-                filling.append(fill)
             elif step[0] == "first" and self.cut[0]:
-                for more in filling:
-                    more()
                 for half in range(self.halves):
                     chain(step[1], half, True)
             elif self.cut[0]:
-                for more in filling:
-                    more()
                 chain(step[1], step[2], False)
-        between()
-        fill()
         if self.cut[1]:
             for half in range(self.halves):
                 for l in reversed(range(n[1])):
@@ -336,7 +329,6 @@
         late()
         if self.cut[0]:
             for half in range(self.halves):
-                fill()
                 self.last(0, 0, 1, me[0], half, me[0], me[1])
         for half in range(self.halves):
             if self.cut[1]:
@@ -649,7 +641,7 @@
     )
 
 
-def run_scatter(grid, sizes, rows, scratch, produce, *hooks):
+def run_scatter(grid, sizes, rows, scratch, produce, *hooks, quick=False):
     cut = scatter_cut(sizes)
     step = rows // HALVES
     parts, b0, b1, b2, b3, s0, s1, s2, s3, send_sems = scratch
@@ -659,16 +651,16 @@
         return parts.at[slot, pl.ds(half * step, step), columns_of(cut, kind)]
 
     scatter = Scatter(
-        grid, sender, part, ((b0, b1), (b2, b3)), ((s0, s1), (s2, s3)), HALVES, cut
+        grid, sender, part, ((b0, b1), (b2, b3)), ((s0, s1), (s2, s3)), HALVES, cut, quick
     )
     scatter.run(produce, *hooks)
     sender.finish()
 
 
-def production_order(grid):
+def production_order(grid, quick=False):
     return [
         grid.index(grid.nearest(0, k), grid.nearest(1, l))
-        for action, k, l in [step for step in scatter_plan(grid.n) if step[0] == "make"]
+        for action, k, l in [step for step in scatter_plan(grid.n, quick) if step[0] == "make"]
     ]
 
 
@@ -1072,28 +1064,44 @@
     )(grad_logits, head_weight, normed, inverse, gain)
 
 
-def branch_grad_rows(own, out_flat, down_weight, slope, sizes, collective):
+def branch_grad_rows(own, out_flat, down_weight, slope, ctx, act, second, sizes, collective):
     rows = own.shape[0]
     shards = sizes[0] * sizes[1]
     inner, hidden = out_flat.shape[0], down_weight.shape[0]
+    half_width = D // 2
 
     def kernel(
-        own_ref, outw_any, downw_any, slope_any, rows_any, ctx_any, up_any, sums_ref,
-        full, send_sems, recv_sems, outw, downw, load_sems, slope, slope_sems, ctx, up, out_sems, row_sems,
+        own_ref, outw_any, downw_any, slope_any, ctx_any, act_any, second_any,
+        grad_ctx_any, grad_up_any, sums_ref, out_away, out_mine, down_away, down_mine, up_away, up_mine,
+        full, send_sems, recv_sems, outw, downw, load_sems, slope, slope_sem, grad_ctx, grad_up, out_sems,
+        ctx, act, second, row_sems, out_total, down_total, up_total, part_sems,
     ):
         grid = Grid2(sizes)
+        core = lax.rem(lax.axis_index("dp"), 2)
         loads = [
             pltpu.make_async_copy(outw_any, outw, load_sems.at[0]),
             pltpu.make_async_copy(downw_any, downw, load_sems.at[1]),
         ]
         for copy in loads:
             copy.start()
-        slopes = pltpu.make_async_copy(slope_any, slope, slope_sems)
+        slopes = pltpu.make_async_copy(slope_any, slope, slope_sem)
         slopes.start()
+        order_of = [
+            grid.index(grid.nearest(0, k), grid.nearest(1, l)) for k in range(sizes[0]) for l in range(sizes[1])
+        ]
+        row_loads = [
+            [
+                pltpu.make_async_copy(there.at[place], here.at[i % 2], row_sems.at[i % 2, j])
+                for j, (there, here) in enumerate(((ctx_any, ctx), (act_any, act), (second_any, second)))
+            ]
+            for i, place in enumerate(order_of)
+        ]
+        for copy in row_loads[0]:
+            copy.start()
         full[grid.index(*grid.me)] = own_ref[...]
         sums_ref[...] = jnp.zeros_like(sums_ref)
         grid.barrier()
-        open_copies, raw_copies = [], []
+        open_copies = []
 
         def ready(slow, fast, order):
             place = grid.index(slow, fast)
@@ -1104,44 +1112,95 @@
             if order >= 2:
                 for copy in open_copies.pop(0):
                     copy.wait()
-            ctx[slot] = dot_nt(full[place], outw[...]).astype(jnp.bfloat16)
+            if order + 1 < shards:
+                for copy in row_loads[order + 1]:
+                    copy.start()
+            grad_ctx[slot] = dot_nt(full[place], outw[...]).astype(jnp.bfloat16)
             tile = tile_of(hidden)
 
             def up_tile(index, _):
                 here = span(index, tile)
                 found = dot_nt(full[place], downw[here, :]) * slope[place, :, here].astype(jnp.float32)
                 rounded = found.astype(jnp.bfloat16)
-                up[slot, :, here] = rounded
+                grad_up[slot, :, here] = rounded
                 sums_ref[0:1, here] += jnp.sum(rounded.astype(jnp.float32), axis=0, keepdims=True)
                 return _
 
             lax.fori_loop(0, hidden // tile, up_tile, 0)
             copies = [
-                pltpu.make_async_copy(ctx.at[slot], ctx_any.at[place], out_sems.at[slot, 0]),
-                pltpu.make_async_copy(up.at[slot], up_any.at[place], out_sems.at[slot, 1]),
+                pltpu.make_async_copy(grad_ctx.at[slot], grad_ctx_any.at[place], out_sems.at[slot, 0]),
+                pltpu.make_async_copy(grad_up.at[slot], grad_up_any.at[place], out_sems.at[slot, 1]),
             ]
             for copy in copies:
                 copy.start()
             open_copies.append(copies)
-            raw = pltpu.make_async_copy(full.at[place], rows_any.at[place], row_sems.at[order])
-            raw.start()
-            raw_copies.append(raw)
+            for copy in row_loads[order]:
+                copy.wait()
+
+            def add(total, here, found):
+                if order == 0:
+                    total[:, here] = found
+                else:
+                    total[:, here] += found
+
+            def stream_tile(index, _):
+                here = span(index, 512)
+                grads = full[place, :, here]
+                add(out_total, here, dot_tn(ctx[slot], grads))
+                add(down_total, here, dot_tn(act[slot], grads))
+                return _
+
+            lax.fori_loop(0, D // 512, stream_tile, 0)
+
+            def up_grad_tile(index, _):
+                here = span(index, tile)
+                add(up_total, here, dot_tn(second[slot], grad_up[slot, :, here]))
+                return _
+
+            lax.fori_loop(0, hidden // tile, up_grad_tile, 0)
 
         run_gather(grid, sizes, rows, full, send_sems, recv_sems, ready)
         for copies in open_copies:
             for copy in copies:
                 copy.wait()
-        for copy in raw_copies:
+        stores = []
+
+        def store(total, there, row, column, height, width):
+            index = len(stores)
+            if index < 2 * shards:
+                here = full.at[index // 2, :, pl.ds((index % 2) * half_width, width)]
+            else:
+                here = slope.at[index - 2 * shards, :, pl.ds(0, width)]
+            here[...] = total[
+                pl.ds(pl.multiple_of(row, rows), rows), pl.ds(pl.multiple_of(column, 128), width)
+            ].astype(jnp.bfloat16)
+            copy = pltpu.make_async_copy(here, there.at[pl.ds(height, rows)], part_sems.at[index])
+            copy.start()
+            stores.append(copy)
+
+        for which, wide in ((1 - core, (out_away, down_away, up_away)), (core, (out_mine, down_mine, up_mine))):
+            for total, there, count in ((out_total, wide[0], inner), (down_total, wide[1], hidden)):
+                for height in range(0, count, rows):
+                    store(total, there, height, which * half_width, height, half_width)
+            for height in range(0, half_width, rows):
+                store(up_total, wide[2], which * half_width + height, 0, height, hidden)
+        for copy in stores:
             copy.wait()
 
     def out(columns):
         return jax.ShapeDtypeStruct((shards, rows, columns), jnp.bfloat16)
 
+    parts = [
+        jax.ShapeDtypeStruct(shape, jnp.bfloat16)
+        for shape in ((inner, half_width), (hidden, half_width), (half_width, hidden))
+        for _ in range(2)
+    ]
+    stores = 2 * (inner // rows + hidden // rows + half_width // rows)
     return row_kernel(
         kernel, collective,
-        [out(D), out(inner), out(hidden), jax.ShapeDtypeStruct((8, hidden), jnp.float32)],
-        [VMEM, ANY, ANY, ANY],
-        [ANY, ANY, ANY, VMEM],
+        [out(inner), out(hidden), jax.ShapeDtypeStruct((8, hidden), jnp.float32)] + parts,
+        [VMEM] + [ANY] * 6,
+        [ANY, ANY, VMEM] + [ANY] * 6,
         gather_scratch(sizes, rows)
         + [
             pltpu.VMEM(out_flat.shape, jnp.bfloat16),
@@ -1152,10 +1211,17 @@
             pltpu.VMEM((2, rows, inner), jnp.bfloat16),
             pltpu.VMEM((2, rows, hidden), jnp.bfloat16),
             pltpu.SemaphoreType.DMA((2, 2)),
-            pltpu.SemaphoreType.DMA((shards,)),
+            pltpu.VMEM((2, rows, inner), jnp.bfloat16),
+            pltpu.VMEM((2, rows, hidden), jnp.bfloat16),
+            pltpu.VMEM((2, rows, D), jnp.bfloat16),
+            pltpu.SemaphoreType.DMA((2, 3)),
+            pltpu.VMEM((inner, D), jnp.float32),
+            pltpu.VMEM((hidden, D), jnp.float32),
+            pltpu.VMEM((D, hidden), jnp.float32),
+            pltpu.SemaphoreType.DMA((stores,)),
         ],
-        2 * BLOCK * D * (inner + hidden),
-    )(own, out_flat, down_weight, slope)
+        4 * BLOCK * D * (inner + hidden) + 2 * BLOCK * D * hidden,
+    )(own, out_flat, down_weight, slope, ctx, act, second)
 
 
 class SmallSum:
@@ -1406,7 +1472,7 @@
             sums_ref[4:8] = end_ref[0:4]
             small.spread()
 
-        run_scatter(grid, sizes, rows, scratch, produce, made, lambda: None, small.collect)
+        run_scatter(grid, sizes, rows, scratch, produce, made, small.collect)
         mine = grid.index(*grid.me)
 
         def norm_tile(index, _):
@@ -1533,15 +1599,11 @@
 
 
 class PairSum:
-    def __init__(self, product=None, made=None):
+    def __init__(self, away, mine):
         self.plain = lax.axis_size("dp") != 4
         self.core = lax.rem(lax.axis_index("dp"), 2)
-        if made is None:
-            away = product(1 - self.core).astype(jnp.bfloat16)
-            came = lax.ppermute(away, "dp", pairs(1))
-            mine = held(product(self.core))
-            made = (mine + came.astype(jnp.float32)).astype(jnp.bfloat16)
-        self.sum = made
+        came = lax.ppermute(away, "dp", pairs(1))
+        self.sum = (mine.astype(jnp.float32) + came.astype(jnp.float32)).astype(jnp.bfloat16)
 
     def cross(self):
         if self.plain:
@@ -1552,11 +1614,8 @@
             self.other = lax.ppermute(self.sum, "dp", pairs(2))
         return self
 
-    def join(self):
-        if self.plain:
-            self.total = self.other
-        else:
-            self.total = (self.sum.astype(jnp.float32) + self.other.astype(jnp.float32)).astype(jnp.bfloat16)
+    def join(self, earlier):
+        self.total = self.other if self.plain else join_halves([self.sum], [self.other], earlier)[0]
         return self
 
 
@@ -1566,6 +1625,11 @@
     for step in (1, 2):
         values = values + lax.ppermute(values, "dp", pairs(step))
     return values
+
+
+def pair_product(product):
+    core = lax.rem(lax.axis_index("dp"), 2)
+    return PairSum(product(1 - core).astype(jnp.bfloat16), held(product(core)))
 
 
 def join_all(sums, earlier):
@@ -1624,34 +1688,22 @@
         - weights.reshape(BLOCK, local_vocab).astype(jnp.float32) * coef[1][:, None]
     ).astype(jnp.bfloat16))
     final_rows = final_full.reshape(BLOCK, D)
-    head_sum = PairSum(lambda which: dot_tn(half_of(final_rows, which), grad_logits)).cross()
+    head_sum = pair_product(lambda which: dot_tn(half_of(final_rows, which), grad_logits)).cross()
 
     grad_stream, grad_own, end_sums = final_grad_rows(
         grad_logits.reshape(shards, rows, local_vocab), head_weight, normed, inverse, row_of(lnf_gain), sizes, 3,
         (head_sum.sum,),
     )
-    grad_full, grad_ctx, grad_up, up_sums = branch_grad_rows(
-        grad_own, out_flat, down_weight, slope, sizes, 4
+    grad_ctx, grad_up, up_sums, *halves = branch_grad_rows(
+        grad_own, out_flat, down_weight, slope, ctx.reshape(shards, rows, inner), act, second_full, sizes, 4
     )
-    grad_rows = grad_full.reshape(BLOCK, D)
-    act_rows = act.reshape(BLOCK, local_hidden)
-    second_rows = second_full.reshape(BLOCK, D)
-    up_rows = grad_up.reshape(BLOCK, local_hidden)
-    sums = [
-        PairSum(lambda which: dot_tn(ctx, half_of(grad_rows, which))),
-        PairSum(lambda which: dot_tn(act_rows, half_of(grad_rows, which))),
-        PairSum(lambda which: dot_tn(half_of(second_rows, which), up_rows)),
-    ]
-    for one in sums:
-        one.cross()
-    made = [one.sum for one in sums]
+    sums = [PairSum(*halves[2 * i : 2 * i + 2]).cross() for i in range(3)]
     grad_qkv, qkv_sums = attention_backward(
         flat_qkv, block_lengths, local_heads, ctx, lse, grad_ctx.reshape(BLOCK, inner), planes,
-        made,
+        (),
     )
     first_rows = first_full.reshape(BLOCK, D)
-    sums.append(PairSum(lambda which: dot_tn(half_of(first_rows, which), grad_qkv)))
-    sums[-1].cross()
+    sums.append(pair_product(lambda which: dot_tn(half_of(first_rows, which), grad_qkv)).cross())
     qkv_sums = qkv_sums[:, 0]
     qv_grad = jnp.concatenate([qkv_sums[:, :HEAD_DIM], qkv_sums[:, 2 * HEAD_DIM :]], axis=-1)
     split = local_heads * 2 * HEAD_DIM
@@ -1660,7 +1712,7 @@
     gains = jnp.concatenate([row_of(ln1_gain), row_of(ln2_gain)], axis=0)
     grad_input, group_sums = input_grad_rows(
         own, grad_stream, plain, grad_qkv.reshape(shards, rows, width), grad_up, qkv_flat, up_weight, gains,
-        end_sums, sizes, 5, (sums[-1].sum, head_sum.join().total),
+        end_sums, sizes, 5, (sums[-1].sum, head_sum.join(up_sums).total),
     )
     (head_grad,) = settle_all([head_sum], [(D, local_vocab)], (group_sums,))
     join_all(sums, head_grad)

time: 917 us -> 888 us (0.968)
  matrix products: 89.8 us -> 54.5 us
  Pallas kernels: 715 us -> 741 us
    dot_general x10 -> x4, matrix products: 89.8 us -> 54.5 us  [dot_tn(): lax.dot_general(left, right, (((0,), (0,)), ((), ())), preferred_element_...]
    pallas_call x6, Pallas kernels: 591 us -> 607 us  [call(): pl.pallas_call(body, out_shape=out_shape, in_specs=[ANY] * len(before) +...]
    pallas_call x1 -> x2, Pallas kernels: 9.12 us -> 19.1 us  [join_halves(): pl.pallas_call(kernel, grid=(steps,), out_shape=[jax.ShapeDtypeStruct(v.s...]
    convert_element_type x6 -> x5, other arithmetic: 24.6 us -> 17 us  [__init__(): (mine.astype(jnp.float32) + came.astype(jnp.float32)).astype(jnp.bfloat16)]
  transfers between devices with their start and end apart: 17 -> 17, of which waited for: 4 -> 4; matrix products, arithmetic and copies ran while one was open for 10% -> 5% of each run, Pallas kernels for 38% -> 41%
where the time goes in v8:
time: 888 us; the launch traced here: 874 us
  Pallas kernels  741 us (83%)
  matrix products  54.5 us (6%)
  other arithmetic  39.7 us (4%)
  local copies, waits for them, and re-layouts  19.7 us (2%)
  starting transfers between devices  9.65 us (1%)
    pallas_call x6, Pallas kernels, call(): pl.pallas_call(body, out_shape=out_shape, in_specs=[ANY] * len(before) +...  607 us
    dot_general x4, matrix products, dot_tn(): lax.dot_general(left, right, (((0,), (0,)), ((), ())), preferred_element_...  54.5 us
    pallas_call x2, Pallas kernels, settle_halves(): pl.pallas_call(kernel, grid_spec=pltpu.PrefetchScalarGridSpec(num_scalar_...  35.9 us
    pallas_call x1, Pallas kernels, attention_backward(): pl.pallas_call(kernel, grid_spec=pltpu.PrefetchScalarGridSpec(num_scalar_...  34.3 us
    pallas_call x1, Pallas kernels, attention_forward(): pl.pallas_call(kernel, grid_spec=pltpu.PrefetchScalarGridSpec(num_scalar_...  23.5 us
    pallas_call x1, Pallas kernels, score_rows(): pl.pallas_call(kernel, out_shape=[jax.ShapeDtypeStruct((8, BLOCK), jnp.fl...  21.3 us
    pallas_call x2, Pallas kernels, join_halves(): pl.pallas_call(kernel, grid=(steps,), out_shape=[jax.ShapeDtypeStruct(v.s...  19.1 us
  transfers between devices with their start and end apart: 17, of which 4 were waited for; matrix products, arithmetic and copies ran while one was open for 5% of the time, Pallas kernels for 41%

profile of v8, /device:TPU:0, one launch (start us, length us, event | category | flops | bytes accessed | tf_op | source)
XLA Modules:
  0.0 874.3 jit_solution(1919888198729948271)
XLA Ops:
  2.6 1.3 broadcast_in_dim.108
  8.7 2.0 copy.36.refs_2_
  10.7 4.2 copy.38
  15.6 97.3 %shard_map.314 = (bf16[8,256,2048]{2,1,0:T(8,128)(2,1)}, bf16[8,256,2048]{2,1,0:T(8,128)(2,1)}, bf16[8,256,2048]{2,1,0:T(8,128)(2,1)}, bf16[8,256,768]{2,1,0:T(8...) custom-call(bf16[256,2048]{1,0:T(8,128)(2,1)} %bitcast.70, ...), custom_call_target="tpu_custom_call" | custom-call | flops 15032385536 | bytes 268435456 | tf_op jit(solution)/shard_map/pallas_call | solution.py:597
  112.9 23.5 %shard_map.315 = (bf16[2048,256]{1,0:T(8,128)(2,1)}, f32[2,2048,1]{2,1,0:T(8,128)}) custom-call(s32[8]{0:T(128)} %bitcast.104, bf16[2048,768]{1,0:T(8,128)(2,1)} %bitcast.58, bf16[2048,768]{1,0:T(8,128)(2,1)} %bitcast.59, bf16[2048,768]{1,0:T(8,128)(2,1)} %bitcast.60), custom_call_target="tpu_custom_call" | custom-call | tf_op jit(solution)/shard_map/pallas_call | solution.py:451
  137.0 108.3 %shard_map.316 = (bf16[256,2048]{1,0:T(8,128)(2,1)}, bf16[256,2048]{1,0:T(8,128)(2,1)}, f32[256,2048]{1,0:T(8,128)}, f32[256,1]{1,0:T(8,128)}) custom-call(bf16[256,2048]{1,0:T(8,128)(2,1)} %bitcast.71, bf16[8,256,256]{2,1,0:T(8,128)(2,1)} %bitcast.73, bf16[8,256,1024]{2,1,0:T(8,128)(2,1)} %get-tuple-element.63.refs_2_.refs_5_, bf16[256,2048]{1,0:T(8,128)(2,1)} %bitcast.114, ...), custom_call_target="tpu_custom_call" | custom-call | flops 10737418240 | bytes 268435456 | tf_op jit(solution)/shard_map/pallas_call | solution.py:597
  245.3 95.6 %shard_map.317 = (bf16[8,256,2048]{2,1,0:T(8,128)(2,1)}, bf16[8,256,3328]{2,1,0:T(8,128)(2,1)}, f32[8,2048]{1,0:T(8,128)}) custom-call(bf16[256,2048]{1,0:T(8,128)(2,1)} %get-tuple-element.64.refs_0_, bf16[2048,3328]{1,0:T(8,128)(2,1)} %refs_2_.2, s32[2048,1]{1,0:T(8,128)} %copy.36.refs_2_), custom_call_target="tpu_custom_call" | custom-call | flops 27917287424 | bytes 268435456 | tf_op jit(solution)/shard_map/pallas_call | solution.py:597
  341.0 21.3 %shard_map.318 = (f32[8,2048]{1,0:T(8,128)}, f32[8,128]{1,0:T(8,128)}) custom-call(f32[8,2048]{1,0:T(8,128)} %get-tuple-element.65.stats_ref, s32[8]{0:T(128)} %bitcast.105, s32[8]{0:T(128)} %bitcast.110, f32[8]{0:T(128)} %bitcast.111), custom_call_target="tpu_custom_call" | custom-call | tf_op jit(solution)/shard_map/pallas_call | solution.py:1386
  363.2 14.7 %fusion.1 = bf16[2048,3328]{1,0:T(8,128)(2,1)} fusion(bf16[8,256,3328]{2,1,0:T(8,128)(2,1)} %get-tuple-element.72, f32[2048]{0:T(1024)S(1)} %bitcast.86, f32[2048]{0:T(1024)S(1)} %bitcast.85, s32[3328]{0:T(1024)S(1)} %iota_add_fusion, s32[2048]{0:T(1024)S(1)} %bitcast.84), kind=kLoop, calls=%fused_computation.2 | loop fusion | flops 40894464 | bytes 27300864 | tf_op jit(solution)/shard_map/convert_element_type | solution.py:1689
  377.9 21.8 %convolution_convert_fusion = bf16[1024,3328]{1,0:T(8,128)(2,1)} fusion(bf16[2048,3328]{1,0:T(8,128)(2,1)} %fusion.1, bf16[2048,2048]{1,0:T(8,128)(2,1)} %bitcast.118, s32[]{:T(128)S(6)} %select_n.14), kind=kOutput, calls=%fused_computation.4 | convolution fusion | flops 13962051584 | bytes 24641540 | tf_op jit(solution)/shard_map/dot_general | solution.py:369
  399.8 20.6 %fusion.5 = f32[1024,3328]{1,0:T(8,128)S(1)} fusion(bf16[2048,3328]{1,0:T(8,128)(2,1)} %fusion.1, bf16[2048,2048]{1,0:T(8,128)(2,1)} %bitcast.119, s32[]{:T(128)S(6)} %select_n.12), kind=kOutput, calls=%fused_computation.10 | convolution fusion | flops 13958643712 | bytes 31457284 | tf_op jit(solution)/shard_map/dot_general | solution.py:369
  420.4 7.7 add_convert_fusion.refs_0_
  428.1 1.7 collective-permute-start.2
  429.8 97.8 %shard_map.319 = (f32[256,2048]{1,0:T(8,128)}, bf16[256,2048]{1,0:T(8,128)(2,1)}, f32[8,2048]{1,0:T(8,128)}) custom-call(bf16[1024,3328]{1,0:T(8,128)(2,1)} %add_convert_fusion.refs_0_, bf16[8,256,3328]{2,1,0:T(8,128)(2,1)} %bitcast.64, bf16[2048,3328]{1,0:T(8,128)(2,1)} %refs_2_.2, f32[256,2048]{1,0:T(8,128)} %get-tuple-element.73.refs_3_, ...), custom_call_target="tpu_custom_call" | custom-call | flops 27917287424 | bytes 268435456 | tf_op jit(solution)/shard_map/pallas_call | solution.py:597
  527.7 102.0 %shard_map.320 = (bf16[8,256,256]{2,1,0:T(8,128)(2,1)}, bf16[8,256,1024]{2,1,0:T(8,128)(2,1)}, f32[8,1024]{1,0:T(8,128)}, bf16[256,1024]{1,0:T(8,128)(2,1)}, bf1...) custom-call(bf16[256,2048]{1,0:T(8,128)(2,1)} %get-tuple-element.75., ...), custom_call_target="tpu_custom_call" | custom-call | flops 30064771072 | bytes 268435456 | tf_op jit(solution)/shard_map/pallas_call | solution.py:597
  629.7 9.9 %shard_map.322.refs_1_.refs_0_ = bf16[1024,3328]{1,0:T(8,128)(2,1)} custom-call(bf16[1024,3328]{1,0:T(8,128)(2,1)} %add_convert_fusion.refs_0_, bf16[1024,3328]{1,0:T(8,128)(2,1)} %collective-permute-done.2.refs_1_, f32[8,1024]{1,0:T(8,128)} %get-tuple-element.83.refs_2_), custom_call_target="tpu_custom_call" | custom-call | tf_op jit(solution)/shard_map/pallas_call | solution.py:1525
  640.1 34.3 %shard_map.321 = (bf16[2048,768]{1,0:T(8,128)(2,1)}, f32[2,1,384]{2,1,0:T(1,128)}) custom-call(s32[8]{0:T(128)} %bitcast.106, bf16[2048,768]{1,0:T(8,128)(2,1)} %bitcast.61, bf16[2048,768]{1,0:T(8,128)(2,1)} %bitcast.62, bf16[2048,768]{1,0:T(8,128)(2,1)} %bitcast.63, bf16[2048,256]{1,0:T(8,128)(2,1)} %get-tuple-element.62.ctx_ref, ...), custom_call_target="tpu_custom_call" | custom-call | tf_op jit(solution)/shard_map/pallas_call | solution.py:533
  674.5 6.8 fusion.9
  681.3 1.6 collective-permute-start.1
  682.9 3.9 add_convert_fusion.2.refs_1_
  687.3 4.1 add_convert_fusion.1.refs_2_
  692.7 5.3 fusion.7
  699.2 1.9 collective-permute-done.5
  702.1 1.3 collective-permute-start.8
  704.0 106.0 %shard_map.323 = (f32[256,2048]{1,0:T(8,128)}, f32[8,2048]{1,0:T(8,128)}) custom-call(bf16[1024,768]{1,0:T(8,128)(2,1)} %copy-done, bf16[1024,3328]{1,0:T(8,128)(2,1)} %shard_map.322.refs_1_.refs_0_, bf16[256,2048]{1,0:T(8,128)(2,1)} %bitcast.72, f32[256,2048]{1,0:T(8,128)} %get-tuple-element.84.refs_3_, bf16[8,256,2048]{2,1,0:T(8,128)(2,1)} %get-tuple-element.85.refs_4_, ...), custom_call_target="tpu_custom_call" | custom-call | flops 1 | bytes 1 | tf_op jit(solution)/shard_map/pallas_call | solution.py:597
  810.1 18.2 %shard_map.324.refs_8_ = f32[2048,3328]{1,0:T(8,128)} custom-call(s32[1]{0:T(128)} %bitcast.32.core_ref, bf16[1024,3328]{1,0:T(8,128)(2,1)} %shard_map.322.refs_1_.refs_0_, bf16[1024,3328]{1,0:T(8,128)(2,1)} %collective-permute-done.12.refs_1_, f32[8,2048]{1,0:T(8,128)} %get-tuple-element.89.refs_2_), custom_call_target="tpu_custom_call" | custom-call | tf_op jit(solution)/shard_map/pallas_call | solution.py:1574
  828.3 9.2 %shard_map.325 = (bf16[256,1024]{1,0:T(8,128)(2,1)}, bf16[1024,1024]{1,0:T(8,128)(2,1)}, bf16[1024,1024]{1,0:T(8,128)(2,1)}, bf16[1024,768]{1,0:T(8,128)(2,1)}) custom-call(bf16[256,1024]{1,0:T(8,128)(2,1)} %add_convert_fusion.4.refs_0_, bf16[1024,1024]{1,0:T(8,128)(2,1)} %add_convert_fusion.2.refs_1_, bf16[1024,1024]{1,0:T(8,128)(2,1)} %add_convert_fusion.1.refs_2_, ...), custom_call_target="tpu_custom_call" | custom-call | tf_op jit(solution)/shard_map/pallas_call | solution.py:1525
  839.4 2.5 collective-permute-done.3
  843.3 3.0 collective-permute-done.4
  850.9 17.7 %shard_map.326 = (f32[256,2048]{1,0:T(8,128)}, f32[1024,2048]{1,0:T(8,128)}, f32[2048,1024]{1,0:T(8,128)}, f32[2048,2,384]{2,1,0:T(2,128)}) custom-call(s32[1]{0:T(128)} %bitcast.32.core_ref, bf16[256,1024]{1,0:T(8,128)(2,1)} %get-tuple-element.97.refs_0_, bf16[1024,1024]{1,0:T(8,128)(2,1)} %get-tuple-element.98.refs_1_, ...), custom_call_target="tpu_custom_call" | custom-call | tf_op jit(solution)/shard_map/pallas_call | solution.py:1574
  868.6 2.3 copy.45
  871.0 3.1 copy.46
  (99 shorter events, 22.2 us)
Async XLA Ops:
  4.5 10.4 %copy-start.8 = (f32[2048]{0:T(1024)}, f32[2048]{0:T(1024)S(1)}, u32[]{:S(2)}) copy-start(f32[2048]{0:T(1024)S(1)} %broadcast_in_dim.104) | copy-start | bytes 24580
  5.9 9.7 %copy-start.10 = (f32[2048]{0:T(1024)}, f32[2048]{0:T(1024)S(1)}, u32[]{:S(2)}) copy-start(f32[2048]{0:T(1024)S(1)} %broadcast_in_dim.106) | copy-start | bytes 24580
  8.0 128.4 %copy-start.13 = (f32[2048]{0:T(1024)}, f32[2048]{0:T(1024)S(1)}, u32[]{:S(2)}) copy-start(f32[2048]{0:T(1024)S(1)} %broadcast_in_dim.109) | copy-start | bytes 24580
  245.3 117.9 %copy-start.12 = (s32[1,2048]{1,0:T(1,128)S(1)}, s32[1,2048]{1,0:T(1,128)}, u32[]{:S(2)}) copy-start(s32[1,2048]{1,0:T(1,128)} %param.20) | copy-start | bytes 24580
  399.7 20.8 %collective-permute-start = (bf16[1024,3328]{1,0:T(8,128)(2,1)}, bf16[1024,3328]{1,0:T(8,128)(2,1)}, u32[]{:S(2)}, u32[]{:S(2)}) collective-permute-start(bf16[1024,3328]{1,0:T(8,128)(2,1)} %convolution_convert_fusion), channel_id=1, source_target_pairs={{0,8},{8,0},{16,24},{24,16},{1,9},{9,1},{17,25},{25,17},{2,10},{10... | collective-permute-start | bytes 20447240 | tf_op jit(solution)/shard_map/ppermute | solution.py:1605
  428.1 201.6 %collective-permute-start.2 = (bf16[1024,3328]{1,0:T(8,128)(2,1)}, bf16[1024,3328]{1,0:T(8,128)(2,1)}, u32[]{:S(2)}, u32[]{:S(2)}) collective-permute-start(bf16[1024,3328]{1,0:T(8,128)(2,1)} %add_convert_fusion.refs_0_), channel_id=1, source_target_pairs={{0,16},{8,24},{16,0},{24,8},{1,17},{9,25},{17,1},{25,9},{2,18},{10... | collective-permute-start | bytes 20447240 | tf_op jit(solution)/shard_map/ppermute | solution.py:1614
  639.6 170.4 %collective-permute-start.12 = (bf16[1024,3328]{1,0:T(8,128)(2,1)}, bf16[1024,3328]{1,0:T(8,128)(2,1)}, u32[]{:S(2)}, u32[]{:S(2)}) collective-permute-start(bf16[1024,3328]{1,0:T(8,128)(2,1)} %shard_map.322.refs_1_.refs_0_), channel_id=1, source_target_pairs={{0,8},{8,0},{16,24},{24,16},{1,9},{9,1},{17,25},{25,17},{2,10},{10... | collective-permute-start | bytes 20447240 | tf_op jit(solution)/shard_map/ppermute | solution.py:1646
  639.6 43.3 %collective-permute-start.6 = (bf16[1024,1024]{1,0:T(8,128)(2,1)}, bf16[1024,1024]{1,0:T(8,128)(2,1)}, u32[]{:S(2)}, u32[]{:S(2)}) collective-permute-start(bf16[1024,1024]{1,0:T(8,128)(2,1)} %get-tuple-element.94), channel_id=1, source_target_pairs={{0,8},{8,0},{16,24},{24,16},{1,9},{9,1},{17,25},{25,17},{2,10},{10... | collective-permute-start | bytes 6291464 | tf_op jit(solution)/shard_map/ppermute | solution.py:1605
  640.1 47.2 %collective-permute-start.7 = (bf16[1024,1024]{1,0:T(8,128)(2,1)}, bf16[1024,1024]{1,0:T(8,128)(2,1)}, u32[]{:S(2)}, u32[]{:S(2)}) collective-permute-start(bf16[1024,1024]{1,0:T(8,128)(2,1)} %get-tuple-element.96), channel_id=1, source_target_pairs={{0,8},{8,0},{16,24},{24,16},{1,9},{9,1},{17,25},{25,17},{2,10},{10... | collective-permute-start | bytes 6291464 | tf_op jit(solution)/shard_map/ppermute | solution.py:1605
  674.5 8.4 copy-start.3
  681.3 6.0 copy-start.2
  681.3 16.7 %collective-permute-start.1 = (bf16[1024,768]{1,0:T(8,128)(2,1)S(1)}, bf16[1024,768]{1,0:T(8,128)(2,1)S(1)}, u32[]{:S(2)}, u32[]{:S(2)}) collective-permute-start(bf16[1024,768]{1,0:T(8,128)(2,1)S(1)} %fusion.9), channel_id=1, source_target_pairs={{0,8},{8,0},{16,24},{24,16},{1,9},{9,1},{17,25},{25,17},{2,10},{10... | collective-permute-start | bytes 4718600 | tf_op jit(solution)/shard_map/ppermute | solution.py:1605
  686.7 5.9 copy-start.1
  686.8 141.5 %collective-permute-start.9 = (bf16[1024,1024]{1,0:T(8,128)(2,1)}, bf16[1024,1024]{1,0:T(8,128)(2,1)}, u32[]{:S(2)}, u32[]{:S(2)}) collective-permute-start(bf16[1024,1024]{1,0:T(8,128)(2,1)} %add_convert_fusion.2.refs_1_), channel_id=1, source_target_pairs={{0,16},{8,24},{16,0},{24,8},{1,17},{9,25},{17,1},{25,9},{2,18},{10... | collective-permute-start | bytes 6291464 | tf_op jit(solution)/shard_map/ppermute | solution.py:1614
  691.4 136.9 %collective-permute-start.10 = (bf16[1024,1024]{1,0:T(8,128)(2,1)}, bf16[1024,1024]{1,0:T(8,128)(2,1)}, u32[]{:S(2)}, u32[]{:S(2)}) collective-permute-start(bf16[1024,1024]{1,0:T(8,128)(2,1)} %add_convert_fusion.1.refs_2_), channel_id=1, source_target_pairs={{0,16},{8,24},{16,0},{24,8},{1,17},{9,25},{17,1},{25,9},{2,18},{10... | collective-permute-start | bytes 6291464 | tf_op jit(solution)/shard_map/ppermute | solution.py:1614
  698.0 1.2 copy-start.16
  698.0 3.1 copy-start.6
  698.0 5.4 copy-start.9
  698.0 5.4 copy-start.11
  698.4 5.6 copy-start
  698.4 129.9 %collective-permute-start.11 = (bf16[1024,768]{1,0:T(8,128)(2,1)S(1)}, bf16[1024,768]{1,0:T(8,128)(2,1)}, u32[]{:S(2)}, u32[]{:S(2)}) collective-permute-start(bf16[1024,768]{1,0:T(8,128)(2,1)S(1)} %add_convert_fusion.3.refs_0_.refs_3_), channel_id=1, source_target_pairs={{0,16},{8,24},{16,0},{24,8},{1,17},{9,25},{17,1},{25,9},{2,18},{10... | collective-permute-start | bytes 4718600 | tf_op jit(solution)/shard_map/ppermute | solution.py:1614
  699.2 1.9 collective-permute-start.5
  702.1 126.1 %collective-permute-start.8 = (bf16[256,1024]{1,0:T(8,128)(2,1)}, bf16[256,1024]{1,0:T(8,128)(2,1)}, u32[]{:S(2)}, u32[]{:S(2)}) collective-permute-start(bf16[256,1024]{1,0:T(8,128)(2,1)} %add_convert_fusion.4.refs_0_), channel_id=1, source_target_pairs={{0,16},{8,24},{16,0},{24,8},{1,17},{9,25},{17,1},{25,9},{2,18},{10... | collective-permute-start | bytes 1572872 | tf_op jit(solution)/shard_map/ppermute | solution.py:1614
  828.2 9.8 %copy-start.15 = (f32[2,1,384]{2,1,0:T(1,128)S(1)}, f32[2,1,384]{2,1,0:T(1,128)}, u32[]{:S(2)}) copy-start(f32[2,1,384]{2,1,0:T(1,128)} %get-tuple-element.90) | copy-start | bytes 9220
  828.2 10.7 %copy-start.5 = (f32[8,2048]{1,0:T(8,128)S(1)}, f32[8,2048]{1,0:T(8,128)}, u32[]{:S(2)}) copy-start(f32[8,2048]{1,0:T(8,128)} %get-tuple-element.89.refs_2_) | copy-start | bytes 196612
  828.2 14.5 %copy-start.14 = (f32[8,128]{1,0:T(8,128)S(1)}, f32[8,128]{1,0:T(8,128)}, u32[]{:S(2)}) copy-start(f32[8,128]{1,0:T(8,128)} %get-tuple-element.66) | copy-start | bytes 12292
  837.4 12.4 %collective-permute-start.14 = (bf16[1024,1024]{1,0:T(8,128)(2,1)}, bf16[1024,1024]{1,0:T(8,128)(2,1)}, u32[]{:S(2)}, u32[]{:S(2)}) collective-permute-start(bf16[1024,1024]{1,0:T(8,128)(2,1)} %get-tuple-element.98.refs_1_), channel_id=1, source_target_pairs={{0,8},{8,0},{16,24},{24,16},{1,9},{9,1},{17,25},{25,17},{2,10},{10... | collective-permute-start | bytes 6291464 | tf_op jit(solution)/shard_map/ppermute | solution.py:1646
  837.5 12.3 %collective-permute-start.15 = (bf16[1024,1024]{1,0:T(8,128)(2,1)}, bf16[1024,1024]{1,0:T(8,128)(2,1)}, u32[]{:S(2)}, u32[]{:S(2)}) collective-permute-start(bf16[1024,1024]{1,0:T(8,128)(2,1)} %get-tuple-element.99.refs_2_), channel_id=1, source_target_pairs={{0,8},{8,0},{16,24},{24,16},{1,9},{9,1},{17,25},{25,17},{2,10},{10... | collective-permute-start | bytes 6291464 | tf_op jit(solution)/shard_map/ppermute | solution.py:1646
  838.0 11.0 %collective-permute-start.16 = (bf16[1024,768]{1,0:T(8,128)(2,1)}, bf16[1024,768]{1,0:T(8,128)(2,1)S(1)}, u32[]{:S(2)}, u32[]{:S(2)}) collective-permute-start(bf16[1024,768]{1,0:T(8,128)(2,1)} %get-tuple-element.100.refs_3_), channel_id=1, source_target_pairs={{0,8},{8,0},{16,24},{24,16},{1,9},{9,1},{17,25},{25,17},{2,10},{10... | collective-permute-start | bytes 4718600 | tf_op jit(solution)/shard_map/ppermute | solution.py:1646
  838.9 3.0 collective-permute-start.3
  841.9 4.3 collective-permute-start.4
  846.9 2.1 collective-permute-start.13
  (2 other events, 1.9 us)

commit v9 on v8

--- a/solution.py
+++ b/solution.py
@@ -358,6 +358,12 @@
 
 
 ATT_TILE = 256
+
+
+def span(index, size):
+    return pl.ds(pl.multiple_of(index * size, size), size)
+
+
 SCALE = HEAD_DIM ** (-0.5)
 
 
@@ -419,48 +425,51 @@
 def attention_forward(qkv, lengths, heads):
     tiles = BLOCK // ATT_TILE
 
-    def kernel(lengths_ref, q_ref, k_ref, v_ref, ctx_ref, lse_ref):
-        tile = pl.program_id(1)
-        queries = q_ref[...]
+    def kernel(lengths_ref, qkv_ref, ctx_ref, lse_ref):
+        tile = pl.program_id(0)
         start, first = tile_starts(lengths_ref, tile)
+        here = span(tile, ATT_TILE)
+        queries = [qkv_ref[here, 3 * head * HEAD_DIM : (3 * head + 1) * HEAD_DIM] for head in range(heads)]
 
         def step(key_tile, carry):
-            top, total, acc = carry
-            rows = pl.ds(pl.multiple_of(key_tile * ATT_TILE, ATT_TILE), ATT_TILE)
-            scores = dot_nt(queries, k_ref[rows, :]) * SCALE
-            scores = jnp.where(tile_mask(start, tile, key_tile), scores, -1e30)
-            new_top = jnp.maximum(top, jnp.max(scores, axis=1, keepdims=True))
-            shrink = jnp.exp(top - new_top)
-            weights = jnp.exp(scores - new_top)
-            total = total * shrink + jnp.sum(weights, axis=1, keepdims=True)
-            acc = acc * shrink + jnp.dot(
-                weights.astype(jnp.bfloat16), v_ref[rows, :], preferred_element_type=jnp.float32
-            )
-            return (new_top, total, acc)
+            rows = span(key_tile, ATT_TILE)
+            allowed = tile_mask(start, tile, key_tile)
+            found = []
+            for head in range(heads):
+                top, total, acc = carry[head]
+                keys = qkv_ref[rows, (3 * head + 1) * HEAD_DIM : (3 * head + 2) * HEAD_DIM]
+                values = qkv_ref[rows, (3 * head + 2) * HEAD_DIM : (3 * head + 3) * HEAD_DIM]
+                scores = jnp.where(allowed, dot_nt(queries[head], keys) * SCALE, -1e30)
+                new_top = jnp.maximum(top, jnp.max(scores, axis=1, keepdims=True))
+                shrink = jnp.exp(top - new_top)
+                weights = jnp.exp(scores - new_top)
+                total = total * shrink + jnp.sum(weights, axis=1, keepdims=True)
+                acc = acc * shrink + jnp.dot(
+                    weights.astype(jnp.bfloat16), values, preferred_element_type=jnp.float32
+                )
+                found.append((new_top, total, acc))
+            return tuple(found)
 
         begin = (
             jnp.full((ATT_TILE, 1), -1e30, jnp.float32),
             jnp.zeros((ATT_TILE, 1), jnp.float32),
             jnp.zeros((ATT_TILE, HEAD_DIM), jnp.float32),
         )
-        begin = step(tile, begin)
-        top, total, acc = lax.fori_loop(first, tile, step, begin)
-        ctx_ref[...] = (acc / total).astype(jnp.bfloat16)
-        lse_ref[...] = top + jnp.log(total)
+        result = lax.fori_loop(first, tile, step, step(tile, (begin,) * heads))
+        for head in range(heads):
+            top, total, acc = result[head]
+            ctx_ref[:, head * HEAD_DIM : (head + 1) * HEAD_DIM] = (acc / total).astype(jnp.bfloat16)
+            lse_ref[head] = top + jnp.log(total)
 
     return pl.pallas_call(
         kernel,
         grid_spec=pltpu.PrefetchScalarGridSpec(
             num_scalar_prefetch=1,
-            grid=(heads, tiles),
-            in_specs=[
-                pl.BlockSpec((ATT_TILE, HEAD_DIM), lambda h, i, first: (i, 3 * h)),
-                pl.BlockSpec((BLOCK, HEAD_DIM), lambda h, i, first: (0, 3 * h + 1)),
-                pl.BlockSpec((BLOCK, HEAD_DIM), lambda h, i, first: (0, 3 * h + 2)),
-            ],
+            grid=(tiles,),
+            in_specs=[pl.BlockSpec(qkv.shape, lambda i, lengths: (0, 0))],
             out_specs=[
-                pl.BlockSpec((ATT_TILE, HEAD_DIM), lambda h, i, first: (i, h)),
-                pl.BlockSpec((pl.squeezed, ATT_TILE, 1), lambda h, i, first: (h, i, 0)),
+                pl.BlockSpec((ATT_TILE, heads * HEAD_DIM), lambda i, lengths: (i, 0)),
+                pl.BlockSpec((heads, ATT_TILE, 1), lambda i, lengths: (0, i, 0)),
             ],
         ),
         out_shape=[
@@ -468,100 +477,106 @@
             jax.ShapeDtypeStruct((heads, BLOCK, 1), jnp.float32),
         ],
         compiler_params=pltpu.CompilerParams(vmem_limit_bytes=VMEM_LIMIT),
-    )(lengths, qkv, qkv, qkv)
-
-
-def attention_backward(qkv, lengths, heads, ctx, lse, grad_ctx, planes, before):
+    )(lengths, qkv)
+
+
+def attention_backward(qkv, lengths, heads, ctx, lse, grad_ctx, planes):
     tiles = BLOCK // ATT_TILE
 
     def kernel(
-        lengths_ref, q_ref, k_ref, v_ref, ctx_ref, lse_ref, do_ref, cos_ref, below_ref,
-        above_ref, *rest,
+        lengths_ref, qkv_ref, ctx_ref, lse_ref, do_ref, cos_ref, below_ref, above_ref, out_ref, sums_ref, dk_ref,
+        dv_ref,
     ):
-        out_ref, sums_ref, dk_ref, dv_ref = rest[len(before) :]
-        tile = pl.program_id(1)
+        tile = pl.program_id(0)
 
         @pl.when(tile == 0)
         def _():
             dk_ref[...] = jnp.zeros_like(dk_ref)
             dv_ref[...] = jnp.zeros_like(dv_ref)
 
-        queries = q_ref[...]
         start, first = tile_starts(lengths_ref, tile)
-        grads = do_ref[...]
-        lse_rows = lse_ref[...]
-        inner = jnp.sum(
-            grads.astype(jnp.float32) * ctx_ref[...].astype(jnp.float32), axis=1, keepdims=True
-        )
-
-        def step(key_tile, dq):
-            rows = pl.ds(pl.multiple_of(key_tile * ATT_TILE, ATT_TILE), ATT_TILE)
-            keys = k_ref[rows, :]
-            scores = dot_nt(queries, keys) * SCALE
-            probs = jnp.where(
-                tile_mask(start, tile, key_tile), jnp.exp(scores - lse_rows), 0.0
+        here = span(tile, ATT_TILE)
+        fixed = []
+        for head in range(heads):
+            lanes = slice(head * HEAD_DIM, (head + 1) * HEAD_DIM)
+            grads = do_ref[:, lanes]
+            inner = jnp.sum(
+                grads.astype(jnp.float32) * ctx_ref[:, lanes].astype(jnp.float32), axis=1, keepdims=True
             )
-            grad_probs = dot_nt(grads, v_ref[rows, :])
-            grad_scores = (probs * (grad_probs - inner)).astype(jnp.bfloat16)
-            dv_ref[rows, :] += dot_tn(probs.astype(jnp.bfloat16), grads)
-            dk_ref[rows, :] += dot_tn(grad_scores, queries)
-            return dq + jnp.dot(grad_scores, keys, preferred_element_type=jnp.float32)
-
-        dq = lax.fori_loop(
-            first, tile + 1, step, jnp.zeros((ATT_TILE, HEAD_DIM), jnp.float32)
-        )
-        here = pl.ds(pl.multiple_of(tile * ATT_TILE, ATT_TILE), ATT_TILE)
-        out_ref[here, :HEAD_DIM] = turn(
-            dq * SCALE, cos_ref[here, :], -below_ref[here, :], -above_ref[here, :]
-        ).astype(jnp.bfloat16)
+            queries = qkv_ref[here, 3 * head * HEAD_DIM : (3 * head + 1) * HEAD_DIM]
+            fixed.append((queries, grads, inner, lse_ref[head]))
+
+        def step(key_tile, carry):
+            rows = span(key_tile, ATT_TILE)
+            allowed = tile_mask(start, tile, key_tile)
+            found = []
+            for head in range(heads):
+                queries, grads, inner, lse_rows = fixed[head]
+                lanes = slice(head * HEAD_DIM, (head + 1) * HEAD_DIM)
+                keys = qkv_ref[rows, (3 * head + 1) * HEAD_DIM : (3 * head + 2) * HEAD_DIM]
+                values = qkv_ref[rows, (3 * head + 2) * HEAD_DIM : (3 * head + 3) * HEAD_DIM]
+                scores = dot_nt(queries, keys) * SCALE
+                probs = jnp.where(allowed, jnp.exp(scores - lse_rows), 0.0)
+                grad_scores = (probs * (dot_nt(grads, values) - inner)).astype(jnp.bfloat16)
+                dv_ref[rows, lanes] += dot_tn(probs.astype(jnp.bfloat16), grads)
+                dk_ref[rows, lanes] += dot_tn(grad_scores, queries)
+                found.append(carry[head] + jnp.dot(grad_scores, keys, preferred_element_type=jnp.float32))
+            return tuple(found)
+
+        none = jnp.zeros((ATT_TILE, HEAD_DIM), jnp.float32)
+        result = lax.fori_loop(first, tile + 1, step, (none,) * heads)
+        for head in range(heads):
+            out_ref[here, 3 * head * HEAD_DIM : (3 * head + 1) * HEAD_DIM] = turn(
+                result[head] * SCALE, cos_ref[here, :], -below_ref[here, :], -above_ref[here, :]
+            ).astype(jnp.bfloat16)
 
         @pl.when(tile == tiles - 1)
         def _():
             def finish(index, sums):
-                rows = pl.ds(pl.multiple_of(index * ATT_TILE, ATT_TILE), ATT_TILE)
-                out_ref[rows, HEAD_DIM : 2 * HEAD_DIM] = turn(
-                    dk_ref[rows, :] * SCALE, cos_ref[rows, :], -below_ref[rows, :], -above_ref[rows, :]
-                ).astype(jnp.bfloat16)
-                out_ref[rows, 2 * HEAD_DIM :] = dv_ref[rows, :].astype(jnp.bfloat16)
+                rows = span(index, ATT_TILE)
+                for head in range(heads):
+                    lanes = slice(head * HEAD_DIM, (head + 1) * HEAD_DIM)
+                    out_ref[rows, (3 * head + 1) * HEAD_DIM : (3 * head + 2) * HEAD_DIM] = turn(
+                        dk_ref[rows, lanes] * SCALE, cos_ref[rows, :], -below_ref[rows, :], -above_ref[rows, :]
+                    ).astype(jnp.bfloat16)
+                    out_ref[rows, (3 * head + 2) * HEAD_DIM : (3 * head + 3) * HEAD_DIM] = dv_ref[rows, lanes].astype(
+                        jnp.bfloat16
+                    )
                 return sums + jnp.sum(out_ref[rows, :].astype(jnp.float32), axis=0, keepdims=True)
 
             sums_ref[...] = lax.fori_loop(
-                0, tiles, finish, jnp.zeros((1, 3 * HEAD_DIM), jnp.float32)
+                0, tiles, finish, jnp.zeros((1, 3 * heads * HEAD_DIM), jnp.float32)
             )
 
-    whole = pl.BlockSpec((BLOCK, HEAD_DIM), lambda h, i, first: (0, 0))
+    def whole(shape):
+        return pl.BlockSpec(shape, lambda i, lengths: (0,) * len(shape))
+
     return pl.pallas_call(
         kernel,
         grid_spec=pltpu.PrefetchScalarGridSpec(
             num_scalar_prefetch=1,
-            grid=(heads, tiles),
+            grid=(tiles,),
             in_specs=[
-                pl.BlockSpec((ATT_TILE, HEAD_DIM), lambda h, i, first: (i, 3 * h)),
-                pl.BlockSpec((BLOCK, HEAD_DIM), lambda h, i, first: (0, 3 * h + 1)),
-                pl.BlockSpec((BLOCK, HEAD_DIM), lambda h, i, first: (0, 3 * h + 2)),
-                pl.BlockSpec((ATT_TILE, HEAD_DIM), lambda h, i, first: (i, h)),
-                pl.BlockSpec((pl.squeezed, ATT_TILE, 1), lambda h, i, first: (h, i, 0)),
-                pl.BlockSpec((ATT_TILE, HEAD_DIM), lambda h, i, first: (i, h)),
-                whole,
-                whole,
-                whole,
-            ]
-            + [pl.BlockSpec(memory_space=pl.ANY)] * len(before),
-            out_specs=[
-                pl.BlockSpec((BLOCK, 3 * HEAD_DIM), lambda h, i, first: (0, h)),
-                pl.BlockSpec((pl.squeezed, 1, 3 * HEAD_DIM), lambda h, i, first: (h, 0, 0)),
+                whole(qkv.shape),
+                pl.BlockSpec((ATT_TILE, heads * HEAD_DIM), lambda i, lengths: (i, 0)),
+                pl.BlockSpec((heads, ATT_TILE, 1), lambda i, lengths: (0, i, 0)),
+                pl.BlockSpec((ATT_TILE, heads * HEAD_DIM), lambda i, lengths: (i, 0)),
+                whole((BLOCK, HEAD_DIM)),
+                whole((BLOCK, HEAD_DIM)),
+                whole((BLOCK, HEAD_DIM)),
             ],
+            out_specs=[whole(qkv.shape), whole((1, qkv.shape[1]))],
             scratch_shapes=[
-                pltpu.VMEM((BLOCK, HEAD_DIM), jnp.float32),
-                pltpu.VMEM((BLOCK, HEAD_DIM), jnp.float32),
+                pltpu.VMEM((BLOCK, heads * HEAD_DIM), jnp.float32),
+                pltpu.VMEM((BLOCK, heads * HEAD_DIM), jnp.float32),
             ],
         ),
         out_shape=[
-            jax.ShapeDtypeStruct((BLOCK, heads * 3 * HEAD_DIM), jnp.bfloat16),
-            jax.ShapeDtypeStruct((heads, 1, 3 * HEAD_DIM), jnp.float32),
+            jax.ShapeDtypeStruct(qkv.shape, jnp.bfloat16),
+            jax.ShapeDtypeStruct((1, qkv.shape[1]), jnp.float32),
         ],
         compiler_params=pltpu.CompilerParams(vmem_limit_bytes=VMEM_LIMIT),
-    )(lengths, qkv, qkv, qkv, ctx, lse, grad_ctx, *planes, *before)
+    )(lengths, qkv, ctx, lse, grad_ctx, *planes)
 
 
 def gather_cut(sizes):
@@ -578,10 +593,6 @@
 
 def tile_of(width):
     return 512 if width % 512 == 0 else 256 if width % 256 == 0 else 128
-
-
-def span(index, size):
-    return pl.ds(pl.multiple_of(index * size, size), size)
 
 
 ANY = pl.BlockSpec(memory_space=pl.ANY)
@@ -1064,7 +1075,7 @@
     )(grad_logits, head_weight, normed, inverse, gain)
 
 
-def branch_grad_rows(own, out_flat, down_weight, slope, ctx, act, second, sizes, collective):
+def branch_grad_rows(own, out_flat, down_weight, slope, ctx, act, second, sizes, collective, before):
     rows = own.shape[0]
     shards = sizes[0] * sizes[1]
     inner, hidden = out_flat.shape[0], down_weight.shape[0]
@@ -1072,7 +1083,7 @@
 
     def kernel(
         own_ref, outw_any, downw_any, slope_any, ctx_any, act_any, second_any,
-        grad_ctx_any, grad_up_any, sums_ref, out_away, out_mine, down_away, down_mine, up_away, up_mine,
+        grad_ctx_any, grad_up_any, sums_ref, stream_away, stream_mine, up_away, up_mine,
         full, send_sems, recv_sems, outw, downw, load_sems, slope, slope_sem, grad_ctx, grad_up, out_sems,
         ctx, act, second, row_sems, out_total, down_total, up_total, part_sems,
     ):
@@ -1178,12 +1189,12 @@
             copy.start()
             stores.append(copy)
 
-        for which, wide in ((1 - core, (out_away, down_away, up_away)), (core, (out_mine, down_mine, up_mine))):
-            for total, there, count in ((out_total, wide[0], inner), (down_total, wide[1], hidden)):
+        for which, wide in ((1 - core, (stream_away, up_away)), (core, (stream_mine, up_mine))):
+            for total, begin, count in ((out_total, 0, inner), (down_total, inner, hidden)):
                 for height in range(0, count, rows):
-                    store(total, there, height, which * half_width, height, half_width)
+                    store(total, wide[0], height, which * half_width, begin + height, half_width)
             for height in range(0, half_width, rows):
-                store(up_total, wide[2], which * half_width + height, 0, height, hidden)
+                store(up_total, wide[1], which * half_width + height, 0, height, hidden)
         for copy in stores:
             copy.wait()
 
@@ -1192,7 +1203,7 @@
 
     parts = [
         jax.ShapeDtypeStruct(shape, jnp.bfloat16)
-        for shape in ((inner, half_width), (hidden, half_width), (half_width, hidden))
+        for shape in ((inner + hidden, half_width), (half_width, hidden))
         for _ in range(2)
     ]
     stores = 2 * (inner // rows + hidden // rows + half_width // rows)
@@ -1200,7 +1211,7 @@
         kernel, collective,
         [out(inner), out(hidden), jax.ShapeDtypeStruct((8, hidden), jnp.float32)] + parts,
         [VMEM] + [ANY] * 6,
-        [ANY, ANY, VMEM] + [ANY] * 6,
+        [ANY, ANY, VMEM] + [ANY] * 4,
         gather_scratch(sizes, rows)
         + [
             pltpu.VMEM(out_flat.shape, jnp.bfloat16),
@@ -1221,6 +1232,7 @@
             pltpu.SemaphoreType.DMA((stores,)),
         ],
         4 * BLOCK * D * (inner + hidden) + 2 * BLOCK * D * hidden,
+        before,
     )(own, out_flat, down_weight, slope, ctx, act, second)
 
 
@@ -1512,73 +1524,100 @@
     )(own, grad_stream, plain, grad_qkv, grad_up, qkv_flat, up_weight, gains, end_sums)
 
 
-def join_halves(sums, others, earlier):
-    steps, count = 8, len(sums)
-
-    def kernel(*refs):
-        for i in range(count):
-            refs[2 * count + 1 + i][...] = (
-                refs[i][...].astype(jnp.float32) + refs[count + i][...].astype(jnp.float32)
-            ).astype(jnp.bfloat16)
-
-    specs = [pl.BlockSpec((v.shape[0] // steps, v.shape[1]), lambda i: (i, 0)) for v in sums]
+def settle_halves(core, mine, backs, shapes, places, before=()):
+    depth, most = 4, 256
+    count = len(mine[0])
+    steps = []
+    for index, (_, _, rows) in enumerate(places):
+        size = min(most, rows)
+        for which in (0, 1):
+            for first in range(0, rows, size):
+                steps.append((index, which, first, size))
+    width = max(arrays[0].shape[1] for arrays in mine)
+    deep = [shape for shape in shapes if len(shape) == 3]
+
+    def kernel(core_ref, *refs):
+        sources = [
+            [refs[(index * 2 + which) * count : (index * 2 + which + 1) * count] for which in (0, 1)]
+            for index, _, _ in places
+        ]
+        rest = refs[2 * count * len(mine) + len(before) :]
+        outs, (taken, given, split, in_sems, out_sems) = rest[: len(shapes)], rest[len(shapes) :]
+
+        def loads(i):
+            index, which, first, size = steps[i]
+            number, begin, _ = places[index]
+            columns = mine[number][0].shape[1]
+            return [
+                pltpu.make_async_copy(
+                    source.at[pl.ds(begin + first, size)],
+                    taken.at[i % depth, j, pl.ds(0, size), pl.ds(0, columns)],
+                    in_sems.at[i % depth, j],
+                )
+                for j, source in enumerate(sources[index][which])
+            ]
+
+        def store(i):
+            index, which, first, size = steps[i]
+            number, _, rows = places[index]
+            columns = mine[number][0].shape[1]
+            place = core_ref[0] if which == 0 else 1 - core_ref[0]
+            if len(shapes[index]) == 2 and shapes[index][0] == rows:
+                there = outs[index].at[pl.ds(first, size), pl.ds(pl.multiple_of(place * columns, columns), columns)]
+            else:
+                there = outs[index].at[pl.ds(pl.multiple_of(place * rows + first, size), size)]
+            here = given.at[i % depth, pl.ds(0, size), pl.ds(0, columns)]
+            if len(shapes[index]) == 3:
+                here = split.at[i % depth, pl.ds(0, size)]
+            return pltpu.make_async_copy(here, there, out_sems.at[i % depth])
+
+        for i in range(min(depth - 1, len(steps))):
+            for copy in loads(i):
+                copy.start()
+        for i, (index, which, first, size) in enumerate(steps):
+            if i + depth - 1 < len(steps):
+                for copy in loads(i + depth - 1):
+                    copy.start()
+            for copy in loads(i):
+                copy.wait()
+            if i >= depth:
+                store(i - depth).wait()
+            columns = mine[places[index][0]][0].shape[1]
+
+            def convert(row, _, i=i, index=index, columns=columns):
+                here = span(row, 32)
+                found = taken[i % depth, 0, here, :columns].astype(jnp.float32)
+                for j in range(1, count):
+                    found = found + taken[i % depth, j, here, :columns].astype(jnp.float32)
+                if len(shapes[index]) == 3:
+                    for head in range(shapes[index][1]):
+                        split[i % depth, here, head, :] = found[
+                            :, head * shapes[index][2] : (head + 1) * shapes[index][2]
+                        ]
+                else:
+                    given[i % depth, here, :columns] = found
+                return _
+
+            lax.fori_loop(0, size // 32, convert, 0)
+            store(i).start()
+        for i in range(max(len(steps) - depth, 0), len(steps)):
+            store(i).wait()
+
+    dma = pltpu.SemaphoreType.DMA
     return pl.pallas_call(
         kernel,
-        grid=(steps,),
-        out_shape=[jax.ShapeDtypeStruct(v.shape, jnp.bfloat16) for v in sums],
-        in_specs=specs + specs + [ANY],
-        out_specs=specs,
+        out_shape=[jax.ShapeDtypeStruct(shape, jnp.float32) for shape in shapes],
+        in_specs=[SMEM] + [ANY] * (2 * count * len(mine) + len(before)),
+        out_specs=[ANY] * len(shapes),
+        scratch_shapes=[
+            pltpu.VMEM((depth, count, most, width), jnp.bfloat16),
+            pltpu.VMEM((depth, most, width), jnp.float32),
+            pltpu.VMEM((depth, most) + deep[0][1:] if deep else (1, 8, 128), jnp.float32),
+            dma((depth, count)),
+            dma((depth,)),
+        ],
         compiler_params=pltpu.CompilerParams(vmem_limit_bytes=VMEM_LIMIT),
-    )(*sums, *others, earlier)
-
-
-def settle_halves(core, totals, backs, shapes, before=()):
-    steps = 8
-
-    def kernel(core_ref, *refs):
-        count = len(totals)
-        mine = pl.program_id(0) == 0
-        for i in range(count):
-            found = jnp.where(mine, refs[i][...].astype(jnp.float32), refs[count + i][...].astype(jnp.float32))
-            out = refs[2 * count + len(before) + i]
-            if len(out.shape) == 3:
-                for head in range(out.shape[1]):
-                    out[:, head, :] = found[:, head * out.shape[2] : (head + 1) * out.shape[2]]
-            else:
-                out[...] = found
-
-    def place(half, core_ref):
-        return jnp.where(half == 0, core_ref[0], 1 - core_ref[0])
-
-    ins, outs = [], []
-    for which in (0, 1):
-        for value in totals:
-            ins.append(
-                pl.BlockSpec(
-                    (value.shape[0] // steps, value.shape[1]),
-                    (lambda h, i, core_ref: (jnp.where(h == 0, i, steps - 1), 0))
-                    if which == 0
-                    else (lambda h, i, core_ref: (jnp.where(h == 0, 0, i), 0)),
-                )
-            )
-    for value, shape in zip(totals, shapes):
-        rows = value.shape[0] // steps
-        if len(shape) == 3:
-            outs.append(
-                pl.BlockSpec((rows,) + shape[1:], lambda h, i, core_ref: (place(h, core_ref) * steps + i, 0, 0))
-            )
-        elif shape[0] == value.shape[0]:
-            outs.append(pl.BlockSpec((rows, value.shape[1]), lambda h, i, core_ref: (i, place(h, core_ref))))
-        else:
-            outs.append(pl.BlockSpec((rows, shape[1]), lambda h, i, core_ref: (place(h, core_ref) * steps + i, 0)))
-    return pl.pallas_call(
-        kernel,
-        grid_spec=pltpu.PrefetchScalarGridSpec(
-            num_scalar_prefetch=1, grid=(2, steps), in_specs=ins + [ANY] * len(before), out_specs=outs
-        ),
-        out_shape=[jax.ShapeDtypeStruct(shape, jnp.float32) for shape in shapes],
-        compiler_params=pltpu.CompilerParams(vmem_limit_bytes=VMEM_LIMIT),
-    )(core, *totals, *backs, *before)
+    )(core, *[array for pair in zip(mine, backs) for half in pair for array in half], *before)
 
 
 def row_of(vector):
@@ -1609,14 +1648,44 @@
         if self.plain:
             none = jnp.zeros_like(self.sum)
             both = jnp.stack([jnp.where(self.core == which, self.sum, none) for which in (0, 1)])
-            self.other = lax.psum(both, "dp")
+            self.other, self.first_back = lax.psum(both, "dp"), self.sum
         else:
             self.other = lax.ppermute(self.sum, "dp", pairs(2))
+            self.first_back = lax.ppermute(self.sum, "dp", pairs(1))
         return self
 
-    def join(self, earlier):
-        self.total = self.other if self.plain else join_halves([self.sum], [self.other], earlier)[0]
-        return self
+
+def after(values, earlier):
+    def kernel(*refs):
+        del refs
+
+    return pl.pallas_call(
+        kernel,
+        out_shape=[jax.ShapeDtypeStruct(v.shape, v.dtype) for v in values],
+        in_specs=[ANY] * (len(values) + 1),
+        out_specs=[ANY] * len(values),
+        input_output_aliases={i: i for i in range(len(values))},
+    )(*values, earlier)
+
+
+def give_back(sums, earlier):
+    if sums[0].plain:
+        for one in sums:
+            one.mine, one.back = [one.other[0]], [one.other[1]]
+        return
+    for one, other in zip(sums, after([one.other for one in sums], earlier)):
+        one.mine = [one.sum, other]
+        one.back = [one.first_back, lax.ppermute(other, "dp", pairs(1))]
+
+
+def settle_all(sums, shapes, places, before=()):
+    core = jnp.zeros((1,), jnp.int32) if sums[0].plain else sums[0].core[None]
+    return settle_halves(core, [one.mine for one in sums], [one.back for one in sums], shapes, places, before)
+
+
+def pair_product(product):
+    core = lax.rem(lax.axis_index("dp"), 2)
+    return PairSum(product(1 - core).astype(jnp.bfloat16), held(product(core)))
 
 
 def sum_over_dp(values):
@@ -1625,26 +1694,6 @@
     for step in (1, 2):
         values = values + lax.ppermute(values, "dp", pairs(step))
     return values
-
-
-def pair_product(product):
-    core = lax.rem(lax.axis_index("dp"), 2)
-    return PairSum(product(1 - core).astype(jnp.bfloat16), held(product(core)))
-
-
-def join_all(sums, earlier):
-    if not sums[0].plain:
-        totals = join_halves([one.sum for one in sums], [one.other for one in sums], earlier)
-        for one, total in zip(sums, totals):
-            one.total = total
-
-
-def settle_all(sums, shapes, before=()):
-    if sums[0].plain:
-        core = jnp.zeros((1,), jnp.int32)
-        return settle_halves(core, [s.other[0] for s in sums], [s.other[1] for s in sums], shapes, before)
-    backs = [lax.ppermute(one.total, "dp", pairs(1)) for one in sums]
-    return settle_halves(sums[0].core[None], [one.total for one in sums], backs, shapes, before)
 
 
 def per_device(
@@ -1695,30 +1744,34 @@
         (head_sum.sum,),
     )
     grad_ctx, grad_up, up_sums, *halves = branch_grad_rows(
-        grad_own, out_flat, down_weight, slope, ctx.reshape(shards, rows, inner), act, second_full, sizes, 4
+        grad_own, out_flat, down_weight, slope, ctx.reshape(shards, rows, inner), act, second_full, sizes, 4,
+        (head_sum.first_back,),
     )
-    sums = [PairSum(*halves[2 * i : 2 * i + 2]).cross() for i in range(3)]
+    sums = [PairSum(*halves[2 * i : 2 * i + 2]).cross() for i in range(2)]
     grad_qkv, qkv_sums = attention_backward(
-        flat_qkv, block_lengths, local_heads, ctx, lse, grad_ctx.reshape(BLOCK, inner), planes,
-        (),
+        flat_qkv, block_lengths, local_heads, ctx, lse, grad_ctx.reshape(BLOCK, inner), planes
     )
     first_rows = first_full.reshape(BLOCK, D)
     sums.append(pair_product(lambda which: dot_tn(half_of(first_rows, which), grad_qkv)).cross())
-    qkv_sums = qkv_sums[:, 0]
+    qkv_sums = qkv_sums.reshape(local_heads, 3 * HEAD_DIM)
     qv_grad = jnp.concatenate([qkv_sums[:, :HEAD_DIM], qkv_sums[:, 2 * HEAD_DIM :]], axis=-1)
     split = local_heads * 2 * HEAD_DIM
     biases = jnp.concatenate([qv_grad.reshape(-1), up_sums[0]])
     biases = jnp.pad(biases[None, :], ((0, 0), (0, D - biases.shape[0])))
+    give_back([head_sum], grad_qkv)
     gains = jnp.concatenate([row_of(ln1_gain), row_of(ln2_gain)], axis=0)
     grad_input, group_sums = input_grad_rows(
         own, grad_stream, plain, grad_qkv.reshape(shards, rows, width), grad_up, qkv_flat, up_weight, gains,
-        end_sums, sizes, 5, (sums[-1].sum, head_sum.join(up_sums).total),
+        end_sums, sizes, 5, [one.first_back for one in sums],
     )
-    (head_grad,) = settle_all([head_sum], [(D, local_vocab)], (group_sums,))
-    join_all(sums, head_grad)
+    give_back(sums[:2], group_sums)
+    (head_grad,) = settle_all([head_sum], [(D, local_vocab)], [(0, 0, D // 2)], (group_sums,))
+    give_back(sums[2:], head_grad)
     small = sum_over_dp(jnp.concatenate([group_sums[:7], biases], axis=0))
     out_grad, down_grad, up_grad, qkv_grad = settle_all(
-        sums, [(inner, D), (local_hidden, D), (D, local_hidden), qkv_weight.shape]
+        sums,
+        [(inner, D), (local_hidden, D), (D, local_hidden), qkv_weight.shape],
+        [(0, 0, inner), (0, inner, local_hidden), (1, 0, D // 2), (2, 0, D // 2)],
     )
     return (
         losses[:, 0][None],

time: 888 us -> 869 us (0.979)
  Pallas kernels: 741 us -> 715 us
    pallas_call x4 -> x5, Pallas kernels: 55 us -> 36.8 us  [the longest x2 36.8 us: settle_halves(): pl.pallas_call(kernel, out_shape=[jax.ShapeDtypeStruct(shape, jnp.float32...]
    convert_element_type x5 -> x4, other arithmetic: 17 us -> 18 us  [__init__(): (mine.astype(jnp.float32) + came.astype(jnp.float32)).astype(jnp.bfloat16)]
  transfers between devices with their start and end apart: 17 -> 18, of which waited for: 4 -> 4; matrix products, arithmetic and copies ran while one was open for 5% -> 5% of each run, Pallas kernels for 41% -> 42%
where the time goes in v9:
time: 869 us; the launch traced here: 852 us
  Pallas kernels  715 us (82%)
  matrix products  53.7 us (6%)
  other arithmetic  40.8 us (5%)
  local copies, waits for them, and re-layouts  20.7 us (2%)
  waiting for transfers between devices  11.6 us (1%)
  starting transfers between devices  9.04 us (1%)
    pallas_call x6, Pallas kernels, call(): pl.pallas_call(body, out_shape=out_shape, in_specs=[ANY] * len(before) +...  603 us
    dot_general x4, matrix products, dot_tn(): lax.dot_general(left, right, (((0,), (0,)), ((), ())), preferred_element_...  53.7 us
    pallas_call x2, Pallas kernels, settle_halves(): pl.pallas_call(kernel, out_shape=[jax.ShapeDtypeStruct(shape, jnp.float32...  36.8 us
    pallas_call x1, Pallas kernels, attention_backward(): pl.pallas_call(kernel, grid_spec=pltpu.PrefetchScalarGridSpec(num_scalar_...  30.1 us
    pallas_call x1, Pallas kernels, score_rows(): pl.pallas_call(kernel, out_shape=[jax.ShapeDtypeStruct((8, BLOCK), jnp.fl...  24.6 us
    pallas_call x1, Pallas kernels, attention_forward(): pl.pallas_call(kernel, grid_spec=pltpu.PrefetchScalarGridSpec(num_scalar_...  20.8 us
    convert_element_type x4, other arithmetic, __init__(): (mine.astype(jnp.float32) + came.astype(jnp.float32)).astype(jnp.bfloat16)  18 us
  transfers between devices with their start and end apart: 18, of which 4 were waited for; matrix products, arithmetic and copies ran while one was open for 5% of the time, Pallas kernels for 42%

profile of v9, /device:TPU:0, one launch (start us, length us, event | category | flops | bytes accessed | tf_op | source)
XLA Modules:
  0.0 852.0 jit_solution(15341591300076406422)
XLA Ops:
  2.6 1.3 broadcast_in_dim.108
  8.7 2.0 copy.40.refs_2_
  10.7 4.2 copy.41
  15.6 97.4 %shard_map.314 = (bf16[8,256,2048]{2,1,0:T(8,128)(2,1)}, bf16[8,256,2048]{2,1,0:T(8,128)(2,1)}, bf16[8,256,2048]{2,1,0:T(8,128)(2,1)}, bf16[8,256,768]{2,1,0:T(8...) custom-call(bf16[256,2048]{1,0:T(8,128)(2,1)} %bitcast.65, ...), custom_call_target="tpu_custom_call" | custom-call | flops 15032385536 | bytes 268435456 | tf_op jit(solution)/shard_map/pallas_call | solution.py:608
  113.0 20.8 %shard_map.315 = (bf16[2048,256]{1,0:T(8,128)(2,1)}, f32[2,2048,1]{2,1,0:T(8,128)}) custom-call(s32[8]{0:T(128)} %bitcast.96, bf16[2048,768]{1,0:T(8,128)(2,1)} %bitcast.59), custom_call_target="tpu_custom_call" | custom-call | tf_op jit(solution)/shard_map/pallas_call | solution.py:464
  134.4 100.0 %shard_map.316 = (bf16[256,2048]{1,0:T(8,128)(2,1)}, bf16[256,2048]{1,0:T(8,128)(2,1)}, f32[256,2048]{1,0:T(8,128)}, f32[256,1]{1,0:T(8,128)}) custom-call(bf16[256,2048]{1,0:T(8,128)(2,1)} %bitcast.66, bf16[8,256,256]{2,1,0:T(8,128)(2,1)} %bitcast.69, bf16[8,256,1024]{2,1,0:T(8,128)(2,1)} %get-tuple-element.59.refs_2_.refs_6_, bf16[256,2048]{1,0:T(8,128)(2,1)} %bitcast.106, ...), custom_call_target="tpu_custom_call" | custom-call | flops 10737418240 | bytes 268435456 | tf_op jit(solution)/shard_map/pallas_call | solution.py:608
  234.4 98.8 %shard_map.317 = (bf16[8,256,2048]{2,1,0:T(8,128)(2,1)}, bf16[8,256,3328]{2,1,0:T(8,128)(2,1)}, f32[8,2048]{1,0:T(8,128)}) custom-call(bf16[256,2048]{1,0:T(8,128)(2,1)} %get-tuple-element.60.refs_0_, bf16[2048,3328]{1,0:T(8,128)(2,1)} %refs_2_.1, s32[2048,1]{1,0:T(8,128)} %copy.40.refs_2_), custom_call_target="tpu_custom_call" | custom-call | flops 27917287424 | bytes 268435456 | tf_op jit(solution)/shard_map/pallas_call | solution.py:608
  333.2 24.6 %shard_map.318 = (f32[8,2048]{1,0:T(8,128)}, f32[8,128]{1,0:T(8,128)}) custom-call(f32[8,2048]{1,0:T(8,128)} %get-tuple-element.61.stats_ref, s32[8]{0:T(128)} %bitcast.97, s32[8]{0:T(128)} %bitcast.102, f32[8]{0:T(128)} %bitcast.103), custom_call_target="tpu_custom_call" | custom-call | tf_op jit(solution)/shard_map/pallas_call | solution.py:1398
  358.8 14.7 %fusion.1 = bf16[2048,3328]{1,0:T(8,128)(2,1)} fusion(bf16[8,256,3328]{2,1,0:T(8,128)(2,1)} %get-tuple-element.66, f32[2048]{0:T(1024)S(1)} %bitcast.79, f32[2048]{0:T(1024)S(1)} %bitcast.78, s32[3328]{0:T(1024)S(1)} %iota_add_fusion, s32[2048]{0:T(1024)S(1)} %bitcast.77), kind=kLoop, calls=%fused_computation.2 | loop fusion | flops 40894464 | bytes 27300864 | tf_op jit(solution)/shard_map/convert_element_type | solution.py:1738
  373.4 21.6 %convolution_convert_fusion = bf16[1024,3328]{1,0:T(8,128)(2,1)} fusion(bf16[2048,3328]{1,0:T(8,128)(2,1)} %fusion.1, bf16[2048,2048]{1,0:T(8,128)(2,1)} %bitcast.110, s32[]{:T(128)S(6)} %select_n.14), kind=kOutput, calls=%fused_computation.4 | convolution fusion | flops 13962051584 | bytes 24641540 | tf_op jit(solution)/shard_map/dot_general | solution.py:375
  395.1 20.7 %fusion.7 = f32[1024,3328]{1,0:T(8,128)S(1)} fusion(bf16[2048,3328]{1,0:T(8,128)(2,1)} %fusion.1, bf16[2048,2048]{1,0:T(8,128)(2,1)} %bitcast.111, s32[]{:T(128)S(6)} %select_n.12), kind=kOutput, calls=%fused_computation.12 | convolution fusion | flops 13958643712 | bytes 31457284 | tf_op jit(solution)/shard_map/dot_general | solution.py:375
  415.8 7.9 add_convert_fusion.refs_0_
  424.1 97.8 %shard_map.319 = (f32[256,2048]{1,0:T(8,128)}, bf16[256,2048]{1,0:T(8,128)(2,1)}, f32[8,2048]{1,0:T(8,128)}) custom-call(bf16[1024,3328]{1,0:T(8,128)(2,1)} %add_convert_fusion.refs_0_, bf16[8,256,3328]{2,1,0:T(8,128)(2,1)} %bitcast.55, bf16[2048,3328]{1,0:T(8,128)(2,1)} %refs_2_.1, f32[256,2048]{1,0:T(8,128)} %get-tuple-element.67.refs_3_, ...), custom_call_target="tpu_custom_call" | custom-call | flops 27917287424 | bytes 268435456 | tf_op jit(solution)/shard_map/pallas_call | solution.py:608
  522.0 102.1 %shard_map.320 = (bf16[8,256,256]{2,1,0:T(8,128)(2,1)}, bf16[8,256,1024]{2,1,0:T(8,128)(2,1)}, f32[8,1024]{1,0:T(8,128)}, bf16[1280,1024]{1,0:T(8,128)(2,1)}, bf...) custom-call(bf16[1024,3328]{1,0:T(8,128)(2,1)} %collective-permute-done.1.refs_0_.refs_2_, ...), custom_call_target="tpu_custom_call" | custom-call | flops 30064771072 | bytes 268435456 | tf_op jit(solution)/shard_map/pallas_call | solution.py:608
  624.6 30.1 %shard_map.321 = (bf16[2048,768]{1,0:T(8,128)(2,1)}, f32[1,768]{1,0:T(1,128)}) custom-call(s32[8]{0:T(128)} %bitcast.98, bf16[2048,768]{1,0:T(8,128)(2,1)} %bitcast.60, bf16[2048,256]{1,0:T(8,128)(2,1)} %get-tuple-element.58.ctx_ref, f32[2,2048,1]{2,1,0:T(8,128)} %get-tuple-element.77.lse_ref, bf16[2048,256]{1,0:T(8,128)(2,1)} %bitcast.71, ...), custom_call_target="tpu_custom_call" | custom-call | tf_op jit(solution)/shard_map/pallas_call | solution.py:554
  654.9 1.7 copy-done
  656.6 5.7 fusion.9
  662.5 5.7 fusion.4
  668.2 1.6 add_convert_fusion.3.refs_8_
  670.2 4.1 add_convert_fusion.2.refs_4_
  674.7 4.5 add_convert_fusion.1.refs_0_
  679.3 1.9 collective-permute-start.10
  681.3 1.8 collective-permute-start.14
  684.4 106.7 %shard_map.322 = (f32[256,2048]{1,0:T(8,128)}, f32[8,2048]{1,0:T(8,128)}) custom-call(bf16[1280,1024]{1,0:T(8,128)(2,1)} %collective-permute-done.3.refs_0_.refs_2_, bf16[1024,1024]{1,0:T(8,128)(2,1)} %collective-permute-done.5.refs_1_.refs_6_, bf16[1024,768]{1,0:T(8,128)(2,1)} %copy-done.1, bf16[256,2048]{1,0:T(8,128)(2,1)} %bitcast.67, ...), custom_call_target="tpu_custom_call" | custom-call | flops 1 | bytes 1 | tf_op jit(solution)/shard_map/pallas_call | solution.py:608
  791.9 18.7 %shard_map.325.refs_1_ = f32[2048,3328]{1,0:T(8,128)} custom-call(s32[1]{0:T(128)} %bitcast.32.core_ref, bf16[1024,3328]{1,0:T(8,128)(2,1)} %add_convert_fusion.refs_0_, bf16[1024,3328]{1,0:T(8,128)(2,1)} %shard_map.324.refs_1_, bf16[1024,3328]{1,0:T(8,128)(2,1)} %collective-permute-done.1.refs_0_.refs_2_, ...), custom_call_target="tpu_custom_call" | custom-call | tf_op jit(solution)/shard_map/pallas_call | solution.py:1607
  810.6 6.8 collective-permute-done.14.refs_0_
  818.8 2.1 collective-permute-done.8
  820.9 1.7 collective-permute-start.9
  823.3 2.0 collective-permute-done.9
  828.3 18.1 %shard_map.327 = (f32[256,2048]{1,0:T(8,128)}, f32[1024,2048]{1,0:T(8,128)}, f32[2048,1024]{1,0:T(8,128)}, f32[2048,2,384]{2,1,0:T(2,128)}) custom-call(s32[1]{0:T(128)} %bitcast.32.core_ref, bf16[1280,1024]{1,0:T(8,128)(2,1)} %add_convert_fusion.1.refs_0_, bf16[1280,1024]{1,0:T(8,128)(2,1)} %get-tuple-element.91.refs_1_, ...), custom_call_target="tpu_custom_call" | custom-call | tf_op jit(solution)/shard_map/pallas_call | solution.py:1607
  846.4 2.3 copy.50
  848.7 3.1 copy.51
  (96 shorter events, 18.5 us)
Async XLA Ops:
  4.5 10.4 %copy-start.6 = (f32[2048]{0:T(1024)}, f32[2048]{0:T(1024)S(1)}, u32[]{:S(2)}) copy-start(f32[2048]{0:T(1024)S(1)} %broadcast_in_dim.104) | copy-start | bytes 24580
  5.9 9.7 %copy-start.8 = (f32[2048]{0:T(1024)}, f32[2048]{0:T(1024)S(1)}, u32[]{:S(2)}) copy-start(f32[2048]{0:T(1024)S(1)} %broadcast_in_dim.106) | copy-start | bytes 24580
  8.0 125.8 %copy-start.11 = (f32[2048]{0:T(1024)}, f32[2048]{0:T(1024)S(1)}, u32[]{:S(2)}) copy-start(f32[2048]{0:T(1024)S(1)} %broadcast_in_dim.109) | copy-start | bytes 24580
  234.4 124.3 %copy-start.10 = (s32[1,2048]{1,0:T(1,128)S(1)}, s32[1,2048]{1,0:T(1,128)}, u32[]{:S(2)}) copy-start(s32[1,2048]{1,0:T(1,128)} %param.20) | copy-start | bytes 24580
  395.0 20.8 %collective-permute-start = (bf16[1024,3328]{1,0:T(8,128)(2,1)}, bf16[1024,3328]{1,0:T(8,128)(2,1)}, u32[]{:S(2)}, u32[]{:S(2)}) collective-permute-start(bf16[1024,3328]{1,0:T(8,128)(2,1)} %convolution_convert_fusion), channel_id=1, source_target_pairs={{0,8},{8,0},{16,24},{24,16},{1,9},{9,1},{17,25},{25,17},{2,10},{10... | collective-permute-start | bytes 20447240 | tf_op jit(solution)/shard_map/ppermute | solution.py:1644
  423.7 98.2 %collective-permute-start.1 = (bf16[1024,3328]{1,0:T(8,128)(2,1)}, bf16[1024,3328]{1,0:T(8,128)(2,1)}, u32[]{:S(2)}, u32[]{:S(2)}) collective-permute-start(bf16[1024,3328]{1,0:T(8,128)(2,1)} %add_convert_fusion.refs_0_), channel_id=1, source_target_pairs={{0,8},{8,0},{16,24},{24,16},{1,9},{9,1},{17,25},{25,17},{2,10},{10... | collective-permute-start | bytes 20447240 | tf_op jit(solution)/shard_map/ppermute | solution.py:1654
  424.1 230.6 %collective-permute-start.15 = (bf16[1024,3328]{1,0:T(8,128)(2,1)}, bf16[1024,3328]{1,0:T(8,128)(2,1)}, u32[]{:S(2)}, u32[]{:S(2)}) collective-permute-start(bf16[1024,3328]{1,0:T(8,128)(2,1)} %add_convert_fusion.refs_0_), channel_id=1, source_target_pairs={{0,16},{8,24},{16,0},{24,8},{1,17},{9,25},{17,1},{25,9},{2,18},{10... | collective-permute-start | bytes 20447240 | tf_op jit(solution)/shard_map/ppermute | solution.py:1653
  624.1 46.2 %collective-permute-start.4 = (bf16[1024,1024]{1,0:T(8,128)(2,1)}, bf16[1024,1024]{1,0:T(8,128)(2,1)}, u32[]{:S(2)}, u32[]{:S(2)}) collective-permute-start(bf16[1024,1024]{1,0:T(8,128)(2,1)} %get-tuple-element.75), channel_id=1, source_target_pairs={{0,8},{8,0},{16,24},{24,16},{1,9},{9,1},{17,25},{25,17},{2,10},{10... | collective-permute-start | bytes 6291464 | tf_op jit(solution)/shard_map/ppermute | solution.py:1644
  624.1 50.5 %collective-permute-start.2 = (bf16[1280,1024]{1,0:T(8,128)(2,1)}, bf16[1280,1024]{1,0:T(8,128)(2,1)}, u32[]{:S(2)}, u32[]{:S(2)}) collective-permute-start(bf16[1280,1024]{1,0:T(8,128)(2,1)} %get-tuple-element.73), channel_id=1, source_target_pairs={{0,8},{8,0},{16,24},{24,16},{1,9},{9,1},{17,25},{25,17},{2,10},{10... | collective-permute-start | bytes 7864328 | tf_op jit(solution)/shard_map/ppermute | solution.py:1644
  654.7 1.9 copy-start
  654.8 137.1 %collective-permute-start.16 = (bf16[1024,3328]{1,0:T(8,128)(2,1)}, bf16[1024,3328]{1,0:T(8,128)(2,1)}, u32[]{:S(2)}, u32[]{:S(2)}) collective-permute-start(bf16[1024,3328]{1,0:T(8,128)(2,1)} %shard_map.324.refs_1_), channel_id=1, source_target_pairs={{0,8},{8,0},{16,24},{24,16},{1,9},{9,1},{17,25},{25,17},{2,10},{10... | collective-permute-start | bytes 20447240 | tf_op jit(solution)/shard_map/ppermute | solution.py:1678
  662.3 5.9 collective-permute-start.6
  668.2 2.0 copy-start.3
  669.8 4.9 copy-start.2
  669.8 11.3 %collective-permute-start.7 = (bf16[1024,768]{1,0:T(8,128)(2,1)}, bf16[1024,768]{1,0:T(8,128)(2,1)S(1)}, u32[]{:S(2)}, u32[]{:S(2)}) collective-permute-start(bf16[1024,768]{1,0:T(8,128)(2,1)} %add_convert_fusion.3.refs_8_), channel_id=1, source_target_pairs={{0,8},{8,0},{16,24},{24,16},{1,9},{9,1},{17,25},{25,17},{2,10},{10... | collective-permute-start | bytes 4718600 | tf_op jit(solution)/shard_map/ppermute | solution.py:1654
  674.3 8.9 %copy-start.7 = (f32[2048]{0:T(1024)S(1)}, f32[2048]{0:T(1024)}, u32[]{:S(2)}) copy-start(f32[2048]{0:T(1024)} %copy-done.6) | copy-start | bytes 24580
  674.3 8.9 %copy-start.9 = (f32[2048]{0:T(1024)S(1)}, f32[2048]{0:T(1024)}, u32[]{:S(2)}) copy-start(f32[2048]{0:T(1024)} %copy-done.8) | copy-start | bytes 24580
  674.3 7.0 collective-permute-start.5
  679.2 5.3 collective-permute-start.3
  679.3 111.9 %collective-permute-start.10 = (bf16[1280,1024]{1,0:T(8,128)(2,1)}, bf16[1280,1024]{1,0:T(8,128)(2,1)}, u32[]{:S(2)}, u32[]{:S(2)}) collective-permute-start(bf16[1280,1024]{1,0:T(8,128)(2,1)} %add_convert_fusion.1.refs_0_), channel_id=1, source_target_pairs={{0,16},{8,24},{16,0},{24,8},{1,17},{9,25},{17,1},{25,9},{2,18},{10... | collective-permute-start | bytes 7864328 | tf_op jit(solution)/shard_map/ppermute | solution.py:1653
  681.1 3.3 copy-start.1
  681.1 110.0 %collective-permute-start.11 = (bf16[1024,1024]{1,0:T(8,128)(2,1)}, bf16[1024,1024]{1,0:T(8,128)(2,1)}, u32[]{:S(2)}, u32[]{:S(2)}) collective-permute-start(bf16[1024,1024]{1,0:T(8,128)(2,1)} %add_convert_fusion.2.refs_4_), channel_id=1, source_target_pairs={{0,16},{8,24},{16,0},{24,8},{1,17},{9,25},{17,1},{25,9},{2,18},{10... | collective-permute-start | bytes 6291464 | tf_op jit(solution)/shard_map/ppermute | solution.py:1653
  681.3 136.1 %collective-permute-start.14 = (bf16[1024,768]{1,0:T(8,128)(2,1)}, bf16[1024,768]{1,0:T(8,128)(2,1)}, u32[]{:S(2)}, u32[]{:S(2)}) collective-permute-start(bf16[1024,768]{1,0:T(8,128)(2,1)} %add_convert_fusion.3.refs_8_), channel_id=1, source_target_pairs={{0,16},{8,24},{16,0},{24,8},{1,17},{9,25},{17,1},{25,9},{2,18},{10... | collective-permute-start | bytes 4718600 | tf_op jit(solution)/shard_map/ppermute | solution.py:1653
  791.1 0.7 copy-start.13
  791.2 36.0 %collective-permute-start.12 = (bf16[1280,1024]{1,0:T(8,128)(2,1)}, bf16[1280,1024]{1,0:T(8,128)(2,1)}, u32[]{:S(2)}, u32[]{:S(2)}) collective-permute-start(bf16[1280,1024]{1,0:T(8,128)(2,1)} %get-tuple-element.91.refs_1_), channel_id=1, source_target_pairs={{0,8},{8,0},{16,24},{24,16},{1,9},{9,1},{17,25},{25,17},{2,10},{10... | collective-permute-start | bytes 7864328 | tf_op jit(solution)/shard_map/ppermute | solution.py:1678
  791.3 35.9 %collective-permute-start.13 = (bf16[1024,1024]{1,0:T(8,128)(2,1)}, bf16[1024,1024]{1,0:T(8,128)(2,1)}, u32[]{:S(2)}, u32[]{:S(2)}) collective-permute-start(bf16[1024,1024]{1,0:T(8,128)(2,1)} %get-tuple-element.92.refs_5_), channel_id=1, source_target_pairs={{0,8},{8,0},{16,24},{24,16},{1,9},{9,1},{17,25},{25,17},{2,10},{10... | collective-permute-start | bytes 6291464 | tf_op jit(solution)/shard_map/ppermute | solution.py:1678
  810.6 7.6 copy-start.5
  810.6 12.1 %copy-start.12 = (f32[8,128]{1,0:T(8,128)S(1)}, f32[8,128]{1,0:T(8,128)}, u32[]{:S(2)}) copy-start(f32[8,128]{1,0:T(8,128)} %get-tuple-element.62) | copy-start | bytes 12292
  817.4 9.7 %collective-permute-start.17 = (bf16[1024,768]{1,0:T(8,128)(2,1)}, bf16[1024,768]{1,0:T(8,128)(2,1)S(1)}, u32[]{:S(2)}, u32[]{:S(2)}) collective-permute-start(bf16[1024,768]{1,0:T(8,128)(2,1)} %shard_map.326.refs_9_), channel_id=1, source_target_pairs={{0,8},{8,0},{16,24},{24,16},{1,9},{9,1},{17,25},{25,17},{2,10},{10... | collective-permute-start | bytes 4718600 | tf_op jit(solution)/shard_map/ppermute | solution.py:1678
  818.2 2.7 collective-permute-start.8
  820.9 4.3 collective-permute-start.9
  827.2 1.2 copy-start.4

commit v10 on v9

--- a/solution.py
+++ b/solution.py
@@ -1524,7 +1524,78 @@
     )(own, grad_stream, plain, grad_qkv, grad_up, qkv_flat, up_weight, gains, end_sums)
 
 
-def settle_halves(core, mine, backs, shapes, places, before=()):
+def head_products(weights, coef, targets_col, final, place):
+    vocab = weights.shape[1]
+    half_width = D // 2
+    tile = 256 if vocab % 256 == 0 else 128
+    chunk = 256
+
+    def away_kernel(place_ref, weights_ref, coef_ref, target_ref, final_ref, grads_ref, away_ref, factors):
+        step = pl.program_id(0)
+
+        @pl.when(step == 0)
+        def _():
+            for block in range(BLOCK // 128):
+                here = pl.ds(block * 128, 128)
+                found = jnp.concatenate([coef_ref[:, here], jnp.zeros((120, 128), jnp.float32)], axis=0)
+                factors[here, :] = found.T
+
+        first = place_ref[1] + step * tile
+
+        def rows_step(index, _):
+            here = span(index, chunk)
+            ids = first + lax.broadcasted_iota(jnp.int32, (chunk, tile), 1)
+            factor = factors[here, :]
+            grads_ref[here, :] = (
+                jnp.where(ids == target_ref[here, :], factor[:, 0:1], 0.0)
+                - weights_ref[here, :].astype(jnp.float32) * factor[:, 1:2]
+            ).astype(jnp.bfloat16)
+            return _
+
+        lax.fori_loop(0, BLOCK // chunk, rows_step, 0)
+        away_ref[...] = dot_tn(final_ref[...], grads_ref[...]).astype(jnp.bfloat16)
+
+    def mine_kernel(place_ref, grads_ref, final_ref, mine_ref):
+        mine_ref[...] = dot_tn(final_ref[...], grads_ref[...]).astype(jnp.bfloat16)
+
+    wide = pl.BlockSpec((BLOCK, tile), lambda j, place_ref: (0, j))
+    narrow = pl.BlockSpec((half_width, tile), lambda j, place_ref: (0, j))
+    cost = pl.CostEstimate(flops=2 * BLOCK * half_width * vocab, bytes_accessed=2**25, transcendentals=0)
+    half = jax.ShapeDtypeStruct((half_width, vocab), jnp.bfloat16)
+    grads, away = pl.pallas_call(
+        away_kernel,
+        grid_spec=pltpu.PrefetchScalarGridSpec(
+            num_scalar_prefetch=1,
+            grid=(vocab // tile,),
+            in_specs=[
+                wide,
+                pl.BlockSpec((8, BLOCK), lambda j, place_ref: (0, 0)),
+                pl.BlockSpec((BLOCK, 1), lambda j, place_ref: (0, 0)),
+                pl.BlockSpec((BLOCK, half_width), lambda j, place_ref: (0, 1 - place_ref[0])),
+            ],
+            out_specs=[wide, narrow],
+            scratch_shapes=[pltpu.VMEM((BLOCK, 128), jnp.float32)],
+        ),
+        out_shape=[jax.ShapeDtypeStruct((BLOCK, vocab), jnp.bfloat16), half],
+        cost_estimate=cost,
+        compiler_params=pltpu.CompilerParams(vmem_limit_bytes=VMEM_LIMIT),
+    )(place, weights, coef, targets_col, final)
+    mine = pl.pallas_call(
+        mine_kernel,
+        grid_spec=pltpu.PrefetchScalarGridSpec(
+            num_scalar_prefetch=1,
+            grid=(vocab // tile,),
+            in_specs=[wide, pl.BlockSpec((BLOCK, half_width), lambda j, place_ref: (0, place_ref[0]))],
+            out_specs=narrow,
+        ),
+        out_shape=half,
+        cost_estimate=cost,
+        compiler_params=pltpu.CompilerParams(vmem_limit_bytes=VMEM_LIMIT),
+    )(place, grads, final)
+    return grads, away, mine
+
+
+def settle_halves(core, mine, backs, shapes, places, passed=()):
     depth, most = 4, 256
     count = len(mine[0])
     steps = []
@@ -1541,8 +1612,16 @@
             [refs[(index * 2 + which) * count : (index * 2 + which + 1) * count] for which in (0, 1)]
             for index, _, _ in places
         ]
-        rest = refs[2 * count * len(mine) + len(before) :]
-        outs, (taken, given, split, in_sems, out_sems) = rest[: len(shapes)], rest[len(shapes) :]
+        rest = refs[2 * count * len(mine) :]
+        through, rest = rest[: len(passed)], rest[len(passed) :]
+        outs, rest = rest[: len(shapes)], rest[len(shapes) :]
+        copies = [
+            pltpu.make_async_copy(here, there, rest[-1].at[i])
+            for i, (here, there) in enumerate(zip(through, rest[: len(passed)]))
+        ]
+        taken, given, split, in_sems, out_sems = rest[len(passed) : -1]
+        for copy in copies:
+            copy.start()
 
         def loads(i):
             index, which, first, size = steps[i]
@@ -1602,22 +1681,26 @@
             store(i).start()
         for i in range(max(len(steps) - depth, 0), len(steps)):
             store(i).wait()
+        for copy in copies:
+            copy.wait()
 
     dma = pltpu.SemaphoreType.DMA
     return pl.pallas_call(
         kernel,
-        out_shape=[jax.ShapeDtypeStruct(shape, jnp.float32) for shape in shapes],
-        in_specs=[SMEM] + [ANY] * (2 * count * len(mine) + len(before)),
-        out_specs=[ANY] * len(shapes),
+        out_shape=[jax.ShapeDtypeStruct(shape, jnp.float32) for shape in shapes]
+        + [jax.ShapeDtypeStruct(array.shape, array.dtype) for array in passed],
+        in_specs=[SMEM] + [ANY] * (2 * count * len(mine) + len(passed)),
+        out_specs=[ANY] * (len(shapes) + len(passed)),
         scratch_shapes=[
             pltpu.VMEM((depth, count, most, width), jnp.bfloat16),
             pltpu.VMEM((depth, most, width), jnp.float32),
             pltpu.VMEM((depth, most) + deep[0][1:] if deep else (1, 8, 128), jnp.float32),
             dma((depth, count)),
             dma((depth,)),
+            dma((max(len(passed), 1),)),
         ],
         compiler_params=pltpu.CompilerParams(vmem_limit_bytes=VMEM_LIMIT),
-    )(core, *[array for pair in zip(mine, backs) for half in pair for array in half], *before)
+    )(core, *[array for pair in zip(mine, backs) for half in pair for array in half], *passed)
 
 
 def row_of(vector):
@@ -1678,9 +1761,9 @@
         one.back = [one.first_back, lax.ppermute(other, "dp", pairs(1))]
 
 
-def settle_all(sums, shapes, places, before=()):
+def settle_all(sums, shapes, places, passed=()):
     core = jnp.zeros((1,), jnp.int32) if sums[0].plain else sums[0].core[None]
-    return settle_halves(core, [one.mine for one in sums], [one.back for one in sums], shapes, places, before)
+    return settle_halves(core, [one.mine for one in sums], [one.back for one in sums], shapes, places, passed)
 
 
 def pair_product(product):
@@ -1731,14 +1814,12 @@
     coef, losses = score_rows(
         stats, block_lengths, labels[0], ref_logps[0], sizes, lax.axis_size("dp"), 6
     )
-    vocab_ids = lax.axis_index("seq") * local_vocab + jnp.arange(local_vocab, dtype=jnp.int32)
-    grad_logits = held((
-        jnp.where(vocab_ids[None, :] == targets[0][:, None], coef[0][:, None], 0.0)
-        - weights.reshape(BLOCK, local_vocab).astype(jnp.float32) * coef[1][:, None]
-    ).astype(jnp.bfloat16))
-    final_rows = final_full.reshape(BLOCK, D)
-    head_sum = pair_product(lambda which: dot_tn(half_of(final_rows, which), grad_logits)).cross()
-
+    core = lax.rem(lax.axis_index("dp"), 2)
+    grad_logits, away, mine = head_products(
+        weights.reshape(BLOCK, local_vocab), coef, targets_col, final_full.reshape(BLOCK, D),
+        jnp.stack([core, lax.axis_index("seq") * local_vocab]),
+    )
+    head_sum = PairSum(away, mine).cross()
     grad_stream, grad_own, end_sums = final_grad_rows(
         grad_logits.reshape(shards, rows, local_vocab), head_weight, normed, inverse, row_of(lnf_gain), sizes, 3,
         (head_sum.sum,),
@@ -1765,7 +1846,9 @@
         end_sums, sizes, 5, [one.first_back for one in sums],
     )
     give_back(sums[:2], group_sums)
-    (head_grad,) = settle_all([head_sum], [(D, local_vocab)], [(0, 0, D // 2)], (group_sums,))
+    head_grad, output, grad_input = settle_all(
+        [head_sum], [(D, local_vocab)], [(0, 0, D // 2)], (output, grad_input)
+    )
     give_back(sums[2:], head_grad)
     small = sum_over_dp(jnp.concatenate([group_sums[:7], biases], axis=0))
     out_grad, down_grad, up_grad, qkv_grad = settle_all(

time: 869 us -> 938 us (1.079)
  Pallas kernels: 715 us -> 854 us
  matrix products: 53.7 us -> 12.3 us
  other arithmetic: 40.8 us -> 26.9 us
    pallas_call x2, Pallas kernels: 36.8 us -> 115 us  [settle_halves(): pl.pallas_call(kernel, out_shape=[jax.ShapeDtypeStruct(shape, jnp.float32...]
    pallas_call x0 -> x2, Pallas kernels: none -> 62.8 us  [the longest x1 40.8 us: head_products(): pl.pallas_call(away_kernel, grid_spec=pltpu.PrefetchScalarGridSpec(num_sc...]
    dot_general x4 -> x2, matrix products: 53.7 us -> 12.3 us  [dot_tn(): lax.dot_general(left, right, (((0,), (0,)), ((), ())), preferred_element_...]
    convert_element_type x1 -> x0, other arithmetic: 14.7 us -> none  [per_device(): grad_logits = held((jnp.where(vocab_ids[None, :] == targets[0][:, None],...]
  transfers between devices with their start and end apart: 18 -> 18, of which waited for: 4 -> 3; matrix products, arithmetic and copies ran while one was open for 5% -> 3% of each run, Pallas kernels for 42% -> 49%
where the time goes in v10:
time: 938 us; the launch traced here: 928 us
  Pallas kernels  854 us (91%)
  other arithmetic  26.9 us (3%)
  local copies, waits for them, and re-layouts  12.5 us (1%)
  matrix products  12.3 us (1%)
  starting transfers between devices  10.2 us (1%)
  waiting for transfers between devices  10 us (1%)
    pallas_call x6, Pallas kernels, call(): pl.pallas_call(body, out_shape=out_shape, in_specs=[ANY] * len(before) +...  598 us
    pallas_call x2, Pallas kernels, settle_halves(): pl.pallas_call(kernel, out_shape=[jax.ShapeDtypeStruct(shape, jnp.float32...  115 us
    pallas_call x1, Pallas kernels, head_products(): pl.pallas_call(away_kernel, grid_spec=pltpu.PrefetchScalarGridSpec(num_sc...  40.8 us
    pallas_call x1, Pallas kernels, attention_backward(): pl.pallas_call(kernel, grid_spec=pltpu.PrefetchScalarGridSpec(num_scalar_...  30.1 us
    pallas_call x1, Pallas kernels, score_rows(): pl.pallas_call(kernel, out_shape=[jax.ShapeDtypeStruct((8, BLOCK), jnp.fl...  27.9 us
    pallas_call x1, Pallas kernels, head_products(): pl.pallas_call(mine_kernel, grid_spec=pltpu.PrefetchScalarGridSpec(num_sc...  22 us
    pallas_call x1, Pallas kernels, attention_forward(): pl.pallas_call(kernel, grid_spec=pltpu.PrefetchScalarGridSpec(num_scalar_...  20.9 us
    convert_element_type x4, other arithmetic, __init__(): (mine.astype(jnp.float32) + came.astype(jnp.float32)).astype(jnp.bfloat16)  20.9 us
  transfers between devices with their start and end apart: 18, of which 3 were waited for; matrix products, arithmetic and copies ran while one was open for 3% of the time, Pallas kernels for 49%

profile of v10, /device:TPU:0, one launch (start us, length us, event | category | flops | bytes accessed | tf_op | source)
XLA Modules:
  0.0 927.5 jit_solution(10320195308628797328)
XLA Ops:
  0.7 0.7 broadcast_in_dim.89
  2.1 0.7 broadcast_in_dim.87
  3.4 4.2 copy.42
  10.1 97.4 %shard_map.314 = (bf16[8,256,2048]{2,1,0:T(8,128)(2,1)}, bf16[8,256,2048]{2,1,0:T(8,128)(2,1)}, bf16[8,256,2048]{2,1,0:T(8,128)(2,1)}, bf16[8,256,768]{2,1,0:T(8...) custom-call(bf16[256,2048]{1,0:T(8,128)(2,1)} %bitcast.55, ...), custom_call_target="tpu_custom_call" | custom-call | flops 15032385536 | bytes 268435456 | tf_op jit(solution)/shard_map/pallas_call | solution.py:608
  107.6 20.9 %shard_map.315 = (bf16[2048,256]{1,0:T(8,128)(2,1)}, f32[2,2048,1]{2,1,0:T(8,128)}) custom-call(s32[8]{0:T(128)} %bitcast.84, bf16[2048,768]{1,0:T(8,128)(2,1)} %bitcast.52), custom_call_target="tpu_custom_call" | custom-call | tf_op jit(solution)/shard_map/pallas_call | solution.py:464
  128.6 1.3 copy.40.refs_2_.target_ref
  131.1 97.5 %shard_map.316 = (bf16[256,2048]{1,0:T(8,128)(2,1)}, bf16[256,2048]{1,0:T(8,128)(2,1)}, f32[256,2048]{1,0:T(8,128)}, f32[256,1]{1,0:T(8,128)}) custom-call(bf16[256,2048]{1,0:T(8,128)(2,1)} %bitcast.56, bf16[8,256,256]{2,1,0:T(8,128)(2,1)} %bitcast.58, bf16[8,256,1024]{2,1,0:T(8,128)(2,1)} %get-tuple-element.64.refs_2_.refs_6_, bf16[256,2048]{1,0:T(8,128)(2,1)} %bitcast.95, ...), custom_call_target="tpu_custom_call" | custom-call | flops 10737418240 | bytes 268435456 | tf_op jit(solution)/shard_map/pallas_call | solution.py:608
  228.6 96.4 %shard_map.317 = (bf16[8,256,2048]{2,1,0:T(8,128)(2,1)}, bf16[8,256,3328]{2,1,0:T(8,128)(2,1)}, f32[8,2048]{1,0:T(8,128)}) custom-call(bf16[256,2048]{1,0:T(8,128)(2,1)} %get-tuple-element.65.refs_0_, bf16[2048,3328]{1,0:T(8,128)(2,1)} %refs_2_.1, s32[2048,1]{1,0:T(8,128)} %copy.40.refs_2_.target_ref), custom_call_target="tpu_custom_call" | custom-call | flops 27917287424 | bytes 268435456 | tf_op jit(solution)/shard_map/pallas_call | solution.py:608
  325.0 27.9 %shard_map.318 = (f32[8,2048]{1,0:T(8,128)}, f32[8,128]{1,0:T(8,128)}) custom-call(f32[8,2048]{1,0:T(8,128)} %get-tuple-element.66.stats_ref, s32[8]{0:T(128)} %bitcast.85, s32[8]{0:T(128)} %bitcast.90, f32[8]{0:T(128)} %bitcast.91), custom_call_target="tpu_custom_call" | custom-call | tf_op jit(solution)/shard_map/pallas_call | solution.py:1398
  352.9 40.8 %shard_map.319 = (bf16[2048,3328]{1,0:T(8,128)(2,1)}, bf16[1024,3328]{1,0:T(8,128)(2,1)}) custom-call(s32[2]{0:T(128)} %pad_add_fusion.place_ref, bf16[2048,3328]{1,0:T(8,128)(2,1)} %bitcast.99, f32[8,2048]{1,0:T(8,128)} %get-tuple-element.69.coef_ref, s32[2048,1]{1,0:T(8,128)} %copy.40.refs_2_.target_ref, bf16[2048,2048]{1,0:T(8,128)(2,1)} %bitcast.102), custom_call_target="tpu_custom_call" | custom-call | flops 13958643712 | bytes 33554432 | tf_op jit(solution)/shard_map/pallas_call | solution.py:1565
  393.8 22.0 %shard_map.320 = bf16[1024,3328]{1,0:T(8,128)(2,1)} custom-call(s32[2]{0:T(128)} %pad_add_fusion.place_ref, bf16[2048,3328]{1,0:T(8,128)(2,1)} %get-tuple-element.71.grads_ref, bf16[2048,2048]{1,0:T(8,128)(2,1)} %bitcast.103), custom_call_target="tpu_custom_call" | custom-call | flops 13958643712 | bytes 33554432 | tf_op jit(solution)/shard_map/pallas_call | solution.py:1583
  415.8 9.4 %add_convert_fusion.refs_0_ = bf16[1024,3328]{1,0:T(8,128)(2,1)} fusion(bf16[1024,3328]{1,0:T(8,128)(2,1)} %collective-permute-done, bf16[1024,3328]{1,0:T(8,128)(2,1)} %shard_map.320), kind=kLoop, calls=%fused_computation | loop fusion | flops 13631488 | bytes 20447232 | tf_op jit(solution)/shard_map/convert_element_type | solution.py:1728
  425.6 97.7 %shard_map.321 = (f32[256,2048]{1,0:T(8,128)}, bf16[256,2048]{1,0:T(8,128)(2,1)}, f32[8,2048]{1,0:T(8,128)}) custom-call(bf16[1024,3328]{1,0:T(8,128)(2,1)} %add_convert_fusion.refs_0_, bf16[8,256,3328]{2,1,0:T(8,128)(2,1)} %bitcast.98, bf16[2048,3328]{1,0:T(8,128)(2,1)} %refs_2_.1, f32[256,2048]{1,0:T(8,128)} %get-tuple-element.74.refs_3_, ...), custom_call_target="tpu_custom_call" | custom-call | flops 27917287424 | bytes 268435456 | tf_op jit(solution)/shard_map/pallas_call | solution.py:608
  523.4 102.5 %shard_map.322 = (bf16[8,256,256]{2,1,0:T(8,128)(2,1)}, bf16[8,256,1024]{2,1,0:T(8,128)(2,1)}, f32[8,1024]{1,0:T(8,128)}, bf16[1280,1024]{1,0:T(8,128)(2,1)}, bf...) custom-call(bf16[1024,3328]{1,0:T(8,128)(2,1)} %collective-permute-done.2.refs_0_.refs_2_, ...), custom_call_target="tpu_custom_call" | custom-call | flops 30064771072 | bytes 268435456 | tf_op jit(solution)/shard_map/pallas_call | solution.py:608
  625.9 30.1 %shard_map.323 = (bf16[2048,768]{1,0:T(8,128)(2,1)}, f32[1,768]{1,0:T(1,128)}) custom-call(s32[8]{0:T(128)} %bitcast.86, bf16[2048,768]{1,0:T(8,128)(2,1)} %bitcast.53, bf16[2048,256]{1,0:T(8,128)(2,1)} %get-tuple-element.63.ctx_ref, f32[2,2048,1]{2,1,0:T(8,128)} %get-tuple-element.73.lse_ref, bf16[2048,256]{1,0:T(8,128)(2,1)} %bitcast.60, ...), custom_call_target="tpu_custom_call" | custom-call | tf_op jit(solution)/shard_map/pallas_call | solution.py:554
  656.7 1.2 copy-done
  657.9 6.8 fusion.4
  664.7 5.5 fusion.2
  670.2 6.1 collective-permute-done.8
  676.3 2.9 add_convert_fusion.3.refs_8_
  679.4 4.1 add_convert_fusion.2.refs_4_
  683.9 4.5 add_convert_fusion.1.refs_0_
  688.5 2.7 collective-permute-start.12
  691.4 2.0 collective-permute-start.16
  694.0 106.4 %shard_map.325 = (f32[256,2048]{1,0:T(8,128)}, f32[8,2048]{1,0:T(8,128)}) custom-call(bf16[1280,1024]{1,0:T(8,128)(2,1)} %collective-permute-done.5.refs_0_.refs_2_, bf16[1024,1024]{1,0:T(8,128)(2,1)} %collective-permute-done.7.refs_1_.refs_6_, bf16[1024,768]{1,0:T(8,128)(2,1)} %copy-done.1, bf16[256,2048]{1,0:T(8,128)(2,1)} %bitcast.57, ...), custom_call_target="tpu_custom_call" | custom-call | flops 1 | bytes 1 | tf_op jit(solution)/shard_map/pallas_call | solution.py:608
  801.2 96.5 %shard_map.326 = (f32[2048,3328]{1,0:T(8,128)}, bf16[256,2048]{1,0:T(8,128)(2,1)}, f32[256,2048]{1,0:T(8,128)}) custom-call(s32[1]{0:T(128)} %bitcast.16.core_ref, bf16[1024,3328]{1,0:T(8,128)(2,1)} %add_convert_fusion.refs_0_, bf16[1024,3328]{1,0:T(8,128)(2,1)} %shard_map.324.refs_1_, bf16[1024,3328]{1,0:T(8,128)(2,1)} %collective-permute-done.2.refs_0_.refs_2_, ...), custom_call_target="tpu_custom_call" | custom-call | tf_op jit(solution)/shard_map/pallas_call | solution.py:1688
  897.8 0.8 slice.54
  899.2 2.1 collective-permute-done.10
  901.3 2.4 collective-permute-start.11
  904.4 1.8 collective-permute-done.11
  908.1 1.1 copy-done.4
  909.2 18.1 %shard_map.329 = (f32[256,2048]{1,0:T(8,128)}, f32[1024,2048]{1,0:T(8,128)}, f32[2048,1024]{1,0:T(8,128)}, f32[2048,2,384]{2,1,0:T(2,128)}) custom-call(s32[1]{0:T(128)} %bitcast.16.core_ref, bf16[1280,1024]{1,0:T(8,128)(2,1)} %add_convert_fusion.1.refs_0_, bf16[1280,1024]{1,0:T(8,128)(2,1)} %get-tuple-element.100.refs_1_, ...), custom_call_target="tpu_custom_call" | custom-call | tf_op jit(solution)/shard_map/pallas_call | solution.py:1688
  (102 shorter events, 11.6 us)
Async XLA Ops:
  2.1 7.4 copy-start.6
  3.4 6.0 copy-start.8
  3.4 4.2 copy-start.16
  3.4 4.8 copy-start.18
  107.5 21.0 %copy-start.12 = (bf16[2048]{0:T(1024)(128)(2,1)S(1)}, bf16[2048]{0:T(1024)(128)(2,1)}, u32[]{:S(2)}) copy-start(bf16[2048]{0:T(1024)(128)(2,1)} %param.34) | copy-start | bytes 12292
  107.5 21.0 %copy-start.13 = (bf16[2048]{0:T(1024)(128)(2,1)S(1)}, bf16[2048]{0:T(1024)(128)(2,1)}, u32[]{:S(2)}) copy-start(bf16[2048]{0:T(1024)(128)(2,1)} %param.36) | copy-start | bytes 12292
  107.5 21.0 %copy-start.14 = (bf16[2048]{0:T(1024)(128)(2,1)S(1)}, bf16[2048]{0:T(1024)(128)(2,1)}, u32[]{:S(2)}) copy-start(bf16[2048]{0:T(1024)(128)(2,1)} %param.35) | copy-start | bytes 12292
  107.6 21.0 %copy-start.11 = (s32[1,2048]{1,0:T(1,128)S(1)}, s32[1,2048]{1,0:T(1,128)}, u32[]{:S(2)}) copy-start(s32[1,2048]{1,0:T(1,128)} %param.20) | copy-start | bytes 24580
  128.5 100.1 %copy-start.10 = (f32[2048]{0:T(1024)}, f32[2048]{0:T(1024)S(1)}, u32[]{:S(2)}) copy-start(f32[2048]{0:T(1024)S(1)} %broadcast_in_dim.91) | copy-start | bytes 24580
  393.7 22.1 %collective-permute-start = (bf16[1024,3328]{1,0:T(8,128)(2,1)}, bf16[1024,3328]{1,0:T(8,128)(2,1)}, u32[]{:S(2)}, u32[]{:S(2)}) collective-permute-start(bf16[1024,3328]{1,0:T(8,128)(2,1)} %get-tuple-element.72), channel_id=1, source_target_pairs={{0,8},{8,0},{16,24},{24,16},{1,9},{9,1},{17,25},{25,17},{2,10},{10... | collective-permute-start | bytes 20447240 | tf_op jit(solution)/shard_map/ppermute | solution.py:1727
  425.2 98.1 %collective-permute-start.2 = (bf16[1024,3328]{1,0:T(8,128)(2,1)}, bf16[1024,3328]{1,0:T(8,128)(2,1)}, u32[]{:S(2)}, u32[]{:S(2)}) collective-permute-start(bf16[1024,3328]{1,0:T(8,128)(2,1)} %add_convert_fusion.refs_0_), channel_id=1, source_target_pairs={{0,8},{8,0},{16,24},{24,16},{1,9},{9,1},{17,25},{25,17},{2,10},{10... | collective-permute-start | bytes 20447240 | tf_op jit(solution)/shard_map/ppermute | solution.py:1737
  425.6 230.4 %collective-permute-start.1 = (bf16[1024,3328]{1,0:T(8,128)(2,1)}, bf16[1024,3328]{1,0:T(8,128)(2,1)}, u32[]{:S(2)}, u32[]{:S(2)}) collective-permute-start(bf16[1024,3328]{1,0:T(8,128)(2,1)} %add_convert_fusion.refs_0_), channel_id=1, source_target_pairs={{0,16},{8,24},{16,0},{24,8},{1,17},{9,25},{17,1},{25,9},{2,18},{10... | collective-permute-start | bytes 20447240 | tf_op jit(solution)/shard_map/ppermute | solution.py:1736
  656.0 145.1 %collective-permute-start.3 = (bf16[1024,3328]{1,0:T(8,128)(2,1)}, bf16[1024,3328]{1,0:T(8,128)(2,1)}, u32[]{:S(2)}, u32[]{:S(2)}) collective-permute-start(bf16[1024,3328]{1,0:T(8,128)(2,1)} %shard_map.324.refs_1_), channel_id=1, source_target_pairs={{0,8},{8,0},{16,24},{24,16},{1,9},{9,1},{17,25},{25,17},{2,10},{10... | collective-permute-start | bytes 20447240 | tf_op jit(solution)/shard_map/ppermute | solution.py:1761
  656.1 27.8 %collective-permute-start.4 = (bf16[1280,1024]{1,0:T(8,128)(2,1)}, bf16[1280,1024]{1,0:T(8,128)(2,1)}, u32[]{:S(2)}, u32[]{:S(2)}) collective-permute-start(bf16[1280,1024]{1,0:T(8,128)(2,1)} %get-tuple-element.86), channel_id=1, source_target_pairs={{0,8},{8,0},{16,24},{24,16},{1,9},{9,1},{17,25},{25,17},{2,10},{10... | collective-permute-start | bytes 7864328 | tf_op jit(solution)/shard_map/ppermute | solution.py:1727
  656.6 22.8 %collective-permute-start.6 = (bf16[1024,1024]{1,0:T(8,128)(2,1)}, bf16[1024,1024]{1,0:T(8,128)(2,1)}, u32[]{:S(2)}, u32[]{:S(2)}) collective-permute-start(bf16[1024,1024]{1,0:T(8,128)(2,1)} %get-tuple-element.88), channel_id=1, source_target_pairs={{0,8},{8,0},{16,24},{24,16},{1,9},{9,1},{17,25},{25,17},{2,10},{10... | collective-permute-start | bytes 6291464 | tf_op jit(solution)/shard_map/ppermute | solution.py:1727
  664.7 11.6 %collective-permute-start.8 = (bf16[1024,768]{1,0:T(8,128)(2,1)}, bf16[1024,768]{1,0:T(8,128)(2,1)}, u32[]{:S(2)}, u32[]{:S(2)}) collective-permute-start(bf16[1024,768]{1,0:T(8,128)(2,1)} %fusion.4), channel_id=1, source_target_pairs={{0,8},{8,0},{16,24},{24,16},{1,9},{9,1},{17,25},{25,17},{2,10},{10... | collective-permute-start | bytes 4718600 | tf_op jit(solution)/shard_map/ppermute | solution.py:1727
  670.2 9.2 copy-start.3
  679.3 12.0 %collective-permute-start.9 = (bf16[1024,768]{1,0:T(8,128)(2,1)}, bf16[1024,768]{1,0:T(8,128)(2,1)S(1)}, u32[]{:S(2)}, u32[]{:S(2)}) collective-permute-start(bf16[1024,768]{1,0:T(8,128)(2,1)} %add_convert_fusion.3.refs_8_), channel_id=1, source_target_pairs={{0,8},{8,0},{16,24},{24,16},{1,9},{9,1},{17,25},{25,17},{2,10},{10... | collective-permute-start | bytes 4718600 | tf_op jit(solution)/shard_map/ppermute | solution.py:1737
  679.4 4.5 copy-start.2
  683.5 7.9 collective-permute-start.7
  683.9 9.4 %copy-start.7 = (f32[2048]{0:T(1024)S(1)}, f32[2048]{0:T(1024)}, u32[]{:S(2)}) copy-start(f32[2048]{0:T(1024)} %copy-done.6) | copy-start | bytes 24580
  683.9 9.4 %copy-start.9 = (f32[2048]{0:T(1024)S(1)}, f32[2048]{0:T(1024)}, u32[]{:S(2)}) copy-start(f32[2048]{0:T(1024)} %copy-done.8) | copy-start | bytes 24580
  688.4 5.5 collective-permute-start.5
  688.5 111.9 %collective-permute-start.12 = (bf16[1280,1024]{1,0:T(8,128)(2,1)}, bf16[1280,1024]{1,0:T(8,128)(2,1)}, u32[]{:S(2)}, u32[]{:S(2)}) collective-permute-start(bf16[1280,1024]{1,0:T(8,128)(2,1)} %add_convert_fusion.1.refs_0_), channel_id=1, source_target_pairs={{0,16},{8,24},{16,0},{24,8},{1,17},{9,25},{17,1},{25,9},{2,18},{10... | collective-permute-start | bytes 7864328 | tf_op jit(solution)/shard_map/ppermute | solution.py:1736
  691.3 109.1 %collective-permute-start.13 = (bf16[1024,1024]{1,0:T(8,128)(2,1)}, bf16[1024,1024]{1,0:T(8,128)(2,1)}, u32[]{:S(2)}, u32[]{:S(2)}) collective-permute-start(bf16[1024,1024]{1,0:T(8,128)(2,1)} %add_convert_fusion.2.refs_4_), channel_id=1, source_target_pairs={{0,16},{8,24},{16,0},{24,8},{1,17},{9,25},{17,1},{25,9},{2,18},{10... | collective-permute-start | bytes 6291464 | tf_op jit(solution)/shard_map/ppermute | solution.py:1736
  691.4 206.3 %collective-permute-start.16 = (bf16[1024,768]{1,0:T(8,128)(2,1)}, bf16[1024,768]{1,0:T(8,128)(2,1)}, u32[]{:S(2)}, u32[]{:S(2)}) collective-permute-start(bf16[1024,768]{1,0:T(8,128)(2,1)} %add_convert_fusion.3.refs_8_), channel_id=1, source_target_pairs={{0,16},{8,24},{16,0},{24,8},{1,17},{9,25},{17,1},{25,9},{2,18},{10... | collective-permute-start | bytes 4718600 | tf_op jit(solution)/shard_map/ppermute | solution.py:1736
  800.5 107.6 %collective-permute-start.14 = (bf16[1280,1024]{1,0:T(8,128)(2,1)}, bf16[1280,1024]{1,0:T(8,128)(2,1)}, u32[]{:S(2)}, u32[]{:S(2)}) collective-permute-start(bf16[1280,1024]{1,0:T(8,128)(2,1)} %get-tuple-element.100.refs_1_), channel_id=1, source_target_pairs={{0,8},{8,0},{16,24},{24,16},{1,9},{9,1},{17,25},{25,17},{2,10},{10... | collective-permute-start | bytes 7864328 | tf_op jit(solution)/shard_map/ppermute | solution.py:1761
  800.5 107.5 %collective-permute-start.15 = (bf16[1024,1024]{1,0:T(8,128)(2,1)}, bf16[1024,1024]{1,0:T(8,128)(2,1)}, u32[]{:S(2)}, u32[]{:S(2)}) collective-permute-start(bf16[1024,1024]{1,0:T(8,128)(2,1)} %get-tuple-element.101.refs_5_), channel_id=1, source_target_pairs={{0,8},{8,0},{16,24},{24,16},{1,9},{9,1},{17,25},{25,17},{2,10},{10... | collective-permute-start | bytes 6291464 | tf_op jit(solution)/shard_map/ppermute | solution.py:1761
  897.7 6.1 copy-start.15
  897.7 10.3 %collective-permute-start.17 = (bf16[1024,768]{1,0:T(8,128)(2,1)}, bf16[1024,768]{1,0:T(8,128)(2,1)S(1)}, u32[]{:S(2)}, u32[]{:S(2)}) collective-permute-start(bf16[1024,768]{1,0:T(8,128)(2,1)} %shard_map.328.refs_9_), channel_id=1, source_target_pairs={{0,8},{8,0},{16,24},{24,16},{1,9},{9,1},{17,25},{25,17},{2,10},{10... | collective-permute-start | bytes 4718600 | tf_op jit(solution)/shard_map/ppermute | solution.py:1761
  898.6 2.7 collective-permute-start.10
  901.3 4.8 collective-permute-start.11
  (5 other events, 7.3 us)

commit v11 on v9

--- a/solution.py
+++ b/solution.py
@@ -1524,7 +1524,7 @@
     )(own, grad_stream, plain, grad_qkv, grad_up, qkv_flat, up_weight, gains, end_sums)
 
 
-def settle_halves(core, mine, backs, shapes, places, before=()):
+def settle_halves(core, mine, backs, shapes, places, passed=(), before=()):
     depth, most = 4, 256
     count = len(mine[0])
     steps = []
@@ -1541,8 +1541,15 @@
             [refs[(index * 2 + which) * count : (index * 2 + which + 1) * count] for which in (0, 1)]
             for index, _, _ in places
         ]
-        rest = refs[2 * count * len(mine) + len(before) :]
-        outs, (taken, given, split, in_sems, out_sems) = rest[: len(shapes)], rest[len(shapes) :]
+        rest = refs[2 * count * len(mine) :]
+        through, rest = rest[: len(passed)], rest[len(passed) + len(before) :]
+        outs, rest = rest[: len(shapes)], rest[len(shapes) :]
+        passed_out, rest = rest[: len(passed)], rest[len(passed) :]
+        taken, given, split, in_sems, out_sems, pass_sems, *staged = rest
+        ins = [pltpu.make_async_copy(through[i], here, pass_sems.at[0, i]) for i, here in enumerate(staged)]
+        copies = [pltpu.make_async_copy(here, passed_out[i], pass_sems.at[1, i]) for i, here in enumerate(staged)]
+        for copy in ins:
+            copy.start()
 
         def loads(i):
             index, which, first, size = steps[i]
@@ -1600,24 +1607,34 @@
 
             lax.fori_loop(0, size // 32, convert, 0)
             store(i).start()
+            if i == 0:
+                for taking, copy in zip(ins, copies):
+                    taking.wait()
+                    copy.start()
         for i in range(max(len(steps) - depth, 0), len(steps)):
             store(i).wait()
+        for copy in copies:
+            copy.wait()
 
     dma = pltpu.SemaphoreType.DMA
     return pl.pallas_call(
         kernel,
-        out_shape=[jax.ShapeDtypeStruct(shape, jnp.float32) for shape in shapes],
-        in_specs=[SMEM] + [ANY] * (2 * count * len(mine) + len(before)),
-        out_specs=[ANY] * len(shapes),
+        out_shape=[jax.ShapeDtypeStruct(shape, jnp.float32) for shape in shapes]
+        + [jax.ShapeDtypeStruct(array.shape, array.dtype) for array in passed],
+        in_specs=[SMEM] + [ANY] * (2 * count * len(mine) + len(passed) + len(before)),
+        out_specs=[ANY] * (len(shapes) + len(passed)),
         scratch_shapes=[
             pltpu.VMEM((depth, count, most, width), jnp.bfloat16),
             pltpu.VMEM((depth, most, width), jnp.float32),
             pltpu.VMEM((depth, most) + deep[0][1:] if deep else (1, 8, 128), jnp.float32),
             dma((depth, count)),
             dma((depth,)),
-        ],
+            dma((2, max(len(passed), 1))),
+        ]
+        + [pltpu.VMEM(array.shape, array.dtype) for array in passed],
+        cost_estimate=pl.CostEstimate(flops=1, bytes_accessed=1, transcendentals=0),
         compiler_params=pltpu.CompilerParams(vmem_limit_bytes=VMEM_LIMIT),
-    )(core, *[array for pair in zip(mine, backs) for half in pair for array in half], *before)
+    )(core, *[array for pair in zip(mine, backs) for half in pair for array in half], *passed, *before)
 
 
 def row_of(vector):
@@ -1655,17 +1672,17 @@
         return self
 
 
-def after(values, earlier):
+def after(values, *earlier):
     def kernel(*refs):
         del refs
 
     return pl.pallas_call(
         kernel,
         out_shape=[jax.ShapeDtypeStruct(v.shape, v.dtype) for v in values],
-        in_specs=[ANY] * (len(values) + 1),
+        in_specs=[ANY] * (len(values) + len(earlier)),
         out_specs=[ANY] * len(values),
         input_output_aliases={i: i for i in range(len(values))},
-    )(*values, earlier)
+    )(*values, *earlier)
 
 
 def give_back(sums, earlier):
@@ -1678,9 +1695,9 @@
         one.back = [one.first_back, lax.ppermute(other, "dp", pairs(1))]
 
 
-def settle_all(sums, shapes, places, before=()):
+def settle_all(sums, shapes, places, passed=(), before=()):
     core = jnp.zeros((1,), jnp.int32) if sums[0].plain else sums[0].core[None]
-    return settle_halves(core, [one.mine for one in sums], [one.back for one in sums], shapes, places, before)
+    return settle_halves(core, [one.mine for one in sums], [one.back for one in sums], shapes, places, passed, before)
 
 
 def pair_product(product):
@@ -1733,7 +1750,7 @@
     )
     vocab_ids = lax.axis_index("seq") * local_vocab + jnp.arange(local_vocab, dtype=jnp.int32)
     grad_logits = held((
-        jnp.where(vocab_ids[None, :] == targets[0][:, None], coef[0][:, None], 0.0)
+        jnp.where(vocab_ids[None, :] == targets_col, coef[0][:, None], 0.0)
         - weights.reshape(BLOCK, local_vocab).astype(jnp.float32) * coef[1][:, None]
     ).astype(jnp.bfloat16))
     final_rows = final_full.reshape(BLOCK, D)
@@ -1751,7 +1768,7 @@
     grad_qkv, qkv_sums = attention_backward(
         flat_qkv, block_lengths, local_heads, ctx, lse, grad_ctx.reshape(BLOCK, inner), planes
     )
-    first_rows = first_full.reshape(BLOCK, D)
+    (first_rows,) = after([first_full.reshape(BLOCK, D)], sums[0].sum, sums[1].sum)
     sums.append(pair_product(lambda which: dot_tn(half_of(first_rows, which), grad_qkv)).cross())
     qkv_sums = qkv_sums.reshape(local_heads, 3 * HEAD_DIM)
     qv_grad = jnp.concatenate([qkv_sums[:, :HEAD_DIM], qkv_sums[:, 2 * HEAD_DIM :]], axis=-1)
@@ -1765,14 +1782,18 @@
         end_sums, sizes, 5, [one.first_back for one in sums],
     )
     give_back(sums[:2], group_sums)
-    (head_grad,) = settle_all([head_sum], [(D, local_vocab)], [(0, 0, D // 2)], (group_sums,))
+    head_grad, output, grad_input = settle_all(
+        [head_sum], [(D, local_vocab)], [(0, 0, D // 2)], (output, grad_input)
+    )
+    out_grad, down_grad, up_grad = settle_all(
+        sums[:2],
+        [(inner, D), (local_hidden, D), (D, local_hidden)],
+        [(0, 0, inner), (0, inner, local_hidden), (1, 0, D // 2)],
+        before=(head_grad,),
+    )
+    small = sum_over_dp(jnp.concatenate([group_sums[:7], biases], axis=0))
     give_back(sums[2:], head_grad)
-    small = sum_over_dp(jnp.concatenate([group_sums[:7], biases], axis=0))
-    out_grad, down_grad, up_grad, qkv_grad = settle_all(
-        sums,
-        [(inner, D), (local_hidden, D), (D, local_hidden), qkv_weight.shape],
-        [(0, 0, inner), (0, inner, local_hidden), (1, 0, D // 2), (2, 0, D // 2)],
-    )
+    (qkv_grad,) = settle_all(sums[2:], [qkv_weight.shape], [(0, 0, D // 2)])
     return (
         losses[:, 0][None],
         output[None],

time: 869 us -> 864 us (level)
    pallas_call x2 -> x3, Pallas kernels: 36.8 us -> 40.5 us  [settle_halves(): pl.pallas_call(kernel, out_shape=[jax.ShapeDtypeStruct(shape, jnp.float32...]
  transfers between devices with their start and end apart: 18 -> 18, of which waited for: 4 -> 4; matrix products, arithmetic and copies ran while one was open for 5% -> 5% of each run, Pallas kernels for 42% -> 43%
where the time goes in v11:
time: 864 us; the launch traced here: 847 us
  Pallas kernels  717 us (83%)
  matrix products  51.6 us (6%)
  other arithmetic  40.7 us (5%)
  local copies, waits for them, and re-layouts  18 us (2%)
  waiting for transfers between devices  10 us (1%)
  starting transfers between devices  8.96 us (1%)
    pallas_call x6, Pallas kernels, call(): pl.pallas_call(body, out_shape=out_shape, in_specs=[ANY] * len(before) +...  602 us
    dot_general x4, matrix products, dot_tn(): lax.dot_general(left, right, (((0,), (0,)), ((), ())), preferred_element_...  51.6 us
    pallas_call x3, Pallas kernels, settle_halves(): pl.pallas_call(kernel, out_shape=[jax.ShapeDtypeStruct(shape, jnp.float32...  40.5 us
    pallas_call x1, Pallas kernels, attention_backward(): pl.pallas_call(kernel, grid_spec=pltpu.PrefetchScalarGridSpec(num_scalar_...  30.5 us
    pallas_call x1, Pallas kernels, score_rows(): pl.pallas_call(kernel, out_shape=[jax.ShapeDtypeStruct((8, BLOCK), jnp.fl...  23.1 us
    pallas_call x1, Pallas kernels, attention_forward(): pl.pallas_call(kernel, grid_spec=pltpu.PrefetchScalarGridSpec(num_scalar_...  20.8 us
    convert_element_type x4, other arithmetic, __init__(): (mine.astype(jnp.float32) + came.astype(jnp.float32)).astype(jnp.bfloat16)  17.9 us
  transfers between devices with their start and end apart: 18, of which 4 were waited for; matrix products, arithmetic and copies ran while one was open for 5% of the time, Pallas kernels for 43%

profile of v11, /device:TPU:0, one launch (start us, length us, event | category | flops | bytes accessed | tf_op | source)
XLA Modules:
  0.0 847.3 jit_solution(9700833437098753124)
XLA Ops:
  8.7 2.0 copy.41.refs_2_
  10.7 4.2 copy.42
  15.6 97.4 %shard_map.314 = (bf16[8,256,2048]{2,1,0:T(8,128)(2,1)}, bf16[8,256,2048]{2,1,0:T(8,128)(2,1)}, bf16[8,256,2048]{2,1,0:T(8,128)(2,1)}, bf16[8,256,768]{2,1,0:T(8...) custom-call(bf16[256,2048]{1,0:T(8,128)(2,1)} %bitcast.63, ...), custom_call_target="tpu_custom_call" | custom-call | flops 15032385536 | bytes 268435456 | tf_op jit(solution)/shard_map/pallas_call | solution.py:608
  113.0 20.8 %shard_map.315 = (bf16[2048,256]{1,0:T(8,128)(2,1)}, f32[2,2048,1]{2,1,0:T(8,128)}) custom-call(s32[8]{0:T(128)} %bitcast.95, bf16[2048,768]{1,0:T(8,128)(2,1)} %bitcast.59), custom_call_target="tpu_custom_call" | custom-call | tf_op jit(solution)/shard_map/pallas_call | solution.py:464
  134.4 99.9 %shard_map.316 = (bf16[256,2048]{1,0:T(8,128)(2,1)}, bf16[256,2048]{1,0:T(8,128)(2,1)}, f32[256,2048]{1,0:T(8,128)}, f32[256,1]{1,0:T(8,128)}) custom-call(bf16[256,2048]{1,0:T(8,128)(2,1)} %bitcast.64, bf16[8,256,256]{2,1,0:T(8,128)(2,1)} %bitcast.66, bf16[8,256,1024]{2,1,0:T(8,128)(2,1)} %get-tuple-element.61.refs_2_.refs_6_, bf16[256,2048]{1,0:T(8,128)(2,1)} %bitcast.106, ...), custom_call_target="tpu_custom_call" | custom-call | flops 10737418240 | bytes 268435456 | tf_op jit(solution)/shard_map/pallas_call | solution.py:608
  234.3 98.6 %shard_map.317 = (bf16[8,256,2048]{2,1,0:T(8,128)(2,1)}, bf16[8,256,3328]{2,1,0:T(8,128)(2,1)}, f32[8,2048]{1,0:T(8,128)}) custom-call(bf16[256,2048]{1,0:T(8,128)(2,1)} %get-tuple-element.62.refs_0_, bf16[2048,3328]{1,0:T(8,128)(2,1)} %refs_2_.1, s32[2048,1]{1,0:T(8,128)} %copy.41.refs_2_), custom_call_target="tpu_custom_call" | custom-call | flops 27917287424 | bytes 268435456 | tf_op jit(solution)/shard_map/pallas_call | solution.py:608
  332.9 23.1 %shard_map.318 = (f32[8,2048]{1,0:T(8,128)}, f32[8,128]{1,0:T(8,128)}) custom-call(f32[8,2048]{1,0:T(8,128)} %get-tuple-element.63.stats_ref, s32[8]{0:T(128)} %bitcast.96, s32[8]{0:T(128)} %bitcast.101, f32[8]{0:T(128)} %bitcast.102), custom_call_target="tpu_custom_call" | custom-call | tf_op jit(solution)/shard_map/pallas_call | solution.py:1398
  357.0 14.7 %fusion.1 = bf16[2048,3328]{1,0:T(8,128)(2,1)} fusion(bf16[8,256,3328]{2,1,0:T(8,128)(2,1)} %get-tuple-element.67, f32[2048]{0:T(1024)S(1)} %bitcast.78, f32[2048]{0:T(1024)S(1)} %bitcast.77, s32[3328]{0:T(1024)S(1)} %iota_add_fusion, s32[2048]{0:T(1024)S(1)} %bitcast.76), kind=kLoop, calls=%fused_computation.2 | loop fusion | flops 40894464 | bytes 27300864 | tf_op jit(solution)/shard_map/convert_element_type | solution.py:1755
  371.6 21.6 %convolution_convert_fusion = bf16[1024,3328]{1,0:T(8,128)(2,1)} fusion(bf16[2048,3328]{1,0:T(8,128)(2,1)} %fusion.1, bf16[2048,2048]{1,0:T(8,128)(2,1)} %bitcast.109, s32[]{:T(128)S(6)} %select_n.14), kind=kOutput, calls=%fused_computation.4 | convolution fusion | flops 13962051584 | bytes 24641540 | tf_op jit(solution)/shard_map/dot_general | solution.py:375
  393.4 20.6 %fusion.7 = f32[1024,3328]{1,0:T(8,128)S(1)} fusion(bf16[2048,3328]{1,0:T(8,128)(2,1)} %fusion.1, bf16[2048,2048]{1,0:T(8,128)(2,1)} %bitcast.110, s32[]{:T(128)S(6)} %select_n.12), kind=kOutput, calls=%fused_computation.12 | convolution fusion | flops 13958643712 | bytes 31457284 | tf_op jit(solution)/shard_map/dot_general | solution.py:375
  414.0 7.9 add_convert_fusion.refs_0_
  422.4 1.3 collective-permute-start.1
  423.7 97.4 %shard_map.319 = (f32[256,2048]{1,0:T(8,128)}, bf16[256,2048]{1,0:T(8,128)(2,1)}, f32[8,2048]{1,0:T(8,128)}) custom-call(bf16[1024,3328]{1,0:T(8,128)(2,1)} %add_convert_fusion.refs_0_, bf16[8,256,3328]{2,1,0:T(8,128)(2,1)} %bitcast.55, bf16[2048,3328]{1,0:T(8,128)(2,1)} %refs_2_.1, f32[256,2048]{1,0:T(8,128)} %get-tuple-element.69.refs_3_, ...), custom_call_target="tpu_custom_call" | custom-call | flops 27917287424 | bytes 268435456 | tf_op jit(solution)/shard_map/pallas_call | solution.py:608
  521.2 102.5 %shard_map.320 = (bf16[8,256,256]{2,1,0:T(8,128)(2,1)}, bf16[8,256,1024]{2,1,0:T(8,128)(2,1)}, f32[8,1024]{1,0:T(8,128)}, bf16[1280,1024]{1,0:T(8,128)(2,1)}, bf...) custom-call(bf16[1024,3328]{1,0:T(8,128)(2,1)} %collective-permute-done.2.refs_0_.refs_2_, ...), custom_call_target="tpu_custom_call" | custom-call | flops 30064771072 | bytes 268435456 | tf_op jit(solution)/shard_map/pallas_call | solution.py:608
  624.3 30.5 %shard_map.321 = (bf16[2048,768]{1,0:T(8,128)(2,1)}, f32[1,768]{1,0:T(1,128)}) custom-call(s32[8]{0:T(128)} %bitcast.97, bf16[2048,768]{1,0:T(8,128)(2,1)} %bitcast.60, bf16[2048,256]{1,0:T(8,128)(2,1)} %get-tuple-element.60.ctx_ref, f32[2,2048,1]{2,1,0:T(8,128)} %get-tuple-element.68.lse_ref, bf16[2048,256]{1,0:T(8,128)(2,1)} %bitcast.68, ...), custom_call_target="tpu_custom_call" | custom-call | tf_op jit(solution)/shard_map/pallas_call | solution.py:554
  655.0 1.4 copy-done.4
  656.4 3.9 add_convert_fusion.2.refs_2_.refs_4_
  660.3 4.5 add_convert_fusion.1.refs_1_.refs_0_
  664.8 1.9 copy-done
  666.7 5.8 fusion.9
  673.2 1.6 collective-permute-start.15
  674.8 2.6 collective-permute-done.8
  677.4 1.3 collective-permute-start.14
  678.8 3.5 fusion.4
  682.3 1.6 add_convert_fusion.3.refs_0_
  685.3 2.2 collective-permute-done.9.refs_2_
  688.7 106.1 %shard_map.324 = (f32[256,2048]{1,0:T(8,128)}, f32[8,2048]{1,0:T(8,128)}) custom-call(bf16[1280,1024]{1,0:T(8,128)(2,1)} %collective-permute-done.5.refs_0_.refs_2_, bf16[1024,1024]{1,0:T(8,128)(2,1)} %collective-permute-done.7.refs_1_.refs_6_, bf16[1024,768]{1,0:T(8,128)(2,1)} %copy-done.2, bf16[256,2048]{1,0:T(8,128)(2,1)} %bitcast.65, ...), custom_call_target="tpu_custom_call" | custom-call | flops 1 | bytes 1 | tf_op jit(solution)/shard_map/pallas_call | solution.py:608
  795.6 21.3 %shard_map.325 = (f32[2048,3328]{1,0:T(8,128)}, bf16[256,2048]{1,0:T(8,128)(2,1)}, f32[256,2048]{1,0:T(8,128)}) custom-call(s32[1]{0:T(128)} %bitcast.16.core_ref, bf16[1024,3328]{1,0:T(8,128)(2,1)} %add_convert_fusion.refs_0_, bf16[1024,3328]{1,0:T(8,128)(2,1)} %shard_map.322.refs_1_, bf16[1024,3328]{1,0:T(8,128)(2,1)} %collective-permute-done.2.refs_0_.refs_2_, ...), custom_call_target="tpu_custom_call" | custom-call | flops 1 | bytes 1 | tf_op jit(solution)/shard_map/pallas_call | solution.py:1620
  818.4 2.1 collective-permute-done.10
  821.9 3.0 collective-permute-done.11
  827.9 5.8 shard_map.327
  833.7 13.4 %shard_map.329 = (f32[256,2048]{1,0:T(8,128)}, f32[1024,2048]{1,0:T(8,128)}, f32[2048,1024]{1,0:T(8,128)}) custom-call(s32[1]{0:T(128)} %bitcast.16.core_ref, bf16[1280,1024]{1,0:T(8,128)(2,1)} %add_convert_fusion.1.refs_1_.refs_0_, bf16[1280,1024]{1,0:T(8,128)(2,1)} %get-tuple-element.96.refs_1_, bf16[1280,1024]{1,0:T(8,128)(2,1)} %collective-permute-done.5.refs_0_.refs_2_, ...), custom_call_target="tpu_custom_call" | custom-call | flops 1 | bytes 1 | tf_op jit(solution)/shard_map/pallas_call | solution.py:1620
  (98 shorter events, 21.4 us)
Async XLA Ops:
  4.5 10.4 %copy-start.7 = (f32[2048]{0:T(1024)}, f32[2048]{0:T(1024)S(1)}, u32[]{:S(2)}) copy-start(f32[2048]{0:T(1024)S(1)} %broadcast_in_dim.105) | copy-start | bytes 24580
  5.9 9.7 %copy-start.9 = (f32[2048]{0:T(1024)}, f32[2048]{0:T(1024)S(1)}, u32[]{:S(2)}) copy-start(f32[2048]{0:T(1024)S(1)} %broadcast_in_dim.107) | copy-start | bytes 24580
  8.0 125.8 %copy-start.12 = (f32[2048]{0:T(1024)}, f32[2048]{0:T(1024)S(1)}, u32[]{:S(2)}) copy-start(f32[2048]{0:T(1024)S(1)} %broadcast_in_dim.110) | copy-start | bytes 24580
  234.3 122.7 %copy-start.11 = (s32[1,2048]{1,0:T(1,128)S(1)}, s32[1,2048]{1,0:T(1,128)}, u32[]{:S(2)}) copy-start(s32[1,2048]{1,0:T(1,128)} %param.20) | copy-start | bytes 24580
  393.2 20.7 %collective-permute-start = (bf16[1024,3328]{1,0:T(8,128)(2,1)}, bf16[1024,3328]{1,0:T(8,128)(2,1)}, u32[]{:S(2)}, u32[]{:S(2)}) collective-permute-start(bf16[1024,3328]{1,0:T(8,128)(2,1)} %convolution_convert_fusion), channel_id=1, source_target_pairs={{0,8},{8,0},{16,24},{24,16},{1,9},{9,1},{17,25},{25,17},{2,10},{10... | collective-permute-start | bytes 20447240 | tf_op jit(solution)/shard_map/ppermute | solution.py:1661
  421.9 99.3 %collective-permute-start.2 = (bf16[1024,3328]{1,0:T(8,128)(2,1)}, bf16[1024,3328]{1,0:T(8,128)(2,1)}, u32[]{:S(2)}, u32[]{:S(2)}) collective-permute-start(bf16[1024,3328]{1,0:T(8,128)(2,1)} %add_convert_fusion.refs_0_), channel_id=1, source_target_pairs={{0,8},{8,0},{16,24},{24,16},{1,9},{9,1},{17,25},{25,17},{2,10},{10... | collective-permute-start | bytes 20447240 | tf_op jit(solution)/shard_map/ppermute | solution.py:1671
  422.4 232.4 %collective-permute-start.1 = (bf16[1024,3328]{1,0:T(8,128)(2,1)}, bf16[1024,3328]{1,0:T(8,128)(2,1)}, u32[]{:S(2)}, u32[]{:S(2)}) collective-permute-start(bf16[1024,3328]{1,0:T(8,128)(2,1)} %add_convert_fusion.refs_0_), channel_id=1, source_target_pairs={{0,16},{8,24},{16,0},{24,8},{1,17},{9,25},{17,1},{25,9},{2,18},{10... | collective-permute-start | bytes 20447240 | tf_op jit(solution)/shard_map/ppermute | solution.py:1670
  623.7 36.6 %collective-permute-start.4 = (bf16[1280,1024]{1,0:T(8,128)(2,1)}, bf16[1280,1024]{1,0:T(8,128)(2,1)}, u32[]{:S(2)}, u32[]{:S(2)}) collective-permute-start(bf16[1280,1024]{1,0:T(8,128)(2,1)} %get-tuple-element.81), channel_id=1, source_target_pairs={{0,8},{8,0},{16,24},{24,16},{1,9},{9,1},{17,25},{25,17},{2,10},{10... | collective-permute-start | bytes 7864328 | tf_op jit(solution)/shard_map/ppermute | solution.py:1661
  623.8 31.2 %collective-permute-start.6 = (bf16[1024,1024]{1,0:T(8,128)(2,1)}, bf16[1024,1024]{1,0:T(8,128)(2,1)}, u32[]{:S(2)}, u32[]{:S(2)}) collective-permute-start(bf16[1024,1024]{1,0:T(8,128)(2,1)} %get-tuple-element.83), channel_id=1, source_target_pairs={{0,8},{8,0},{16,24},{24,16},{1,9},{9,1},{17,25},{25,17},{2,10},{10... | collective-permute-start | bytes 6291464 | tf_op jit(solution)/shard_map/ppermute | solution.py:1661
  654.8 1.6 copy-start.4
  654.8 5.5 copy-start.3
  654.8 140.7 %collective-permute-start.3 = (bf16[1024,3328]{1,0:T(8,128)(2,1)}, bf16[1024,3328]{1,0:T(8,128)(2,1)}, u32[]{:S(2)}, u32[]{:S(2)}) collective-permute-start(bf16[1024,3328]{1,0:T(8,128)(2,1)} %shard_map.322.refs_1_), channel_id=1, source_target_pairs={{0,8},{8,0},{16,24},{24,16},{1,9},{9,1},{17,25},{25,17},{2,10},{10... | collective-permute-start | bytes 20447240 | tf_op jit(solution)/shard_map/ppermute | solution.py:1695
  664.8 1.9 copy-start
  666.7 12.1 %copy-start.1 = (bf16[2048,2048]{1,0:T(8,128)(2,1)S(1)}, bf16[2048,2048]{1,0:T(8,128)(2,1)}, u32[]{:S(2)}) copy-start(bf16[2048,2048]{1,0:T(8,128)(2,1)} %shard_map.323) | copy-start | bytes 25165828
  672.5 4.9 collective-permute-start.8
  672.7 11.2 %collective-permute-start.7 = (bf16[1024,1024]{1,0:T(8,128)(2,1)}, bf16[1024,1024]{1,0:T(8,128)(2,1)}, u32[]{:S(2)}, u32[]{:S(2)}) collective-permute-start(bf16[1024,1024]{1,0:T(8,128)(2,1)} %add_convert_fusion.2.refs_2_.refs_4_), channel_id=1, source_target_pairs={{0,8},{8,0},{16,24},{24,16},{1,9},{9,1},{17,25},{25,17},{2,10},{10... | collective-permute-start | bytes 6291464 | tf_op jit(solution)/shard_map/ppermute | solution.py:1671
  673.1 10.9 %collective-permute-start.5 = (bf16[1280,1024]{1,0:T(8,128)(2,1)}, bf16[1280,1024]{1,0:T(8,128)(2,1)}, u32[]{:S(2)}, u32[]{:S(2)}) collective-permute-start(bf16[1280,1024]{1,0:T(8,128)(2,1)} %add_convert_fusion.1.refs_1_.refs_0_), channel_id=1, source_target_pairs={{0,8},{8,0},{16,24},{24,16},{1,9},{9,1},{17,25},{25,17},{2,10},{10... | collective-permute-start | bytes 7864328 | tf_op jit(solution)/shard_map/ppermute | solution.py:1671
  673.2 121.6 %collective-permute-start.15 = (bf16[1024,1024]{1,0:T(8,128)(2,1)}, bf16[1024,1024]{1,0:T(8,128)(2,1)}, u32[]{:S(2)}, u32[]{:S(2)}) collective-permute-start(bf16[1024,1024]{1,0:T(8,128)(2,1)} %add_convert_fusion.2.refs_2_.refs_4_), channel_id=1, source_target_pairs={{0,16},{8,24},{16,0},{24,8},{1,17},{9,25},{17,1},{25,9},{2,18},{10... | collective-permute-start | bytes 6291464 | tf_op jit(solution)/shard_map/ppermute | solution.py:1670
  677.4 117.4 %collective-permute-start.14 = (bf16[1280,1024]{1,0:T(8,128)(2,1)}, bf16[1280,1024]{1,0:T(8,128)(2,1)}, u32[]{:S(2)}, u32[]{:S(2)}) collective-permute-start(bf16[1280,1024]{1,0:T(8,128)(2,1)} %add_convert_fusion.1.refs_1_.refs_0_), channel_id=1, source_target_pairs={{0,16},{8,24},{16,0},{24,8},{1,17},{9,25},{17,1},{25,9},{2,18},{10... | collective-permute-start | bytes 7864328 | tf_op jit(solution)/shard_map/ppermute | solution.py:1670
  682.3 2.4 copy-start.8
  682.3 2.3 copy-start.10
  683.9 3.6 collective-permute-start.9
  684.0 132.9 %collective-permute-start.12 = (bf16[1024,768]{1,0:T(8,128)(2,1)}, bf16[1024,768]{1,0:T(8,128)(2,1)}, u32[]{:S(2)}, u32[]{:S(2)}) collective-permute-start(bf16[1024,768]{1,0:T(8,128)(2,1)} %add_convert_fusion.3.refs_0_), channel_id=1, source_target_pairs={{0,16},{8,24},{16,0},{24,8},{1,17},{9,25},{17,1},{25,9},{2,18},{10... | collective-permute-start | bytes 4718600 | tf_op jit(solution)/shard_map/ppermute | solution.py:1670
  687.5 1.1 copy-start.2
  794.9 38.8 %collective-permute-start.16 = (bf16[1280,1024]{1,0:T(8,128)(2,1)}, bf16[1280,1024]{1,0:T(8,128)(2,1)}, u32[]{:S(2)}, u32[]{:S(2)}) collective-permute-start(bf16[1280,1024]{1,0:T(8,128)(2,1)} %get-tuple-element.96.refs_1_), channel_id=1, source_target_pairs={{0,8},{8,0},{16,24},{24,16},{1,9},{9,1},{17,25},{25,17},{2,10},{10... | collective-permute-start | bytes 7864328 | tf_op jit(solution)/shard_map/ppermute | solution.py:1695
  794.9 38.7 %collective-permute-start.17 = (bf16[1024,1024]{1,0:T(8,128)(2,1)}, bf16[1024,1024]{1,0:T(8,128)(2,1)}, u32[]{:S(2)}, u32[]{:S(2)}) collective-permute-start(bf16[1024,1024]{1,0:T(8,128)(2,1)} %get-tuple-element.97.refs_5_), channel_id=1, source_target_pairs={{0,8},{8,0},{16,24},{24,16},{1,9},{9,1},{17,25},{25,17},{2,10},{10... | collective-permute-start | bytes 6291464 | tf_op jit(solution)/shard_map/ppermute | solution.py:1695
  816.9 0.9 copy-start.6
  816.9 4.4 copy-start.13
  816.9 9.8 %collective-permute-start.13 = (bf16[1024,768]{1,0:T(8,128)(2,1)}, bf16[1024,768]{1,0:T(8,128)(2,1)S(1)}, u32[]{:S(2)}, u32[]{:S(2)}) collective-permute-start(bf16[1024,768]{1,0:T(8,128)(2,1)} %shard_map.326.refs_1_), channel_id=1, source_target_pairs={{0,8},{8,0},{16,24},{24,16},{1,9},{9,1},{17,25},{25,17},{2,10},{10... | collective-permute-start | bytes 4718600 | tf_op jit(solution)/shard_map/ppermute | solution.py:1695
  817.8 2.7 collective-permute-start.10
  820.5 4.3 collective-permute-start.11
  826.7 1.1 copy-start.5
  (1 other events, 0.7 us)
